TPU v7x, 32 devices: a whole 2x2x4 slice. The times are simulated.
32 devices in a mesh: dp: 8 (over y, x, core), fsdp: 4 (over z).
Axes of the slice: x: 2, y: 2, z: 4, core: 2. Of those that a mesh axis runs over, the one named last changes fastest.
Arguments:
- events: bfloat16 [96, 128, 1024], P(('dp', 'fsdp')), may hold values from -6 to 6
- query_weight: bfloat16 [1024, 512], P('fsdp'), may hold values from -0.1875 to 0.1875
- keys: bfloat16 [96, 128, 512], P(('dp', 'fsdp')), may hold values from -6 to 6
- values: bfloat16 [96, 128, 512], P(('dp', 'fsdp')), may hold values from -48 to 48
- gates: bfloat16 [96, 128, 512], P(('dp', 'fsdp')), may hold values from -6 to 6
- cotangent: bfloat16 [96, 128, 512], P(('dp', 'fsdp')), may hold values from -6 to 6
- lengths: int32 [96], replicated, may hold values from 1 to 128, as said below
Outputs:
- grad_keys: bfloat16 [96, 128, 512], P(('dp', 'fsdp'))
- grad_values: bfloat16 [96, 128, 512], P(('dp', 'fsdp'))
- grad_gates: bfloat16 [96, 128, 512], P(('dp', 'fsdp'))
- grad_weight: float32 [1024, 512], P('fsdp')
Inputs may be any that keep to these rules, and one draw needn't show every extreme that they name: Each sequence fills the first lengths[b] events of its slot of 128 events; the rest is padding that no output reads.
All inputs are finite; a program needn't handle non-finite values.
Results may differ from a plain program's by a relative error of at most 0.015.
Values may be sent and summed in bfloat16 or wider, within the bound.
No kernel may reach another device: no remote copies, remote signals or barrier semaphores. Data moves between devices by JAX's collectives and lax.ppermute only.
A program may use at most 64 MiB of HBM per device.

v0:
```python
import math

import jax
import jax.numpy as jnp
from jax import lax
from jax.sharding import PartitionSpec as P

HEADS = 4
BLK = 64


EPSILON = 1e-06


def slot_grads(queries, key_rows, value_rows, gate_rows, upstream_rows, length, head_count):
    row_count = queries.shape[0]
    head_width = queries.shape[1]
    head_depth = head_width // head_count
    score_scale = 1.0 / math.sqrt(head_depth)
    query_h = queries.reshape(row_count, head_count, head_depth)
    keys_h = key_rows.reshape(row_count, head_count, head_depth)
    values_h = value_rows.reshape(row_count, head_count, head_depth)
    scores = (
        jnp.einsum("qhd,khd->hqk", query_h, keys_h, preferred_element_type=jnp.float32)
        * score_scale
    )
    places = lax.iota(jnp.int32, row_count)
    causal = (places[None, :] <= places[:, None]) & (places[:, None] < length)
    weight_mask = causal.astype(jnp.float32)[None]
    inverse = 1.0 / length.astype(jnp.float32)
    sigmoid = jax.nn.sigmoid(scores)
    attention = (scores * sigmoid * weight_mask * inverse).astype(jnp.bfloat16)
    mixed_rows = jnp.einsum(
        "hqk,khd->qhd", attention, values_h, preferred_element_type=jnp.float32
    ).reshape(row_count, head_width)
    centred = mixed_rows - jnp.mean(mixed_rows, axis=1, keepdims=True)
    inv_std = lax.rsqrt(jnp.mean(centred * centred, axis=1, keepdims=True) + EPSILON)
    normed = centred * inv_std
    upstream = upstream_rows.astype(jnp.float32)
    grad_gates = (upstream * normed).astype(jnp.bfloat16)
    valid_rows = (places < length).astype(jnp.float32)[:, None]
    grad_normed = upstream * gate_rows.astype(jnp.float32) * valid_rows
    grad_mixed = inv_std * (
        grad_normed
        - jnp.mean(grad_normed, axis=1, keepdims=True)
        - normed * jnp.mean(grad_normed * normed, axis=1, keepdims=True)
    )
    grad_mixed = grad_mixed.astype(jnp.bfloat16).reshape(row_count, head_count, head_depth)
    grad_values = jnp.einsum(
        "hqk,qhd->khd", attention, grad_mixed, preferred_element_type=jnp.float32
    )
    grad_attention = jnp.einsum(
        "qhd,khd->hqk", grad_mixed, values_h, preferred_element_type=jnp.float32
    )
    grad_scores = (
        grad_attention * sigmoid * (1.0 + scores * (1.0 - sigmoid)) * weight_mask * inverse
    ).astype(jnp.bfloat16)
    grad_query = (
        jnp.einsum("hqk,khd->qhd", grad_scores, keys_h, preferred_element_type=jnp.float32)
        * score_scale
    )
    grad_keys = (
        jnp.einsum("hqk,qhd->khd", grad_scores, query_h, preferred_element_type=jnp.float32)
        * score_scale
    )
    return (
        grad_query.reshape(row_count, head_width).astype(jnp.bfloat16),
        grad_keys.reshape(row_count, head_width).astype(jnp.bfloat16),
        grad_values.reshape(row_count, head_width).astype(jnp.bfloat16),
        grad_gates,
    )


def prefix_branch(row_count, slot_span):

    def run_prefix(operands):
        queries, key_rows, value_rows, gate_rows, upstream_rows, length = operands
        if row_count == 0:
            empty = jnp.zeros((slot_span, queries.shape[1]), jnp.bfloat16)
            return (empty, empty, empty, empty)
        results = slot_grads(
            queries[:row_count],
            key_rows[:row_count],
            value_rows[:row_count],
            gate_rows[:row_count],
            upstream_rows[:row_count],
            length,
            HEADS,
        )
        return tuple((jnp.pad(result, ((0, slot_span - row_count), (0, 0))) for result in results))

    return run_prefix


def attend(operands):
    slot_span = operands[0].shape[0]
    block_count = slot_span // BLK
    live_blocks = jnp.minimum((operands[5] + BLK - 1) // BLK, block_count)
    branches = [prefix_branch(blocks * BLK, slot_span) for blocks in range(block_count + 1)]
    return lax.switch(live_blocks, branches, operands)


def shards(events, query_weight, keys, values, gates, cotangent, lengths):
    slot_count, slot_span, model_width = events.shape
    head_width = query_weight.shape[1]
    flat_events = events.reshape(slot_count * slot_span, model_width)
    columns = flat_events
    queries = jnp.dot(
        columns,
        lax.all_gather(query_weight, "fsdp", axis=0, tiled=True),
        preferred_element_type=jnp.float32,
    )
    queries = queries.astype(jnp.bfloat16).reshape(slot_count, slot_span, head_width)
    dp_count = lax.axis_size("dp")
    fsdp_count = lax.axis_size("fsdp")
    dp_place = lax.axis_index("dp")
    fsdp_place = lax.axis_index("fsdp")
    device_row = dp_place * fsdp_count + fsdp_place
    own_lengths = lax.dynamic_slice_in_dim(lengths, device_row * slot_count, slot_count)
    operands = (queries, keys, values, gates, cotangent)
    merged = lax.map(attend, operands + (own_lengths,))
    grad_query, grad_keys, grad_values, grad_gates = merged
    grad_flat = grad_query.reshape(slot_count * slot_span, head_width)
    total_seqs = slot_count * dp_count * fsdp_count
    contract = (((0,), (0,)), ((), ()))
    columns = flat_events
    shard_rows = lax.psum_scatter(
        lax.dot_general(columns, grad_flat, contract, preferred_element_type=jnp.float32),
        "fsdp",
        scatter_dimension=0,
        tiled=True,
    )
    summed = lax.psum(shard_rows, "dp")
    return (grad_keys, grad_values, grad_gates, summed / total_seqs)


def solution(mesh):
    in_specs = (
        P(("dp", "fsdp"), None, None),
        P("fsdp", None),
        P(("dp", "fsdp"), None, None),
        P(("dp", "fsdp"), None, None),
        P(("dp", "fsdp"), None, None),
        P(("dp", "fsdp"), None, None),
        P(),
    )
    out_specs = (
        P(("dp", "fsdp"), None, None),
        P(("dp", "fsdp"), None, None),
        P(("dp", "fsdp"), None, None),
        P("fsdp", None),
    )
    return jax.shard_map(shards, mesh=mesh, in_specs=in_specs, out_specs=out_specs, check_vma=False)
```

profile of v0, /device:TPU:0, one launch (start us, length us, event | category | flops | bytes accessed | tf_op | source)
XLA Modules:
  0.0 188.6 jit_solution(6257932496541887362)
XLA Ops:
  7.2 0.7 all-gather.2.cloned.1.call-update
  8.0 0.7 dynamic_slice.65
  8.8 31.5 %all-gather.2.cloned.1.call-done = bf16[1024,512]{1,0:T(8,128)(2,1)} async-done(((bf16[256,512]{1,0:T(8,128)(2,1)}), bf16[1024,512]{1,0:T(8,128)(2,1)}) %all-gather.2.cloned.1.call-update) | async-done | bytes 1048592 | tf_op jit(solution)/shard_map/all_gather | solution.py:110
  40.3 1.8 convolution_convert_fusion.2
  42.1 23.8 %while.21 = (s32[]{:T(128)}, bf16[3,128,512]{2,1,0:T(8,128)(2,1)}, bf16[3,128,512]{2,1,0:T(8,128)(2,1)}, bf16[3,128,512]{2,1,0:T(8,128)(2,1)}, bf16[3,128,512]{2...) while((s32[]{:T(128)}, bf16[3,128,512]{2,1,0:T(8,128)(2,1)}, ...), condition=%wide.region_12.13_spmd, body=%wide.region_0.12_spmd.sunk | while | flops 103989648 | bytes 11088631 | solution.py:121
  42.1 0.6 dynamic_slice.117
  43.4 5.2 %conditional.2 = (bf16[1,128,512]{2,1,0:T(8,128)(2,1)S(1)}, bf16[1,128,512]{2,1,0:T(8,128)(2,1)S(1)}, bf16[1,128,512]{2,1,0:T(8,128)(2,1)S(1)}, bf16[1,128,512]{2,1,0:T(8,128)(2,1)S(1)}) conditional(s32[]{:T(128)} %clamp.11, () %tuple.99, (bf16[3,128,512]{2,1,0:T(8,128)(2,1)S(1)}, bf16[3,128,512]{2,1,0:T(8,128)(2,1)S(1)}, ...), branch_computations={%region_1.1_spmd, %region_2.6_spmd.clone.clone, %region_7.11_spmd.... | conditional | flops 103989632 | bytes 10038608 | solution.py:100
  44.1 0.6 iota_compare_fusion.1
  45.1 0.2 fusion.47
  45.6 1.1 fusion.14
  46.7 1.0 fusion.10
  48.6 0.7 constant_dynamic-update-slice_fusion.6
  49.3 0.7 constant_dynamic-update-slice_fusion.7
  50.0 0.6 dynamic_slice.117
  51.3 5.2 %conditional.2 = (bf16[1,128,512]{2,1,0:T(8,128)(2,1)S(1)}, bf16[1,128,512]{2,1,0:T(8,128)(2,1)S(1)}, bf16[1,128,512]{2,1,0:T(8,128)(2,1)S(1)}, bf16[1,128,512]{2,1,0:T(8,128)(2,1)S(1)}) conditional(s32[]{:T(128)} %clamp.11, () %tuple.99, (bf16[3,128,512]{2,1,0:T(8,128)(2,1)S(1)}, bf16[3,128,512]{2,1,0:T(8,128)(2,1)S(1)}, ...), branch_computations={%region_1.1_spmd, %region_2.6_spmd.clone.clone, %region_7.11_spmd.... | conditional | flops 103989632 | bytes 10038608 | solution.py:100
  52.0 0.6 iota_compare_fusion.1
  53.5 1.1 fusion.14
  54.6 1.0 fusion.10
  56.5 0.7 constant_dynamic-update-slice_fusion.6
  57.2 0.7 constant_dynamic-update-slice_fusion.7
  58.0 0.6 dynamic_slice.117
  59.2 5.2 %conditional.2 = (bf16[1,128,512]{2,1,0:T(8,128)(2,1)S(1)}, bf16[1,128,512]{2,1,0:T(8,128)(2,1)S(1)}, bf16[1,128,512]{2,1,0:T(8,128)(2,1)S(1)}, bf16[1,128,512]{2,1,0:T(8,128)(2,1)S(1)}) conditional(s32[]{:T(128)} %clamp.11, () %tuple.99, (bf16[3,128,512]{2,1,0:T(8,128)(2,1)S(1)}, bf16[3,128,512]{2,1,0:T(8,128)(2,1)S(1)}, ...), branch_computations={%region_1.1_spmd, %region_2.6_spmd.clone.clone, %region_7.11_spmd.... | conditional | flops 103989632 | bytes 10038608 | solution.py:100
  59.9 0.6 iota_compare_fusion.1
  61.4 1.1 fusion.14
  62.5 1.0 fusion.10
  64.4 0.7 constant_dynamic-update-slice_fusion.6
  65.2 0.7 constant_dynamic-update-slice_fusion.7
  65.9 3.1 %convolution_bitcast_fusion = f32[1024,512]{0,1:T(8,128)} fusion(bf16[3,128,512]{2,1,0:T(8,128)(2,1)} %get-tuple-element.326, bf16[3,128,1024]{2,1,0:T(8,128)(2,1)S(1)} %copy-done), kind=kOutput, calls=%fused_computation.104 | convolution fusion | flops 402653184 | bytes 3276800 | tf_op jit(solution)/shard_map/dot_general | solution.py:128
  69.0 53.7 %reduce-scatter.2.cloned.1.call-done = f32[256,512]{0,1:T(8,128)} async-done(((f32[1024,512]{0,1:T(8,128)}), f32[256,512]{0,1:T(8,128)}) %reduce-scatter.2.cloned.1.call-update) | async-done | bytes 524304 | tf_op jit(solution)/shard_map/reduce_scatter | solution.py:127
  122.7 57.3 %all-reduce.6.cloned.1.call-done = f32[256,512]{0,1:T(8,128)} async-done(((f32[256,512]{0,1:T(8,128)}), f32[256,512]{0,1:T(8,128)}) %all-reduce.6.cloned.1.call-update) | async-done | bytes 524304 | tf_op jit(solution)/shard_map/psum | solution.py:133
  180.0 1.1 broadcast_multiply_fusion.6
  181.1 1.0 copy.58
  (86 shorter events, 4.8 us)
Async XLA Ops:
  7.2 33.1 %copy-start = (bf16[3,128,1024]{2,1,0:T(8,128)(2,1)S(1)}, bf16[3,128,1024]{2,1,0:T(8,128)(2,1)}, u32[]{:S(2)}) copy-start(bf16[3,128,1024]{2,1,0:T(8,128)(2,1)} %param.12) | copy-start | bytes 2359300
  7.2 34.9 %copy-start.2 = (bf16[3,128,512]{2,1,0:T(8,128)(2,1)S(1)}, bf16[3,128,512]{2,1,0:T(8,128)(2,1)}, u32[]{:S(2)}) copy-start(bf16[3,128,512]{2,1,0:T(8,128)(2,1)} %param.15) | copy-start | bytes 1179652
  7.2 34.9 %copy-start.1 = (bf16[3,128,512]{2,1,0:T(8,128)(2,1)S(1)}, bf16[3,128,512]{2,1,0:T(8,128)(2,1)}, u32[]{:S(2)}) copy-start(bf16[3,128,512]{2,1,0:T(8,128)(2,1)} %param.14) | copy-start | bytes 1179652
  7.2 33.1 %all-gather.2.cloned.1.call-start = ((), (), s32[]{:S(2)}) async-start(), calls=%async_computation.1 | async-start | bytes 1310720 | tf_op jit(solution)/shard_map/all_gather | solution.py:110
  7.9 114.8 %reduce-scatter.2.cloned.1.call-start = ((), (), s32[]{:S(2)}) async-start(), calls=%async_computation.2 | async-start | bytes 2621440 | tf_op jit(solution)/shard_map/reduce_scatter | solution.py:127
  69.0 111.0 %all-reduce.6.cloned.1.call-start = ((), (), s32[]{:S(2)}) async-start(), calls=%async_computation.3 | async-start | bytes 1048576 | tf_op jit(solution)/shard_map/psum | solution.py:133
Sparse Core Ops, SparseCore 0:
  9.6 30.6 all-gather.1
  69.1 53.5 reduce-scatter.1
  126.1 53.8 all-reduce.5
where the time goes:
time: 189 us
  waiting for transfers between devices  143 us (76%)
  between operations  13.8 us (7%)
  other arithmetic  10.1 us (5%)
  local copies, waits for them, and re-layouts  8.38 us (4%)
  matrix products  8.38 us (4%)
  loops' own time  4.64 us (2%)
    psum x1, waiting for transfers between devices, shards(): summed = lax.psum(shard_rows, 'dp')  57.3 us
    reduce_scatter x1, waiting for transfers between devices, shards(): lax.psum_scatter(lax.dot_general(columns, grad_flat, contract, preferred_...  53.7 us
    all_gather x1, waiting for transfers between devices, shards(): lax.all_gather(query_weight, 'fsdp', axis=0, tiled=True)  31.5 us
    dynamic_update_slice x6, local copies, waits for them, and re-layouts, shards(): merged = lax.map(attend, operands + (own_lengths,))  4.31 us
  transfers between devices with their start and end apart: 3, of which 3 were waited for; matrix products, arithmetic and copies ran while one was open for 0% of the time, Pallas kernels for 0%

commit v1 on v0

v1 whole, which is shorter than its diff:
```python
import functools
import math

import jax
import jax.numpy as jnp
from jax import lax
from jax.experimental import pallas as pl
from jax.experimental.pallas import tpu as pltpu
from jax.sharding import PartitionSpec as P

HEADS = 4
EPSILON = 1e-06
CORES = 2
BOTH = ("dp", "fsdp")
VMEM_LIMIT = 24 * 1024 * 1024

LAST = (((1,), (1,)), ((), ()))
FIRST = (((0,), (0,)), ((), ()))


def dot(lhs, rhs, dims=(((1,), (0,)), ((), ()))):
    return lax.dot_general(lhs, rhs, dims, preferred_element_type=jnp.float32)


def vmem():
    return pl.BlockSpec(memory_space=pltpu.VMEM)


def params():
    return pltpu.CompilerParams(vmem_limit_bytes=VMEM_LIMIT)


def cost(flops, bytes_accessed):
    return pl.CostEstimate(flops=flops, bytes_accessed=bytes_accessed, transcendentals=0)


def transpose_kernel(own_ref, sibling_ref, out_ref):
    rows = own_ref.shape[0]
    out_ref[:, :rows] = own_ref[...].T
    out_ref[:, rows:] = sibling_ref[...].T


def attend_slot(slot, span, length, query_ref, key_ref, value_ref, gate_ref, upstream_ref,
                grad_key_ref, grad_value_ref, grad_gate_ref, halves_ref):
    width = key_ref.shape[1]
    depth = width // HEADS
    scale = 1.0 / math.sqrt(depth)
    rows = slice(slot * span, (slot + 1) * span)
    columns = [slice(h * depth, (h + 1) * depth) for h in range(HEADS)]
    row = lax.broadcasted_iota(jnp.int32, (span, span), 0)
    column = lax.broadcasted_iota(jnp.int32, (span, span), 1)
    inverse = 1.0 / jnp.full((span, span), length, jnp.int32).astype(jnp.float32)
    weight = jnp.where((column <= row) & (row < length), inverse, 0.0)
    live = lax.broadcasted_iota(jnp.int32, (span, 1), 0) < length

    attention, slopes, mixed = [], [], []
    for h in range(HEADS):
        scores = dot(query_ref[rows, columns[h]], key_ref[rows, columns[h]], LAST) * scale
        sigmoid = 0.5 * jnp.tanh(0.5 * scores) + 0.5
        silu = scores * sigmoid
        attention.append((silu * weight).astype(jnp.bfloat16))
        slopes.append((sigmoid + silu * (1.0 - sigmoid)) * weight)
        mixed.append(dot(attention[h], value_ref[rows, columns[h]]))

    mean = sum(jnp.sum(m, axis=1, keepdims=True) for m in mixed) / width
    centred = [m - mean for m in mixed]
    var = sum(jnp.sum(c * c, axis=1, keepdims=True) for c in centred) / width
    inv_std = lax.rsqrt(var + EPSILON)
    normed = [c * inv_std for c in centred]
    grad_normed = []
    for h in range(HEADS):
        upstream = upstream_ref[rows, columns[h]].astype(jnp.float32)
        grad_gate_ref[rows, columns[h]] = (upstream * normed[h]).astype(jnp.bfloat16)
        gated = upstream * gate_ref[rows, columns[h]].astype(jnp.float32)
        grad_normed.append(jnp.where(live, gated, 0.0))
    first = sum(jnp.sum(g, axis=1, keepdims=True) for g in grad_normed) / width
    second = sum(
        jnp.sum(g * n, axis=1, keepdims=True) for g, n in zip(grad_normed, normed)
    ) / width

    for h in range(HEADS):
        grad_mixed = (inv_std * (grad_normed[h] - first - normed[h] * second)).astype(jnp.bfloat16)
        grad_value_ref[rows, columns[h]] = dot(attention[h], grad_mixed, FIRST).astype(jnp.bfloat16)
        grad_attention = dot(grad_mixed, value_ref[rows, columns[h]], LAST)
        grad_scores = (grad_attention * slopes[h]).astype(jnp.bfloat16)
        grad_query = dot(grad_scores, key_ref[rows, columns[h]]) * scale
        per_half = HEADS // CORES
        place = slice((h % per_half) * depth, (h % per_half + 1) * depth)
        halves_ref[h // per_half, rows, place] = grad_query.astype(jnp.bfloat16)
        grad_key = dot(grad_scores, query_ref[rows, columns[h]], FIRST) * scale
        grad_key_ref[rows, columns[h]] = grad_key.astype(jnp.bfloat16)


def attention_kernel(slots, piece_count, *refs):
    starts_ref, lengths_ref = refs[:2]
    pieces = refs[2 : 2 + piece_count]
    (events_ref, key_ref, value_ref, gate_ref, upstream_ref, grad_key_ref, grad_value_ref,
     grad_gate_ref, keep_ref, send_ref, weight_ref, query_ref, halves_ref, sems) = refs[2 + piece_count :]
    copies = []
    for p, piece in enumerate(pieces):
        rows = piece.shape[0]
        start = pl.multiple_of(starts_ref[p], 16)
        copy = pltpu.make_async_copy(piece, weight_ref.at[pl.ds(start, rows)], sems.at[p])
        copy.start()
        copies.append(copy)
    for copy in copies:
        copy.wait()
    query_ref[...] = dot(events_ref[...], weight_ref[...]).astype(jnp.bfloat16)
    span = key_ref.shape[0] // slots
    for slot in range(slots):
        attend_slot(slot, span, lengths_ref[slot], query_ref, key_ref, value_ref, gate_ref,
                    upstream_ref, grad_key_ref, grad_value_ref, grad_gate_ref, halves_ref)
    core = starts_ref[piece_count]
    keep_ref[...] = halves_ref[core]
    send_ref[...] = halves_ref[1 - core]


def gradient_kernel(shards, chips, place_ref, events_ref, keep_ref, got_ref, *refs):
    outs, both_ref, total_ref = refs[:chips], refs[chips], refs[chips + 1]
    rows = keep_ref.shape[0]
    both_ref[:rows] = keep_ref[...]
    both_ref[rows:] = got_ref[...]
    total_ref[...] = dot(events_ref[...], both_ref[...]).reshape(total_ref.shape)
    for k, out in enumerate(outs):
        chip = lax.rem(place_ref[0] + k, chips)
        for s in range(shards):
            out[s] = total_ref[s, chip].astype(out.dtype)


def shard_sum_kernel(shards, place_ref, *refs):
    terms, outs = refs[: len(refs) - shards], refs[len(refs) - shards :]
    for k, out in enumerate(outs):
        shard = lax.rem(place_ref[0] + k, shards)
        total = terms[0][shard].astype(jnp.float32)
        for term in terms[1:]:
            total = total + term[shard].astype(jnp.float32)
        out[...] = total.astype(out.dtype)


def mean_kernel(count, *refs):
    total = refs[0][...].astype(jnp.float32)
    for term in refs[1:-1]:
        total = total + term[...].astype(jnp.float32)
    refs[-1][...] = (total / count).astype(refs[-1].dtype)


def place_kernel(dp_count, place_ref, *refs):
    out = refs[-1]
    rows, columns = refs[0].shape
    for k, piece in enumerate(refs[:-1]):
        source = lax.rem(place_ref[0] + dp_count - k, dp_count)
        row = pl.multiple_of((source // CORES) * rows, 16)
        column = pl.multiple_of((source % CORES) * columns, 128)
        out[pl.ds(row, rows), pl.ds(column, columns)] = piece[...].astype(out.dtype)


def gather_weight(weight, dp_count, fsdp_count, sibling):
    core = lax.axis_index("dp") % CORES
    here = lax.axis_index("fsdp")
    rows = weight.shape[0]
    pieces, starts = [weight], [here * rows]

    def move(block, forward, backward):
        perm = []
        for d in range(dp_count):
            step = forward if d % CORES == 0 else backward
            for z in range(fsdp_count):
                perm.append((d * fsdp_count + z, d * fsdp_count + (z + step) % fsdp_count))
        return lax.ppermute(block, BOTH, perm)

    for step in range(1, (fsdp_count + 1) // 2):
        got = move(weight, step, fsdp_count - step)
        source = jnp.where(core == 0, here - step, here + step) % fsdp_count
        other = jnp.where(core == 0, here + step, here - step) % fsdp_count
        pieces += [got, sibling(got)]
        starts += [source * rows, other * rows]
    if fsdp_count % 2 == 0:
        step, half = fsdp_count // 2, rows // CORES
        got = move(lax.dynamic_slice_in_dim(weight, core * half, half), step, step)
        source = (here + step) % fsdp_count * rows
        pieces += [got, sibling(got)]
        starts += [source + core * half, source + (1 - core) * half]
    return pieces, starts


def shards(events, query_weight, keys, values, gates, cotangent, lengths):
    slots, span, model_width = events.shape
    width = query_weight.shape[1]
    half_width = width // CORES
    rows = slots * span
    dp_count, fsdp_count = lax.axis_size("dp"), lax.axis_size("fsdp")
    dp_place, fsdp_place = lax.axis_index("dp"), lax.axis_index("fsdp")
    core, chip, chips = dp_place % CORES, dp_place // CORES, dp_count // CORES
    shard_rows = model_width // fsdp_count
    total_seqs = slots * dp_count * fsdp_count
    bf16, f32 = jnp.bfloat16, jnp.float32
    smem = pl.BlockSpec(memory_space=pltpu.SMEM)

    def sibling(block):
        return lax.ppermute(block, "dp", [(d, d ^ 1) for d in range(dp_count)])

    flat_events = events.reshape(rows, model_width)
    pieces, starts = gather_weight(query_weight, dp_count, fsdp_count, sibling)
    events_t = pl.pallas_call(
        transpose_kernel,
        out_shape=jax.ShapeDtypeStruct((model_width, CORES * rows), bf16),
        in_specs=[vmem(), vmem()],
        out_specs=vmem(),
        compiler_params=params(),
        cost_estimate=cost(0, 8 * rows * model_width),
        name="events_transposed",
    )(flat_events, sibling(flat_events))

    device = dp_place * fsdp_count + fsdp_place
    own_lengths = lax.dynamic_slice_in_dim(lengths, device * slots, slots)
    own = [a.reshape(rows, width) for a in (keys, values, gates, cotangent)]
    wide = jax.ShapeDtypeStruct((rows, width), bf16)
    half = jax.ShapeDtypeStruct((rows, half_width), bf16)
    piece_count = len(pieces)
    grad_keys, grad_values, grad_gates, keep, send = pl.pallas_call(
        functools.partial(attention_kernel, slots, piece_count),
        out_shape=(wide, wide, wide, half, half),
        in_specs=[smem, smem] + [pl.BlockSpec(memory_space=pl.ANY)] * piece_count + [vmem()] * 5,
        out_specs=(vmem(),) * 5,
        scratch_shapes=[
            pltpu.VMEM((model_width, width), bf16),
            pltpu.VMEM((rows, width), bf16),
            pltpu.VMEM((CORES, rows, half_width), bf16),
            pltpu.SemaphoreType.DMA((piece_count,)),
        ],
        compiler_params=params(),
        cost_estimate=cost(2 * rows * width * (model_width + 5 * span), 12 * rows * width * 2),
        name="attention_both_ways",
    )(jnp.stack(starts + [core]).astype(jnp.int32), own_lengths, *pieces, flat_events, *own)
    got = sibling(send)

    piece_rows = shard_rows // chips
    staged = piece_rows % 16 == 0
    parts = chips if staged else 1
    part_rows = shard_rows // parts
    first_type = f32
    terms = pl.pallas_call(
        functools.partial(gradient_kernel, fsdp_count, parts),
        out_shape=tuple(
            jax.ShapeDtypeStruct((fsdp_count, part_rows, half_width), bf16 if k else first_type)
            for k in range(parts)
        ),
        in_specs=[smem] + [vmem()] * 3,
        out_specs=(vmem(),) * parts,
        scratch_shapes=[
            pltpu.VMEM((CORES * rows, half_width), bf16),
            pltpu.VMEM((fsdp_count, parts, part_rows, half_width), f32),
        ],
        compiler_params=params(),
        cost_estimate=cost(
            4 * rows * model_width * half_width, 2 * model_width * (2 * rows + half_width)
        ),
        name="weight_gradient",
    )(jnp.reshape(chip if staged else 0 * chip, (1,)), events_t, keep, got)

    if not staged:
        own_half = terms[0].reshape(model_width, half_width)
        whole = lax.dynamic_update_slice_in_dim(
            jnp.zeros((model_width, width), f32), own_half, core * half_width, axis=1
        )
        mine = lax.psum_scatter(whole, "fsdp", scatter_dimension=0, tiled=True)
        grad_weight = lax.psum(mine, "dp") / total_seqs
    else:
        terms = [terms[0]] + [
            lax.ppermute(
                terms[k],
                "dp",
                [
                    (c * CORES + e, (c + k) % chips * CORES + e)
                    for c in range(chips)
                    for e in range(CORES)
                ],
            )
            for k in range(1, chips)
        ]
        block = (part_rows, half_width)
        sums = pl.pallas_call(
            functools.partial(shard_sum_kernel, fsdp_count),
            out_shape=tuple(
                jax.ShapeDtypeStruct(block, bf16 if k else f32) for k in range(fsdp_count)
            ),
            in_specs=[smem] + [vmem()] * len(terms),
            out_specs=(vmem(),) * fsdp_count,
            compiler_params=params(),
            name="sum_over_chips",
        )(jnp.reshape(fsdp_place, (1,)), *terms)
        sums = [sums[0]] + [
            lax.ppermute(sums[k], "fsdp", [(z, (z + k) % fsdp_count) for z in range(fsdp_count)])
            for k in range(1, fsdp_count)
        ]
        mean = pl.pallas_call(
            functools.partial(mean_kernel, total_seqs),
            out_shape=jax.ShapeDtypeStruct(block, bf16),
            in_specs=[vmem()] * len(sums),
            out_specs=vmem(),
            compiler_params=params(),
            name="mean_over_shards",
        )(*sums)
        blocks = [mean] + [
            lax.ppermute(mean, "dp", [(d, (d + k) % dp_count) for d in range(dp_count)])
            for k in range(1, dp_count)
        ]
        grad_weight = pl.pallas_call(
            functools.partial(place_kernel, dp_count),
            out_shape=jax.ShapeDtypeStruct((shard_rows, width), f32),
            in_specs=[smem] + [vmem()] * len(blocks),
            out_specs=vmem(),
            compiler_params=params(),
            name="blocks_in_place",
        )(jnp.reshape(dp_place, (1,)), *blocks)

    shape = (slots, span, width)
    return (
        grad_keys.reshape(shape),
        grad_values.reshape(shape),
        grad_gates.reshape(shape),
        grad_weight,
    )


def solution(mesh):
    split = P(BOTH, None, None)
    return jax.shard_map(
        shards,
        mesh=mesh,
        in_specs=(split, P("fsdp", None), split, split, split, split, P()),
        out_specs=(split, split, split, P("fsdp", None)),
        check_vma=False,
    )
```

time: 189 us -> 63.5 us (0.34)
  waiting for transfers between devices: 143 us -> 23.3 us
  starting transfers between devices: 0.12 us -> 21.6 us
  between operations: 13.8 us -> 0.7 us
  other arithmetic: 10.1 us -> 0 us
  Pallas kernels: 0 us -> 9.81 us
  matrix products: 8.38 us -> 0 us
  loops' own time: 4.64 us -> 0 us
    psum x1 -> x0, waiting for transfers between devices: 57.3 us -> none  [shards(): summed = lax.psum(shard_rows, 'dp')]
    reduce_scatter x1 -> x0, waiting for transfers between devices: 53.7 us -> none  [shards(): lax.psum_scatter(lax.dot_general(columns, grad_flat, contract, preferred_...]
    all_gather x1 -> x0, waiting for transfers between devices: 31.5 us -> none  [shards(): lax.all_gather(query_weight, 'fsdp', axis=0, tiled=True)]
    ppermute x0 -> x19, waiting for transfers between devices: none -> 23.3 us  [the longest x2 9.51 us: move(): return lax.ppermute(block, BOTH, perm)]
    ppermute x0 -> x19, starting transfers between devices: none -> 21.6 us  [the longest x7 5.94 us: shards(): lax.ppermute(mean, 'dp', [(d, (d + k) % dp_count) for d in range(dp_count)])]
    pallas_call x0 -> x6, Pallas kernels: none -> 9.81 us  [the longest x1 7.73 us: shards(): pl.pallas_call(functools.partial(attention_kernel, slots, piece_count), o...]
    dot_general x20 -> x0, matrix products: 8.38 us -> none  [the longest x1 3.08 us: shards(): lax.dot_general(columns, grad_flat, contract, preferred_element_type=jnp....]
    unnamed x7 -> x14, local copies, waits for them, and re-layouts: 1.01 us -> 6.07 us
  transfers between devices with their start and end apart: 3 -> 19, of which waited for: 3 -> 13; matrix products, arithmetic and copies ran while one was open for 0% -> 3% of each run, Pallas kernels for 0% -> 13%
where the time goes in v1:
time: 63.5 us; the launch traced here: 63.1 us
  waiting for transfers between devices  23.3 us (37%)
  starting transfers between devices  21.6 us (34%)
  Pallas kernels  9.81 us (15%)
  local copies, waits for them, and re-layouts  7.82 us (12%)
  between operations  0.7 us (1%)
    ppermute x2, waiting for transfers between devices, move(): return lax.ppermute(block, BOTH, perm)  9.51 us
    pallas_call x1, Pallas kernels, shards(): pl.pallas_call(functools.partial(attention_kernel, slots, piece_count), o...  7.73 us
    unnamed x14, local copies, waits for them, and re-layouts  6.07 us
    ppermute x7, starting transfers between devices, shards(): lax.ppermute(mean, 'dp', [(d, (d + k) % dp_count) for d in range(dp_count)])  5.94 us
    ppermute x2, starting transfers between devices, move(): return lax.ppermute(block, BOTH, perm)  5.29 us
    ppermute x3, waiting for transfers between devices, shards(): lax.ppermute(terms[k], 'dp', [(c * CORES + e, (c + k) % chips * CORES + e...  5.11 us
    ppermute x3, starting transfers between devices, shards(): lax.ppermute(terms[k], 'dp', [(c * CORES + e, (c + k) % chips * CORES + e...  4.51 us
    ppermute x3, starting transfers between devices, shards(): lax.ppermute(sums[k], 'fsdp', [(z, (z + k) % fsdp_count) for z in range(f...  4.24 us
  transfers between devices with their start and end apart: 19, of which 13 were waited for; matrix products, arithmetic and copies ran while one was open for 3% of the time, Pallas kernels for 13%

profile of v1, /device:TPU:0, one launch (start us, length us, event | category | flops | bytes accessed | tf_op | source)
XLA Modules:
  0.0 63.1 jit_solution(9286755513854058239)
XLA Ops:
  1.1 2.6 %collective-permute-start = (bf16[256,512]{1,0:T(8,128)(2,1)}, bf16[256,512]{1,0:T(8,128)(2,1)S(1)}, u32[]{:S(2)}, u32[]{:S(2)}) collective-permute-start(bf16[256,512]{1,0:T(8,128)(2,1)} %refs_2_.1), channel_id=1, source_target_pairs={{0,1},{1,2},{2,3},{3,0},{4,7},{5,4},{6,5},{7,6},{8,9},{9,10},{10,1... | collective-permute-start | bytes 786440 | tf_op jit(solution)/shard_map/ppermute | solution.py:169
  3.8 0.9 %constant_dynamic-slice_fusion = bf16[128,512]{1,0:T(8,128)(2,1)S(1)} fusion(bf16[256,512]{1,0:T(8,128)(2,1)} %refs_2_.1, s32[]{:T(128)S(6)} %select_n.44), kind=kLoop, calls=%fused_computation | loop fusion | bytes 262148 | tf_op jit(solution)/shard_map/dynamic_slice | solution.py:179
  4.7 2.7 %collective-permute-start.2 = (bf16[128,512]{1,0:T(8,128)(2,1)S(1)}, bf16[128,512]{1,0:T(8,128)(2,1)S(1)}, u32[]{:S(2)}, u32[]{:S(2)}) collective-permute-start(bf16[128,512]{1,0:T(8,128)(2,1)S(1)} %constant_dynamic-slice_fusion), channel_id=1, source_target_pairs={{0,2},{1,3},{2,0},{3,1},{4,6},{5,7},{6,4},{7,5},{8,10},{9,11},{10,... | collective-permute-start | bytes 393224 | tf_op jit(solution)/shard_map/ppermute | solution.py:169
  7.4 5.9 %collective-permute-done.refs_3_ = bf16[256,512]{1,0:T(8,128)(2,1)S(1)} collective-permute-done((bf16[256,512]{1,0:T(8,128)(2,1)}, bf16[256,512]{1,0:T(8,128)(2,1)S(1)}, u32[]{:S(2)}, u32[]{:S(2)}) %collective-permute-start) | collective-permute-done | bytes 262176 | tf_op jit(solution)/shard_map/ppermute | solution.py:169
  13.3 3.6 %collective-permute-done.2.refs_5_ = bf16[128,512]{1,0:T(8,128)(2,1)S(1)} collective-permute-done((bf16[128,512]{1,0:T(8,128)(2,1)S(1)}, bf16[128,512]{1,0:T(8,128)(2,1)S(1)}, u32[]{:S(2)}, u32[]{:S(2)}) %collective-permute-start.2) | collective-permute-done | bytes 131104 | tf_op jit(solution)/shard_map/ppermute | solution.py:169
  16.9 0.6 collective-permute-start.3
  17.5 0.7 %dynamic_slice.6.refs_1_ = s32[3]{0:T(128)S(1)} dynamic-slice(s32[96]{0:T(128)} %param.13, s32[]{:T(128)S(6)} %select_n.43), dynamic_slice_sizes={3} | dynamic-slice | bytes 28 | tf_op jit(solution)/shard_map/dynamic_slice | solution.py:215
  18.5 1.1 %copy-done = bf16[3,128,1024]{2,1,0:T(8,128)(2,1)S(1)} copy-done((bf16[3,128,1024]{2,1,0:T(8,128)(2,1)S(1)}, bf16[3,128,1024]{2,1,0:T(8,128)(2,1)}, u32[]{:S(2)}) %copy-start) | copy-done | bytes 786456
  19.7 0.9 %copy-done.2 = bf16[256,512]{1,0:T(8,128)(2,1)S(1)} copy-done((bf16[256,512]{1,0:T(8,128)(2,1)S(1)}, bf16[256,512]{1,0:T(8,128)(2,1)}, u32[]{:S(2)}) %copy-start.2) | copy-done | bytes 262168
  20.6 1.0 %copy-done.3 = bf16[3,128,512]{2,1,0:T(8,128)(2,1)S(1)} copy-done((bf16[3,128,512]{2,1,0:T(8,128)(2,1)S(1)}, bf16[3,128,512]{2,1,0:T(8,128)(2,1)}, u32[]{:S(2)}) %copy-start.3) | copy-done | bytes 393240
  21.6 1.0 %copy-done.4 = bf16[3,128,512]{2,1,0:T(8,128)(2,1)S(1)} copy-done((bf16[3,128,512]{2,1,0:T(8,128)(2,1)S(1)}, bf16[3,128,512]{2,1,0:T(8,128)(2,1)}, u32[]{:S(2)}) %copy-start.4) | copy-done | bytes 393240
  22.6 1.0 %copy-done.5 = bf16[3,128,512]{2,1,0:T(8,128)(2,1)S(1)} copy-done((bf16[3,128,512]{2,1,0:T(8,128)(2,1)S(1)}, bf16[3,128,512]{2,1,0:T(8,128)(2,1)}, u32[]{:S(2)}) %copy-start.5) | copy-done | bytes 393240
  23.6 1.0 %copy-done.6 = bf16[3,128,512]{2,1,0:T(8,128)(2,1)S(1)} copy-done((bf16[3,128,512]{2,1,0:T(8,128)(2,1)S(1)}, bf16[3,128,512]{2,1,0:T(8,128)(2,1)}, u32[]{:S(2)}) %copy-start.6) | copy-done | bytes 393240
  24.6 7.7 %attention_both_ways.1 = (bf16[384,512]{1,0:T(8,128)(2,1)}, bf16[384,512]{1,0:T(8,128)(2,1)}, bf16[384,512]{1,0:T(8,128)(2,1)}, bf16[384,256]{1,0:T(8,128)(2,1)S(1)}, bf16[384,256]{1,0:T(8,128)(2,1)S(1)}) custom-call(s32[6]{0:T(128)S(1)} %stack.27.refs_0_, s32[3]{0:T(128)S(1)} %dynamic_slice.6.refs_1_, bf16[256,512]{1,0:T(8,128)(2,1)S(1)} %copy-done.2, ...), custom_call_target="tpu_custom_call" | custom-call | flops 654311424 | bytes 4718592 | tf_op jit(solution)/shard_map/attention_both_ways/pallas_call | solution.py:220
  33.2 0.6 collective-permute-done.5.got_ref
  33.8 0.7 %weight_gradient.1 = (f32[4,64,256]{2,1,0:T(8,128)S(1)}, bf16[4,64,256]{2,1,0:T(8,128)(2,1)S(1)}, bf16[4,64,256]{2,1,0:T(8,128)(2,1)S(1)}, bf16[4,64,256]{2,1,0:T(8,128)(2,1)S(1)}) custom-call(s32[1]{0:T(128)} %bitcast.16.place_ref, bf16[1024,768]{1,0:T(8,128)(2,1)S(1)} %events_transposed.1.events_ref, bf16[384,256]{1,0:T(8,128)(2,1)S(1)} %get-tuple-element.20.keep_ref, ...), custom_call_target="tpu_custom_call" | custom-call | flops 402653184 | bytes 2097152 | tf_op jit(solution)/shard_map/weight_gradient/pallas_call | solution.py:242
  34.5 1.6 %collective-permute-start.6 = (bf16[4,64,256]{2,1,0:T(8,128)(2,1)S(1)}, bf16[4,64,256]{2,1,0:T(8,128)(2,1)S(1)}, u32[]{:S(2)}, u32[]{:S(2)}) collective-permute-start(bf16[4,64,256]{2,1,0:T(8,128)(2,1)S(1)} %get-tuple-element.23), channel_id=1, source_target_pairs={{0,8},{4,12},{8,16},{12,20},{16,24},{20,28},{24,0},{28,4},{1,9},{5... | collective-permute-start | bytes 393224 | tf_op jit(solution)/shard_map/ppermute | solution.py:270
  36.1 1.5 %collective-permute-start.7 = (bf16[4,64,256]{2,1,0:T(8,128)(2,1)S(1)}, bf16[4,64,256]{2,1,0:T(8,128)(2,1)S(1)}, u32[]{:S(2)}, u32[]{:S(2)}) collective-permute-start(bf16[4,64,256]{2,1,0:T(8,128)(2,1)S(1)} %get-tuple-element.24), channel_id=1, source_target_pairs={{0,16},{4,20},{8,24},{12,28},{16,0},{20,4},{24,8},{28,12},{1,17},{... | collective-permute-start | bytes 393224 | tf_op jit(solution)/shard_map/ppermute | solution.py:270
  37.6 1.4 %collective-permute-start.8 = (bf16[4,64,256]{2,1,0:T(8,128)(2,1)S(1)}, bf16[4,64,256]{2,1,0:T(8,128)(2,1)S(1)}, u32[]{:S(2)}, u32[]{:S(2)}) collective-permute-start(bf16[4,64,256]{2,1,0:T(8,128)(2,1)S(1)} %get-tuple-element.25), channel_id=1, source_target_pairs={{0,24},{4,28},{8,0},{12,4},{16,8},{20,12},{24,16},{28,20},{1,25},{... | collective-permute-start | bytes 393224 | tf_op jit(solution)/shard_map/ppermute | solution.py:270
  39.0 2.8 %collective-permute-done.6.refs_1_ = bf16[4,64,256]{2,1,0:T(8,128)(2,1)S(1)} collective-permute-done((bf16[4,64,256]{2,1,0:T(8,128)(2,1)S(1)}, bf16[4,64,256]{2,1,0:T(8,128)(2,1)S(1)}, u32[]{:S(2)}, u32[]{:S(2)}) %collective-permute-start.6) | collective-permute-done | bytes 131104 | tf_op jit(solution)/shard_map/ppermute | solution.py:270
  41.8 2.2 %collective-permute-done.7.refs_2_ = bf16[4,64,256]{2,1,0:T(8,128)(2,1)S(1)} collective-permute-done((bf16[4,64,256]{2,1,0:T(8,128)(2,1)S(1)}, bf16[4,64,256]{2,1,0:T(8,128)(2,1)S(1)}, u32[]{:S(2)}, u32[]{:S(2)}) %collective-permute-start.7) | collective-permute-done | bytes 131104 | tf_op jit(solution)/shard_map/ppermute | solution.py:270
  44.8 3.4 %collective-permute-start.10 = (bf16[64,256]{1,0:T(8,128)(2,1)S(1)}, bf16[64,256]{1,0:T(8,128)(2,1)S(1)}, u32[]{:S(2)}, u32[]{:S(2)}) collective-permute-start(bf16[64,256]{1,0:T(8,128)(2,1)S(1)} %get-tuple-element.28), channel_id=1, source_target_pairs={{0,2},{1,3},{2,0},{3,1},{4,6},{5,7},{6,4},{7,5},{8,10},{9,11},{10,... | collective-permute-start | bytes 98312 | tf_op jit(solution)/shard_map/ppermute | solution.py:293
  48.5 1.7 %collective-permute-done.9.refs_1_ = bf16[64,256]{1,0:T(8,128)(2,1)S(1)} collective-permute-done((bf16[64,256]{1,0:T(8,128)(2,1)S(1)}, bf16[64,256]{1,0:T(8,128)(2,1)S(1)}, u32[]{:S(2)}, u32[]{:S(2)}) %collective-permute-start.9) | collective-permute-done | bytes 32800 | tf_op jit(solution)/shard_map/ppermute | solution.py:293
  50.1 0.8 %collective-permute-done.10.refs_2_ = bf16[64,256]{1,0:T(8,128)(2,1)S(1)} collective-permute-done((bf16[64,256]{1,0:T(8,128)(2,1)S(1)}, bf16[64,256]{1,0:T(8,128)(2,1)S(1)}, u32[]{:S(2)}, u32[]{:S(2)}) %collective-permute-start.10) | collective-permute-done | bytes 32800 | tf_op jit(solution)/shard_map/ppermute | solution.py:293
  50.9 1.1 %collective-permute-done.11.refs_3_ = bf16[64,256]{1,0:T(8,128)(2,1)S(1)} collective-permute-done((bf16[64,256]{1,0:T(8,128)(2,1)S(1)}, bf16[64,256]{1,0:T(8,128)(2,1)S(1)}, u32[]{:S(2)}, u32[]{:S(2)}) %collective-permute-start.11) | collective-permute-done | bytes 32800 | tf_op jit(solution)/shard_map/ppermute | solution.py:293
  52.2 1.7 %collective-permute-start.17 = (bf16[64,256]{1,0:T(8,128)(2,1)S(1)}, bf16[64,256]{1,0:T(8,128)(2,1)S(1)}, u32[]{:S(2)}, u32[]{:S(2)}) collective-permute-start(bf16[64,256]{1,0:T(8,128)(2,1)S(1)} %mean_over_shards.1.refs_0_), channel_id=1, source_target_pairs={{0,24},{4,28},{8,0},{12,4},{16,8},{20,12},{24,16},{28,20},{1,25},{... | collective-permute-start | bytes 98312 | tf_op jit(solution)/shard_map/ppermute | solution.py:305
  53.9 1.3 %collective-permute-start.16 = (bf16[64,256]{1,0:T(8,128)(2,1)S(1)}, bf16[64,256]{1,0:T(8,128)(2,1)S(1)}, u32[]{:S(2)}, u32[]{:S(2)}) collective-permute-start(bf16[64,256]{1,0:T(8,128)(2,1)S(1)} %mean_over_shards.1.refs_0_), channel_id=1, source_target_pairs={{0,20},{4,24},{8,28},{12,0},{16,4},{20,8},{24,12},{28,16},{1,21},{... | collective-permute-start | bytes 98312 | tf_op jit(solution)/shard_map/ppermute | solution.py:305
  55.7 1.2 %collective-permute-start.14 = (bf16[64,256]{1,0:T(8,128)(2,1)S(1)}, bf16[64,256]{1,0:T(8,128)(2,1)S(1)}, u32[]{:S(2)}, u32[]{:S(2)}) collective-permute-start(bf16[64,256]{1,0:T(8,128)(2,1)S(1)} %mean_over_shards.1.refs_0_), channel_id=1, source_target_pairs={{0,12},{4,16},{8,20},{12,24},{16,28},{20,0},{24,4},{28,8},{1,13},{... | collective-permute-start | bytes 98312 | tf_op jit(solution)/shard_map/ppermute | solution.py:305
  56.9 1.2 %collective-permute-start.13 = (bf16[64,256]{1,0:T(8,128)(2,1)S(1)}, bf16[64,256]{1,0:T(8,128)(2,1)S(1)}, u32[]{:S(2)}, u32[]{:S(2)}) collective-permute-start(bf16[64,256]{1,0:T(8,128)(2,1)S(1)} %mean_over_shards.1.refs_0_), channel_id=1, source_target_pairs={{0,8},{4,12},{8,16},{12,20},{16,24},{20,28},{24,0},{28,4},{1,9},{5... | collective-permute-start | bytes 98312 | tf_op jit(solution)/shard_map/ppermute | solution.py:305
  58.1 1.3 %collective-permute-done.15.refs_4_ = bf16[64,256]{1,0:T(8,128)(2,1)S(1)} collective-permute-done((bf16[64,256]{1,0:T(8,128)(2,1)S(1)}, bf16[64,256]{1,0:T(8,128)(2,1)S(1)}, u32[]{:S(2)}, u32[]{:S(2)}) %collective-permute-start.15) | collective-permute-done | bytes 32800 | tf_op jit(solution)/shard_map/ppermute | solution.py:305
  59.4 2.3 %collective-permute-done.13.refs_2_ = bf16[64,256]{1,0:T(8,128)(2,1)S(1)} collective-permute-done((bf16[64,256]{1,0:T(8,128)(2,1)S(1)}, bf16[64,256]{1,0:T(8,128)(2,1)S(1)}, u32[]{:S(2)}, u32[]{:S(2)}) %collective-permute-start.13) | collective-permute-done | bytes 32800 | tf_op jit(solution)/shard_map/ppermute | solution.py:305
  62.3 0.9 %blocks_in_place.1 = f32[256,512]{1,0:T(8,128)} custom-call(s32[1]{0:T(128)} %bitcast.14.place_ref, bf16[64,256]{1,0:T(8,128)(2,1)S(1)} %mean_over_shards.1.refs_0_, bf16[64,256]{1,0:T(8,128)(2,1)S(1)} %collective-permute-done.12.refs_1_, bf16[64,256]{1,0:T(8,128)(2,1)S(1)} %collective-permute-done.13.refs_2_, ...), custom_call_target="tpu_custom_call" | custom-call | tf_op jit(solution)/shard_map/blocks_in_place/pallas_call | solution.py:308
  (29 shorter events, 3.9 us)
Async XLA Ops:
  0.6 32.1 %collective-permute-start.4 = (bf16[384,1024]{1,0:T(8,128)(2,1)}, bf16[384,1024]{1,0:T(8,128)(2,1)S(1)}, u32[]{:S(2)}, u32[]{:S(2)}) collective-permute-start(bf16[384,1024]{1,0:T(8,128)(2,1)} %bitcast.17), channel_id=1, source_target_pairs={{0,4},{4,0},{8,12},{12,8},{16,20},{20,16},{24,28},{28,24},{1,5},{5... | collective-permute-start | bytes 2359304 | tf_op jit(solution)/shard_map/ppermute | solution.py:200
  1.1 12.1 %collective-permute-start = (bf16[256,512]{1,0:T(8,128)(2,1)}, bf16[256,512]{1,0:T(8,128)(2,1)S(1)}, u32[]{:S(2)}, u32[]{:S(2)}) collective-permute-start(bf16[256,512]{1,0:T(8,128)(2,1)} %refs_2_.1), channel_id=1, source_target_pairs={{0,1},{1,2},{2,3},{3,0},{4,7},{5,4},{6,5},{7,6},{8,9},{9,10},{10,1... | collective-permute-start | bytes 786440 | tf_op jit(solution)/shard_map/ppermute | solution.py:169
  4.7 12.2 %collective-permute-start.2 = (bf16[128,512]{1,0:T(8,128)(2,1)S(1)}, bf16[128,512]{1,0:T(8,128)(2,1)S(1)}, u32[]{:S(2)}, u32[]{:S(2)}) collective-permute-start(bf16[128,512]{1,0:T(8,128)(2,1)S(1)} %constant_dynamic-slice_fusion), channel_id=1, source_target_pairs={{0,2},{1,3},{2,0},{3,1},{4,6},{5,7},{6,4},{7,5},{8,10},{9,11},{10,... | collective-permute-start | bytes 393224 | tf_op jit(solution)/shard_map/ppermute | solution.py:169
  13.3 5.2 %collective-permute-start.1 = (bf16[256,512]{1,0:T(8,128)(2,1)S(1)}, bf16[256,512]{1,0:T(8,128)(2,1)S(1)}, u32[]{:S(2)}, u32[]{:S(2)}) collective-permute-start(bf16[256,512]{1,0:T(8,128)(2,1)S(1)} %collective-permute-done.refs_3_), channel_id=1, source_target_pairs={{0,4},{4,0},{8,12},{12,8},{16,20},{20,16},{24,28},{28,24},{1,5},{5... | collective-permute-start | bytes 786440 | tf_op jit(solution)/shard_map/ppermute | solution.py:200
  16.9 1.6 %collective-permute-start.3 = (bf16[128,512]{1,0:T(8,128)(2,1)S(1)}, bf16[128,512]{1,0:T(8,128)(2,1)S(1)}, u32[]{:S(2)}, u32[]{:S(2)}) collective-permute-start(bf16[128,512]{1,0:T(8,128)(2,1)S(1)} %collective-permute-done.2.refs_5_), channel_id=1, source_target_pairs={{0,4},{4,0},{8,12},{12,8},{16,20},{20,16},{24,28},{28,24},{1,5},{5... | collective-permute-start | bytes 393224 | tf_op jit(solution)/shard_map/ppermute | solution.py:200
  18.5 1.1 %copy-start = (bf16[3,128,1024]{2,1,0:T(8,128)(2,1)S(1)}, bf16[3,128,1024]{2,1,0:T(8,128)(2,1)}, u32[]{:S(2)}) copy-start(bf16[3,128,1024]{2,1,0:T(8,128)(2,1)} %param.7) | copy-start | bytes 2359300
  19.7 0.9 %copy-start.2 = (bf16[256,512]{1,0:T(8,128)(2,1)S(1)}, bf16[256,512]{1,0:T(8,128)(2,1)}, u32[]{:S(2)}) copy-start(bf16[256,512]{1,0:T(8,128)(2,1)} %refs_2_.1) | copy-start | bytes 786436
  20.6 1.0 %copy-start.3 = (bf16[3,128,512]{2,1,0:T(8,128)(2,1)S(1)}, bf16[3,128,512]{2,1,0:T(8,128)(2,1)}, u32[]{:S(2)}) copy-start(bf16[3,128,512]{2,1,0:T(8,128)(2,1)} %param.9) | copy-start | bytes 1179652
  21.6 1.0 %copy-start.4 = (bf16[3,128,512]{2,1,0:T(8,128)(2,1)S(1)}, bf16[3,128,512]{2,1,0:T(8,128)(2,1)}, u32[]{:S(2)}) copy-start(bf16[3,128,512]{2,1,0:T(8,128)(2,1)} %param.10) | copy-start | bytes 1179652
  22.6 1.0 %copy-start.5 = (bf16[3,128,512]{2,1,0:T(8,128)(2,1)S(1)}, bf16[3,128,512]{2,1,0:T(8,128)(2,1)}, u32[]{:S(2)}) copy-start(bf16[3,128,512]{2,1,0:T(8,128)(2,1)} %param.11) | copy-start | bytes 1179652
  23.6 1.0 %copy-start.6 = (bf16[3,128,512]{2,1,0:T(8,128)(2,1)S(1)}, bf16[3,128,512]{2,1,0:T(8,128)(2,1)}, u32[]{:S(2)}) copy-start(bf16[3,128,512]{2,1,0:T(8,128)(2,1)} %param.12) | copy-start | bytes 1179652
  24.6 8.2 %copy-start.1 = (bf16[3,128,1024]{2,1,0:T(8,128)(2,1)S(1)}, bf16[3,128,1024]{2,1,0:T(8,128)(2,1)}, u32[]{:S(2)}) copy-start(bf16[3,128,1024]{2,1,0:T(8,128)(2,1)} %param.7) | copy-start | bytes 2359300
  32.3 1.5 %collective-permute-start.5 = (bf16[384,256]{1,0:T(8,128)(2,1)S(1)}, bf16[384,256]{1,0:T(8,128)(2,1)S(1)}, u32[]{:S(2)}, u32[]{:S(2)}) collective-permute-start(bf16[384,256]{1,0:T(8,128)(2,1)S(1)} %get-tuple-element.21), channel_id=1, source_target_pairs={{0,4},{4,0},{8,12},{12,8},{16,20},{20,16},{24,28},{28,24},{1,5},{5... | collective-permute-start | bytes 589832 | tf_op jit(solution)/shard_map/ppermute | solution.py:200
  34.5 7.3 %collective-permute-start.6 = (bf16[4,64,256]{2,1,0:T(8,128)(2,1)S(1)}, bf16[4,64,256]{2,1,0:T(8,128)(2,1)S(1)}, u32[]{:S(2)}, u32[]{:S(2)}) collective-permute-start(bf16[4,64,256]{2,1,0:T(8,128)(2,1)S(1)} %get-tuple-element.23), channel_id=1, source_target_pairs={{0,8},{4,12},{8,16},{12,20},{16,24},{20,28},{24,0},{28,4},{1,9},{5... | collective-permute-start | bytes 393224 | tf_op jit(solution)/shard_map/ppermute | solution.py:270
  36.1 8.0 %collective-permute-start.7 = (bf16[4,64,256]{2,1,0:T(8,128)(2,1)S(1)}, bf16[4,64,256]{2,1,0:T(8,128)(2,1)S(1)}, u32[]{:S(2)}, u32[]{:S(2)}) collective-permute-start(bf16[4,64,256]{2,1,0:T(8,128)(2,1)S(1)} %get-tuple-element.24), channel_id=1, source_target_pairs={{0,16},{4,20},{8,24},{12,28},{16,0},{20,4},{24,8},{28,12},{1,17},{... | collective-permute-start | bytes 393224 | tf_op jit(solution)/shard_map/ppermute | solution.py:270
  37.6 6.5 %collective-permute-start.8 = (bf16[4,64,256]{2,1,0:T(8,128)(2,1)S(1)}, bf16[4,64,256]{2,1,0:T(8,128)(2,1)S(1)}, u32[]{:S(2)}, u32[]{:S(2)}) collective-permute-start(bf16[4,64,256]{2,1,0:T(8,128)(2,1)S(1)} %get-tuple-element.25), channel_id=1, source_target_pairs={{0,24},{4,28},{8,0},{12,4},{16,8},{20,12},{24,16},{28,20},{1,25},{... | collective-permute-start | bytes 393224 | tf_op jit(solution)/shard_map/ppermute | solution.py:270
  44.2 5.9 %collective-permute-start.9 = (bf16[64,256]{1,0:T(8,128)(2,1)S(1)}, bf16[64,256]{1,0:T(8,128)(2,1)S(1)}, u32[]{:S(2)}, u32[]{:S(2)}) collective-permute-start(bf16[64,256]{1,0:T(8,128)(2,1)S(1)} %get-tuple-element.27), channel_id=1, source_target_pairs={{0,1},{1,2},{2,3},{3,0},{4,5},{5,6},{6,7},{7,4},{8,9},{9,10},{10,1... | collective-permute-start | bytes 98312 | tf_op jit(solution)/shard_map/ppermute | solution.py:293
  44.8 6.2 %collective-permute-start.10 = (bf16[64,256]{1,0:T(8,128)(2,1)S(1)}, bf16[64,256]{1,0:T(8,128)(2,1)S(1)}, u32[]{:S(2)}, u32[]{:S(2)}) collective-permute-start(bf16[64,256]{1,0:T(8,128)(2,1)S(1)} %get-tuple-element.28), channel_id=1, source_target_pairs={{0,2},{1,3},{2,0},{3,1},{4,6},{5,7},{6,4},{7,5},{8,10},{9,11},{10,... | collective-permute-start | bytes 98312 | tf_op jit(solution)/shard_map/ppermute | solution.py:293
  48.1 3.9 %collective-permute-start.11 = (bf16[64,256]{1,0:T(8,128)(2,1)S(1)}, bf16[64,256]{1,0:T(8,128)(2,1)S(1)}, u32[]{:S(2)}, u32[]{:S(2)}) collective-permute-start(bf16[64,256]{1,0:T(8,128)(2,1)S(1)} %get-tuple-element.29), channel_id=1, source_target_pairs={{0,3},{1,0},{2,1},{3,2},{4,7},{5,4},{6,5},{7,6},{8,11},{9,8},{10,9... | collective-permute-start | bytes 98312 | tf_op jit(solution)/shard_map/ppermute | solution.py:293
  52.1 4.8 %collective-permute-start.18 = (bf16[64,256]{1,0:T(8,128)(2,1)S(1)}, bf16[64,256]{1,0:T(8,128)(2,1)S(1)}, u32[]{:S(2)}, u32[]{:S(2)}) collective-permute-start(bf16[64,256]{1,0:T(8,128)(2,1)S(1)} %mean_over_shards.1.refs_0_), channel_id=1, source_target_pairs={{0,28},{4,0},{8,4},{12,8},{16,12},{20,16},{24,20},{28,24},{1,29},{... | collective-permute-start | bytes 98312 | tf_op jit(solution)/shard_map/ppermute | solution.py:305
  52.2 5.9 %collective-permute-start.17 = (bf16[64,256]{1,0:T(8,128)(2,1)S(1)}, bf16[64,256]{1,0:T(8,128)(2,1)S(1)}, u32[]{:S(2)}, u32[]{:S(2)}) collective-permute-start(bf16[64,256]{1,0:T(8,128)(2,1)S(1)} %mean_over_shards.1.refs_0_), channel_id=1, source_target_pairs={{0,24},{4,28},{8,0},{12,4},{16,8},{20,12},{24,16},{28,20},{1,25},{... | collective-permute-start | bytes 98312 | tf_op jit(solution)/shard_map/ppermute | solution.py:305
  53.9 4.2 %collective-permute-start.16 = (bf16[64,256]{1,0:T(8,128)(2,1)S(1)}, bf16[64,256]{1,0:T(8,128)(2,1)S(1)}, u32[]{:S(2)}, u32[]{:S(2)}) collective-permute-start(bf16[64,256]{1,0:T(8,128)(2,1)S(1)} %mean_over_shards.1.refs_0_), channel_id=1, source_target_pairs={{0,20},{4,24},{8,28},{12,0},{16,4},{20,8},{24,12},{28,16},{1,21},{... | collective-permute-start | bytes 98312 | tf_op jit(solution)/shard_map/ppermute | solution.py:305
  55.2 4.2 %collective-permute-start.15 = (bf16[64,256]{1,0:T(8,128)(2,1)S(1)}, bf16[64,256]{1,0:T(8,128)(2,1)S(1)}, u32[]{:S(2)}, u32[]{:S(2)}) collective-permute-start(bf16[64,256]{1,0:T(8,128)(2,1)S(1)} %mean_over_shards.1.refs_0_), channel_id=1, source_target_pairs={{0,16},{4,20},{8,24},{12,28},{16,0},{20,4},{24,8},{28,12},{1,17},{... | collective-permute-start | bytes 98312 | tf_op jit(solution)/shard_map/ppermute | solution.py:305
  55.7 3.7 %collective-permute-start.14 = (bf16[64,256]{1,0:T(8,128)(2,1)S(1)}, bf16[64,256]{1,0:T(8,128)(2,1)S(1)}, u32[]{:S(2)}, u32[]{:S(2)}) collective-permute-start(bf16[64,256]{1,0:T(8,128)(2,1)S(1)} %mean_over_shards.1.refs_0_), channel_id=1, source_target_pairs={{0,12},{4,16},{8,20},{12,24},{16,28},{20,0},{24,4},{28,8},{1,13},{... | collective-permute-start | bytes 98312 | tf_op jit(solution)/shard_map/ppermute | solution.py:305
  56.9 4.8 %collective-permute-start.13 = (bf16[64,256]{1,0:T(8,128)(2,1)S(1)}, bf16[64,256]{1,0:T(8,128)(2,1)S(1)}, u32[]{:S(2)}, u32[]{:S(2)}) collective-permute-start(bf16[64,256]{1,0:T(8,128)(2,1)S(1)} %mean_over_shards.1.refs_0_), channel_id=1, source_target_pairs={{0,8},{4,12},{8,16},{12,20},{16,24},{20,28},{24,0},{28,4},{1,9},{5... | collective-permute-start | bytes 98312 | tf_op jit(solution)/shard_map/ppermute | solution.py:305
  58.0 4.2 %collective-permute-start.12 = (bf16[64,256]{1,0:T(8,128)(2,1)S(1)}, bf16[64,256]{1,0:T(8,128)(2,1)S(1)}, u32[]{:S(2)}, u32[]{:S(2)}) collective-permute-start(bf16[64,256]{1,0:T(8,128)(2,1)S(1)} %mean_over_shards.1.refs_0_), channel_id=1, source_target_pairs={{0,4},{4,8},{8,12},{12,16},{16,20},{20,24},{24,28},{28,0},{1,5},{5... | collective-permute-start | bytes 98312 | tf_op jit(solution)/shard_map/ppermute | solution.py:305

commit v2 on v0

v2 whole, which is shorter than its diff:
```python
import functools
import math

import jax
import jax.numpy as jnp
from jax import lax
from jax.experimental import pallas as pl
from jax.experimental.pallas import tpu as pltpu
from jax.sharding import PartitionSpec as P

HEADS = 4
EPSILON = 1e-06
CORES = 2
BOTH = ("dp", "fsdp")
VMEM_LIMIT = 24 * 1024 * 1024

LAST = (((1,), (1,)), ((), ()))
FIRST = (((0,), (0,)), ((), ()))


def dot(lhs, rhs, dims=(((1,), (0,)), ((), ()))):
    return lax.dot_general(lhs, rhs, dims, preferred_element_type=jnp.float32)


def call(kernel, name, operands, in_specs, out_shape, scratch=(), flops=0, moved=0,
         out_specs=None):
    vmem = pl.BlockSpec(memory_space=pltpu.VMEM)
    many = isinstance(out_shape, tuple)
    operands = [
        pltpu.with_memory_space_constraint(a, pltpu.HBM) if spec is FAR else a
        for a, spec in zip(operands, in_specs)
    ]
    return pl.pallas_call(
        kernel,
        out_shape=out_shape,
        in_specs=in_specs,
        out_specs=out_specs or ((vmem,) * len(out_shape) if many else vmem),
        scratch_shapes=list(scratch),
        compiler_params=pltpu.CompilerParams(vmem_limit_bytes=VMEM_LIMIT),
        cost_estimate=pl.CostEstimate(flops=flops, bytes_accessed=moved, transcendentals=0),
        name=name,
    )(*operands)


NEAR = pl.BlockSpec(memory_space=pltpu.VMEM)
ANYWHERE = pl.BlockSpec(memory_space=pl.ANY)
FAR = pl.BlockSpec(memory_space=pltpu.HBM)


def head_columns(width):
    depth = width // HEADS
    return [slice(h * depth, (h + 1) * depth) for h in range(HEADS)]


def slot_rows(rows, slots):
    span = rows // slots
    return [slice(s * span, (s + 1) * span) for s in range(slots)]


def row_mean(blocks, width):
    return jnp.sum(sum(blocks[1:], blocks[0]), axis=1, keepdims=True) / width


def slice_kernel(group, block_ref, out_ref, sem):
    rows = out_ref.shape[0]
    start = pl.multiple_of(lax.rem(lax.axis_index("dp"), group) * rows, rows)
    copy = pltpu.make_async_copy(block_ref.at[pl.ds(start, rows)], out_ref, sem)
    copy.start()
    copy.wait()


def prepare_kernel(slots, _, lengths_ref, sibling_ref, *refs):
    inputs, held = refs[:6], refs[6:11]
    (events_t_ref, key_t_ref, value_t_ref, weight_ref, gated_ref, first_ref,
     gate_ref, own_lengths_ref, sems) = refs[11:]
    events_ref, key_ref, value_ref, upstream_ref, _ = held
    copies = [
        pltpu.make_async_copy(source, target, sems.at[i])
        for i, (source, target) in enumerate(zip(inputs, held + (gate_ref,)))
    ]
    copies.append(pltpu.make_async_copy(lengths_ref, own_lengths_ref, sems.at[len(copies)]))
    for copy in copies:
        copy.start()
    rows, width = key_ref.shape
    events_t_ref[:, rows:] = sibling_ref[...].T
    for copy in copies:
        copy.wait()
    events_t_ref[:, :rows] = events_ref[...].T
    key_t_ref[...] = key_ref[...].T
    value_t_ref[...] = value_ref[...].T
    span = rows // slots
    row = lax.broadcasted_iota(jnp.int32, (span, span), 0)
    column = lax.broadcasted_iota(jnp.int32, (span, span), 1)
    first_slot = (lax.axis_index("dp") * lax.axis_size("fsdp") + lax.axis_index("fsdp")) * slots
    for s, place in enumerate(slot_rows(rows, slots)):
        length = own_lengths_ref[first_slot + s]
        inverse = 1.0 / jnp.full((span, span), length, jnp.int32).astype(jnp.float32)
        weight_ref[s] = jnp.where((column <= row) & (row < length), inverse, 0.0)
        live = lax.broadcasted_iota(jnp.int32, (span, width), 0) < length
        gated = upstream_ref[place].astype(jnp.float32) * gate_ref[place].astype(jnp.float32)
        gated = jnp.where(live, gated, 0.0)
        gated_ref[place] = gated
        first = row_mean([gated[:, c] for c in head_columns(width)], width)
        first_ref[place] = jnp.broadcast_to(first, (span, first_ref.shape[1]))


def piece_start(origin, shard_rows, group, part_rows):
    flips, member_flip = origin
    device = lax.axis_index("dp")
    flip = jnp.where(lax.rem(device, CORES) == 0, flips[0], flips[1])
    start = (lax.axis_index("fsdp") ^ flip) * shard_rows
    if member_flip is not None:
        start = start + (lax.rem(device, group) ^ member_flip) * part_rows
    return pl.multiple_of(start, 16)


def attention_kernel(slots, group, origins, *refs):
    piece_count = len(origins)
    pieces = refs[:piece_count]
    (events_ref, key_ref, value_ref, key_t_ref, value_t_ref, weight_ref, gated_ref, first_ref,
     grad_query_ref, query_ref, normed_ref, mixed_grad_ref, attention_ref, scores_grad_ref,
     projection_ref, sems) = refs[piece_count:]
    copies = []
    for p, (piece, origin) in enumerate(zip(pieces, origins)):
        rows = piece.shape[0]
        start = piece_start(origin, pieces[0].shape[0], group, rows)
        copies.append(
            pltpu.make_async_copy(piece, projection_ref.at[pl.ds(start, rows)], sems.at[p])
        )
    for copy in copies:
        copy.start()
    for copy in copies:
        copy.wait()
    query_ref[...] = dot(events_ref[...], projection_ref[...]).astype(jnp.bfloat16)

    rows, width = key_ref.shape
    scale = 1.0 / math.sqrt(width // HEADS)
    columns = head_columns(width)
    places = slot_rows(rows, slots)
    each = [(s, h, s * HEADS + h) for s in range(slots) for h in range(HEADS)]
    slopes, mixed, grad_mixed = [], [], []
    for s, h, i in each:
        scores = dot(query_ref[places[s], columns[h]], key_t_ref[columns[h], places[s]]) * scale
        sigmoid = 0.5 * jnp.tanh(0.5 * scores) + 0.5
        silu = scores * sigmoid
        attention_ref[i] = (silu * weight_ref[s]).astype(jnp.bfloat16)
        slopes.append((sigmoid + silu * (1.0 - sigmoid)) * weight_ref[s])
    for s, h, i in each:
        mixed.append(dot(attention_ref[i], value_ref[places[s], columns[h]]))
    for s in range(slots):
        own = mixed[s * HEADS : (s + 1) * HEADS]
        mean = row_mean(own, width)
        centred = [m - mean for m in own]
        inv_std = lax.rsqrt(row_mean([c * c for c in centred], width) + EPSILON)
        normed = [c * inv_std for c in centred]
        gated = [gated_ref[places[s], c] for c in columns]
        second = row_mean([g * n for g, n in zip(gated, normed)], width)
        first = first_ref[places[s]]
        for h in range(HEADS):
            normed_ref[places[s], columns[h]] = normed[h]
            grad = inv_std * (gated[h] - first - normed[h] * second)
            mixed_grad_ref[places[s], columns[h]] = grad.astype(jnp.bfloat16)
    for s, h, i in each:
        grad_attention = dot(
            mixed_grad_ref[places[s], columns[h]], value_t_ref[columns[h], places[s]]
        )
        scores_grad_ref[i] = (grad_attention * slopes[i]).astype(jnp.bfloat16)
    for s, h, i in each:
        grad_query = dot(scores_grad_ref[i], key_ref[places[s], columns[h]]) * scale
        grad_query_ref[places[s], columns[h]] = grad_query.astype(jnp.bfloat16)


def outputs_kernel(slots, _, query_ref, normed_ref, mixed_grad_ref, attention_ref, scores_grad_ref,
                   upstream_ref, grad_key_ref, grad_value_ref, grad_gate_ref):
    rows, width = query_ref.shape
    scale = 1.0 / math.sqrt(width // HEADS)
    columns = head_columns(width)
    places = slot_rows(rows, slots)
    grad_gate_ref[...] = (upstream_ref[...].astype(jnp.float32) * normed_ref[...]).astype(
        jnp.bfloat16
    )
    for s in range(slots):
        for h in range(HEADS):
            i = s * HEADS + h
            grad_value = dot(attention_ref[i], mixed_grad_ref[places[s], columns[h]], FIRST)
            grad_value_ref[places[s], columns[h]] = grad_value.astype(jnp.bfloat16)
            grad_key = dot(scores_grad_ref[i], query_ref[places[s], columns[h]], FIRST) * scale
            grad_key_ref[places[s], columns[h]] = grad_key.astype(jnp.bfloat16)


def gradient_kernel(pairs, events_ref, own_ref, got_ref, *refs):
    outs, both_ref, total_ref = refs[:-2], refs[-2], refs[-1]
    rows, width = own_ref.shape
    shard_rows = total_ref.shape[0]
    half = width // CORES
    both_ref[:rows] = own_ref[...]
    both_ref[rows:] = got_ref[...]
    core, here = lax.rem(lax.axis_index("dp"), CORES), lax.axis_index("fsdp")

    def term(shard, columns):
        place = pl.ds(pl.multiple_of(shard * shard_rows, shard_rows), shard_rows)
        return dot(events_ref[place], both_ref[:, columns])

    at = 0
    for flips in pairs:
        total_ref[:, at : at + width] = term(
            here ^ jnp.where(core == 0, flips[0], flips[1]), slice(None)
        )
        at += width
    columns = pl.ds(pl.multiple_of(core * half, half), half)
    for shard in (here, here ^ (lax.axis_size("fsdp") // 2)):
        total_ref[:, at : at + half] = term(shard, columns)
        at += half
    part_rows = outs[0].shape[0]
    chip = lax.div(lax.axis_index("dp"), CORES)
    for k, out in enumerate(outs):
        start = pl.multiple_of((chip ^ k) * part_rows, part_rows)
        out[...] = total_ref[pl.ds(start, part_rows)].astype(out.dtype)


def chip_sum_kernel(term_count, _, *refs):
    terms, outs = refs[:term_count], refs[term_count:]
    at = 0
    for out in outs:
        columns = slice(at, at + out.shape[1])
        total = terms[0][:, columns].astype(jnp.float32)
        for term in terms[1:]:
            total = total + term[:, columns].astype(jnp.float32)
        out[...] = total.astype(out.dtype)
        at += out.shape[1]


def shard_sum_kernel(own_ref, middle_ref, *refs):
    wholes, out_ref, total_ref = refs[:-2], refs[-2], refs[-1]
    total = wholes[0][...].astype(jnp.float32)
    for whole in wholes[1:]:
        total = total + whole[...].astype(jnp.float32)
    total_ref[...] = total
    half = own_ref.shape[1]
    core = lax.rem(lax.axis_index("dp"), CORES)
    columns = pl.ds(pl.multiple_of(core * half, half), half)
    total_ref[:, columns] += own_ref[...] + middle_ref[...].astype(jnp.float32)
    out_ref[...] = total_ref[...].astype(out_ref.dtype)


def mean_kernel(count, own_ref, sibling_ref, out_ref, half_ref):
    total = own_ref[...].astype(jnp.float32) + sibling_ref[...].astype(jnp.float32)
    out_ref[...] = (total / count).astype(out_ref.dtype)
    rows = half_ref.shape[0]
    core = lax.rem(lax.axis_index("dp"), CORES)
    half_ref[...] = out_ref[pl.ds(pl.multiple_of(core * rows, rows), rows)]


def place_kernel(own_ref, near_ref, sibling_near_ref, half_ref, sibling_half_ref, out_ref, held_ref,
                 sems):
    rows, half = own_ref.shape[0], half_ref.shape[0]
    core, chip = lax.rem(lax.axis_index("dp"), CORES), lax.div(lax.axis_index("dp"), CORES)
    blocks = (
        (own_ref, chip * rows),
        (near_ref, (chip ^ (1 + core)) * rows),
        (sibling_near_ref, (chip ^ (2 - core)) * rows),
        (half_ref, (chip ^ 3) * rows + core * half),
        (sibling_half_ref, (chip ^ 3) * rows + (1 - core) * half),
    )
    copies = []
    for i, (block_ref, start) in enumerate(blocks):
        place = pl.ds(pl.multiple_of(start, half), block_ref.shape[0])
        held_ref[place] = block_ref[...].astype(held_ref.dtype)
        copies.append(pltpu.make_async_copy(held_ref.at[place], out_ref.at[place], sems.at[i]))
        copies[i].start()
    for copy in copies:
        copy.wait()


def flip(block, axis, count, bits):
    return lax.ppermute(block, axis, [(i, i ^ bits) for i in range(count)])


def far_first(count, send):
    return [send(k) for k in range(count - 1, 0, -1)][::-1]


def shard_pairs(fsdp_count):
    others = [d for d in range(1, fsdp_count) if d != fsdp_count // 2]
    return list(zip(others[::2], others[1::2]))


def flip_by_core(block, flips, dp_count, fsdp_count):
    pairs = [
        (d * fsdp_count + z, d * fsdp_count + (z ^ flips[d % CORES]))
        for d in range(dp_count)
        for z in range(fsdp_count)
    ]
    return lax.ppermute(block, BOTH, pairs)


def across_z(weight, dp_count, fsdp_count):
    rows = weight.shape[0]
    group = 4 if dp_count % 4 == 0 and rows % 64 == 0 else 2
    part = call(
        functools.partial(slice_kernel, group),
        "own_part_of_weight",
        [weight],
        [FAR],
        jax.ShapeDtypeStruct((rows // group, weight.shape[1]), weight.dtype),
        [pltpu.SemaphoreType.DMA],
    )
    middle = fsdp_count // 2
    weight, part = lax.optimization_barrier((weight, part))
    arrived = [(flip(part, "fsdp", fsdp_count, middle), (middle, middle), 0)]
    for flips in shard_pairs(fsdp_count):
        arrived.append((flip_by_core(weight, flips, dp_count, fsdp_count), flips, None))
    return group, arrived


def share(group, arrived, ready, dp_count):
    block, flips, member = arrived[0]
    own = [(block, flips, member)]
    if group == 4:
        own.append((flip(block, "dp", dp_count, 2), flips, member ^ 2))
    for block, flips, member in arrived[1:]:
        own.append((lax.optimization_barrier((block, own[-1][0], ready))[0], flips, member))
    found = []
    for block, source, place in own:
        moved = flip(block, "dp", dp_count, 1)
        found.append((block, (source, place)))
        found.append((moved, (source[::-1], None if place is None else place ^ 1)))
    return found


def shards(events, query_weight, keys, values, gates, cotangent, lengths):
    slots, span, model_width = events.shape
    width = query_weight.shape[1]
    half_width = width // CORES
    rows = slots * span
    dp_count, fsdp_count = lax.axis_size("dp"), lax.axis_size("fsdp")
    chips = dp_count // CORES
    shard_rows = model_width // fsdp_count
    total_seqs = slots * dp_count * fsdp_count
    bf16, f32 = jnp.bfloat16, jnp.float32

    def shape(*dims, dtype=bf16):
        return jax.ShapeDtypeStruct(dims, dtype)

    flat_events = events.reshape(rows, model_width)
    keys, values, gates, cotangent = (
        a.reshape(rows, width) for a in (keys, values, gates, cotangent)
    )
    sibling_events = flip(flat_events, "dp", dp_count, 1)
    group, arrived = across_z(query_weight, dp_count, fsdp_count)
    prepared = call(
        functools.partial(prepare_kernel, slots),
        "prepared_operands",
        [arrived[0][0], lengths, sibling_events]
        + [flat_events, keys, values, cotangent, query_weight, gates],
        [ANYWHERE, FAR, NEAR] + [FAR] * 6,
        (
            shape(rows, model_width),
            shape(rows, width),
            shape(rows, width),
            shape(rows, width),
            shape(shard_rows, width),
            shape(model_width, CORES * rows),
            shape(width, rows),
            shape(width, rows),
            shape(slots, span, span, dtype=f32),
            shape(rows, width, dtype=f32),
            shape(rows, span, dtype=f32),
        ),
        [
            pltpu.VMEM((rows, width), bf16),
            pltpu.SMEM(lengths.shape, jnp.int32),
            pltpu.SemaphoreType.DMA((7,)),
        ],
        flops=10**10,
    )
    near_events, near_keys, near_values, near_cotangent, near_weight = prepared[:5]
    events_t, keys_t, values_t, weight, gated, first = prepared[5:]
    found = [(near_weight, ((0, 0), None))] + share(group, arrived, first, dp_count)
    pieces, origins = zip(*found)
    blocks = shape(slots * HEADS, span, span)
    grad_query, query, normed, grad_mixed, attention, grad_scores = call(
        functools.partial(attention_kernel, slots, group, origins),
        "attention_to_grad_query",
        list(pieces)
        + [near_events, near_keys, near_values, keys_t, values_t, weight, gated, first],
        [ANYWHERE] * len(pieces) + [NEAR] * 8,
        (
            shape(rows, width),
            shape(rows, width),
            shape(rows, width, dtype=f32),
            shape(rows, width),
            blocks,
            blocks,
        ),
        [
            pltpu.VMEM((model_width, width), bf16),
            pltpu.SemaphoreType.DMA((len(pieces),)),
        ],
        flops=2 * rows * width * (model_width + 4 * span),
        moved=24 * rows * width,
    )
    part_rows = shard_rows // chips
    staged = chips == 4 and part_rows % 32 == 0 and fsdp_count % 4 == 0
    terms = [grad_query]
    if staged:
        pairs = shard_pairs(fsdp_count)
        columns = len(pairs) * width + 2 * half_width
        terms = call(
            functools.partial(gradient_kernel, pairs),
            "weight_gradient",
            [events_t, grad_query, flip(grad_query, "dp", dp_count, 1)],
            [NEAR] * 3,
            tuple(shape(part_rows, columns, dtype=bf16 if k else f32) for k in range(chips)),
            [
                pltpu.VMEM((CORES * rows, width), bf16),
                pltpu.VMEM((shard_rows, columns), f32),
            ],
            flops=4 * rows * shard_rows * columns,
            moved=2 * model_width * (2 * rows + half_width),
        )
    grad_keys, grad_values, grad_gates = call(
        functools.partial(outputs_kernel, slots),
        "key_value_gate_gradients",
        [terms[0], query, normed, grad_mixed, attention, grad_scores, near_cotangent],
        [ANYWHERE] + [NEAR] * 6,
        (shape(rows, width),) * 3,
        flops=4 * rows * width * span,
        moved=12 * rows * width,
    )
    if staged:
        terms = [terms[0]] + far_first(chips, lambda k: flip(terms[k], "dp", dp_count, k * CORES))
        sums = call(
            functools.partial(chip_sum_kernel, chips),
            "sum_over_chips",
            [grad_keys] + terms,
            [FAR] + [NEAR] * chips,
            (shape(part_rows, width),) * len(pairs)
            + (shape(part_rows, half_width, dtype=f32), shape(part_rows, half_width)),
        )
        wholes = [flip_by_core(a, p, dp_count, fsdp_count) for a, p in zip(sums, pairs)]
        middle = flip(sums[-1], "fsdp", fsdp_count, fsdp_count // 2)
        total = call(
            shard_sum_kernel,
            "sum_over_shards",
            [sums[-2], middle] + wholes,
            [NEAR] * (2 + len(wholes)),
            shape(part_rows, width),
            [pltpu.VMEM((part_rows, width), f32)],
        )
        mean, half = call(
            functools.partial(mean_kernel, total_seqs),
            "mean_of_both_cores",
            [total, flip(total, "dp", dp_count, 1)],
            [NEAR] * 2,
            (shape(part_rows, width), shape(part_rows // CORES, width)),
        )
        half = flip(half, "dp", dp_count, 3 * CORES)
        near = lax.ppermute(
            mean, "dp", [(d, d ^ (CORES * (1 + d % CORES))) for d in range(dp_count)]
        )
        grad_weight = call(
            place_kernel,
            "blocks_in_place",
            [mean, near, flip(near, "dp", dp_count, 1), half, flip(half, "dp", dp_count, 1)],
            [NEAR] * 5,
            shape(shard_rows, width, dtype=f32),
            [pltpu.VMEM((shard_rows, width), f32), pltpu.SemaphoreType.DMA((5,))],
            out_specs=FAR,
        )
    else:
        whole = lax.dot_general(flat_events, grad_query, FIRST, preferred_element_type=f32)
        mine = lax.psum_scatter(whole, "fsdp", scatter_dimension=0, tiled=True)
        grad_weight = lax.psum(mine, "dp") / total_seqs

    full = (slots, span, width)
    return (
        grad_keys.reshape(full),
        grad_values.reshape(full),
        grad_gates.reshape(full),
        grad_weight,
    )


def solution(mesh):
    split = P(BOTH, None, None)
    return jax.shard_map(
        shards,
        mesh=mesh,
        in_specs=(split, P("fsdp", None), split, split, split, split, P()),
        out_specs=(split, split, split, P("fsdp", None)),
        check_vma=False,
    )
```

time: 189 us -> 48.9 us (0.26)
  waiting for transfers between devices: 143 us -> 19.6 us
  starting transfers between devices: 0.12 us -> 19.9 us
  between operations: 13.8 us -> 0.69 us
  other arithmetic: 10.1 us -> 0 us
  Pallas kernels: 0 us -> 8.49 us
  matrix products: 8.38 us -> 0 us
  local copies, waits for them, and re-layouts: 8.38 us -> 0 us
  loops' own time: 4.64 us -> 0 us
    psum x1 -> x0, waiting for transfers between devices: 57.3 us -> none  [shards(): summed = lax.psum(shard_rows, 'dp')]
    reduce_scatter x1 -> x0, waiting for transfers between devices: 53.7 us -> none  [shards(): lax.psum_scatter(lax.dot_general(columns, grad_flat, contract, preferred_...]
    all_gather x1 -> x0, waiting for transfers between devices: 31.5 us -> none  [shards(): lax.all_gather(query_weight, 'fsdp', axis=0, tiled=True)]
    ppermute x0 -> x18, starting transfers between devices: none -> 19.9 us  [the longest x15 15.7 us: flip(): return lax.ppermute(block, axis, [(i, i ^ bits) for i in range(count)])]
    ppermute x0 -> x18, waiting for transfers between devices: none -> 19.6 us  [the longest x15 16.7 us: flip(): return lax.ppermute(block, axis, [(i, i ^ bits) for i in range(count)])]
    pallas_call x0 -> x9, Pallas kernels: none -> 8.49 us  [call(): pl.pallas_call(kernel, out_shape=out_shape, in_specs=in_specs, out_specs=...]
    dot_general x20 -> x0, matrix products: 8.38 us -> none  [the longest x1 3.08 us: shards(): lax.dot_general(columns, grad_flat, contract, preferred_element_type=jnp....]
    another operation x4 -> x0, loops' own time: 4.64 us -> none  [the longest x3 2.6 us: attend(): return lax.switch(live_blocks, branches, operands)]
  transfers between devices with their start and end apart: 3 -> 18, of which waited for: 3 -> 13; matrix products, arithmetic and copies ran while one was open for 0% -> 0% of each run, Pallas kernels for 0% -> 9%
where the time goes in v2:
time: 48.9 us; the launch traced here: 48.7 us
  starting transfers between devices  19.9 us (41%)
  waiting for transfers between devices  19.6 us (40%)
  Pallas kernels  8.49 us (17%)
  between operations  0.69 us (1%)
    ppermute x15, waiting for transfers between devices, flip(): return lax.ppermute(block, axis, [(i, i ^ bits) for i in range(count)])  16.7 us
    ppermute x15, starting transfers between devices, flip(): return lax.ppermute(block, axis, [(i, i ^ bits) for i in range(count)])  15.7 us
    pallas_call x9, Pallas kernels, call(): pl.pallas_call(kernel, out_shape=out_shape, in_specs=in_specs, out_specs=...  8.49 us
    ppermute x2, starting transfers between devices, flip_by_core(): return lax.ppermute(block, BOTH, pairs)  3.13 us
    ppermute x1, waiting for transfers between devices, shards(): lax.ppermute(mean, 'dp', [(d, d ^ CORES * (1 + d % CORES)) for d in range...  1.75 us
    ppermute x2, waiting for transfers between devices, flip_by_core(): return lax.ppermute(block, BOTH, pairs)  1.12 us
    ppermute x1, starting transfers between devices, shards(): lax.ppermute(mean, 'dp', [(d, d ^ CORES * (1 + d % CORES)) for d in range...  1.07 us
  transfers between devices with their start and end apart: 18, of which 13 were waited for; matrix products, arithmetic and copies ran while one was open for 0% of the time, Pallas kernels for 9%

profile of v2, /device:TPU:0, one launch (start us, length us, event | category | flops | bytes accessed | tf_op | source)
XLA Modules:
  0.0 48.7 jit_solution(10299321066053928356)
XLA Ops:
  0.6 0.5 %collective-permute-start.1 = (bf16[384,1024]{1,0:T(8,128)(2,1)}, bf16[384,1024]{1,0:T(8,128)(2,1)S(1)}, u32[]{:S(2)}, u32[]{:S(2)}) collective-permute-start(bf16[384,1024]{1,0:T(8,128)(2,1)} %bitcast.9), channel_id=1, source_target_pairs={{0,4},{4,0},{8,12},{12,8},{16,20},{20,16},{24,28},{28,24},{1,5},{5... | collective-permute-start | bytes 2359304 | tf_op jit(solution)/shard_map/ppermute | solution.py:276
  1.1 0.8 %own_part_of_weight.1 = bf16[64,512]{1,0:T(8,128)(2,1)S(1)} custom-call(bf16[256,512]{1,0:T(8,128)(2,1)} %refs_4_.1), custom_call_target="tpu_custom_call" | custom-call | tf_op jit(solution)/shard_map/own_part_of_weight/pallas_call | solution.py:33
  2.0 3.7 %collective-permute-start = (bf16[64,512]{1,0:T(8,128)(2,1)S(1)}, bf16[64,512]{1,0:T(8,128)(2,1)S(1)}, u32[]{:S(2)}, u32[]{:S(2)}) collective-permute-start(bf16[64,512]{1,0:T(8,128)(2,1)S(1)} %own_part_of_weight.1), channel_id=1, source_target_pairs={{0,2},{1,3},{2,0},{3,1},{4,6},{5,7},{6,4},{7,5},{8,10},{9,11},{10,... | collective-permute-start | bytes 196616 | tf_op jit(solution)/shard_map/ppermute | solution.py:276
  5.7 1.6 %collective-permute-start.5 = (bf16[256,512]{1,0:T(8,128)(2,1)}, bf16[256,512]{1,0:T(8,128)(2,1)S(1)}, u32[]{:S(2)}, u32[]{:S(2)}) collective-permute-start(bf16[256,512]{1,0:T(8,128)(2,1)} %refs_4_.1), channel_id=1, source_target_pairs={{0,1},{1,0},{2,3},{3,2},{4,7},{5,6},{6,5},{7,4},{8,9},{9,8},{10,11... | collective-permute-start | bytes 786440 | tf_op jit(solution)/shard_map/ppermute | solution.py:294
  7.3 2.7 %collective-permute-done._.refs_1_ = bf16[64,512]{1,0:T(8,128)(2,1)S(1)} collective-permute-done((bf16[64,512]{1,0:T(8,128)(2,1)S(1)}, bf16[64,512]{1,0:T(8,128)(2,1)S(1)}, u32[]{:S(2)}, u32[]{:S(2)}) %collective-permute-start) | collective-permute-done | bytes 65568 | tf_op jit(solution)/shard_map/ppermute | solution.py:276
  9.9 1.6 %collective-permute-start.3 = (bf16[64,512]{1,0:T(8,128)(2,1)S(1)}, bf16[64,512]{1,0:T(8,128)(2,1)S(1)}, u32[]{:S(2)}, u32[]{:S(2)}) collective-permute-start(bf16[64,512]{1,0:T(8,128)(2,1)S(1)} %collective-permute-done._.refs_1_), channel_id=1, source_target_pairs={{0,8},{4,12},{8,0},{12,4},{16,24},{20,28},{24,16},{28,20},{1,9},{5... | collective-permute-start | bytes 196616 | tf_op jit(solution)/shard_map/ppermute | solution.py:276
  11.5 2.3 %prepared_operands.1 = (bf16[384,1024]{1,0:T(8,128)(2,1)S(1)}, bf16[384,512]{1,0:T(8,128)(2,1)S(1)}, bf16[384,512]{1,0:T(8,128)(2,1)S(1)}, bf16[384,512]{1,0:T(8...) custom-call(bf16[64,512]{1,0:T(8,128)(2,1)S(1)} %collective-permute-, ...), custom_call_target="tpu_custom_call" | custom-call | flops 10000000000 | tf_op jit(solution)/shard_map/prepared_operands/pallas_call | solution.py:33
  13.8 0.4 collective-permute-done.3.refs_3_
  14.2 1.1 %collective-permute-done.5.refs_5_ = bf16[256,512]{1,0:T(8,128)(2,1)S(1)} collective-permute-done((bf16[256,512]{1,0:T(8,128)(2,1)}, bf16[256,512]{1,0:T(8,128)(2,1)S(1)}, u32[]{:S(2)}, u32[]{:S(2)}) %collective-permute-start.5) | collective-permute-done | bytes 262176 | tf_op jit(solution)/shard_map/ppermute | solution.py:294
  15.3 0.5 %collective-permute-start.2 = (bf16[64,512]{1,0:T(8,128)(2,1)S(1)}, bf16[64,512]{1,0:T(8,128)(2,1)S(1)}, u32[]{:S(2)}, u32[]{:S(2)}) collective-permute-start(bf16[64,512]{1,0:T(8,128)(2,1)S(1)} %collective-permute-done._.refs_1_), channel_id=1, source_target_pairs={{0,4},{4,0},{8,12},{12,8},{16,20},{20,16},{24,28},{28,24},{1,5},{5... | collective-permute-start | bytes 196616 | tf_op jit(solution)/shard_map/ppermute | solution.py:276
  15.8 1.1 %collective-permute-done.2.refs_2_ = bf16[64,512]{1,0:T(8,128)(2,1)S(1)} collective-permute-done((bf16[64,512]{1,0:T(8,128)(2,1)S(1)}, bf16[64,512]{1,0:T(8,128)(2,1)S(1)}, u32[]{:S(2)}, u32[]{:S(2)}) %collective-permute-start.2) | collective-permute-done | bytes 65568 | tf_op jit(solution)/shard_map/ppermute | solution.py:276
  17.1 2.3 %attention_to_grad_query.1 = (bf16[384,512]{1,0:T(8,128)(2,1)S(1)}, bf16[384,512]{1,0:T(8,128)(2,1)S(1)}, f32[384,512]{1,0:T(8,128)S(1)}, bf16[384,512]{1,0:T(8,...) custom-call(bf16[256,512]{1,0:T(8,128)(2,1)S(1)} %get-tuple-element.38.refs_0_, ...), custom_call_target="tpu_custom_call" | custom-call | flops 603979776 | bytes 4718592 | tf_op jit(solution)/shard_map/attention_to_grad_query/pallas_call | solution.py:33
  19.4 0.2 collective-permute-start.7
  19.6 1.6 %collective-permute-done.7.got_ref = bf16[384,512]{1,0:T(8,128)(2,1)S(1)} collective-permute-done((bf16[384,512]{1,0:T(8,128)(2,1)S(1)}, bf16[384,512]{1,0:T(8,128)(2,1)S(1)}, u32[]{:S(2)}, u32[]{:S(2)}) %collective-permute-start.7) | collective-permute-done | bytes 393248 | tf_op jit(solution)/shard_map/ppermute | solution.py:276
  21.2 0.6 %weight_gradient.1 = (f32[64,1024]{1,0:T(8,128)S(1)}, bf16[64,1024]{1,0:T(8,128)(2,1)S(1)}, bf16[64,1024]{1,0:T(8,128)(2,1)S(1)}, bf16[64,1024]{1,0:T(8,128)(2,1)S(1)}) custom-call(bf16[1024,768]{1,0:T(8,128)(2,1)S(1)} %get-tuple-element.37.events_ref, bf16[384,512]{1,0:T(8,128)(2,1)S(1)} %get-tuple-element.49.own_ref, ...), custom_call_target="tpu_custom_call" | custom-call | flops 402653184 | bytes 2097152 | tf_op jit(solution)/shard_map/weight_gradient/pallas_call | solution.py:33
  21.8 1.6 %collective-permute-start.8 = (bf16[64,1024]{1,0:T(8,128)(2,1)S(1)}, bf16[64,1024]{1,0:T(8,128)(2,1)S(1)}, u32[]{:S(2)}, u32[]{:S(2)}) collective-permute-start(bf16[64,1024]{1,0:T(8,128)(2,1)S(1)} %get-tuple-element.60), channel_id=1, source_target_pairs={{0,8},{4,12},{8,0},{12,4},{16,24},{20,28},{24,16},{28,20},{1,9},{5... | collective-permute-start | bytes 393224 | tf_op jit(solution)/shard_map/ppermute | solution.py:276
  23.4 1.5 %collective-permute-start.9 = (bf16[64,1024]{1,0:T(8,128)(2,1)S(1)}, bf16[64,1024]{1,0:T(8,128)(2,1)S(1)}, u32[]{:S(2)}, u32[]{:S(2)}) collective-permute-start(bf16[64,1024]{1,0:T(8,128)(2,1)S(1)} %get-tuple-element.61), channel_id=1, source_target_pairs={{0,16},{4,20},{8,24},{12,28},{16,0},{20,4},{24,8},{28,12},{1,17},{... | collective-permute-start | bytes 393224 | tf_op jit(solution)/shard_map/ppermute | solution.py:276
  24.9 0.4 collective-permute-start.10
  25.4 1.4 %key_value_gate_gradients.1 = (bf16[384,512]{1,0:T(8,128)(2,1)}, bf16[384,512]{1,0:T(8,128)(2,1)}, bf16[384,512]{1,0:T(8,128)(2,1)}) custom-call(f32[64,1024]{1,0:T(8,128)S(1)} %get-tuple-element.50._.refs_0_, bf16[384,512]{1,0:T(8,128)(2,1)S(1)} %get-tuple-element.51.query_ref, f32[384,512]{1,0:T(8,128)S(1)} %get-tuple-element.52.normed_ref, ...), custom_call_target="tpu_custom_call" | custom-call | flops 100663296 | bytes 2359296 | tf_op jit(solution)/shard_map/key_value_gate_gradients/pallas_call | solution.py:33
  26.8 0.9 %collective-permute-done.8.refs_1_ = bf16[64,1024]{1,0:T(8,128)(2,1)S(1)} collective-permute-done((bf16[64,1024]{1,0:T(8,128)(2,1)S(1)}, bf16[64,1024]{1,0:T(8,128)(2,1)S(1)}, u32[]{:S(2)}, u32[]{:S(2)}) %collective-permute-start.8) | collective-permute-done | bytes 131104 | tf_op jit(solution)/shard_map/ppermute | solution.py:276
  27.8 3.8 %collective-permute-done.9.refs_2_ = bf16[64,1024]{1,0:T(8,128)(2,1)S(1)} collective-permute-done((bf16[64,1024]{1,0:T(8,128)(2,1)S(1)}, bf16[64,1024]{1,0:T(8,128)(2,1)S(1)}, u32[]{:S(2)}, u32[]{:S(2)}) %collective-permute-start.9) | collective-permute-done | bytes 131104 | tf_op jit(solution)/shard_map/ppermute | solution.py:276
  31.6 1.6 %collective-permute-start.12 = (bf16[64,512]{1,0:T(8,128)(2,1)S(1)}, bf16[64,512]{1,0:T(8,128)(2,1)S(1)}, u32[]{:S(2)}, u32[]{:S(2)}) collective-permute-start(bf16[64,512]{1,0:T(8,128)(2,1)S(1)} %get-tuple-element.65), channel_id=1, source_target_pairs={{0,1},{1,0},{2,3},{3,2},{4,7},{5,6},{6,5},{7,4},{8,9},{9,8},{10,11... | collective-permute-start | bytes 196616 | tf_op jit(solution)/shard_map/ppermute | solution.py:294
  33.1 3.6 %collective-permute-start.11 = (bf16[64,256]{1,0:T(8,128)(2,1)S(1)}, bf16[64,256]{1,0:T(8,128)(2,1)S(1)}, u32[]{:S(2)}, u32[]{:S(2)}) collective-permute-start(bf16[64,256]{1,0:T(8,128)(2,1)S(1)} %get-tuple-element.64), channel_id=1, source_target_pairs={{0,2},{1,3},{2,0},{3,1},{4,6},{5,7},{6,4},{7,5},{8,10},{9,11},{10,... | collective-permute-start | bytes 98312 | tf_op jit(solution)/shard_map/ppermute | solution.py:276
  36.8 2.6 %collective-permute-done.11.middle_ref = bf16[64,256]{1,0:T(8,128)(2,1)S(1)} collective-permute-done((bf16[64,256]{1,0:T(8,128)(2,1)S(1)}, bf16[64,256]{1,0:T(8,128)(2,1)S(1)}, u32[]{:S(2)}, u32[]{:S(2)}) %collective-permute-start.11) | collective-permute-done | bytes 32800 | tf_op jit(solution)/shard_map/ppermute | solution.py:276
  39.4 0.2 collective-permute-start.13
  39.6 1.1 %collective-permute-done.13.sibling_ref = bf16[64,512]{1,0:T(8,128)(2,1)S(1)} collective-permute-done((bf16[64,512]{1,0:T(8,128)(2,1)S(1)}, bf16[64,512]{1,0:T(8,128)(2,1)S(1)}, u32[]{:S(2)}, u32[]{:S(2)}) %collective-permute-start.13) | collective-permute-done | bytes 65568 | tf_op jit(solution)/shard_map/ppermute | solution.py:276
  40.7 1.1 %collective-permute-start.14 = (bf16[64,512]{1,0:T(8,128)(2,1)S(1)}, bf16[64,512]{1,0:T(8,128)(2,1)S(1)}, u32[]{:S(2)}, u32[]{:S(2)}) collective-permute-start(bf16[64,512]{1,0:T(8,128)(2,1)S(1)} %get-tuple-element.66.own_ref), channel_id=1, source_target_pairs={{0,8},{4,20},{8,0},{12,28},{16,24},{20,4},{24,16},{28,12},{1,9},{5... | collective-permute-start | bytes 196616 | tf_op jit(solution)/shard_map/ppermute | solution.py:459
  41.8 1.9 %collective-permute-start.16 = (bf16[32,512]{1,0:T(8,128)(2,1)S(1)}, bf16[32,512]{1,0:T(8,128)(2,1)S(1)}, u32[]{:S(2)}, u32[]{:S(2)}) collective-permute-start(bf16[32,512]{1,0:T(8,128)(2,1)S(1)} %get-tuple-element.67), channel_id=1, source_target_pairs={{0,24},{4,28},{8,16},{12,20},{16,8},{20,12},{24,0},{28,4},{1,25},{... | collective-permute-start | bytes 98312 | tf_op jit(solution)/shard_map/ppermute | solution.py:276
  43.7 1.8 %collective-permute-done.14.near_ref = bf16[64,512]{1,0:T(8,128)(2,1)S(1)} collective-permute-done((bf16[64,512]{1,0:T(8,128)(2,1)S(1)}, bf16[64,512]{1,0:T(8,128)(2,1)S(1)}, u32[]{:S(2)}, u32[]{:S(2)}) %collective-permute-start.14) | collective-permute-done | bytes 65568 | tf_op jit(solution)/shard_map/ppermute | solution.py:459
  45.4 1.2 %collective-permute-done.16.half_ref = bf16[32,512]{1,0:T(8,128)(2,1)S(1)} collective-permute-done((bf16[32,512]{1,0:T(8,128)(2,1)S(1)}, bf16[32,512]{1,0:T(8,128)(2,1)S(1)}, u32[]{:S(2)}, u32[]{:S(2)}) %collective-permute-start.16) | collective-permute-done | bytes 32800 | tf_op jit(solution)/shard_map/ppermute | solution.py:276
  46.6 1.2 %collective-permute-done.17.sibling_half_ref = bf16[32,512]{1,0:T(8,128)(2,1)S(1)} collective-permute-done((bf16[32,512]{1,0:T(8,128)(2,1)S(1)}, bf16[32,512]{1,0:T(8,128)(2,1)S(1)}, u32[]{:S(2)}, u32[]{:S(2)}) %collective-permute-start.17) | collective-permute-done | bytes 32800 | tf_op jit(solution)/shard_map/ppermute | solution.py:276
  47.8 0.8 %blocks_in_place.1 = f32[256,512]{1,0:T(8,128)} custom-call(bf16[64,512]{1,0:T(8,128)(2,1)S(1)} %get-tuple-element.66.own_ref, bf16[64,512]{1,0:T(8,128)(2,1)S(1)} %collective-permute-done.14.near_ref, bf16[64,512]{1,0:T(8,128)(2,1)S(1)} %collective-permute-done.15.sibling_near_ref, bf16[32,512]{1,0:T(8,128)(2,1)S(1)} %collective-permute-done.16.half_ref, ...), custom_call_target="tpu_custom_call" | custom-call | tf_op jit(solution)/shard_map/blocks_in_place/pallas_call | solution.py:33
  (13 shorter events, 0.3 us)
Async XLA Ops:
  0.6 10.9 %collective-permute-start.1 = (bf16[384,1024]{1,0:T(8,128)(2,1)}, bf16[384,1024]{1,0:T(8,128)(2,1)S(1)}, u32[]{:S(2)}, u32[]{:S(2)}) collective-permute-start(bf16[384,1024]{1,0:T(8,128)(2,1)} %bitcast.9), channel_id=1, source_target_pairs={{0,4},{4,0},{8,12},{12,8},{16,20},{20,16},{24,28},{28,24},{1,5},{5... | collective-permute-start | bytes 2359304 | tf_op jit(solution)/shard_map/ppermute | solution.py:276
  2.0 7.9 %collective-permute-start = (bf16[64,512]{1,0:T(8,128)(2,1)S(1)}, bf16[64,512]{1,0:T(8,128)(2,1)S(1)}, u32[]{:S(2)}, u32[]{:S(2)}) collective-permute-start(bf16[64,512]{1,0:T(8,128)(2,1)S(1)} %own_part_of_weight.1), channel_id=1, source_target_pairs={{0,2},{1,3},{2,0},{3,1},{4,6},{5,7},{6,4},{7,5},{8,10},{9,11},{10,... | collective-permute-start | bytes 196616 | tf_op jit(solution)/shard_map/ppermute | solution.py:276
  5.7 9.6 %collective-permute-start.5 = (bf16[256,512]{1,0:T(8,128)(2,1)}, bf16[256,512]{1,0:T(8,128)(2,1)S(1)}, u32[]{:S(2)}, u32[]{:S(2)}) collective-permute-start(bf16[256,512]{1,0:T(8,128)(2,1)} %refs_4_.1), channel_id=1, source_target_pairs={{0,1},{1,0},{2,3},{3,2},{4,7},{5,6},{6,5},{7,4},{8,9},{9,8},{10,11... | collective-permute-start | bytes 786440 | tf_op jit(solution)/shard_map/ppermute | solution.py:294
  9.9 4.3 %collective-permute-start.3 = (bf16[64,512]{1,0:T(8,128)(2,1)S(1)}, bf16[64,512]{1,0:T(8,128)(2,1)S(1)}, u32[]{:S(2)}, u32[]{:S(2)}) collective-permute-start(bf16[64,512]{1,0:T(8,128)(2,1)S(1)} %collective-permute-done._.refs_1_), channel_id=1, source_target_pairs={{0,8},{4,12},{8,0},{12,4},{16,24},{20,28},{24,16},{28,20},{1,9},{5... | collective-permute-start | bytes 196616 | tf_op jit(solution)/shard_map/ppermute | solution.py:276
  15.3 1.8 %collective-permute-start.6 = (bf16[256,512]{1,0:T(8,128)(2,1)S(1)}, bf16[256,512]{1,0:T(8,128)(2,1)S(1)}, u32[]{:S(2)}, u32[]{:S(2)}) collective-permute-start(bf16[256,512]{1,0:T(8,128)(2,1)S(1)} %collective-permute-done.5.refs_5_), channel_id=1, source_target_pairs={{0,4},{4,0},{8,12},{12,8},{16,20},{20,16},{24,28},{28,24},{1,5},{5... | collective-permute-start | bytes 786440 | tf_op jit(solution)/shard_map/ppermute | solution.py:276
  15.3 1.6 %collective-permute-start.2 = (bf16[64,512]{1,0:T(8,128)(2,1)S(1)}, bf16[64,512]{1,0:T(8,128)(2,1)S(1)}, u32[]{:S(2)}, u32[]{:S(2)}) collective-permute-start(bf16[64,512]{1,0:T(8,128)(2,1)S(1)} %collective-permute-done._.refs_1_), channel_id=1, source_target_pairs={{0,4},{4,0},{8,12},{12,8},{16,20},{20,16},{24,28},{28,24},{1,5},{5... | collective-permute-start | bytes 196616 | tf_op jit(solution)/shard_map/ppermute | solution.py:276
  15.8 1.3 %collective-permute-start.4 = (bf16[64,512]{1,0:T(8,128)(2,1)S(1)}, bf16[64,512]{1,0:T(8,128)(2,1)S(1)}, u32[]{:S(2)}, u32[]{:S(2)}) collective-permute-start(bf16[64,512]{1,0:T(8,128)(2,1)S(1)} %collective-permute-done.3.refs_3_), channel_id=1, source_target_pairs={{0,4},{4,0},{8,12},{12,8},{16,20},{20,16},{24,28},{28,24},{1,5},{5... | collective-permute-start | bytes 196616 | tf_op jit(solution)/shard_map/ppermute | solution.py:276
  19.4 1.8 %collective-permute-start.7 = (bf16[384,512]{1,0:T(8,128)(2,1)S(1)}, bf16[384,512]{1,0:T(8,128)(2,1)S(1)}, u32[]{:S(2)}, u32[]{:S(2)}) collective-permute-start(bf16[384,512]{1,0:T(8,128)(2,1)S(1)} %get-tuple-element.49.own_ref), channel_id=1, source_target_pairs={{0,4},{4,0},{8,12},{12,8},{16,20},{20,16},{24,28},{28,24},{1,5},{5... | collective-permute-start | bytes 1179656 | tf_op jit(solution)/shard_map/ppermute | solution.py:276
  21.8 5.9 %collective-permute-start.8 = (bf16[64,1024]{1,0:T(8,128)(2,1)S(1)}, bf16[64,1024]{1,0:T(8,128)(2,1)S(1)}, u32[]{:S(2)}, u32[]{:S(2)}) collective-permute-start(bf16[64,1024]{1,0:T(8,128)(2,1)S(1)} %get-tuple-element.60), channel_id=1, source_target_pairs={{0,8},{4,12},{8,0},{12,4},{16,24},{20,28},{24,16},{28,20},{1,9},{5... | collective-permute-start | bytes 393224 | tf_op jit(solution)/shard_map/ppermute | solution.py:276
  23.4 8.1 %collective-permute-start.9 = (bf16[64,1024]{1,0:T(8,128)(2,1)S(1)}, bf16[64,1024]{1,0:T(8,128)(2,1)S(1)}, u32[]{:S(2)}, u32[]{:S(2)}) collective-permute-start(bf16[64,1024]{1,0:T(8,128)(2,1)S(1)} %get-tuple-element.61), channel_id=1, source_target_pairs={{0,16},{4,20},{8,24},{12,28},{16,0},{20,4},{24,8},{28,12},{1,17},{... | collective-permute-start | bytes 393224 | tf_op jit(solution)/shard_map/ppermute | solution.py:276
  24.9 6.6 %collective-permute-start.10 = (bf16[64,1024]{1,0:T(8,128)(2,1)S(1)}, bf16[64,1024]{1,0:T(8,128)(2,1)S(1)}, u32[]{:S(2)}, u32[]{:S(2)}) collective-permute-start(bf16[64,1024]{1,0:T(8,128)(2,1)S(1)} %get-tuple-element.62), channel_id=1, source_target_pairs={{0,24},{4,28},{8,16},{12,20},{16,8},{20,12},{24,0},{28,4},{1,25},{... | collective-permute-start | bytes 393224 | tf_op jit(solution)/shard_map/ppermute | solution.py:276
  31.6 7.8 %collective-permute-start.12 = (bf16[64,512]{1,0:T(8,128)(2,1)S(1)}, bf16[64,512]{1,0:T(8,128)(2,1)S(1)}, u32[]{:S(2)}, u32[]{:S(2)}) collective-permute-start(bf16[64,512]{1,0:T(8,128)(2,1)S(1)} %get-tuple-element.65), channel_id=1, source_target_pairs={{0,1},{1,0},{2,3},{3,2},{4,7},{5,6},{6,5},{7,4},{8,9},{9,8},{10,11... | collective-permute-start | bytes 196616 | tf_op jit(solution)/shard_map/ppermute | solution.py:294
  33.1 6.2 %collective-permute-start.11 = (bf16[64,256]{1,0:T(8,128)(2,1)S(1)}, bf16[64,256]{1,0:T(8,128)(2,1)S(1)}, u32[]{:S(2)}, u32[]{:S(2)}) collective-permute-start(bf16[64,256]{1,0:T(8,128)(2,1)S(1)} %get-tuple-element.64), channel_id=1, source_target_pairs={{0,2},{1,3},{2,0},{3,1},{4,6},{5,7},{6,4},{7,5},{8,10},{9,11},{10,... | collective-permute-start | bytes 98312 | tf_op jit(solution)/shard_map/ppermute | solution.py:276
  39.4 1.3 %collective-permute-start.13 = (bf16[64,512]{1,0:T(8,128)(2,1)S(1)}, bf16[64,512]{1,0:T(8,128)(2,1)S(1)}, u32[]{:S(2)}, u32[]{:S(2)}) collective-permute-start(bf16[64,512]{1,0:T(8,128)(2,1)S(1)} %sum_over_shards.1.own_ref), channel_id=1, source_target_pairs={{0,4},{4,0},{8,12},{12,8},{16,20},{20,16},{24,28},{28,24},{1,5},{5... | collective-permute-start | bytes 196616 | tf_op jit(solution)/shard_map/ppermute | solution.py:276
  40.7 4.7 %collective-permute-start.14 = (bf16[64,512]{1,0:T(8,128)(2,1)S(1)}, bf16[64,512]{1,0:T(8,128)(2,1)S(1)}, u32[]{:S(2)}, u32[]{:S(2)}) collective-permute-start(bf16[64,512]{1,0:T(8,128)(2,1)S(1)} %get-tuple-element.66.own_ref), channel_id=1, source_target_pairs={{0,8},{4,20},{8,0},{12,28},{16,24},{20,4},{24,16},{28,12},{1,9},{5... | collective-permute-start | bytes 196616 | tf_op jit(solution)/shard_map/ppermute | solution.py:459
  41.8 4.8 %collective-permute-start.16 = (bf16[32,512]{1,0:T(8,128)(2,1)S(1)}, bf16[32,512]{1,0:T(8,128)(2,1)S(1)}, u32[]{:S(2)}, u32[]{:S(2)}) collective-permute-start(bf16[32,512]{1,0:T(8,128)(2,1)S(1)} %get-tuple-element.67), channel_id=1, source_target_pairs={{0,24},{4,28},{8,16},{12,20},{16,8},{20,12},{24,0},{28,4},{1,25},{... | collective-permute-start | bytes 98312 | tf_op jit(solution)/shard_map/ppermute | solution.py:276
  45.4 2.4 %collective-permute-start.15 = (bf16[64,512]{1,0:T(8,128)(2,1)S(1)}, bf16[64,512]{1,0:T(8,128)(2,1)S(1)}, u32[]{:S(2)}, u32[]{:S(2)}) collective-permute-start(bf16[64,512]{1,0:T(8,128)(2,1)S(1)} %collective-permute-done.14.near_ref), channel_id=1, source_target_pairs={{0,4},{4,0},{8,12},{12,8},{16,20},{20,16},{24,28},{28,24},{1,5},{5... | collective-permute-start | bytes 196616 | tf_op jit(solution)/shard_map/ppermute | solution.py:276
  46.6 1.2 %collective-permute-start.17 = (bf16[32,512]{1,0:T(8,128)(2,1)S(1)}, bf16[32,512]{1,0:T(8,128)(2,1)S(1)}, u32[]{:S(2)}, u32[]{:S(2)}) collective-permute-start(bf16[32,512]{1,0:T(8,128)(2,1)S(1)} %collective-permute-done.16.half_ref), channel_id=1, source_target_pairs={{0,4},{4,0},{8,12},{12,8},{16,20},{20,16},{24,28},{28,24},{1,5},{5... | collective-permute-start | bytes 98312 | tf_op jit(solution)/shard_map/ppermute | solution.py:276

commit v3 on v2

--- a/solution.py
+++ b/solution.py
@@ -189,33 +189,38 @@
 
 
 def gradient_kernel(pairs, events_ref, own_ref, got_ref, *refs):
-    outs, both_ref, total_ref = refs[:-2], refs[-2], refs[-1]
+    outs, both_ref, picked_ref = refs[:-2], refs[-2], refs[-1]
     rows, width = own_ref.shape
-    shard_rows = total_ref.shape[0]
     half = width // CORES
     both_ref[:rows] = own_ref[...]
     both_ref[rows:] = got_ref[...]
-    core, here = lax.rem(lax.axis_index("dp"), CORES), lax.axis_index("fsdp")
-
-    def term(shard, columns):
-        place = pl.ds(pl.multiple_of(shard * shard_rows, shard_rows), shard_rows)
-        return dot(events_ref[place], both_ref[:, columns])
-
-    at = 0
-    for flips in pairs:
-        total_ref[:, at : at + width] = term(
-            here ^ jnp.where(core == 0, flips[0], flips[1]), slice(None)
-        )
-        at += width
-    columns = pl.ds(pl.multiple_of(core * half, half), half)
-    for shard in (here, here ^ (lax.axis_size("fsdp") // 2)):
-        total_ref[:, at : at + half] = term(shard, columns)
-        at += half
+    device, here = lax.axis_index("dp"), lax.axis_index("fsdp")
     part_rows = outs[0].shape[0]
-    chip = lax.div(lax.axis_index("dp"), CORES)
-    for k, out in enumerate(outs):
-        start = pl.multiple_of((chip ^ k) * part_rows, part_rows)
-        out[...] = total_ref[pl.ds(start, part_rows)].astype(out.dtype)
+    shard_rows = events_ref.shape[0] // lax.axis_size("fsdp")
+
+    def core_of(k):
+        return lax.rem(device, CORES) ^ (1 if k else 0)
+
+    def add(picks, columns, at, wide):
+        for i, (k, shard) in enumerate(picks):
+            start = shard * shard_rows + (lax.div(device, CORES) ^ k) * part_rows
+            place = pl.ds(pl.multiple_of(start, part_rows), part_rows)
+            picked_ref[i * part_rows : (i + 1) * part_rows] = events_ref[place]
+        total = dot(picked_ref[: len(picks) * part_rows], both_ref[:, columns])
+        for i, (k, _) in enumerate(picks):
+            block = total[i * part_rows : (i + 1) * part_rows]
+            outs[k][:, at(i) : at(i) + wide] = block.astype(outs[k].dtype)
+
+    chips = range(len(outs))
+    for p, flips in enumerate(pairs):
+        picks = [(k, here ^ jnp.where(core_of(k) == 0, flips[0], flips[1])) for k in chips]
+        add(picks, slice(None), lambda i: p * width, width)
+    after = len(pairs) * width
+    for group in (chips[:1], chips[1:]):
+        columns = pl.ds(pl.multiple_of(core_of(group[0]) * half, half), half)
+        shards = (here, here ^ (lax.axis_size("fsdp") // 2))
+        picks = [(k, shard) for k in group for shard in shards]
+        add(picks, columns, lambda i: after + i % 2 * half, half)
 
 
 def chip_sum_kernel(term_count, _, *refs):
@@ -239,35 +244,27 @@
     half = own_ref.shape[1]
     core = lax.rem(lax.axis_index("dp"), CORES)
     columns = pl.ds(pl.multiple_of(core * half, half), half)
-    total_ref[:, columns] += own_ref[...] + middle_ref[...].astype(jnp.float32)
+    total_ref[:, columns] += own_ref[...]
+    columns = pl.ds(pl.multiple_of((1 - core) * half, half), half)
+    total_ref[:, columns] += middle_ref[...].astype(jnp.float32)
     out_ref[...] = total_ref[...].astype(out_ref.dtype)
 
 
-def mean_kernel(count, own_ref, sibling_ref, out_ref, half_ref):
+def mean_kernel(count, own_ref, sibling_ref, out_ref):
     total = own_ref[...].astype(jnp.float32) + sibling_ref[...].astype(jnp.float32)
     out_ref[...] = (total / count).astype(out_ref.dtype)
-    rows = half_ref.shape[0]
-    core = lax.rem(lax.axis_index("dp"), CORES)
-    half_ref[...] = out_ref[pl.ds(pl.multiple_of(core * rows, rows), rows)]
-
-
-def place_kernel(own_ref, near_ref, sibling_near_ref, half_ref, sibling_half_ref, out_ref, held_ref,
-                 sems):
-    rows, half = own_ref.shape[0], half_ref.shape[0]
-    core, chip = lax.rem(lax.axis_index("dp"), CORES), lax.div(lax.axis_index("dp"), CORES)
-    blocks = (
-        (own_ref, chip * rows),
-        (near_ref, (chip ^ (1 + core)) * rows),
-        (sibling_near_ref, (chip ^ (2 - core)) * rows),
-        (half_ref, (chip ^ 3) * rows + core * half),
-        (sibling_half_ref, (chip ^ 3) * rows + (1 - core) * half),
-    )
+
+
+def place_kernel(*refs):
+    blocks, (out_ref, held_ref, sems) = refs[:-3], refs[-3:]
+    rows = blocks[0].shape[0]
+    chip = lax.div(lax.axis_index("dp"), CORES)
     copies = []
-    for i, (block_ref, start) in enumerate(blocks):
-        place = pl.ds(pl.multiple_of(start, half), block_ref.shape[0])
+    for k, block_ref in enumerate(blocks):
+        place = pl.ds(pl.multiple_of((chip ^ k) * rows, rows), rows)
         held_ref[place] = block_ref[...].astype(held_ref.dtype)
-        copies.append(pltpu.make_async_copy(held_ref.at[place], out_ref.at[place], sems.at[i]))
-        copies[i].start()
+        copies.append(pltpu.make_async_copy(held_ref.at[place], out_ref.at[place], sems.at[k]))
+        copies[k].start()
     for copy in copies:
         copy.wait()
 
@@ -276,22 +273,25 @@
     return lax.ppermute(block, axis, [(i, i ^ bits) for i in range(count)])
 
 
-def far_first(count, send):
-    return [send(k) for k in range(count - 1, 0, -1)][::-1]
-
-
-def shard_pairs(fsdp_count):
-    others = [d for d in range(1, fsdp_count) if d != fsdp_count // 2]
-    return list(zip(others[::2], others[1::2]))
-
-
-def flip_by_core(block, flips, dp_count, fsdp_count):
+def cross(block, dp_count, fsdp_count, chip_bits, shard_bits):
     pairs = [
-        (d * fsdp_count + z, d * fsdp_count + (z ^ flips[d % CORES]))
+        (
+            d * fsdp_count + z,
+            (d ^ (chip_bits * CORES) ^ 1) * fsdp_count + (z ^ shard_bits[d % CORES]),
+        )
         for d in range(dp_count)
         for z in range(fsdp_count)
     ]
     return lax.ppermute(block, BOTH, pairs)
+
+
+def far_first(count, send):
+    return [send(k) for k in range(count - 1, 0, -1)][::-1]
+
+
+def shard_pairs(fsdp_count):
+    others = [d for d in range(1, fsdp_count) if d != fsdp_count // 2]
+    return list(zip(others[::2], others[1::2]))
 
 
 def across_z(weight, dp_count, fsdp_count):
@@ -305,19 +305,21 @@
         jax.ShapeDtypeStruct((rows // group, weight.shape[1]), weight.dtype),
         [pltpu.SemaphoreType.DMA],
     )
-    middle = fsdp_count // 2
     weight, part = lax.optimization_barrier((weight, part))
-    arrived = [(flip(part, "fsdp", fsdp_count, middle), (middle, middle), 0)]
+    middle = (fsdp_count // 2,) * CORES
+    arrived = [(cross(part, dp_count, fsdp_count, 0, middle), middle, 1)]
     for flips in shard_pairs(fsdp_count):
-        arrived.append((flip_by_core(weight, flips, dp_count, fsdp_count), flips, None))
+        block = cross(weight, dp_count, fsdp_count, 0, flips)
+        arrived.append((block, flips[::-1], None))
     return group, arrived
 
 
-def share(group, arrived, ready, dp_count):
+def share(group, arrived, ready, dp_count, fsdp_count):
     block, flips, member = arrived[0]
     own = [(block, flips, member)]
     if group == 4:
-        own.append((flip(block, "dp", dp_count, 2), flips, member ^ 2))
+        passed = cross(block, dp_count, fsdp_count, 1, (0,) * CORES)
+        own.append((passed, flips, member ^ 3))
     for block, flips, member in arrived[1:]:
         own.append((lax.optimization_barrier((block, own[-1][0], ready))[0], flips, member))
     found = []
@@ -376,7 +378,7 @@
     )
     near_events, near_keys, near_values, near_cotangent, near_weight = prepared[:5]
     events_t, keys_t, values_t, weight, gated, first = prepared[5:]
-    found = [(near_weight, ((0, 0), None))] + share(group, arrived, first, dp_count)
+    found = [(near_weight, ((0, 0), None))] + share(group, arrived, first, dp_count, fsdp_count)
     pieces, origins = zip(*found)
     blocks = shape(slots * HEADS, span, span)
     grad_query, query, normed, grad_mixed, attention, grad_scores = call(
@@ -401,7 +403,7 @@
         moved=24 * rows * width,
     )
     part_rows = shard_rows // chips
-    staged = chips == 4 and part_rows % 32 == 0 and fsdp_count % 4 == 0
+    staged = part_rows % 16 == 0 and fsdp_count % 4 == 0
     terms = [grad_query]
     if staged:
         pairs = shard_pairs(fsdp_count)
@@ -414,7 +416,7 @@
             tuple(shape(part_rows, columns, dtype=bf16 if k else f32) for k in range(chips)),
             [
                 pltpu.VMEM((CORES * rows, width), bf16),
-                pltpu.VMEM((shard_rows, columns), f32),
+                pltpu.VMEM((2 * chips * part_rows, CORES * rows), bf16),
             ],
             flops=4 * rows * shard_rows * columns,
             moved=2 * model_width * (2 * rows + half_width),
@@ -429,7 +431,12 @@
         moved=12 * rows * width,
     )
     if staged:
-        terms = [terms[0]] + far_first(chips, lambda k: flip(terms[k], "dp", dp_count, k * CORES))
+        alike = (0,) * CORES
+
+        def to_chip(block, k):
+            return cross(block, dp_count, fsdp_count, k, alike)
+
+        terms = [terms[0]] + far_first(chips, lambda k: to_chip(terms[k], k))
         sums = call(
             functools.partial(chip_sum_kernel, chips),
             "sum_over_chips",
@@ -438,8 +445,8 @@
             (shape(part_rows, width),) * len(pairs)
             + (shape(part_rows, half_width, dtype=f32), shape(part_rows, half_width)),
         )
-        wholes = [flip_by_core(a, p, dp_count, fsdp_count) for a, p in zip(sums, pairs)]
-        middle = flip(sums[-1], "fsdp", fsdp_count, fsdp_count // 2)
+        wholes = [cross(a, dp_count, fsdp_count, 0, p) for a, p in zip(sums, pairs)]
+        middle = cross(sums[-1], dp_count, fsdp_count, 0, (fsdp_count // 2,) * CORES)
         total = call(
             shard_sum_kernel,
             "sum_over_shards",
@@ -448,24 +455,21 @@
             shape(part_rows, width),
             [pltpu.VMEM((part_rows, width), f32)],
         )
-        mean, half = call(
+        mean = call(
             functools.partial(mean_kernel, total_seqs),
             "mean_of_both_cores",
             [total, flip(total, "dp", dp_count, 1)],
             [NEAR] * 2,
-            (shape(part_rows, width), shape(part_rows // CORES, width)),
-        )
-        half = flip(half, "dp", dp_count, 3 * CORES)
-        near = lax.ppermute(
-            mean, "dp", [(d, d ^ (CORES * (1 + d % CORES))) for d in range(dp_count)]
-        )
+            shape(part_rows, width),
+        )
+        found = [mean] + far_first(chips, lambda k: to_chip(mean, k))
         grad_weight = call(
             place_kernel,
             "blocks_in_place",
-            [mean, near, flip(near, "dp", dp_count, 1), half, flip(half, "dp", dp_count, 1)],
-            [NEAR] * 5,
+            found,
+            [NEAR] * chips,
             shape(shard_rows, width, dtype=f32),
-            [pltpu.VMEM((shard_rows, width), f32), pltpu.SemaphoreType.DMA((5,))],
+            [pltpu.VMEM((shard_rows, width), f32), pltpu.SemaphoreType.DMA((chips,))],
             out_specs=FAR,
         )
     else:

time: 48.9 us -> 48 us (0.982)
  starting transfers between devices: 19.9 us -> 18.3 us
  waiting for transfers between devices: 19.6 us -> 20.4 us
    ppermute x3 -> x11, waiting for transfers between devices: 2.88 us -> 16.6 us  [cross(): return lax.ppermute(block, BOTH, pairs)]
    ppermute x15 -> x6, waiting for transfers between devices: 16.7 us -> 3.72 us  [flip(): return lax.ppermute(block, axis, [(i, i ^ bits) for i in range(count)])]
    ppermute x15 -> x6, starting transfers between devices: 15.7 us -> 3.11 us  [flip(): return lax.ppermute(block, axis, [(i, i ^ bits) for i in range(count)])]
    ppermute x3 -> x11, starting transfers between devices: 4.2 us -> 15.2 us  [cross(): return lax.ppermute(block, BOTH, pairs)]
  transfers between devices with their start and end apart: 18 -> 17, of which waited for: 13 -> 13; matrix products, arithmetic and copies ran while one was open for 0% -> 0% of each run, Pallas kernels for 9% -> 10%
where the time goes in v3:
time: 48 us; the launch traced here: 47.8 us
  waiting for transfers between devices  20.4 us (42%)
  starting transfers between devices  18.3 us (38%)
  Pallas kernels  8.44 us (18%)
  between operations  0.69 us (1%)
    ppermute x11, waiting for transfers between devices, cross(): return lax.ppermute(block, BOTH, pairs)  16.6 us
    ppermute x11, starting transfers between devices, cross(): return lax.ppermute(block, BOTH, pairs)  15.2 us
    pallas_call x9, Pallas kernels, call(): pl.pallas_call(kernel, out_shape=out_shape, in_specs=in_specs, out_specs=...  8.44 us
    ppermute x6, waiting for transfers between devices, flip(): return lax.ppermute(block, axis, [(i, i ^ bits) for i in range(count)])  3.72 us
    ppermute x6, starting transfers between devices, flip(): return lax.ppermute(block, axis, [(i, i ^ bits) for i in range(count)])  3.11 us
  transfers between devices with their start and end apart: 17, of which 13 were waited for; matrix products, arithmetic and copies ran while one was open for 0% of the time, Pallas kernels for 10%

profile of v3, /device:TPU:0, one launch (start us, length us, event | category | flops | bytes accessed | tf_op | source)
XLA Modules:
  0.0 47.8 jit_solution(14021860771436515945)
XLA Ops:
  0.6 0.5 %collective-permute-start.1 = (bf16[384,1024]{1,0:T(8,128)(2,1)}, bf16[384,1024]{1,0:T(8,128)(2,1)S(1)}, u32[]{:S(2)}, u32[]{:S(2)}) collective-permute-start(bf16[384,1024]{1,0:T(8,128)(2,1)} %bitcast.9), channel_id=1, source_target_pairs={{0,4},{4,0},{8,12},{12,8},{16,20},{20,16},{24,28},{28,24},{1,5},{5... | collective-permute-start | bytes 2359304 | tf_op jit(solution)/shard_map/ppermute | solution.py:273
  1.1 0.8 %own_part_of_weight.1 = bf16[64,512]{1,0:T(8,128)(2,1)S(1)} custom-call(bf16[256,512]{1,0:T(8,128)(2,1)} %refs_4_.1), custom_call_target="tpu_custom_call" | custom-call | tf_op jit(solution)/shard_map/own_part_of_weight/pallas_call | solution.py:33
  2.0 3.8 %collective-permute-start = (bf16[64,512]{1,0:T(8,128)(2,1)S(1)}, bf16[64,512]{1,0:T(8,128)(2,1)S(1)}, u32[]{:S(2)}, u32[]{:S(2)}) collective-permute-start(bf16[64,512]{1,0:T(8,128)(2,1)S(1)} %own_part_of_weight.1), channel_id=1, source_target_pairs={{0,6},{1,7},{2,4},{3,5},{4,2},{5,3},{6,0},{7,1},{8,14},{9,15},{10,... | collective-permute-start | bytes 196616 | tf_op jit(solution)/shard_map/ppermute | solution.py:285
  5.8 1.2 %collective-permute-start.5 = (bf16[256,512]{1,0:T(8,128)(2,1)}, bf16[256,512]{1,0:T(8,128)(2,1)S(1)}, u32[]{:S(2)}, u32[]{:S(2)}) collective-permute-start(bf16[256,512]{1,0:T(8,128)(2,1)} %refs_4_.1), channel_id=1, source_target_pairs={{0,5},{1,4},{2,7},{3,6},{4,3},{5,2},{6,1},{7,0},{8,13},{9,12},{10,... | collective-permute-start | bytes 786440 | tf_op jit(solution)/shard_map/ppermute | solution.py:285
  7.0 2.7 %collective-permute-done._.refs_1_ = bf16[64,512]{1,0:T(8,128)(2,1)S(1)} collective-permute-done((bf16[64,512]{1,0:T(8,128)(2,1)S(1)}, bf16[64,512]{1,0:T(8,128)(2,1)S(1)}, u32[]{:S(2)}, u32[]{:S(2)}) %collective-permute-start) | collective-permute-done | bytes 65568 | tf_op jit(solution)/shard_map/ppermute | solution.py:285
  9.7 1.1 %collective-permute-start.3 = (bf16[64,512]{1,0:T(8,128)(2,1)S(1)}, bf16[64,512]{1,0:T(8,128)(2,1)S(1)}, u32[]{:S(2)}, u32[]{:S(2)}) collective-permute-start(bf16[64,512]{1,0:T(8,128)(2,1)S(1)} %collective-permute-done._.refs_1_), channel_id=1, source_target_pairs={{0,12},{1,13},{2,14},{3,15},{4,8},{5,9},{6,10},{7,11},{8,4},{9,5},... | collective-permute-start | bytes 196616 | tf_op jit(solution)/shard_map/ppermute | solution.py:285
  10.8 2.3 %prepared_operands.1 = (bf16[384,1024]{1,0:T(8,128)(2,1)S(1)}, bf16[384,512]{1,0:T(8,128)(2,1)S(1)}, bf16[384,512]{1,0:T(8,128)(2,1)S(1)}, bf16[384,512]{1,0:T(8...) custom-call(bf16[64,512]{1,0:T(8,128)(2,1)S(1)} %collective-permute-, ...), custom_call_target="tpu_custom_call" | custom-call | flops 10000000000 | tf_op jit(solution)/shard_map/prepared_operands/pallas_call | solution.py:33
  13.2 0.7 %collective-permute-done.3.refs_3_ = bf16[64,512]{1,0:T(8,128)(2,1)S(1)} collective-permute-done((bf16[64,512]{1,0:T(8,128)(2,1)S(1)}, bf16[64,512]{1,0:T(8,128)(2,1)S(1)}, u32[]{:S(2)}, u32[]{:S(2)}) %collective-permute-start.3) | collective-permute-done | bytes 65568 | tf_op jit(solution)/shard_map/ppermute | solution.py:285
  13.9 1.3 %collective-permute-done.5.refs_5_ = bf16[256,512]{1,0:T(8,128)(2,1)S(1)} collective-permute-done((bf16[256,512]{1,0:T(8,128)(2,1)}, bf16[256,512]{1,0:T(8,128)(2,1)S(1)}, u32[]{:S(2)}, u32[]{:S(2)}) %collective-permute-start.5) | collective-permute-done | bytes 262176 | tf_op jit(solution)/shard_map/ppermute | solution.py:285
  15.2 0.5 %collective-permute-start.2 = (bf16[64,512]{1,0:T(8,128)(2,1)S(1)}, bf16[64,512]{1,0:T(8,128)(2,1)S(1)}, u32[]{:S(2)}, u32[]{:S(2)}) collective-permute-start(bf16[64,512]{1,0:T(8,128)(2,1)S(1)} %collective-permute-done._.refs_1_), channel_id=1, source_target_pairs={{0,4},{4,0},{8,12},{12,8},{16,20},{20,16},{24,28},{28,24},{1,5},{5... | collective-permute-start | bytes 196616 | tf_op jit(solution)/shard_map/ppermute | solution.py:273
  15.7 1.1 %collective-permute-done.2.refs_2_ = bf16[64,512]{1,0:T(8,128)(2,1)S(1)} collective-permute-done((bf16[64,512]{1,0:T(8,128)(2,1)S(1)}, bf16[64,512]{1,0:T(8,128)(2,1)S(1)}, u32[]{:S(2)}, u32[]{:S(2)}) %collective-permute-start.2) | collective-permute-done | bytes 65568 | tf_op jit(solution)/shard_map/ppermute | solution.py:273
  17.0 2.3 %attention_to_grad_query.1 = (bf16[384,512]{1,0:T(8,128)(2,1)S(1)}, bf16[384,512]{1,0:T(8,128)(2,1)S(1)}, f32[384,512]{1,0:T(8,128)S(1)}, bf16[384,512]{1,0:T(8,...) custom-call(bf16[256,512]{1,0:T(8,128)(2,1)S(1)} %get-tuple-element.36.refs_0_, ...), custom_call_target="tpu_custom_call" | custom-call | flops 603979776 | bytes 4718592 | tf_op jit(solution)/shard_map/attention_to_grad_query/pallas_call | solution.py:33
  19.5 1.6 %collective-permute-done.7.got_ref = bf16[384,512]{1,0:T(8,128)(2,1)S(1)} collective-permute-done((bf16[384,512]{1,0:T(8,128)(2,1)S(1)}, bf16[384,512]{1,0:T(8,128)(2,1)S(1)}, u32[]{:S(2)}, u32[]{:S(2)}) %collective-permute-start.7) | collective-permute-done | bytes 393248 | tf_op jit(solution)/shard_map/ppermute | solution.py:273
  21.1 0.6 %weight_gradient.1 = (f32[64,1024]{1,0:T(8,128)S(1)}, bf16[64,1024]{1,0:T(8,128)(2,1)S(1)}, bf16[64,1024]{1,0:T(8,128)(2,1)S(1)}, bf16[64,1024]{1,0:T(8,128)(2,1)S(1)}) custom-call(bf16[1024,768]{1,0:T(8,128)(2,1)S(1)} %get-tuple-element.35.events_ref, bf16[384,512]{1,0:T(8,128)(2,1)S(1)} %get-tuple-element.47.own_ref, ...), custom_call_target="tpu_custom_call" | custom-call | flops 402653184 | bytes 2097152 | tf_op jit(solution)/shard_map/weight_gradient/pallas_call | solution.py:33
  21.7 1.3 %collective-permute-start.8 = (bf16[64,1024]{1,0:T(8,128)(2,1)S(1)}, bf16[64,1024]{1,0:T(8,128)(2,1)S(1)}, u32[]{:S(2)}, u32[]{:S(2)}) collective-permute-start(bf16[64,1024]{1,0:T(8,128)(2,1)S(1)} %get-tuple-element.58), channel_id=1, source_target_pairs={{0,12},{1,13},{2,14},{3,15},{4,8},{5,9},{6,10},{7,11},{8,4},{9,5},... | collective-permute-start | bytes 393224 | tf_op jit(solution)/shard_map/ppermute | solution.py:285
  23.0 1.5 %collective-permute-start.9 = (bf16[64,1024]{1,0:T(8,128)(2,1)S(1)}, bf16[64,1024]{1,0:T(8,128)(2,1)S(1)}, u32[]{:S(2)}, u32[]{:S(2)}) collective-permute-start(bf16[64,1024]{1,0:T(8,128)(2,1)S(1)} %get-tuple-element.59), channel_id=1, source_target_pairs={{0,20},{1,21},{2,22},{3,23},{4,16},{5,17},{6,18},{7,19},{8,28},{9,... | collective-permute-start | bytes 393224 | tf_op jit(solution)/shard_map/ppermute | solution.py:285
  24.5 0.2 collective-permute-start.10
  24.7 1.4 %key_value_gate_gradients.1 = (bf16[384,512]{1,0:T(8,128)(2,1)}, bf16[384,512]{1,0:T(8,128)(2,1)}, bf16[384,512]{1,0:T(8,128)(2,1)}) custom-call(f32[64,1024]{1,0:T(8,128)S(1)} %get-tuple-element.48._.refs_0_, bf16[384,512]{1,0:T(8,128)(2,1)S(1)} %get-tuple-element.49.query_ref, f32[384,512]{1,0:T(8,128)S(1)} %get-tuple-element.50.normed_ref, ...), custom_call_target="tpu_custom_call" | custom-call | flops 100663296 | bytes 2359296 | tf_op jit(solution)/shard_map/key_value_gate_gradients/pallas_call | solution.py:33
  26.1 1.0 %collective-permute-done.8.refs_1_ = bf16[64,1024]{1,0:T(8,128)(2,1)S(1)} collective-permute-done((bf16[64,1024]{1,0:T(8,128)(2,1)S(1)}, bf16[64,1024]{1,0:T(8,128)(2,1)S(1)}, u32[]{:S(2)}, u32[]{:S(2)}) %collective-permute-start.8) | collective-permute-done | bytes 131104 | tf_op jit(solution)/shard_map/ppermute | solution.py:285
  27.2 3.5 %collective-permute-done.9.refs_2_ = bf16[64,1024]{1,0:T(8,128)(2,1)S(1)} collective-permute-done((bf16[64,1024]{1,0:T(8,128)(2,1)S(1)}, bf16[64,1024]{1,0:T(8,128)(2,1)S(1)}, u32[]{:S(2)}, u32[]{:S(2)}) %collective-permute-start.9) | collective-permute-done | bytes 131104 | tf_op jit(solution)/shard_map/ppermute | solution.py:285
  30.6 0.5 %collective-permute-done.10.refs_3_ = bf16[64,1024]{1,0:T(8,128)(2,1)S(1)} collective-permute-done((bf16[64,1024]{1,0:T(8,128)(2,1)S(1)}, bf16[64,1024]{1,0:T(8,128)(2,1)S(1)}, u32[]{:S(2)}, u32[]{:S(2)}) %collective-permute-start.10) | collective-permute-done | bytes 131104 | tf_op jit(solution)/shard_map/ppermute | solution.py:285
  31.2 0.9 %collective-permute-start.12 = (bf16[64,512]{1,0:T(8,128)(2,1)S(1)}, bf16[64,512]{1,0:T(8,128)(2,1)S(1)}, u32[]{:S(2)}, u32[]{:S(2)}) collective-permute-start(bf16[64,512]{1,0:T(8,128)(2,1)S(1)} %get-tuple-element.63), channel_id=1, source_target_pairs={{0,5},{1,4},{2,7},{3,6},{4,3},{5,2},{6,1},{7,0},{8,13},{9,12},{10,... | collective-permute-start | bytes 196616 | tf_op jit(solution)/shard_map/ppermute | solution.py:285
  32.1 1.9 %collective-permute-start.11 = (bf16[64,256]{1,0:T(8,128)(2,1)S(1)}, bf16[64,256]{1,0:T(8,128)(2,1)S(1)}, u32[]{:S(2)}, u32[]{:S(2)}) collective-permute-start(bf16[64,256]{1,0:T(8,128)(2,1)S(1)} %get-tuple-element.62), channel_id=1, source_target_pairs={{0,6},{1,7},{2,4},{3,5},{4,2},{5,3},{6,0},{7,1},{8,14},{9,15},{10,... | collective-permute-start | bytes 98312 | tf_op jit(solution)/shard_map/ppermute | solution.py:285
  34.0 3.4 %collective-permute-done.11.middle_ref = bf16[64,256]{1,0:T(8,128)(2,1)S(1)} collective-permute-done((bf16[64,256]{1,0:T(8,128)(2,1)S(1)}, bf16[64,256]{1,0:T(8,128)(2,1)S(1)}, u32[]{:S(2)}, u32[]{:S(2)}) %collective-permute-start.11) | collective-permute-done | bytes 32800 | tf_op jit(solution)/shard_map/ppermute | solution.py:285
  37.4 1.9 %collective-permute-start.13 = (bf16[64,512]{1,0:T(8,128)(2,1)S(1)}, bf16[64,512]{1,0:T(8,128)(2,1)S(1)}, u32[]{:S(2)}, u32[]{:S(2)}) collective-permute-start(bf16[64,512]{1,0:T(8,128)(2,1)S(1)} %sum_over_shards.1.own_ref), channel_id=1, source_target_pairs={{0,4},{4,0},{8,12},{12,8},{16,20},{20,16},{24,28},{28,24},{1,5},{5... | collective-permute-start | bytes 196616 | tf_op jit(solution)/shard_map/ppermute | solution.py:273
  39.3 0.9 %collective-permute-done.13.sibling_ref = bf16[64,512]{1,0:T(8,128)(2,1)S(1)} collective-permute-done((bf16[64,512]{1,0:T(8,128)(2,1)S(1)}, bf16[64,512]{1,0:T(8,128)(2,1)S(1)}, u32[]{:S(2)}, u32[]{:S(2)}) %collective-permute-start.13) | collective-permute-done | bytes 65568 | tf_op jit(solution)/shard_map/ppermute | solution.py:273
  40.2 1.4 %collective-permute-start.16 = (bf16[64,512]{1,0:T(8,128)(2,1)S(1)}, bf16[64,512]{1,0:T(8,128)(2,1)S(1)}, u32[]{:S(2)}, u32[]{:S(2)}) collective-permute-start(bf16[64,512]{1,0:T(8,128)(2,1)S(1)} %mean_of_both_cores.1.refs_0_), channel_id=1, source_target_pairs={{0,28},{1,29},{2,30},{3,31},{4,24},{5,25},{6,26},{7,27},{8,20},{9,... | collective-permute-start | bytes 196616 | tf_op jit(solution)/shard_map/ppermute | solution.py:285
  41.7 1.2 %collective-permute-start.15 = (bf16[64,512]{1,0:T(8,128)(2,1)S(1)}, bf16[64,512]{1,0:T(8,128)(2,1)S(1)}, u32[]{:S(2)}, u32[]{:S(2)}) collective-permute-start(bf16[64,512]{1,0:T(8,128)(2,1)S(1)} %mean_of_both_cores.1.refs_0_), channel_id=1, source_target_pairs={{0,20},{1,21},{2,22},{3,23},{4,16},{5,17},{6,18},{7,19},{8,28},{9,... | collective-permute-start | bytes 196616 | tf_op jit(solution)/shard_map/ppermute | solution.py:285
  42.8 0.6 %collective-permute-start.14 = (bf16[64,512]{1,0:T(8,128)(2,1)S(1)}, bf16[64,512]{1,0:T(8,128)(2,1)S(1)}, u32[]{:S(2)}, u32[]{:S(2)}) collective-permute-start(bf16[64,512]{1,0:T(8,128)(2,1)S(1)} %mean_of_both_cores.1.refs_0_), channel_id=1, source_target_pairs={{0,12},{1,13},{2,14},{3,15},{4,8},{5,9},{6,10},{7,11},{8,4},{9,5},... | collective-permute-start | bytes 196616 | tf_op jit(solution)/shard_map/ppermute | solution.py:285
  43.5 1.7 %collective-permute-done.16.refs_3_ = bf16[64,512]{1,0:T(8,128)(2,1)S(1)} collective-permute-done((bf16[64,512]{1,0:T(8,128)(2,1)S(1)}, bf16[64,512]{1,0:T(8,128)(2,1)S(1)}, u32[]{:S(2)}, u32[]{:S(2)}) %collective-permute-start.16) | collective-permute-done | bytes 65568 | tf_op jit(solution)/shard_map/ppermute | solution.py:285
  45.2 1.8 %collective-permute-done.15.refs_2_ = bf16[64,512]{1,0:T(8,128)(2,1)S(1)} collective-permute-done((bf16[64,512]{1,0:T(8,128)(2,1)S(1)}, bf16[64,512]{1,0:T(8,128)(2,1)S(1)}, u32[]{:S(2)}, u32[]{:S(2)}) %collective-permute-start.15) | collective-permute-done | bytes 65568 | tf_op jit(solution)/shard_map/ppermute | solution.py:285
  47.0 0.8 %blocks_in_place.1 = f32[256,512]{1,0:T(8,128)} custom-call(bf16[64,512]{1,0:T(8,128)(2,1)S(1)} %mean_of_both_cores.1.refs_0_, bf16[64,512]{1,0:T(8,128)(2,1)S(1)} %collective-permute-done.14.refs_1_, bf16[64,512]{1,0:T(8,128)(2,1)S(1)} %collective-permute-done.15.refs_2_, bf16[64,512]{1,0:T(8,128)(2,1)S(1)} %collective-permute-done.16.refs_3_), custom_call_target="tpu_custom_call" | custom-call | tf_op jit(solution)/shard_map/blocks_in_place/pallas_call | solution.py:33
  (11 shorter events, 0.5 us)
Async XLA Ops:
  0.6 10.2 %collective-permute-start.1 = (bf16[384,1024]{1,0:T(8,128)(2,1)}, bf16[384,1024]{1,0:T(8,128)(2,1)S(1)}, u32[]{:S(2)}, u32[]{:S(2)}) collective-permute-start(bf16[384,1024]{1,0:T(8,128)(2,1)} %bitcast.9), channel_id=1, source_target_pairs={{0,4},{4,0},{8,12},{12,8},{16,20},{20,16},{24,28},{28,24},{1,5},{5... | collective-permute-start | bytes 2359304 | tf_op jit(solution)/shard_map/ppermute | solution.py:273
  2.0 7.7 %collective-permute-start = (bf16[64,512]{1,0:T(8,128)(2,1)S(1)}, bf16[64,512]{1,0:T(8,128)(2,1)S(1)}, u32[]{:S(2)}, u32[]{:S(2)}) collective-permute-start(bf16[64,512]{1,0:T(8,128)(2,1)S(1)} %own_part_of_weight.1), channel_id=1, source_target_pairs={{0,6},{1,7},{2,4},{3,5},{4,2},{5,3},{6,0},{7,1},{8,14},{9,15},{10,... | collective-permute-start | bytes 196616 | tf_op jit(solution)/shard_map/ppermute | solution.py:285
  5.8 9.4 %collective-permute-start.5 = (bf16[256,512]{1,0:T(8,128)(2,1)}, bf16[256,512]{1,0:T(8,128)(2,1)S(1)}, u32[]{:S(2)}, u32[]{:S(2)}) collective-permute-start(bf16[256,512]{1,0:T(8,128)(2,1)} %refs_4_.1), channel_id=1, source_target_pairs={{0,5},{1,4},{2,7},{3,6},{4,3},{5,2},{6,1},{7,0},{8,13},{9,12},{10,... | collective-permute-start | bytes 786440 | tf_op jit(solution)/shard_map/ppermute | solution.py:285
  9.7 4.2 %collective-permute-start.3 = (bf16[64,512]{1,0:T(8,128)(2,1)S(1)}, bf16[64,512]{1,0:T(8,128)(2,1)S(1)}, u32[]{:S(2)}, u32[]{:S(2)}) collective-permute-start(bf16[64,512]{1,0:T(8,128)(2,1)S(1)} %collective-permute-done._.refs_1_), channel_id=1, source_target_pairs={{0,12},{1,13},{2,14},{3,15},{4,8},{5,9},{6,10},{7,11},{8,4},{9,5},... | collective-permute-start | bytes 196616 | tf_op jit(solution)/shard_map/ppermute | solution.py:285
  15.2 1.8 %collective-permute-start.6 = (bf16[256,512]{1,0:T(8,128)(2,1)S(1)}, bf16[256,512]{1,0:T(8,128)(2,1)S(1)}, u32[]{:S(2)}, u32[]{:S(2)}) collective-permute-start(bf16[256,512]{1,0:T(8,128)(2,1)S(1)} %collective-permute-done.5.refs_5_), channel_id=1, source_target_pairs={{0,4},{4,0},{8,12},{12,8},{16,20},{20,16},{24,28},{28,24},{1,5},{5... | collective-permute-start | bytes 786440 | tf_op jit(solution)/shard_map/ppermute | solution.py:273
  15.2 1.6 %collective-permute-start.2 = (bf16[64,512]{1,0:T(8,128)(2,1)S(1)}, bf16[64,512]{1,0:T(8,128)(2,1)S(1)}, u32[]{:S(2)}, u32[]{:S(2)}) collective-permute-start(bf16[64,512]{1,0:T(8,128)(2,1)S(1)} %collective-permute-done._.refs_1_), channel_id=1, source_target_pairs={{0,4},{4,0},{8,12},{12,8},{16,20},{20,16},{24,28},{28,24},{1,5},{5... | collective-permute-start | bytes 196616 | tf_op jit(solution)/shard_map/ppermute | solution.py:273
  15.7 1.3 %collective-permute-start.4 = (bf16[64,512]{1,0:T(8,128)(2,1)S(1)}, bf16[64,512]{1,0:T(8,128)(2,1)S(1)}, u32[]{:S(2)}, u32[]{:S(2)}) collective-permute-start(bf16[64,512]{1,0:T(8,128)(2,1)S(1)} %collective-permute-done.3.refs_3_), channel_id=1, source_target_pairs={{0,4},{4,0},{8,12},{12,8},{16,20},{20,16},{24,28},{28,24},{1,5},{5... | collective-permute-start | bytes 196616 | tf_op jit(solution)/shard_map/ppermute | solution.py:273
  19.3 1.8 %collective-permute-start.7 = (bf16[384,512]{1,0:T(8,128)(2,1)S(1)}, bf16[384,512]{1,0:T(8,128)(2,1)S(1)}, u32[]{:S(2)}, u32[]{:S(2)}) collective-permute-start(bf16[384,512]{1,0:T(8,128)(2,1)S(1)} %get-tuple-element.47.own_ref), channel_id=1, source_target_pairs={{0,4},{4,0},{8,12},{12,8},{16,20},{20,16},{24,28},{28,24},{1,5},{5... | collective-permute-start | bytes 1179656 | tf_op jit(solution)/shard_map/ppermute | solution.py:273
  21.7 5.5 %collective-permute-start.8 = (bf16[64,1024]{1,0:T(8,128)(2,1)S(1)}, bf16[64,1024]{1,0:T(8,128)(2,1)S(1)}, u32[]{:S(2)}, u32[]{:S(2)}) collective-permute-start(bf16[64,1024]{1,0:T(8,128)(2,1)S(1)} %get-tuple-element.58), channel_id=1, source_target_pairs={{0,12},{1,13},{2,14},{3,15},{4,8},{5,9},{6,10},{7,11},{8,4},{9,5},... | collective-permute-start | bytes 393224 | tf_op jit(solution)/shard_map/ppermute | solution.py:285
  23.0 7.7 %collective-permute-start.9 = (bf16[64,1024]{1,0:T(8,128)(2,1)S(1)}, bf16[64,1024]{1,0:T(8,128)(2,1)S(1)}, u32[]{:S(2)}, u32[]{:S(2)}) collective-permute-start(bf16[64,1024]{1,0:T(8,128)(2,1)S(1)} %get-tuple-element.59), channel_id=1, source_target_pairs={{0,20},{1,21},{2,22},{3,23},{4,16},{5,17},{6,18},{7,19},{8,28},{9,... | collective-permute-start | bytes 393224 | tf_op jit(solution)/shard_map/ppermute | solution.py:285
  24.5 6.7 %collective-permute-start.10 = (bf16[64,1024]{1,0:T(8,128)(2,1)S(1)}, bf16[64,1024]{1,0:T(8,128)(2,1)S(1)}, u32[]{:S(2)}, u32[]{:S(2)}) collective-permute-start(bf16[64,1024]{1,0:T(8,128)(2,1)S(1)} %get-tuple-element.60), channel_id=1, source_target_pairs={{0,28},{1,29},{2,30},{3,31},{4,24},{5,25},{6,26},{7,27},{8,20},{9,... | collective-permute-start | bytes 393224 | tf_op jit(solution)/shard_map/ppermute | solution.py:285
  31.2 6.2 %collective-permute-start.12 = (bf16[64,512]{1,0:T(8,128)(2,1)S(1)}, bf16[64,512]{1,0:T(8,128)(2,1)S(1)}, u32[]{:S(2)}, u32[]{:S(2)}) collective-permute-start(bf16[64,512]{1,0:T(8,128)(2,1)S(1)} %get-tuple-element.63), channel_id=1, source_target_pairs={{0,5},{1,4},{2,7},{3,6},{4,3},{5,2},{6,1},{7,0},{8,13},{9,12},{10,... | collective-permute-start | bytes 196616 | tf_op jit(solution)/shard_map/ppermute | solution.py:285
  32.1 5.3 %collective-permute-start.11 = (bf16[64,256]{1,0:T(8,128)(2,1)S(1)}, bf16[64,256]{1,0:T(8,128)(2,1)S(1)}, u32[]{:S(2)}, u32[]{:S(2)}) collective-permute-start(bf16[64,256]{1,0:T(8,128)(2,1)S(1)} %get-tuple-element.62), channel_id=1, source_target_pairs={{0,6},{1,7},{2,4},{3,5},{4,2},{5,3},{6,0},{7,1},{8,14},{9,15},{10,... | collective-permute-start | bytes 98312 | tf_op jit(solution)/shard_map/ppermute | solution.py:285
  37.4 2.8 %collective-permute-start.13 = (bf16[64,512]{1,0:T(8,128)(2,1)S(1)}, bf16[64,512]{1,0:T(8,128)(2,1)S(1)}, u32[]{:S(2)}, u32[]{:S(2)}) collective-permute-start(bf16[64,512]{1,0:T(8,128)(2,1)S(1)} %sum_over_shards.1.own_ref), channel_id=1, source_target_pairs={{0,4},{4,0},{8,12},{12,8},{16,20},{20,16},{24,28},{28,24},{1,5},{5... | collective-permute-start | bytes 196616 | tf_op jit(solution)/shard_map/ppermute | solution.py:273
  40.2 4.9 %collective-permute-start.16 = (bf16[64,512]{1,0:T(8,128)(2,1)S(1)}, bf16[64,512]{1,0:T(8,128)(2,1)S(1)}, u32[]{:S(2)}, u32[]{:S(2)}) collective-permute-start(bf16[64,512]{1,0:T(8,128)(2,1)S(1)} %mean_of_both_cores.1.refs_0_), channel_id=1, source_target_pairs={{0,28},{1,29},{2,30},{3,31},{4,24},{5,25},{6,26},{7,27},{8,20},{9,... | collective-permute-start | bytes 196616 | tf_op jit(solution)/shard_map/ppermute | solution.py:285
  41.7 5.3 %collective-permute-start.15 = (bf16[64,512]{1,0:T(8,128)(2,1)S(1)}, bf16[64,512]{1,0:T(8,128)(2,1)S(1)}, u32[]{:S(2)}, u32[]{:S(2)}) collective-permute-start(bf16[64,512]{1,0:T(8,128)(2,1)S(1)} %mean_of_both_cores.1.refs_0_), channel_id=1, source_target_pairs={{0,20},{1,21},{2,22},{3,23},{4,16},{5,17},{6,18},{7,19},{8,28},{9,... | collective-permute-start | bytes 196616 | tf_op jit(solution)/shard_map/ppermute | solution.py:285
  42.8 4.1 %collective-permute-start.14 = (bf16[64,512]{1,0:T(8,128)(2,1)S(1)}, bf16[64,512]{1,0:T(8,128)(2,1)S(1)}, u32[]{:S(2)}, u32[]{:S(2)}) collective-permute-start(bf16[64,512]{1,0:T(8,128)(2,1)S(1)} %mean_of_both_cores.1.refs_0_), channel_id=1, source_target_pairs={{0,12},{1,13},{2,14},{3,15},{4,8},{5,9},{6,10},{7,11},{8,4},{9,5},... | collective-permute-start | bytes 196616 | tf_op jit(solution)/shard_map/ppermute | solution.py:285

commit v4 on v3

--- a/solution.py
+++ b/solution.py
@@ -104,29 +104,33 @@
         first_ref[place] = jnp.broadcast_to(first, (span, first_ref.shape[1]))
 
 
-def piece_start(origin, shard_rows, group, part_rows):
-    flips, member_flip = origin
+def piece_start(shard_rows, group, part_rows, flips, member_flip):
     device = lax.axis_index("dp")
-    flip = jnp.where(lax.rem(device, CORES) == 0, flips[0], flips[1])
-    start = (lax.axis_index("fsdp") ^ flip) * shard_rows
+    start = (
+        lax.axis_index("fsdp") ^ jnp.where(lax.rem(device, CORES) == 0, flips[0], flips[1])
+    ) * shard_rows
     if member_flip is not None:
         start = start + (lax.rem(device, group) ^ member_flip) * part_rows
     return pl.multiple_of(start, 16)
 
 
 def attention_kernel(slots, group, origins, *refs):
-    piece_count = len(origins)
-    pieces = refs[:piece_count]
+    pieces = refs[: len(origins)]
     (events_ref, key_ref, value_ref, key_t_ref, value_t_ref, weight_ref, gated_ref, first_ref,
      grad_query_ref, query_ref, normed_ref, mixed_grad_ref, attention_ref, scores_grad_ref,
-     projection_ref, sems) = refs[piece_count:]
+     projection_ref, sems) = refs[len(origins) :]
     copies = []
-    for p, (piece, origin) in enumerate(zip(pieces, origins)):
-        rows = piece.shape[0]
-        start = piece_start(origin, pieces[0].shape[0], group, rows)
-        copies.append(
-            pltpu.make_async_copy(piece, projection_ref.at[pl.ds(start, rows)], sems.at[p])
-        )
+    for piece, (flips, members) in zip(pieces, origins):
+        rows = piece.shape[0] // len(members)
+        for i, member in enumerate(members):
+            start = piece_start(pieces[0].shape[0], group, rows, flips, member)
+            copies.append(
+                pltpu.make_async_copy(
+                    piece.at[pl.ds(i * rows, rows)],
+                    projection_ref.at[pl.ds(start, rows)],
+                    sems.at[len(copies)],
+                )
+            )
     for copy in copies:
         copy.start()
     for copy in copies:
@@ -188,39 +192,48 @@
             grad_key_ref[places[s], columns[h]] = grad_key.astype(jnp.bfloat16)
 
 
-def gradient_kernel(pairs, events_ref, own_ref, got_ref, *refs):
-    outs, both_ref, picked_ref = refs[:-2], refs[-2], refs[-1]
+def add_gradient(picks, events_ref, both_ref, columns, picked_ref, outs, at):
+    part_rows = outs[0].shape[0]
+    shard_rows = events_ref.shape[0] // lax.axis_size("fsdp")
+    chip = lax.div(lax.axis_index("dp"), CORES)
+    for i, (k, shard) in enumerate(picks):
+        start = pl.multiple_of(shard * shard_rows + (chip ^ k) * part_rows, part_rows)
+        picked_ref[i * part_rows : (i + 1) * part_rows] = events_ref[pl.ds(start, part_rows)]
+    total = dot(picked_ref[: len(picks) * part_rows], both_ref[:, columns])
+    for i, (k, _) in enumerate(picks):
+        block = total[i * part_rows : (i + 1) * part_rows]
+        outs[k][:, at(i) : at(i) + total.shape[1]] = block.astype(outs[k].dtype)
+
+
+def summing_core(k):
+    return lax.rem(lax.axis_index("dp"), CORES) ^ (1 if k else 0)
+
+
+def whole_gradient_kernel(pairs, events_ref, own_ref, got_ref, both_ref, *refs):
+    outs, picked_ref = refs[:-1], refs[-1]
     rows, width = own_ref.shape
-    half = width // CORES
     both_ref[:rows] = own_ref[...]
     both_ref[rows:] = got_ref[...]
-    device, here = lax.axis_index("dp"), lax.axis_index("fsdp")
-    part_rows = outs[0].shape[0]
-    shard_rows = events_ref.shape[0] // lax.axis_size("fsdp")
-
-    def core_of(k):
-        return lax.rem(device, CORES) ^ (1 if k else 0)
-
-    def add(picks, columns, at, wide):
-        for i, (k, shard) in enumerate(picks):
-            start = shard * shard_rows + (lax.div(device, CORES) ^ k) * part_rows
-            place = pl.ds(pl.multiple_of(start, part_rows), part_rows)
-            picked_ref[i * part_rows : (i + 1) * part_rows] = events_ref[place]
-        total = dot(picked_ref[: len(picks) * part_rows], both_ref[:, columns])
-        for i, (k, _) in enumerate(picks):
-            block = total[i * part_rows : (i + 1) * part_rows]
-            outs[k][:, at(i) : at(i) + wide] = block.astype(outs[k].dtype)
-
+    here = lax.axis_index("fsdp")
+    for p, flips in enumerate(pairs):
+        picks = [
+            (k, here ^ jnp.where(summing_core(k) == 0, flips[0], flips[1]))
+            for k in range(len(outs))
+        ]
+        add_gradient(picks, events_ref, both_ref, slice(None), picked_ref, outs,
+                     lambda i: p * width)
+
+
+def half_gradient_kernel(events_ref, both_ref, *refs):
+    outs, picked_ref = refs[:-1], refs[-1]
+    half = both_ref.shape[1] // CORES
+    here = lax.axis_index("fsdp")
     chips = range(len(outs))
-    for p, flips in enumerate(pairs):
-        picks = [(k, here ^ jnp.where(core_of(k) == 0, flips[0], flips[1])) for k in chips]
-        add(picks, slice(None), lambda i: p * width, width)
-    after = len(pairs) * width
     for group in (chips[:1], chips[1:]):
-        columns = pl.ds(pl.multiple_of(core_of(group[0]) * half, half), half)
-        shards = (here, here ^ (lax.axis_size("fsdp") // 2))
-        picks = [(k, shard) for k in group for shard in shards]
-        add(picks, columns, lambda i: after + i % 2 * half, half)
+        columns = pl.ds(pl.multiple_of(summing_core(group[0]) * half, half), half)
+        picks = [(k, here ^ z) for k in group for z in (0, lax.axis_size("fsdp") // 2)]
+        add_gradient(picks, events_ref, both_ref, columns, picked_ref, outs,
+                     lambda i: i % 2 * half)
 
 
 def chip_sum_kernel(term_count, _, *refs):
@@ -296,7 +309,7 @@
 
 def across_z(weight, dp_count, fsdp_count):
     rows = weight.shape[0]
-    group = 4 if dp_count % 4 == 0 and rows % 64 == 0 else 2
+    group = max(g for g in (2, 4, 8) if dp_count % g == 0 and rows % (16 * g) == 0)
     part = call(
         functools.partial(slice_kernel, group),
         "own_part_of_weight",
@@ -307,26 +320,44 @@
     )
     weight, part = lax.optimization_barrier((weight, part))
     middle = (fsdp_count // 2,) * CORES
-    arrived = [(cross(part, dp_count, fsdp_count, 0, middle), middle, 1)]
-    for flips in shard_pairs(fsdp_count):
-        block = cross(weight, dp_count, fsdp_count, 0, flips)
-        arrived.append((block, flips[::-1], None))
-    return group, arrived
-
-
-def share(group, arrived, ready, dp_count, fsdp_count):
-    block, flips, member = arrived[0]
-    own = [(block, flips, member)]
-    if group == 4:
-        passed = cross(block, dp_count, fsdp_count, 1, (0,) * CORES)
-        own.append((passed, flips, member ^ 3))
-    for block, flips, member in arrived[1:]:
-        own.append((lax.optimization_barrier((block, own[-1][0], ready))[0], flips, member))
+    part = cross(part, dp_count, fsdp_count, 0, middle)
+    wholes = [
+        (cross(weight, dp_count, fsdp_count, 0, flips), flips[::-1])
+        for flips in shard_pairs(fsdp_count)
+    ]
+    return group, part, wholes
+
+
+def stack_kernel(*refs):
+    out_ref = refs[-1]
+    rows = refs[0].shape[0]
+    for i, block_ref in enumerate(refs[:-1]):
+        out_ref[i * rows : (i + 1) * rows] = block_ref[...]
+
+
+def share(group, part, wholes, ready, dp_count, fsdp_count):
+    alike = (0,) * CORES
+    parts, members = [part], [1]
+    for chip_bits in range(1, group // CORES):
+        parts.append(cross(part, dp_count, fsdp_count, chip_bits, alike))
+        members.append(CORES * chip_bits)
+    if len(parts) > 1:
+        rows, columns = part.shape
+        part = call(
+            stack_kernel,
+            "parts_of_weight",
+            parts,
+            [NEAR] * len(parts),
+            jax.ShapeDtypeStruct((len(parts) * rows, columns), part.dtype),
+        )
+    held = [(part, (fsdp_count // 2,) * CORES, members)]
+    for block, flips in wholes:
+        held.append((lax.optimization_barrier((block, part, ready))[0], flips, [None]))
     found = []
-    for block, source, place in own:
-        moved = flip(block, "dp", dp_count, 1)
-        found.append((block, (source, place)))
-        found.append((moved, (source[::-1], None if place is None else place ^ 1)))
+    for block, flips, members in held:
+        moved = [m if m is None else m ^ 1 for m in members]
+        found.append((block, (flips, members)))
+        found.append((flip(block, "dp", dp_count, 1), (flips[::-1], moved)))
     return found
 
 
@@ -349,11 +380,11 @@
         a.reshape(rows, width) for a in (keys, values, gates, cotangent)
     )
     sibling_events = flip(flat_events, "dp", dp_count, 1)
-    group, arrived = across_z(query_weight, dp_count, fsdp_count)
+    group, part, wholes = across_z(query_weight, dp_count, fsdp_count)
     prepared = call(
         functools.partial(prepare_kernel, slots),
         "prepared_operands",
-        [arrived[0][0], lengths, sibling_events]
+        [part, lengths, sibling_events]
         + [flat_events, keys, values, cotangent, query_weight, gates],
         [ANYWHERE, FAR, NEAR] + [FAR] * 6,
         (
@@ -374,11 +405,12 @@
             pltpu.SMEM(lengths.shape, jnp.int32),
             pltpu.SemaphoreType.DMA((7,)),
         ],
-        flops=10**10,
+        flops=22 * 10**8,
     )
     near_events, near_keys, near_values, near_cotangent, near_weight = prepared[:5]
     events_t, keys_t, values_t, weight, gated, first = prepared[5:]
-    found = [(near_weight, ((0, 0), None))] + share(group, arrived, first, dp_count, fsdp_count)
+    found = [(near_weight, ((0, 0), [None]))]
+    found += share(group, part, wholes, first, dp_count, fsdp_count)
     pieces, origins = zip(*found)
     blocks = shape(slots * HEADS, span, span)
     grad_query, query, normed, grad_mixed, attention, grad_scores = call(
@@ -397,7 +429,7 @@
         ),
         [
             pltpu.VMEM((model_width, width), bf16),
-            pltpu.SemaphoreType.DMA((len(pieces),)),
+            pltpu.SemaphoreType.DMA((sum(len(members) for _, members in origins),)),
         ],
         flops=2 * rows * width * (model_width + 4 * span),
         moved=24 * rows * width,
@@ -407,19 +439,31 @@
     terms = [grad_query]
     if staged:
         pairs = shard_pairs(fsdp_count)
-        columns = len(pairs) * width + 2 * half_width
+        got = flip(grad_query, "dp", dp_count, 1)
+        picked = pltpu.VMEM((2 * chips * part_rows, CORES * rows), bf16)
+
+        def for_chips(columns):
+            return tuple(shape(part_rows, columns, dtype=bf16 if k else f32) for k in range(chips))
+
+        both, *whole_terms = call(
+            functools.partial(whole_gradient_kernel, pairs),
+            "weight_gradient_of_whole_shards",
+            [events_t, grad_query, got],
+            [NEAR] * 3,
+            (shape(CORES * rows, width),) + for_chips(len(pairs) * width),
+            [picked],
+            flops=4 * rows * shard_rows * len(pairs) * width,
+            moved=2 * model_width * (rows + width),
+        )
         terms = call(
-            functools.partial(gradient_kernel, pairs),
-            "weight_gradient",
-            [events_t, grad_query, flip(grad_query, "dp", dp_count, 1)],
-            [NEAR] * 3,
-            tuple(shape(part_rows, columns, dtype=bf16 if k else f32) for k in range(chips)),
-            [
-                pltpu.VMEM((CORES * rows, width), bf16),
-                pltpu.VMEM((2 * chips * part_rows, CORES * rows), bf16),
-            ],
-            flops=4 * rows * shard_rows * columns,
-            moved=2 * model_width * (2 * rows + half_width),
+            half_gradient_kernel,
+            "weight_gradient_of_halves",
+            [events_t, both],
+            [NEAR] * 2,
+            for_chips(2 * half_width),
+            [picked],
+            flops=4 * rows * shard_rows * width,
+            moved=2 * model_width * (rows + width),
         )
     grad_keys, grad_values, grad_gates = call(
         functools.partial(outputs_kernel, slots),
@@ -436,21 +480,28 @@
         def to_chip(block, k):
             return cross(block, dp_count, fsdp_count, k, alike)
 
+        whole_terms[1:] = far_first(chips, lambda k: to_chip(whole_terms[k], k))
+        wholes = call(
+            functools.partial(chip_sum_kernel, chips),
+            "sum_of_whole_shards_over_chips",
+            [both] + whole_terms,
+            [ANYWHERE] + [NEAR] * chips,
+            (shape(part_rows, width),) * len(pairs),
+        )
+        wholes = [cross(a, dp_count, fsdp_count, 0, p) for a, p in zip(wholes, pairs)]
         terms = [terms[0]] + far_first(chips, lambda k: to_chip(terms[k], k))
-        sums = call(
+        own_half, middle = call(
             functools.partial(chip_sum_kernel, chips),
-            "sum_over_chips",
+            "sum_of_halves_over_chips",
             [grad_keys] + terms,
             [FAR] + [NEAR] * chips,
-            (shape(part_rows, width),) * len(pairs)
-            + (shape(part_rows, half_width, dtype=f32), shape(part_rows, half_width)),
-        )
-        wholes = [cross(a, dp_count, fsdp_count, 0, p) for a, p in zip(sums, pairs)]
-        middle = cross(sums[-1], dp_count, fsdp_count, 0, (fsdp_count // 2,) * CORES)
+            (shape(part_rows, half_width, dtype=f32), shape(part_rows, half_width)),
+        )
+        middle = cross(middle, dp_count, fsdp_count, 0, (fsdp_count // 2,) * CORES)
         total = call(
             shard_sum_kernel,
             "sum_over_shards",
-            [sums[-2], middle] + wholes,
+            [own_half, middle] + wholes,
             [NEAR] * (2 + len(wholes)),
             shape(part_rows, width),
             [pltpu.VMEM((part_rows, width), f32)],

time: 48 us -> 48.2 us (level)
  starting transfers between devices: 18.3 us -> 25.6 us
  waiting for transfers between devices: 20.4 us -> 13.1 us
    ppermute x11 -> x16, waiting for transfers between devices: 16.6 us -> 9.54 us  [cross(): return lax.ppermute(block, BOTH, pairs)]
    ppermute x11 -> x16, starting transfers between devices: 15.2 us -> 21.4 us  [cross(): return lax.ppermute(block, BOTH, pairs)]
    ppermute x6 -> x5, starting transfers between devices: 3.11 us -> 4.18 us  [flip(): return lax.ppermute(block, axis, [(i, i ^ bits) for i in range(count)])]
    ppermute x6 -> x5, waiting for transfers between devices: 3.72 us -> 3.53 us  [flip(): return lax.ppermute(block, axis, [(i, i ^ bits) for i in range(count)])]
    pallas_call x9 -> x12, Pallas kernels: 8.44 us -> 8.59 us  [call(): pl.pallas_call(kernel, out_shape=out_shape, in_specs=in_specs, out_specs=...]
  transfers between devices with their start and end apart: 17 -> 21, of which waited for: 13 -> 11; matrix products, arithmetic and copies ran while one was open for 0% -> 0% of each run, Pallas kernels for 10% -> 10%
where the time goes in v4:
time: 48.2 us; the launch traced here: 48 us
  starting transfers between devices  25.6 us (53%)
  waiting for transfers between devices  13.1 us (27%)
  Pallas kernels  8.59 us (18%)
  between operations  0.72 us (1%)
    ppermute x16, starting transfers between devices, cross(): return lax.ppermute(block, BOTH, pairs)  21.4 us
    ppermute x16, waiting for transfers between devices, cross(): return lax.ppermute(block, BOTH, pairs)  9.54 us
    pallas_call x12, Pallas kernels, call(): pl.pallas_call(kernel, out_shape=out_shape, in_specs=in_specs, out_specs=...  8.59 us
    ppermute x5, starting transfers between devices, flip(): return lax.ppermute(block, axis, [(i, i ^ bits) for i in range(count)])  4.18 us
    ppermute x5, waiting for transfers between devices, flip(): return lax.ppermute(block, axis, [(i, i ^ bits) for i in range(count)])  3.53 us
  transfers between devices with their start and end apart: 21, of which 11 were waited for; matrix products, arithmetic and copies ran while one was open for 0% of the time, Pallas kernels for 10%

profile of v4, /device:TPU:0, one launch (start us, length us, event | category | flops | bytes accessed | tf_op | source)
XLA Modules:
  0.0 48.0 jit_solution(13230815670395402574)
XLA Ops:
  0.6 0.5 %collective-permute-start.1 = (bf16[384,1024]{1,0:T(8,128)(2,1)}, bf16[384,1024]{1,0:T(8,128)(2,1)S(1)}, u32[]{:S(2)}, u32[]{:S(2)}) collective-permute-start(bf16[384,1024]{1,0:T(8,128)(2,1)} %bitcast.9), channel_id=1, source_target_pairs={{0,4},{4,0},{8,12},{12,8},{16,20},{20,16},{24,28},{28,24},{1,5},{5... | collective-permute-start | bytes 2359304 | tf_op jit(solution)/shard_map/ppermute | solution.py:286
  1.1 0.8 %own_part_of_weight.1 = bf16[32,512]{1,0:T(8,128)(2,1)S(1)} custom-call(bf16[256,512]{1,0:T(8,128)(2,1)} %refs_4_.1), custom_call_target="tpu_custom_call" | custom-call | tf_op jit(solution)/shard_map/own_part_of_weight/pallas_call | solution.py:33
  1.9 3.8 %collective-permute-start = (bf16[32,512]{1,0:T(8,128)(2,1)S(1)}, bf16[32,512]{1,0:T(8,128)(2,1)S(1)}, u32[]{:S(2)}, u32[]{:S(2)}) collective-permute-start(bf16[32,512]{1,0:T(8,128)(2,1)S(1)} %own_part_of_weight.1), channel_id=1, source_target_pairs={{0,6},{1,7},{2,4},{3,5},{4,2},{5,3},{6,0},{7,1},{8,14},{9,15},{10,... | collective-permute-start | bytes 98312 | tf_op jit(solution)/shard_map/ppermute | solution.py:298
  5.7 1.2 %collective-permute-start.6 = (bf16[256,512]{1,0:T(8,128)(2,1)}, bf16[256,512]{1,0:T(8,128)(2,1)S(1)}, u32[]{:S(2)}, u32[]{:S(2)}) collective-permute-start(bf16[256,512]{1,0:T(8,128)(2,1)} %refs_4_.1), channel_id=1, source_target_pairs={{0,5},{1,4},{2,7},{3,6},{4,3},{5,2},{6,1},{7,0},{8,13},{9,12},{10,... | collective-permute-start | bytes 786440 | tf_op jit(solution)/shard_map/ppermute | solution.py:298
  6.9 0.5 %collective-permute-done._.refs_0_ = bf16[32,512]{1,0:T(8,128)(2,1)S(1)} collective-permute-done((bf16[32,512]{1,0:T(8,128)(2,1)S(1)}, bf16[32,512]{1,0:T(8,128)(2,1)S(1)}, u32[]{:S(2)}, u32[]{:S(2)}) %collective-permute-start) | collective-permute-done | bytes 32800 | tf_op jit(solution)/shard_map/ppermute | solution.py:298
  7.4 2.4 %collective-permute-start.4 = (bf16[32,512]{1,0:T(8,128)(2,1)S(1)}, bf16[32,512]{1,0:T(8,128)(2,1)S(1)}, u32[]{:S(2)}, u32[]{:S(2)}) collective-permute-start(bf16[32,512]{1,0:T(8,128)(2,1)S(1)} %collective-permute-done._.refs_0_), channel_id=1, source_target_pairs={{0,28},{1,29},{2,30},{3,31},{4,24},{5,25},{6,26},{7,27},{8,20},{9,... | collective-permute-start | bytes 98312 | tf_op jit(solution)/shard_map/ppermute | solution.py:298
  10.4 1.4 %collective-permute-done.4.refs_3_ = bf16[32,512]{1,0:T(8,128)(2,1)S(1)} collective-permute-done((bf16[32,512]{1,0:T(8,128)(2,1)S(1)}, bf16[32,512]{1,0:T(8,128)(2,1)S(1)}, u32[]{:S(2)}, u32[]{:S(2)}) %collective-permute-start.4) | collective-permute-done | bytes 32800 | tf_op jit(solution)/shard_map/ppermute | solution.py:298
  11.7 1.5 %collective-permute-done.3.refs_2_ = bf16[32,512]{1,0:T(8,128)(2,1)S(1)} collective-permute-done((bf16[32,512]{1,0:T(8,128)(2,1)S(1)}, bf16[32,512]{1,0:T(8,128)(2,1)S(1)}, u32[]{:S(2)}, u32[]{:S(2)}) %collective-permute-start.3) | collective-permute-done | bytes 32800 | tf_op jit(solution)/shard_map/ppermute | solution.py:298
  13.3 2.3 %prepared_operands.1 = (bf16[384,1024]{1,0:T(8,128)(2,1)S(1)}, bf16[384,512]{1,0:T(8,128)(2,1)S(1)}, bf16[384,512]{1,0:T(8,128)(2,1)S(1)}, bf16[384,512]{1,0:T(8...) custom-call(bf16[32,512]{1,0:T(8,128)(2,1)S(1)} %collective-permute-, ...), custom_call_target="tpu_custom_call" | custom-call | flops 2200000000 | tf_op jit(solution)/shard_map/prepared_operands/pallas_call | solution.py:33
  15.7 0.8 %collective-permute-start.7 = (bf16[256,512]{1,0:T(8,128)(2,1)S(1)}, bf16[256,512]{1,0:T(8,128)(2,1)S(1)}, u32[]{:S(2)}, u32[]{:S(2)}) collective-permute-start(bf16[256,512]{1,0:T(8,128)(2,1)S(1)} %collective-permute-done.6.refs_3_), channel_id=1, source_target_pairs={{0,4},{4,0},{8,12},{12,8},{16,20},{20,16},{24,28},{28,24},{1,5},{5... | collective-permute-start | bytes 786440 | tf_op jit(solution)/shard_map/ppermute | solution.py:286
  16.6 1.3 %collective-permute-done.5.refs_2_ = bf16[128,512]{1,0:T(8,128)(2,1)S(1)} collective-permute-done((bf16[128,512]{1,0:T(8,128)(2,1)S(1)}, bf16[128,512]{1,0:T(8,128)(2,1)S(1)}, u32[]{:S(2)}, u32[]{:S(2)}) %collective-permute-start.5) | collective-permute-done | bytes 131104 | tf_op jit(solution)/shard_map/ppermute | solution.py:286
  17.8 2.4 %attention_to_grad_query.1 = (bf16[384,512]{1,0:T(8,128)(2,1)S(1)}, bf16[384,512]{1,0:T(8,128)(2,1)S(1)}, f32[384,512]{1,0:T(8,128)S(1)}, bf16[384,512]{1,0:T(8,...) custom-call(bf16[256,512]{1,0:T(8,128)(2,1)S(1)} %get-tuple-element.40.refs_0_, ...), custom_call_target="tpu_custom_call" | custom-call | flops 603979776 | bytes 4718592 | tf_op jit(solution)/shard_map/attention_to_grad_query/pallas_call | solution.py:33
  20.6 1.4 %collective-permute-done.8.got_ref = bf16[384,512]{1,0:T(8,128)(2,1)S(1)} collective-permute-done((bf16[384,512]{1,0:T(8,128)(2,1)S(1)}, bf16[384,512]{1,0:T(8,128)(2,1)S(1)}, u32[]{:S(2)}, u32[]{:S(2)}) %collective-permute-start.8) | collective-permute-done | bytes 393248 | tf_op jit(solution)/shard_map/ppermute | solution.py:286
  22.4 0.5 %collective-permute-start.13 = (bf16[64,512]{1,0:T(8,128)(2,1)S(1)}, bf16[64,512]{1,0:T(8,128)(2,1)S(1)}, u32[]{:S(2)}, u32[]{:S(2)}) collective-permute-start(bf16[64,512]{1,0:T(8,128)(2,1)S(1)} %get-tuple-element.69), channel_id=1, source_target_pairs={{0,12},{1,13},{2,14},{3,15},{4,8},{5,9},{6,10},{7,11},{8,4},{9,5},... | collective-permute-start | bytes 196616 | tf_op jit(solution)/shard_map/ppermute | solution.py:298
  22.9 1.3 %collective-permute-start.14 = (bf16[64,512]{1,0:T(8,128)(2,1)S(1)}, bf16[64,512]{1,0:T(8,128)(2,1)S(1)}, u32[]{:S(2)}, u32[]{:S(2)}) collective-permute-start(bf16[64,512]{1,0:T(8,128)(2,1)S(1)} %get-tuple-element.70), channel_id=1, source_target_pairs={{0,20},{1,21},{2,22},{3,23},{4,16},{5,17},{6,18},{7,19},{8,28},{9,... | collective-permute-start | bytes 196616 | tf_op jit(solution)/shard_map/ppermute | solution.py:298
  24.2 1.4 %collective-permute-start.15 = (bf16[64,512]{1,0:T(8,128)(2,1)S(1)}, bf16[64,512]{1,0:T(8,128)(2,1)S(1)}, u32[]{:S(2)}, u32[]{:S(2)}) collective-permute-start(bf16[64,512]{1,0:T(8,128)(2,1)S(1)} %get-tuple-element.71), channel_id=1, source_target_pairs={{0,28},{1,29},{2,30},{3,31},{4,24},{5,25},{6,26},{7,27},{8,20},{9,... | collective-permute-start | bytes 196616 | tf_op jit(solution)/shard_map/ppermute | solution.py:298
  26.0 0.5 collective-permute-start.9
  26.5 1.4 %collective-permute-start.10 = (bf16[64,512]{1,0:T(8,128)(2,1)S(1)}, bf16[64,512]{1,0:T(8,128)(2,1)S(1)}, u32[]{:S(2)}, u32[]{:S(2)}) collective-permute-start(bf16[64,512]{1,0:T(8,128)(2,1)S(1)} %get-tuple-element.64), channel_id=1, source_target_pairs={{0,20},{1,21},{2,22},{3,23},{4,16},{5,17},{6,18},{7,19},{8,28},{9,... | collective-permute-start | bytes 196616 | tf_op jit(solution)/shard_map/ppermute | solution.py:298
  27.8 1.2 %collective-permute-start.11 = (bf16[64,512]{1,0:T(8,128)(2,1)S(1)}, bf16[64,512]{1,0:T(8,128)(2,1)S(1)}, u32[]{:S(2)}, u32[]{:S(2)}) collective-permute-start(bf16[64,512]{1,0:T(8,128)(2,1)S(1)} %get-tuple-element.65), channel_id=1, source_target_pairs={{0,28},{1,29},{2,30},{3,31},{4,24},{5,25},{6,26},{7,27},{8,20},{9,... | collective-permute-start | bytes 196616 | tf_op jit(solution)/shard_map/ppermute | solution.py:298
  29.1 1.6 %collective-permute-start.16 = (bf16[64,512]{1,0:T(8,128)(2,1)S(1)}, bf16[64,512]{1,0:T(8,128)(2,1)S(1)}, u32[]{:S(2)}, u32[]{:S(2)}) collective-permute-start(bf16[64,512]{1,0:T(8,128)(2,1)S(1)} %sum_of_whole_shards_over_chips.1), channel_id=1, source_target_pairs={{0,5},{1,4},{2,7},{3,6},{4,3},{5,2},{6,1},{7,0},{8,13},{9,12},{10,... | collective-permute-start | bytes 196616 | tf_op jit(solution)/shard_map/ppermute | solution.py:298
  30.7 1.4 %key_value_gate_gradients.1 = (bf16[384,512]{1,0:T(8,128)(2,1)}, bf16[384,512]{1,0:T(8,128)(2,1)}, bf16[384,512]{1,0:T(8,128)(2,1)}) custom-call(f32[64,512]{1,0:T(8,128)S(1)} %get-tuple-element.53._.refs_0_, bf16[384,512]{1,0:T(8,128)(2,1)S(1)} %get-tuple-element.54.query_ref, f32[384,512]{1,0:T(8,128)S(1)} %get-tuple-element.55.normed_ref, ...), custom_call_target="tpu_custom_call" | custom-call | flops 100663296 | bytes 2359296 | tf_op jit(solution)/shard_map/key_value_gate_gradients/pallas_call | solution.py:33
  32.1 0.7 %collective-permute-done.11.refs_3_ = bf16[64,512]{1,0:T(8,128)(2,1)S(1)} collective-permute-done((bf16[64,512]{1,0:T(8,128)(2,1)S(1)}, bf16[64,512]{1,0:T(8,128)(2,1)S(1)}, u32[]{:S(2)}, u32[]{:S(2)}) %collective-permute-start.11) | collective-permute-done | bytes 65568 | tf_op jit(solution)/shard_map/ppermute | solution.py:298
  32.8 2.4 %collective-permute-start.12 = (bf16[64,256]{1,0:T(8,128)(2,1)S(1)}, bf16[64,256]{1,0:T(8,128)(2,1)S(1)}, u32[]{:S(2)}, u32[]{:S(2)}) collective-permute-start(bf16[64,256]{1,0:T(8,128)(2,1)S(1)} %get-tuple-element.67), channel_id=1, source_target_pairs={{0,6},{1,7},{2,4},{3,5},{4,2},{5,3},{6,0},{7,1},{8,14},{9,15},{10,... | collective-permute-start | bytes 98312 | tf_op jit(solution)/shard_map/ppermute | solution.py:298
  35.3 1.9 %collective-permute-done.12.middle_ref = bf16[64,256]{1,0:T(8,128)(2,1)S(1)} collective-permute-done((bf16[64,256]{1,0:T(8,128)(2,1)S(1)}, bf16[64,256]{1,0:T(8,128)(2,1)S(1)}, u32[]{:S(2)}, u32[]{:S(2)}) %collective-permute-start.12) | collective-permute-done | bytes 32800 | tf_op jit(solution)/shard_map/ppermute | solution.py:298
  37.2 2.3 %collective-permute-start.17 = (bf16[64,512]{1,0:T(8,128)(2,1)S(1)}, bf16[64,512]{1,0:T(8,128)(2,1)S(1)}, u32[]{:S(2)}, u32[]{:S(2)}) collective-permute-start(bf16[64,512]{1,0:T(8,128)(2,1)S(1)} %sum_over_shards.1.own_ref), channel_id=1, source_target_pairs={{0,4},{4,0},{8,12},{12,8},{16,20},{20,16},{24,28},{28,24},{1,5},{5... | collective-permute-start | bytes 196616 | tf_op jit(solution)/shard_map/ppermute | solution.py:286
  39.5 0.9 %collective-permute-done.17.sibling_ref = bf16[64,512]{1,0:T(8,128)(2,1)S(1)} collective-permute-done((bf16[64,512]{1,0:T(8,128)(2,1)S(1)}, bf16[64,512]{1,0:T(8,128)(2,1)S(1)}, u32[]{:S(2)}, u32[]{:S(2)}) %collective-permute-start.17) | collective-permute-done | bytes 65568 | tf_op jit(solution)/shard_map/ppermute | solution.py:286
  40.4 1.5 %collective-permute-start.20 = (bf16[64,512]{1,0:T(8,128)(2,1)S(1)}, bf16[64,512]{1,0:T(8,128)(2,1)S(1)}, u32[]{:S(2)}, u32[]{:S(2)}) collective-permute-start(bf16[64,512]{1,0:T(8,128)(2,1)S(1)} %mean_of_both_cores.1.refs_0_), channel_id=1, source_target_pairs={{0,28},{1,29},{2,30},{3,31},{4,24},{5,25},{6,26},{7,27},{8,20},{9,... | collective-permute-start | bytes 196616 | tf_op jit(solution)/shard_map/ppermute | solution.py:298
  41.9 1.1 %collective-permute-start.19 = (bf16[64,512]{1,0:T(8,128)(2,1)S(1)}, bf16[64,512]{1,0:T(8,128)(2,1)S(1)}, u32[]{:S(2)}, u32[]{:S(2)}) collective-permute-start(bf16[64,512]{1,0:T(8,128)(2,1)S(1)} %mean_of_both_cores.1.refs_0_), channel_id=1, source_target_pairs={{0,20},{1,21},{2,22},{3,23},{4,16},{5,17},{6,18},{7,19},{8,28},{9,... | collective-permute-start | bytes 196616 | tf_op jit(solution)/shard_map/ppermute | solution.py:298
  43.0 0.6 %collective-permute-start.18 = (bf16[64,512]{1,0:T(8,128)(2,1)S(1)}, bf16[64,512]{1,0:T(8,128)(2,1)S(1)}, u32[]{:S(2)}, u32[]{:S(2)}) collective-permute-start(bf16[64,512]{1,0:T(8,128)(2,1)S(1)} %mean_of_both_cores.1.refs_0_), channel_id=1, source_target_pairs={{0,12},{1,13},{2,14},{3,15},{4,8},{5,9},{6,10},{7,11},{8,4},{9,5},... | collective-permute-start | bytes 196616 | tf_op jit(solution)/shard_map/ppermute | solution.py:298
  43.7 1.7 %collective-permute-done.20.refs_3_ = bf16[64,512]{1,0:T(8,128)(2,1)S(1)} collective-permute-done((bf16[64,512]{1,0:T(8,128)(2,1)S(1)}, bf16[64,512]{1,0:T(8,128)(2,1)S(1)}, u32[]{:S(2)}, u32[]{:S(2)}) %collective-permute-start.20) | collective-permute-done | bytes 65568 | tf_op jit(solution)/shard_map/ppermute | solution.py:298
  45.4 1.8 %collective-permute-done.19.refs_2_ = bf16[64,512]{1,0:T(8,128)(2,1)S(1)} collective-permute-done((bf16[64,512]{1,0:T(8,128)(2,1)S(1)}, bf16[64,512]{1,0:T(8,128)(2,1)S(1)}, u32[]{:S(2)}, u32[]{:S(2)}) %collective-permute-start.19) | collective-permute-done | bytes 65568 | tf_op jit(solution)/shard_map/ppermute | solution.py:298
  47.2 0.8 %blocks_in_place.1 = f32[256,512]{1,0:T(8,128)} custom-call(bf16[64,512]{1,0:T(8,128)(2,1)S(1)} %mean_of_both_cores.1.refs_0_, bf16[64,512]{1,0:T(8,128)(2,1)S(1)} %collective-permute-done.18.refs_1_, bf16[64,512]{1,0:T(8,128)(2,1)S(1)} %collective-permute-done.19.refs_2_, bf16[64,512]{1,0:T(8,128)(2,1)S(1)} %collective-permute-done.20.refs_3_), custom_call_target="tpu_custom_call" | custom-call | tf_op jit(solution)/shard_map/blocks_in_place/pallas_call | solution.py:33
  (22 shorter events, 2.1 us)
Async XLA Ops:
  0.6 12.7 %collective-permute-start.1 = (bf16[384,1024]{1,0:T(8,128)(2,1)}, bf16[384,1024]{1,0:T(8,128)(2,1)S(1)}, u32[]{:S(2)}, u32[]{:S(2)}) collective-permute-start(bf16[384,1024]{1,0:T(8,128)(2,1)} %bitcast.9), channel_id=1, source_target_pairs={{0,4},{4,0},{8,12},{12,8},{16,20},{20,16},{24,28},{28,24},{1,5},{5... | collective-permute-start | bytes 2359304 | tf_op jit(solution)/shard_map/ppermute | solution.py:286
  1.9 5.5 %collective-permute-start = (bf16[32,512]{1,0:T(8,128)(2,1)S(1)}, bf16[32,512]{1,0:T(8,128)(2,1)S(1)}, u32[]{:S(2)}, u32[]{:S(2)}) collective-permute-start(bf16[32,512]{1,0:T(8,128)(2,1)S(1)} %own_part_of_weight.1), channel_id=1, source_target_pairs={{0,6},{1,7},{2,4},{3,5},{4,2},{5,3},{6,0},{7,1},{8,14},{9,15},{10,... | collective-permute-start | bytes 98312 | tf_op jit(solution)/shard_map/ppermute | solution.py:298
  5.7 10.0 %collective-permute-start.6 = (bf16[256,512]{1,0:T(8,128)(2,1)}, bf16[256,512]{1,0:T(8,128)(2,1)S(1)}, u32[]{:S(2)}, u32[]{:S(2)}) collective-permute-start(bf16[256,512]{1,0:T(8,128)(2,1)} %refs_4_.1), channel_id=1, source_target_pairs={{0,5},{1,4},{2,7},{3,6},{4,3},{5,2},{6,1},{7,0},{8,13},{9,12},{10,... | collective-permute-start | bytes 786440 | tf_op jit(solution)/shard_map/ppermute | solution.py:298
  7.4 4.3 %collective-permute-start.4 = (bf16[32,512]{1,0:T(8,128)(2,1)S(1)}, bf16[32,512]{1,0:T(8,128)(2,1)S(1)}, u32[]{:S(2)}, u32[]{:S(2)}) collective-permute-start(bf16[32,512]{1,0:T(8,128)(2,1)S(1)} %collective-permute-done._.refs_0_), channel_id=1, source_target_pairs={{0,28},{1,29},{2,30},{3,31},{4,24},{5,25},{6,26},{7,27},{8,20},{9,... | collective-permute-start | bytes 98312 | tf_op jit(solution)/shard_map/ppermute | solution.py:298
  9.8 3.4 %collective-permute-start.3 = (bf16[32,512]{1,0:T(8,128)(2,1)S(1)}, bf16[32,512]{1,0:T(8,128)(2,1)S(1)}, u32[]{:S(2)}, u32[]{:S(2)}) collective-permute-start(bf16[32,512]{1,0:T(8,128)(2,1)S(1)} %collective-permute-done._.refs_0_), channel_id=1, source_target_pairs={{0,20},{1,21},{2,22},{3,23},{4,16},{5,17},{6,18},{7,19},{8,28},{9,... | collective-permute-start | bytes 98312 | tf_op jit(solution)/shard_map/ppermute | solution.py:298
  10.0 3.3 %collective-permute-start.2 = (bf16[32,512]{1,0:T(8,128)(2,1)S(1)}, bf16[32,512]{1,0:T(8,128)(2,1)S(1)}, u32[]{:S(2)}, u32[]{:S(2)}) collective-permute-start(bf16[32,512]{1,0:T(8,128)(2,1)S(1)} %collective-permute-done._.refs_0_), channel_id=1, source_target_pairs={{0,12},{1,13},{2,14},{3,15},{4,8},{5,9},{6,10},{7,11},{8,4},{9,5},... | collective-permute-start | bytes 98312 | tf_op jit(solution)/shard_map/ppermute | solution.py:298
  15.7 2.2 %collective-permute-start.7 = (bf16[256,512]{1,0:T(8,128)(2,1)S(1)}, bf16[256,512]{1,0:T(8,128)(2,1)S(1)}, u32[]{:S(2)}, u32[]{:S(2)}) collective-permute-start(bf16[256,512]{1,0:T(8,128)(2,1)S(1)} %collective-permute-done.6.refs_3_), channel_id=1, source_target_pairs={{0,4},{4,0},{8,12},{12,8},{16,20},{20,16},{24,28},{28,24},{1,5},{5... | collective-permute-start | bytes 786440 | tf_op jit(solution)/shard_map/ppermute | solution.py:286
  16.5 1.3 %collective-permute-start.5 = (bf16[128,512]{1,0:T(8,128)(2,1)S(1)}, bf16[128,512]{1,0:T(8,128)(2,1)S(1)}, u32[]{:S(2)}, u32[]{:S(2)}) collective-permute-start(bf16[128,512]{1,0:T(8,128)(2,1)S(1)} %parts_of_weight.1.refs_1_), channel_id=1, source_target_pairs={{0,4},{4,0},{8,12},{12,8},{16,20},{20,16},{24,28},{28,24},{1,5},{5... | collective-permute-start | bytes 393224 | tf_op jit(solution)/shard_map/ppermute | solution.py:286
  20.2 1.8 %collective-permute-start.8 = (bf16[384,512]{1,0:T(8,128)(2,1)S(1)}, bf16[384,512]{1,0:T(8,128)(2,1)S(1)}, u32[]{:S(2)}, u32[]{:S(2)}) collective-permute-start(bf16[384,512]{1,0:T(8,128)(2,1)S(1)} %get-tuple-element.51.own_ref), channel_id=1, source_target_pairs={{0,4},{4,0},{8,12},{12,8},{16,20},{20,16},{24,28},{28,24},{1,5},{5... | collective-permute-start | bytes 1179656 | tf_op jit(solution)/shard_map/ppermute | solution.py:286
  22.4 5.5 %collective-permute-start.13 = (bf16[64,512]{1,0:T(8,128)(2,1)S(1)}, bf16[64,512]{1,0:T(8,128)(2,1)S(1)}, u32[]{:S(2)}, u32[]{:S(2)}) collective-permute-start(bf16[64,512]{1,0:T(8,128)(2,1)S(1)} %get-tuple-element.69), channel_id=1, source_target_pairs={{0,12},{1,13},{2,14},{3,15},{4,8},{5,9},{6,10},{7,11},{8,4},{9,5},... | collective-permute-start | bytes 196616 | tf_op jit(solution)/shard_map/ppermute | solution.py:298
  22.9 6.2 %collective-permute-start.14 = (bf16[64,512]{1,0:T(8,128)(2,1)S(1)}, bf16[64,512]{1,0:T(8,128)(2,1)S(1)}, u32[]{:S(2)}, u32[]{:S(2)}) collective-permute-start(bf16[64,512]{1,0:T(8,128)(2,1)S(1)} %get-tuple-element.70), channel_id=1, source_target_pairs={{0,20},{1,21},{2,22},{3,23},{4,16},{5,17},{6,18},{7,19},{8,28},{9,... | collective-permute-start | bytes 196616 | tf_op jit(solution)/shard_map/ppermute | solution.py:298
  24.2 4.9 %collective-permute-start.15 = (bf16[64,512]{1,0:T(8,128)(2,1)S(1)}, bf16[64,512]{1,0:T(8,128)(2,1)S(1)}, u32[]{:S(2)}, u32[]{:S(2)}) collective-permute-start(bf16[64,512]{1,0:T(8,128)(2,1)S(1)} %get-tuple-element.71), channel_id=1, source_target_pairs={{0,28},{1,29},{2,30},{3,31},{4,24},{5,25},{6,26},{7,27},{8,20},{9,... | collective-permute-start | bytes 196616 | tf_op jit(solution)/shard_map/ppermute | solution.py:298
  26.0 6.1 %collective-permute-start.9 = (bf16[64,512]{1,0:T(8,128)(2,1)S(1)}, bf16[64,512]{1,0:T(8,128)(2,1)S(1)}, u32[]{:S(2)}, u32[]{:S(2)}) collective-permute-start(bf16[64,512]{1,0:T(8,128)(2,1)S(1)} %get-tuple-element.63), channel_id=1, source_target_pairs={{0,12},{1,13},{2,14},{3,15},{4,8},{5,9},{6,10},{7,11},{8,4},{9,5},... | collective-permute-start | bytes 196616 | tf_op jit(solution)/shard_map/ppermute | solution.py:298
  26.5 5.7 %collective-permute-start.10 = (bf16[64,512]{1,0:T(8,128)(2,1)S(1)}, bf16[64,512]{1,0:T(8,128)(2,1)S(1)}, u32[]{:S(2)}, u32[]{:S(2)}) collective-permute-start(bf16[64,512]{1,0:T(8,128)(2,1)S(1)} %get-tuple-element.64), channel_id=1, source_target_pairs={{0,20},{1,21},{2,22},{3,23},{4,16},{5,17},{6,18},{7,19},{8,28},{9,... | collective-permute-start | bytes 196616 | tf_op jit(solution)/shard_map/ppermute | solution.py:298
  27.8 4.9 %collective-permute-start.11 = (bf16[64,512]{1,0:T(8,128)(2,1)S(1)}, bf16[64,512]{1,0:T(8,128)(2,1)S(1)}, u32[]{:S(2)}, u32[]{:S(2)}) collective-permute-start(bf16[64,512]{1,0:T(8,128)(2,1)S(1)} %get-tuple-element.65), channel_id=1, source_target_pairs={{0,28},{1,29},{2,30},{3,31},{4,24},{5,25},{6,26},{7,27},{8,20},{9,... | collective-permute-start | bytes 196616 | tf_op jit(solution)/shard_map/ppermute | solution.py:298
  29.1 8.0 %collective-permute-start.16 = (bf16[64,512]{1,0:T(8,128)(2,1)S(1)}, bf16[64,512]{1,0:T(8,128)(2,1)S(1)}, u32[]{:S(2)}, u32[]{:S(2)}) collective-permute-start(bf16[64,512]{1,0:T(8,128)(2,1)S(1)} %sum_of_whole_shards_over_chips.1), channel_id=1, source_target_pairs={{0,5},{1,4},{2,7},{3,6},{4,3},{5,2},{6,1},{7,0},{8,13},{9,12},{10,... | collective-permute-start | bytes 196616 | tf_op jit(solution)/shard_map/ppermute | solution.py:298
  32.8 4.3 %collective-permute-start.12 = (bf16[64,256]{1,0:T(8,128)(2,1)S(1)}, bf16[64,256]{1,0:T(8,128)(2,1)S(1)}, u32[]{:S(2)}, u32[]{:S(2)}) collective-permute-start(bf16[64,256]{1,0:T(8,128)(2,1)S(1)} %get-tuple-element.67), channel_id=1, source_target_pairs={{0,6},{1,7},{2,4},{3,5},{4,2},{5,3},{6,0},{7,1},{8,14},{9,15},{10,... | collective-permute-start | bytes 98312 | tf_op jit(solution)/shard_map/ppermute | solution.py:298
  37.2 3.2 %collective-permute-start.17 = (bf16[64,512]{1,0:T(8,128)(2,1)S(1)}, bf16[64,512]{1,0:T(8,128)(2,1)S(1)}, u32[]{:S(2)}, u32[]{:S(2)}) collective-permute-start(bf16[64,512]{1,0:T(8,128)(2,1)S(1)} %sum_over_shards.1.own_ref), channel_id=1, source_target_pairs={{0,4},{4,0},{8,12},{12,8},{16,20},{20,16},{24,28},{28,24},{1,5},{5... | collective-permute-start | bytes 196616 | tf_op jit(solution)/shard_map/ppermute | solution.py:286
  40.4 4.9 %collective-permute-start.20 = (bf16[64,512]{1,0:T(8,128)(2,1)S(1)}, bf16[64,512]{1,0:T(8,128)(2,1)S(1)}, u32[]{:S(2)}, u32[]{:S(2)}) collective-permute-start(bf16[64,512]{1,0:T(8,128)(2,1)S(1)} %mean_of_both_cores.1.refs_0_), channel_id=1, source_target_pairs={{0,28},{1,29},{2,30},{3,31},{4,24},{5,25},{6,26},{7,27},{8,20},{9,... | collective-permute-start | bytes 196616 | tf_op jit(solution)/shard_map/ppermute | solution.py:298
  41.9 5.2 %collective-permute-start.19 = (bf16[64,512]{1,0:T(8,128)(2,1)S(1)}, bf16[64,512]{1,0:T(8,128)(2,1)S(1)}, u32[]{:S(2)}, u32[]{:S(2)}) collective-permute-start(bf16[64,512]{1,0:T(8,128)(2,1)S(1)} %mean_of_both_cores.1.refs_0_), channel_id=1, source_target_pairs={{0,20},{1,21},{2,22},{3,23},{4,16},{5,17},{6,18},{7,19},{8,28},{9,... | collective-permute-start | bytes 196616 | tf_op jit(solution)/shard_map/ppermute | solution.py:298
  43.0 4.1 %collective-permute-start.18 = (bf16[64,512]{1,0:T(8,128)(2,1)S(1)}, bf16[64,512]{1,0:T(8,128)(2,1)S(1)}, u32[]{:S(2)}, u32[]{:S(2)}) collective-permute-start(bf16[64,512]{1,0:T(8,128)(2,1)S(1)} %mean_of_both_cores.1.refs_0_), channel_id=1, source_target_pairs={{0,12},{1,13},{2,14},{3,15},{4,8},{5,9},{6,10},{7,11},{8,4},{9,5},... | collective-permute-start | bytes 196616 | tf_op jit(solution)/shard_map/ppermute | solution.py:298

commit v5 on v4

--- a/solution.py
+++ b/solution.py
@@ -69,7 +69,7 @@
     copy.wait()
 
 
-def prepare_kernel(slots, _, lengths_ref, sibling_ref, *refs):
+def prepare_kernel(slots, lengths_ref, sibling_ref, *refs):
     inputs, held = refs[:6], refs[6:11]
     (events_t_ref, key_t_ref, value_t_ref, weight_ref, gated_ref, first_ref,
      gate_ref, own_lengths_ref, sems) = refs[11:]
@@ -192,51 +192,65 @@
             grad_key_ref[places[s], columns[h]] = grad_key.astype(jnp.bfloat16)
 
 
-def add_gradient(picks, events_ref, both_ref, columns, picked_ref, outs, at):
-    part_rows = outs[0].shape[0]
+def gradient_rows(picks, part_rows, events_ref, both_ref, columns, picked_ref):
     shard_rows = events_ref.shape[0] // lax.axis_size("fsdp")
     chip = lax.div(lax.axis_index("dp"), CORES)
     for i, (k, shard) in enumerate(picks):
         start = pl.multiple_of(shard * shard_rows + (chip ^ k) * part_rows, part_rows)
         picked_ref[i * part_rows : (i + 1) * part_rows] = events_ref[pl.ds(start, part_rows)]
     total = dot(picked_ref[: len(picks) * part_rows], both_ref[:, columns])
-    for i, (k, _) in enumerate(picks):
-        block = total[i * part_rows : (i + 1) * part_rows]
-        outs[k][:, at(i) : at(i) + total.shape[1]] = block.astype(outs[k].dtype)
+    return [total[i * part_rows : (i + 1) * part_rows] for i in range(len(picks))]
 
 
 def summing_core(k):
     return lax.rem(lax.axis_index("dp"), CORES) ^ (1 if k else 0)
 
 
-def whole_gradient_kernel(pairs, events_ref, own_ref, got_ref, both_ref, *refs):
-    outs, picked_ref = refs[:-1], refs[-1]
-    rows, width = own_ref.shape
+def half_gradient(shard, core_flip, events_ref, both_ref, out_ref, picked_ref):
+    chips, part_rows, half = out_ref.shape
+    for group in (range(1), range(1, chips)):
+        core = summing_core(group[0]) ^ core_flip
+        columns = pl.ds(pl.multiple_of(core * half, half), half)
+        picks = [(k, shard) for k in group]
+        blocks = gradient_rows(picks, part_rows, events_ref, both_ref, columns, picked_ref)
+        for k, block in zip(group, blocks):
+            out_ref[k] = block.astype(out_ref.dtype)
+
+
+def middle_gradient_kernel(events_ref, own_ref, got_ref, both_ref, out_ref, picked_ref):
+    rows = own_ref.shape[0]
     both_ref[:rows] = own_ref[...]
     both_ref[rows:] = got_ref[...]
+    shard = lax.axis_index("fsdp") ^ (lax.axis_size("fsdp") // 2)
+    half_gradient(shard, 1, events_ref, both_ref, out_ref, picked_ref)
+
+
+def own_gradient_kernel(events_ref, both_ref, out_ref, picked_ref):
+    half_gradient(lax.axis_index("fsdp"), 0, events_ref, both_ref, out_ref, picked_ref)
+
+
+def whole_gradient_kernel(pairs, events_ref, both_ref, *refs):
+    outs, picked_ref = refs[:-1], refs[-1]
+    width = both_ref.shape[1]
     here = lax.axis_index("fsdp")
     for p, flips in enumerate(pairs):
         picks = [
             (k, here ^ jnp.where(summing_core(k) == 0, flips[0], flips[1]))
             for k in range(len(outs))
         ]
-        add_gradient(picks, events_ref, both_ref, slice(None), picked_ref, outs,
-                     lambda i: p * width)
-
-
-def half_gradient_kernel(events_ref, both_ref, *refs):
-    outs, picked_ref = refs[:-1], refs[-1]
-    half = both_ref.shape[1] // CORES
-    here = lax.axis_index("fsdp")
-    chips = range(len(outs))
-    for group in (chips[:1], chips[1:]):
-        columns = pl.ds(pl.multiple_of(summing_core(group[0]) * half, half), half)
-        picks = [(k, here ^ z) for k in group for z in (0, lax.axis_size("fsdp") // 2)]
-        add_gradient(picks, events_ref, both_ref, columns, picked_ref, outs,
-                     lambda i: i % 2 * half)
-
-
-def chip_sum_kernel(term_count, _, *refs):
+        part_rows = outs[0].shape[0]
+        blocks = gradient_rows(picks, part_rows, events_ref, both_ref, slice(None), picked_ref)
+        for out, block in zip(outs, blocks):
+            out[:, p * width : (p + 1) * width] = block.astype(out.dtype)
+
+
+def with_middle_kernel(_, own_ref, middle_ref, *outs):
+    for k, out in enumerate(outs):
+        total = own_ref[k] + middle_ref[k].astype(jnp.float32)
+        out[...] = total.astype(out.dtype)
+
+
+def chip_sum_kernel(term_count, *refs):
     terms, outs = refs[:term_count], refs[term_count:]
     at = 0
     for out in outs:
@@ -248,18 +262,19 @@
         at += out.shape[1]
 
 
-def shard_sum_kernel(own_ref, middle_ref, *refs):
-    wholes, out_ref, total_ref = refs[:-2], refs[-2], refs[-1]
+def shard_sum_kernel(chips, *refs):
+    halves, wholes, (out_ref, total_ref) = refs[:chips], refs[chips:-2], refs[-2:]
     total = wholes[0][...].astype(jnp.float32)
     for whole in wholes[1:]:
         total = total + whole[...].astype(jnp.float32)
     total_ref[...] = total
-    half = own_ref.shape[1]
+    half = halves[0].shape[1]
     core = lax.rem(lax.axis_index("dp"), CORES)
     columns = pl.ds(pl.multiple_of(core * half, half), half)
-    total_ref[:, columns] += own_ref[...]
-    columns = pl.ds(pl.multiple_of((1 - core) * half, half), half)
-    total_ref[:, columns] += middle_ref[...].astype(jnp.float32)
+    own = halves[0][...]
+    for term in halves[1:]:
+        own = own + term[...].astype(jnp.float32)
+    total_ref[:, columns] += own
     out_ref[...] = total_ref[...].astype(out_ref.dtype)
 
 
@@ -337,6 +352,7 @@
 
 def share(group, part, wholes, ready, dp_count, fsdp_count):
     alike = (0,) * CORES
+    part, ready = lax.optimization_barrier((part, ready))
     parts, members = [part], [1]
     for chip_bits in range(1, group // CORES):
         parts.append(cross(part, dp_count, fsdp_count, chip_bits, alike))
@@ -352,7 +368,7 @@
         )
     held = [(part, (fsdp_count // 2,) * CORES, members)]
     for block, flips in wholes:
-        held.append((lax.optimization_barrier((block, part, ready))[0], flips, [None]))
+        held.append((lax.optimization_barrier((block, part))[0], flips, [None]))
     found = []
     for block, flips, members in held:
         moved = [m if m is None else m ^ 1 for m in members]
@@ -384,9 +400,9 @@
     prepared = call(
         functools.partial(prepare_kernel, slots),
         "prepared_operands",
-        [part, lengths, sibling_events]
+        [lengths, sibling_events]
         + [flat_events, keys, values, cotangent, query_weight, gates],
-        [ANYWHERE, FAR, NEAR] + [FAR] * 6,
+        [FAR, NEAR] + [FAR] * 6,
         (
             shape(rows, model_width),
             shape(rows, width),
@@ -405,7 +421,7 @@
             pltpu.SMEM(lengths.shape, jnp.int32),
             pltpu.SemaphoreType.DMA((7,)),
         ],
-        flops=22 * 10**8,
+        flops=5 * 10**9,
     )
     near_events, near_keys, near_values, near_cotangent, near_weight = prepared[:5]
     events_t, keys_t, values_t, weight, gated, first = prepared[5:]
@@ -440,31 +456,44 @@
     if staged:
         pairs = shard_pairs(fsdp_count)
         got = flip(grad_query, "dp", dp_count, 1)
-        picked = pltpu.VMEM((2 * chips * part_rows, CORES * rows), bf16)
-
-        def for_chips(columns):
-            return tuple(shape(part_rows, columns, dtype=bf16 if k else f32) for k in range(chips))
-
-        both, *whole_terms = call(
+        picked = pltpu.VMEM((chips * part_rows, CORES * rows), bf16)
+        halves = (chips, part_rows, half_width)
+        work = dict(
+            flops=4 * rows * shard_rows * half_width,
+            moved=2 * (shard_rows + half_width) * CORES * rows,
+        )
+        both, middle = call(
+            middle_gradient_kernel,
+            "weight_gradient_of_middle_shard",
+            [events_t, grad_query, got],
+            [NEAR] * 3,
+            (shape(CORES * rows, width), shape(*halves)),
+            [picked],
+            **work,
+        )
+        middle = cross(middle, dp_count, fsdp_count, 0, (fsdp_count // 2,) * CORES)
+        whole_terms = call(
             functools.partial(whole_gradient_kernel, pairs),
             "weight_gradient_of_whole_shards",
-            [events_t, grad_query, got],
-            [NEAR] * 3,
-            (shape(CORES * rows, width),) + for_chips(len(pairs) * width),
-            [picked],
-            flops=4 * rows * shard_rows * len(pairs) * width,
-            moved=2 * model_width * (rows + width),
-        )
-        terms = call(
-            half_gradient_kernel,
-            "weight_gradient_of_halves",
             [events_t, both],
             [NEAR] * 2,
-            for_chips(2 * half_width),
+            tuple(
+                shape(part_rows, len(pairs) * width, dtype=bf16 if k else f32)
+                for k in range(chips)
+            ),
             [picked],
-            flops=4 * rows * shard_rows * width,
-            moved=2 * model_width * (rows + width),
-        )
+            **work,
+        )
+        terms = call(
+            own_gradient_kernel,
+            "weight_gradient_of_own_shard",
+            [events_t, both],
+            [NEAR] * 2,
+            shape(*halves, dtype=f32),
+            [picked],
+            **work,
+        )
+        terms = [terms]
     grad_keys, grad_values, grad_gates = call(
         functools.partial(outputs_kernel, slots),
         "key_value_gate_gradients",
@@ -480,29 +509,28 @@
         def to_chip(block, k):
             return cross(block, dp_count, fsdp_count, k, alike)
 
-        whole_terms[1:] = far_first(chips, lambda k: to_chip(whole_terms[k], k))
+        whole_terms = [whole_terms[0]] + far_first(chips, lambda k: to_chip(whole_terms[k], k))
         wholes = call(
             functools.partial(chip_sum_kernel, chips),
             "sum_of_whole_shards_over_chips",
-            [both] + whole_terms,
-            [ANYWHERE] + [NEAR] * chips,
+            whole_terms,
+            [NEAR] * chips,
             (shape(part_rows, width),) * len(pairs),
         )
         wholes = [cross(a, dp_count, fsdp_count, 0, p) for a, p in zip(wholes, pairs)]
+        terms = call(
+            with_middle_kernel,
+            "own_and_middle_shard",
+            [grad_keys, terms[0], middle],
+            [FAR] + [NEAR] * 2,
+            tuple(shape(part_rows, half_width, dtype=bf16 if k else f32) for k in range(chips)),
+        )
         terms = [terms[0]] + far_first(chips, lambda k: to_chip(terms[k], k))
-        own_half, middle = call(
-            functools.partial(chip_sum_kernel, chips),
-            "sum_of_halves_over_chips",
-            [grad_keys] + terms,
-            [FAR] + [NEAR] * chips,
-            (shape(part_rows, half_width, dtype=f32), shape(part_rows, half_width)),
-        )
-        middle = cross(middle, dp_count, fsdp_count, 0, (fsdp_count // 2,) * CORES)
         total = call(
-            shard_sum_kernel,
+            functools.partial(shard_sum_kernel, chips),
             "sum_over_shards",
-            [own_half, middle] + wholes,
-            [NEAR] * (2 + len(wholes)),
+            terms + wholes,
+            [NEAR] * (chips + len(wholes)),
             shape(part_rows, width),
             [pltpu.VMEM((part_rows, width), f32)],
         )

time: 48.2 us -> 48.9 us (1.015)
  waiting for transfers between devices: 13.1 us -> 16.8 us
  starting transfers between devices: 25.6 us -> 22.3 us
    ppermute x16, waiting for transfers between devices: 9.54 us -> 13 us  [cross(): return lax.ppermute(block, BOTH, pairs)]
    ppermute x5, starting transfers between devices: 4.18 us -> 1.59 us  [flip(): return lax.ppermute(block, axis, [(i, i ^ bits) for i in range(count)])]
    ppermute x16, starting transfers between devices: 21.4 us -> 20.7 us  [cross(): return lax.ppermute(block, BOTH, pairs)]
    pallas_call x12 -> x13, Pallas kernels: 8.59 us -> 8.85 us  [call(): pl.pallas_call(kernel, out_shape=out_shape, in_specs=in_specs, out_specs=...]
  transfers between devices with their start and end apart: 21 -> 21, of which waited for: 11 -> 13; matrix products, arithmetic and copies ran while one was open for 0% -> 0% of each run, Pallas kernels for 10% -> 11%
where the time goes in v5:
time: 48.9 us; the launch traced here: 48.7 us
  starting transfers between devices  22.3 us (46%)
  waiting for transfers between devices  16.8 us (34%)
  Pallas kernels  8.85 us (18%)
  between operations  0.72 us (1%)
    ppermute x16, starting transfers between devices, cross(): return lax.ppermute(block, BOTH, pairs)  20.7 us
    ppermute x16, waiting for transfers between devices, cross(): return lax.ppermute(block, BOTH, pairs)  13 us
    pallas_call x13, Pallas kernels, call(): pl.pallas_call(kernel, out_shape=out_shape, in_specs=in_specs, out_specs=...  8.85 us
    ppermute x5, waiting for transfers between devices, flip(): return lax.ppermute(block, axis, [(i, i ^ bits) for i in range(count)])  3.83 us
    ppermute x5, starting transfers between devices, flip(): return lax.ppermute(block, axis, [(i, i ^ bits) for i in range(count)])  1.59 us
  transfers between devices with their start and end apart: 21, of which 13 were waited for; matrix products, arithmetic and copies ran while one was open for 0% of the time, Pallas kernels for 11%

profile of v5, /device:TPU:0, one launch (start us, length us, event | category | flops | bytes accessed | tf_op | source)
XLA Modules:
  0.0 48.7 jit_solution(10893519110235920343)
XLA Ops:
  0.6 0.5 %collective-permute-start = (bf16[384,1024]{1,0:T(8,128)(2,1)}, bf16[384,1024]{1,0:T(8,128)(2,1)S(1)}, u32[]{:S(2)}, u32[]{:S(2)}) collective-permute-start(bf16[384,1024]{1,0:T(8,128)(2,1)} %bitcast.9), channel_id=1, source_target_pairs={{0,4},{4,0},{8,12},{12,8},{16,20},{20,16},{24,28},{28,24},{1,5},{5... | collective-permute-start | bytes 2359304 | tf_op jit(solution)/shard_map/ppermute | solution.py:301
  1.1 0.8 %own_part_of_weight.1 = bf16[32,512]{1,0:T(8,128)(2,1)S(1)} custom-call(bf16[256,512]{1,0:T(8,128)(2,1)} %block_ref.1), custom_call_target="tpu_custom_call" | custom-call | tf_op jit(solution)/shard_map/own_part_of_weight/pallas_call | solution.py:33
  1.9 3.8 %collective-permute-start.1 = (bf16[32,512]{1,0:T(8,128)(2,1)S(1)}, bf16[32,512]{1,0:T(8,128)(2,1)S(1)}, u32[]{:S(2)}, u32[]{:S(2)}) collective-permute-start(bf16[32,512]{1,0:T(8,128)(2,1)S(1)} %own_part_of_weight.1), channel_id=1, source_target_pairs={{0,6},{1,7},{2,4},{3,5},{4,2},{5,3},{6,0},{7,1},{8,14},{9,15},{10,... | collective-permute-start | bytes 98312 | tf_op jit(solution)/shard_map/ppermute | solution.py:313
  5.7 1.2 %collective-permute-start.6 = (bf16[256,512]{1,0:T(8,128)(2,1)}, bf16[256,512]{1,0:T(8,128)(2,1)S(1)}, u32[]{:S(2)}, u32[]{:S(2)}) collective-permute-start(bf16[256,512]{1,0:T(8,128)(2,1)} %block_ref.1), channel_id=1, source_target_pairs={{0,5},{1,4},{2,7},{3,6},{4,3},{5,2},{6,1},{7,0},{8,13},{9,12},{10,... | collective-permute-start | bytes 786440 | tf_op jit(solution)/shard_map/ppermute | solution.py:313
  6.9 2.3 %prepared_operands.1 = (bf16[384,1024]{1,0:T(8,128)(2,1)S(1)}, bf16[384,512]{1,0:T(8,128)(2,1)S(1)}, bf16[384,512]{1,0:T(8,128)(2,1)S(1)}, bf16[384,512]{1,0:T(8...) custom-call(s32[96]{0:T(128)} %lengths_ref.1, ...), custom_call_target="tpu_custom_call" | custom-call | flops 5000000000 | tf_op jit(solution)/shard_map/prepared_operands/pallas_call | solution.py:33
  9.2 2.4 %collective-permute-start.4 = (bf16[32,512]{1,0:T(8,128)(2,1)S(1)}, bf16[32,512]{1,0:T(8,128)(2,1)S(1)}, u32[]{:S(2)}, u32[]{:S(2)}) collective-permute-start(bf16[32,512]{1,0:T(8,128)(2,1)S(1)} %collective-permute-done.1.refs_0_), channel_id=1, source_target_pairs={{0,28},{1,29},{2,30},{3,31},{4,24},{5,25},{6,26},{7,27},{8,20},{9,... | collective-permute-start | bytes 98312 | tf_op jit(solution)/shard_map/ppermute | solution.py:313
  12.0 0.4 collective-permute-start.2
  12.4 1.2 %collective-permute-done.4.refs_3_ = bf16[32,512]{1,0:T(8,128)(2,1)S(1)} collective-permute-done((bf16[32,512]{1,0:T(8,128)(2,1)S(1)}, bf16[32,512]{1,0:T(8,128)(2,1)S(1)}, u32[]{:S(2)}, u32[]{:S(2)}) %collective-permute-start.4) | collective-permute-done | bytes 32800 | tf_op jit(solution)/shard_map/ppermute | solution.py:313
  13.5 1.4 %collective-permute-done.3.refs_2_ = bf16[32,512]{1,0:T(8,128)(2,1)S(1)} collective-permute-done((bf16[32,512]{1,0:T(8,128)(2,1)S(1)}, bf16[32,512]{1,0:T(8,128)(2,1)S(1)}, u32[]{:S(2)}, u32[]{:S(2)}) %collective-permute-start.3) | collective-permute-done | bytes 32800 | tf_op jit(solution)/shard_map/ppermute | solution.py:313
  15.9 1.2 %collective-permute-done.5.refs_2_ = bf16[128,512]{1,0:T(8,128)(2,1)S(1)} collective-permute-done((bf16[128,512]{1,0:T(8,128)(2,1)S(1)}, bf16[128,512]{1,0:T(8,128)(2,1)S(1)}, u32[]{:S(2)}, u32[]{:S(2)}) %collective-permute-start.5) | collective-permute-done | bytes 131104 | tf_op jit(solution)/shard_map/ppermute | solution.py:301
  17.1 2.4 %attention_to_grad_query.1 = (bf16[384,512]{1,0:T(8,128)(2,1)S(1)}, bf16[384,512]{1,0:T(8,128)(2,1)S(1)}, f32[384,512]{1,0:T(8,128)S(1)}, bf16[384,512]{1,0:T(8,...) custom-call(bf16[256,512]{1,0:T(8,128)(2,1)S(1)} %get-tuple-element.39.refs_0_, ...), custom_call_target="tpu_custom_call" | custom-call | flops 603979776 | bytes 4718592 | tf_op jit(solution)/shard_map/attention_to_grad_query/pallas_call | solution.py:33
  19.8 1.5 %collective-permute-done.8.got_ref = bf16[384,512]{1,0:T(8,128)(2,1)S(1)} collective-permute-done((bf16[384,512]{1,0:T(8,128)(2,1)S(1)}, bf16[384,512]{1,0:T(8,128)(2,1)S(1)}, u32[]{:S(2)}, u32[]{:S(2)}) %collective-permute-start.8) | collective-permute-done | bytes 393248 | tf_op jit(solution)/shard_map/ppermute | solution.py:301
  21.6 1.6 %collective-permute-start.9 = (bf16[4,64,256]{2,1,0:T(8,128)(2,1)S(1)}, bf16[4,64,256]{2,1,0:T(8,128)(2,1)S(1)}, u32[]{:S(2)}, u32[]{:S(2)}) collective-permute-start(bf16[4,64,256]{2,1,0:T(8,128)(2,1)S(1)} %get-tuple-element.63), channel_id=1, source_target_pairs={{0,6},{1,7},{2,4},{3,5},{4,2},{5,3},{6,0},{7,1},{8,14},{9,15},{10,... | collective-permute-start | bytes 393224 | tf_op jit(solution)/shard_map/ppermute | solution.py:313
  23.6 0.8 %collective-permute-start.13 = (bf16[64,512]{1,0:T(8,128)(2,1)S(1)}, bf16[64,512]{1,0:T(8,128)(2,1)S(1)}, u32[]{:S(2)}, u32[]{:S(2)}) collective-permute-start(bf16[64,512]{1,0:T(8,128)(2,1)S(1)} %get-tuple-element.69), channel_id=1, source_target_pairs={{0,12},{1,13},{2,14},{3,15},{4,8},{5,9},{6,10},{7,11},{8,4},{9,5},... | collective-permute-start | bytes 196616 | tf_op jit(solution)/shard_map/ppermute | solution.py:313
  24.5 1.3 %collective-permute-start.14 = (bf16[64,512]{1,0:T(8,128)(2,1)S(1)}, bf16[64,512]{1,0:T(8,128)(2,1)S(1)}, u32[]{:S(2)}, u32[]{:S(2)}) collective-permute-start(bf16[64,512]{1,0:T(8,128)(2,1)S(1)} %get-tuple-element.70), channel_id=1, source_target_pairs={{0,20},{1,21},{2,22},{3,23},{4,16},{5,17},{6,18},{7,19},{8,28},{9,... | collective-permute-start | bytes 196616 | tf_op jit(solution)/shard_map/ppermute | solution.py:313
  25.8 0.9 %collective-permute-start.15 = (bf16[64,512]{1,0:T(8,128)(2,1)S(1)}, bf16[64,512]{1,0:T(8,128)(2,1)S(1)}, u32[]{:S(2)}, u32[]{:S(2)}) collective-permute-start(bf16[64,512]{1,0:T(8,128)(2,1)S(1)} %get-tuple-element.71), channel_id=1, source_target_pairs={{0,28},{1,29},{2,30},{3,31},{4,24},{5,25},{6,26},{7,27},{8,20},{9,... | collective-permute-start | bytes 196616 | tf_op jit(solution)/shard_map/ppermute | solution.py:313
  26.7 1.1 %collective-permute-done.13.refs_1_ = bf16[64,512]{1,0:T(8,128)(2,1)S(1)} collective-permute-done((bf16[64,512]{1,0:T(8,128)(2,1)S(1)}, bf16[64,512]{1,0:T(8,128)(2,1)S(1)}, u32[]{:S(2)}, u32[]{:S(2)}) %collective-permute-start.13) | collective-permute-done | bytes 65568 | tf_op jit(solution)/shard_map/ppermute | solution.py:313
  27.7 0.8 %collective-permute-done.14.refs_2_ = bf16[64,512]{1,0:T(8,128)(2,1)S(1)} collective-permute-done((bf16[64,512]{1,0:T(8,128)(2,1)S(1)}, bf16[64,512]{1,0:T(8,128)(2,1)S(1)}, u32[]{:S(2)}, u32[]{:S(2)}) %collective-permute-start.14) | collective-permute-done | bytes 65568 | tf_op jit(solution)/shard_map/ppermute | solution.py:313
  28.6 2.0 %collective-permute-done.15.refs_3_ = bf16[64,512]{1,0:T(8,128)(2,1)S(1)} collective-permute-done((bf16[64,512]{1,0:T(8,128)(2,1)S(1)}, bf16[64,512]{1,0:T(8,128)(2,1)S(1)}, u32[]{:S(2)}, u32[]{:S(2)}) %collective-permute-start.15) | collective-permute-done | bytes 65568 | tf_op jit(solution)/shard_map/ppermute | solution.py:313
  30.6 1.3 %collective-permute-start.16 = (bf16[64,512]{1,0:T(8,128)(2,1)S(1)}, bf16[64,512]{1,0:T(8,128)(2,1)S(1)}, u32[]{:S(2)}, u32[]{:S(2)}) collective-permute-start(bf16[64,512]{1,0:T(8,128)(2,1)S(1)} %sum_of_whole_shards_over_chips.1), channel_id=1, source_target_pairs={{0,5},{1,4},{2,7},{3,6},{4,3},{5,2},{6,1},{7,0},{8,13},{9,12},{10,... | collective-permute-start | bytes 196616 | tf_op jit(solution)/shard_map/ppermute | solution.py:313
  32.2 1.4 %key_value_gate_gradients.1 = (bf16[384,512]{1,0:T(8,128)(2,1)}, bf16[384,512]{1,0:T(8,128)(2,1)}, bf16[384,512]{1,0:T(8,128)(2,1)}) custom-call(f32[4,64,256]{2,1,0:T(8,128)S(1)} %weight_gradient_of_own_shard.1._.own_ref, bf16[384,512]{1,0:T(8,128)(2,1)S(1)} %get-tuple-element.54.query_ref, f32[384,512]{1,0:T(8,128)S(1)} %get-tuple-element.55.normed_ref, ...), custom_call_target="tpu_custom_call" | custom-call | flops 100663296 | bytes 2359296 | tf_op jit(solution)/shard_map/key_value_gate_gradients/pallas_call | solution.py:33
  33.7 1.1 %collective-permute-start.10 = (bf16[64,256]{1,0:T(8,128)(2,1)S(1)}, bf16[64,256]{1,0:T(8,128)(2,1)S(1)}, u32[]{:S(2)}, u32[]{:S(2)}) collective-permute-start(bf16[64,256]{1,0:T(8,128)(2,1)S(1)} %get-tuple-element.65), channel_id=1, source_target_pairs={{0,12},{1,13},{2,14},{3,15},{4,8},{5,9},{6,10},{7,11},{8,4},{9,5},... | collective-permute-start | bytes 98312 | tf_op jit(solution)/shard_map/ppermute | solution.py:313
  34.8 0.6 %collective-permute-start.11 = (bf16[64,256]{1,0:T(8,128)(2,1)S(1)}, bf16[64,256]{1,0:T(8,128)(2,1)S(1)}, u32[]{:S(2)}, u32[]{:S(2)}) collective-permute-start(bf16[64,256]{1,0:T(8,128)(2,1)S(1)} %get-tuple-element.66), channel_id=1, source_target_pairs={{0,20},{1,21},{2,22},{3,23},{4,16},{5,17},{6,18},{7,19},{8,28},{9,... | collective-permute-start | bytes 98312 | tf_op jit(solution)/shard_map/ppermute | solution.py:313
  35.4 1.9 %collective-permute-start.12 = (bf16[64,256]{1,0:T(8,128)(2,1)S(1)}, bf16[64,256]{1,0:T(8,128)(2,1)S(1)}, u32[]{:S(2)}, u32[]{:S(2)}) collective-permute-start(bf16[64,256]{1,0:T(8,128)(2,1)S(1)} %get-tuple-element.67), channel_id=1, source_target_pairs={{0,28},{1,29},{2,30},{3,31},{4,24},{5,25},{6,26},{7,27},{8,20},{9,... | collective-permute-start | bytes 98312 | tf_op jit(solution)/shard_map/ppermute | solution.py:313
  37.4 0.8 %collective-permute-done.11.refs_2_ = bf16[64,256]{1,0:T(8,128)(2,1)S(1)} collective-permute-done((bf16[64,256]{1,0:T(8,128)(2,1)S(1)}, bf16[64,256]{1,0:T(8,128)(2,1)S(1)}, u32[]{:S(2)}, u32[]{:S(2)}) %collective-permute-start.11) | collective-permute-done | bytes 32800 | tf_op jit(solution)/shard_map/ppermute | solution.py:313
  38.1 1.6 %collective-permute-done.12.refs_3_ = bf16[64,256]{1,0:T(8,128)(2,1)S(1)} collective-permute-done((bf16[64,256]{1,0:T(8,128)(2,1)S(1)}, bf16[64,256]{1,0:T(8,128)(2,1)S(1)}, u32[]{:S(2)}, u32[]{:S(2)}) %collective-permute-start.12) | collective-permute-done | bytes 32800 | tf_op jit(solution)/shard_map/ppermute | solution.py:313
  40.0 1.1 %collective-permute-done.17.sibling_ref = bf16[64,512]{1,0:T(8,128)(2,1)S(1)} collective-permute-done((bf16[64,512]{1,0:T(8,128)(2,1)S(1)}, bf16[64,512]{1,0:T(8,128)(2,1)S(1)}, u32[]{:S(2)}, u32[]{:S(2)}) %collective-permute-start.17) | collective-permute-done | bytes 65568 | tf_op jit(solution)/shard_map/ppermute | solution.py:301
  41.1 1.9 %collective-permute-start.20 = (bf16[64,512]{1,0:T(8,128)(2,1)S(1)}, bf16[64,512]{1,0:T(8,128)(2,1)S(1)}, u32[]{:S(2)}, u32[]{:S(2)}) collective-permute-start(bf16[64,512]{1,0:T(8,128)(2,1)S(1)} %mean_of_both_cores.1.refs_0_), channel_id=1, source_target_pairs={{0,28},{1,29},{2,30},{3,31},{4,24},{5,25},{6,26},{7,27},{8,20},{9,... | collective-permute-start | bytes 196616 | tf_op jit(solution)/shard_map/ppermute | solution.py:313
  43.4 0.8 %collective-permute-start.18 = (bf16[64,512]{1,0:T(8,128)(2,1)S(1)}, bf16[64,512]{1,0:T(8,128)(2,1)S(1)}, u32[]{:S(2)}, u32[]{:S(2)}) collective-permute-start(bf16[64,512]{1,0:T(8,128)(2,1)S(1)} %mean_of_both_cores.1.refs_0_), channel_id=1, source_target_pairs={{0,12},{1,13},{2,14},{3,15},{4,8},{5,9},{6,10},{7,11},{8,4},{9,5},... | collective-permute-start | bytes 196616 | tf_op jit(solution)/shard_map/ppermute | solution.py:313
  44.2 2.0 %collective-permute-done.20.refs_3_ = bf16[64,512]{1,0:T(8,128)(2,1)S(1)} collective-permute-done((bf16[64,512]{1,0:T(8,128)(2,1)S(1)}, bf16[64,512]{1,0:T(8,128)(2,1)S(1)}, u32[]{:S(2)}, u32[]{:S(2)}) %collective-permute-start.20) | collective-permute-done | bytes 65568 | tf_op jit(solution)/shard_map/ppermute | solution.py:313
  46.2 1.7 %collective-permute-done.19.refs_2_ = bf16[64,512]{1,0:T(8,128)(2,1)S(1)} collective-permute-done((bf16[64,512]{1,0:T(8,128)(2,1)S(1)}, bf16[64,512]{1,0:T(8,128)(2,1)S(1)}, u32[]{:S(2)}, u32[]{:S(2)}) %collective-permute-start.19) | collective-permute-done | bytes 65568 | tf_op jit(solution)/shard_map/ppermute | solution.py:313
  47.9 0.8 %blocks_in_place.1 = f32[256,512]{1,0:T(8,128)} custom-call(bf16[64,512]{1,0:T(8,128)(2,1)S(1)} %mean_of_both_cores.1.refs_0_, bf16[64,512]{1,0:T(8,128)(2,1)S(1)} %collective-permute-done.18.refs_1_, bf16[64,512]{1,0:T(8,128)(2,1)S(1)} %collective-permute-done.19.refs_2_, bf16[64,512]{1,0:T(8,128)(2,1)S(1)} %collective-permute-done.20.refs_3_), custom_call_target="tpu_custom_call" | custom-call | tf_op jit(solution)/shard_map/blocks_in_place/pallas_call | solution.py:33
  (23 shorter events, 3.3 us)
Async XLA Ops:
  0.6 6.3 %collective-permute-start = (bf16[384,1024]{1,0:T(8,128)(2,1)}, bf16[384,1024]{1,0:T(8,128)(2,1)S(1)}, u32[]{:S(2)}, u32[]{:S(2)}) collective-permute-start(bf16[384,1024]{1,0:T(8,128)(2,1)} %bitcast.9), channel_id=1, source_target_pairs={{0,4},{4,0},{8,12},{12,8},{16,20},{20,16},{24,28},{28,24},{1,5},{5... | collective-permute-start | bytes 2359304 | tf_op jit(solution)/shard_map/ppermute | solution.py:301
  1.9 7.3 %collective-permute-start.1 = (bf16[32,512]{1,0:T(8,128)(2,1)S(1)}, bf16[32,512]{1,0:T(8,128)(2,1)S(1)}, u32[]{:S(2)}, u32[]{:S(2)}) collective-permute-start(bf16[32,512]{1,0:T(8,128)(2,1)S(1)} %own_part_of_weight.1), channel_id=1, source_target_pairs={{0,6},{1,7},{2,4},{3,5},{4,2},{5,3},{6,0},{7,1},{8,14},{9,15},{10,... | collective-permute-start | bytes 98312 | tf_op jit(solution)/shard_map/ppermute | solution.py:313
  5.7 9.7 %collective-permute-start.6 = (bf16[256,512]{1,0:T(8,128)(2,1)}, bf16[256,512]{1,0:T(8,128)(2,1)S(1)}, u32[]{:S(2)}, u32[]{:S(2)}) collective-permute-start(bf16[256,512]{1,0:T(8,128)(2,1)} %block_ref.1), channel_id=1, source_target_pairs={{0,5},{1,4},{2,7},{3,6},{4,3},{5,2},{6,1},{7,0},{8,13},{9,12},{10,... | collective-permute-start | bytes 786440 | tf_op jit(solution)/shard_map/ppermute | solution.py:313
  9.2 4.3 %collective-permute-start.4 = (bf16[32,512]{1,0:T(8,128)(2,1)S(1)}, bf16[32,512]{1,0:T(8,128)(2,1)S(1)}, u32[]{:S(2)}, u32[]{:S(2)}) collective-permute-start(bf16[32,512]{1,0:T(8,128)(2,1)S(1)} %collective-permute-done.1.refs_0_), channel_id=1, source_target_pairs={{0,28},{1,29},{2,30},{3,31},{4,24},{5,25},{6,26},{7,27},{8,20},{9,... | collective-permute-start | bytes 98312 | tf_op jit(solution)/shard_map/ppermute | solution.py:313
  11.6 3.3 %collective-permute-start.3 = (bf16[32,512]{1,0:T(8,128)(2,1)S(1)}, bf16[32,512]{1,0:T(8,128)(2,1)S(1)}, u32[]{:S(2)}, u32[]{:S(2)}) collective-permute-start(bf16[32,512]{1,0:T(8,128)(2,1)S(1)} %collective-permute-done.1.refs_0_), channel_id=1, source_target_pairs={{0,20},{1,21},{2,22},{3,23},{4,16},{5,17},{6,18},{7,19},{8,28},{9,... | collective-permute-start | bytes 98312 | tf_op jit(solution)/shard_map/ppermute | solution.py:313
  12.0 3.3 %collective-permute-start.2 = (bf16[32,512]{1,0:T(8,128)(2,1)S(1)}, bf16[32,512]{1,0:T(8,128)(2,1)S(1)}, u32[]{:S(2)}, u32[]{:S(2)}) collective-permute-start(bf16[32,512]{1,0:T(8,128)(2,1)S(1)} %collective-permute-done.1.refs_0_), channel_id=1, source_target_pairs={{0,12},{1,13},{2,14},{3,15},{4,8},{5,9},{6,10},{7,11},{8,4},{9,5},... | collective-permute-start | bytes 98312 | tf_op jit(solution)/shard_map/ppermute | solution.py:313
  15.3 1.8 %collective-permute-start.7 = (bf16[256,512]{1,0:T(8,128)(2,1)S(1)}, bf16[256,512]{1,0:T(8,128)(2,1)S(1)}, u32[]{:S(2)}, u32[]{:S(2)}) collective-permute-start(bf16[256,512]{1,0:T(8,128)(2,1)S(1)} %collective-permute-done.6.refs_3_), channel_id=1, source_target_pairs={{0,4},{4,0},{8,12},{12,8},{16,20},{20,16},{24,28},{28,24},{1,5},{5... | collective-permute-start | bytes 786440 | tf_op jit(solution)/shard_map/ppermute | solution.py:301
  15.7 1.5 %collective-permute-start.5 = (bf16[128,512]{1,0:T(8,128)(2,1)S(1)}, bf16[128,512]{1,0:T(8,128)(2,1)S(1)}, u32[]{:S(2)}, u32[]{:S(2)}) collective-permute-start(bf16[128,512]{1,0:T(8,128)(2,1)S(1)} %parts_of_weight.1.refs_1_), channel_id=1, source_target_pairs={{0,4},{4,0},{8,12},{12,8},{16,20},{20,16},{24,28},{28,24},{1,5},{5... | collective-permute-start | bytes 393224 | tf_op jit(solution)/shard_map/ppermute | solution.py:301
  19.5 1.8 %collective-permute-start.8 = (bf16[384,512]{1,0:T(8,128)(2,1)S(1)}, bf16[384,512]{1,0:T(8,128)(2,1)S(1)}, u32[]{:S(2)}, u32[]{:S(2)}) collective-permute-start(bf16[384,512]{1,0:T(8,128)(2,1)S(1)} %get-tuple-element.52.own_ref), channel_id=1, source_target_pairs={{0,4},{4,0},{8,12},{12,8},{16,20},{20,16},{24,28},{28,24},{1,5},{5... | collective-permute-start | bytes 1179656 | tf_op jit(solution)/shard_map/ppermute | solution.py:301
  21.6 12.0 %collective-permute-start.9 = (bf16[4,64,256]{2,1,0:T(8,128)(2,1)S(1)}, bf16[4,64,256]{2,1,0:T(8,128)(2,1)S(1)}, u32[]{:S(2)}, u32[]{:S(2)}) collective-permute-start(bf16[4,64,256]{2,1,0:T(8,128)(2,1)S(1)} %get-tuple-element.63), channel_id=1, source_target_pairs={{0,6},{1,7},{2,4},{3,5},{4,2},{5,3},{6,0},{7,1},{8,14},{9,15},{10,... | collective-permute-start | bytes 393224 | tf_op jit(solution)/shard_map/ppermute | solution.py:313
  23.6 4.1 %collective-permute-start.13 = (bf16[64,512]{1,0:T(8,128)(2,1)S(1)}, bf16[64,512]{1,0:T(8,128)(2,1)S(1)}, u32[]{:S(2)}, u32[]{:S(2)}) collective-permute-start(bf16[64,512]{1,0:T(8,128)(2,1)S(1)} %get-tuple-element.69), channel_id=1, source_target_pairs={{0,12},{1,13},{2,14},{3,15},{4,8},{5,9},{6,10},{7,11},{8,4},{9,5},... | collective-permute-start | bytes 196616 | tf_op jit(solution)/shard_map/ppermute | solution.py:313
  24.5 4.1 %collective-permute-start.14 = (bf16[64,512]{1,0:T(8,128)(2,1)S(1)}, bf16[64,512]{1,0:T(8,128)(2,1)S(1)}, u32[]{:S(2)}, u32[]{:S(2)}) collective-permute-start(bf16[64,512]{1,0:T(8,128)(2,1)S(1)} %get-tuple-element.70), channel_id=1, source_target_pairs={{0,20},{1,21},{2,22},{3,23},{4,16},{5,17},{6,18},{7,19},{8,28},{9,... | collective-permute-start | bytes 196616 | tf_op jit(solution)/shard_map/ppermute | solution.py:313
  25.8 4.8 %collective-permute-start.15 = (bf16[64,512]{1,0:T(8,128)(2,1)S(1)}, bf16[64,512]{1,0:T(8,128)(2,1)S(1)}, u32[]{:S(2)}, u32[]{:S(2)}) collective-permute-start(bf16[64,512]{1,0:T(8,128)(2,1)S(1)} %get-tuple-element.71), channel_id=1, source_target_pairs={{0,28},{1,29},{2,30},{3,31},{4,24},{5,25},{6,26},{7,27},{8,20},{9,... | collective-permute-start | bytes 196616 | tf_op jit(solution)/shard_map/ppermute | solution.py:313
  30.6 6.7 %collective-permute-start.16 = (bf16[64,512]{1,0:T(8,128)(2,1)S(1)}, bf16[64,512]{1,0:T(8,128)(2,1)S(1)}, u32[]{:S(2)}, u32[]{:S(2)}) collective-permute-start(bf16[64,512]{1,0:T(8,128)(2,1)S(1)} %sum_of_whole_shards_over_chips.1), channel_id=1, source_target_pairs={{0,5},{1,4},{2,7},{3,6},{4,3},{5,2},{6,1},{7,0},{8,13},{9,12},{10,... | collective-permute-start | bytes 196616 | tf_op jit(solution)/shard_map/ppermute | solution.py:313
  33.7 3.7 %collective-permute-start.10 = (bf16[64,256]{1,0:T(8,128)(2,1)S(1)}, bf16[64,256]{1,0:T(8,128)(2,1)S(1)}, u32[]{:S(2)}, u32[]{:S(2)}) collective-permute-start(bf16[64,256]{1,0:T(8,128)(2,1)S(1)} %get-tuple-element.65), channel_id=1, source_target_pairs={{0,12},{1,13},{2,14},{3,15},{4,8},{5,9},{6,10},{7,11},{8,4},{9,5},... | collective-permute-start | bytes 98312 | tf_op jit(solution)/shard_map/ppermute | solution.py:313
  34.8 3.3 %collective-permute-start.11 = (bf16[64,256]{1,0:T(8,128)(2,1)S(1)}, bf16[64,256]{1,0:T(8,128)(2,1)S(1)}, u32[]{:S(2)}, u32[]{:S(2)}) collective-permute-start(bf16[64,256]{1,0:T(8,128)(2,1)S(1)} %get-tuple-element.66), channel_id=1, source_target_pairs={{0,20},{1,21},{2,22},{3,23},{4,16},{5,17},{6,18},{7,19},{8,28},{9,... | collective-permute-start | bytes 98312 | tf_op jit(solution)/shard_map/ppermute | solution.py:313
  35.4 4.3 %collective-permute-start.12 = (bf16[64,256]{1,0:T(8,128)(2,1)S(1)}, bf16[64,256]{1,0:T(8,128)(2,1)S(1)}, u32[]{:S(2)}, u32[]{:S(2)}) collective-permute-start(bf16[64,256]{1,0:T(8,128)(2,1)S(1)} %get-tuple-element.67), channel_id=1, source_target_pairs={{0,28},{1,29},{2,30},{3,31},{4,24},{5,25},{6,26},{7,27},{8,20},{9,... | collective-permute-start | bytes 98312 | tf_op jit(solution)/shard_map/ppermute | solution.py:313
  39.8 1.3 %collective-permute-start.17 = (bf16[64,512]{1,0:T(8,128)(2,1)S(1)}, bf16[64,512]{1,0:T(8,128)(2,1)S(1)}, u32[]{:S(2)}, u32[]{:S(2)}) collective-permute-start(bf16[64,512]{1,0:T(8,128)(2,1)S(1)} %sum_over_shards.1.own_ref), channel_id=1, source_target_pairs={{0,4},{4,0},{8,12},{12,8},{16,20},{20,16},{24,28},{28,24},{1,5},{5... | collective-permute-start | bytes 196616 | tf_op jit(solution)/shard_map/ppermute | solution.py:301
  41.1 5.0 %collective-permute-start.20 = (bf16[64,512]{1,0:T(8,128)(2,1)S(1)}, bf16[64,512]{1,0:T(8,128)(2,1)S(1)}, u32[]{:S(2)}, u32[]{:S(2)}) collective-permute-start(bf16[64,512]{1,0:T(8,128)(2,1)S(1)} %mean_of_both_cores.1.refs_0_), channel_id=1, source_target_pairs={{0,28},{1,29},{2,30},{3,31},{4,24},{5,25},{6,26},{7,27},{8,20},{9,... | collective-permute-start | bytes 196616 | tf_op jit(solution)/shard_map/ppermute | solution.py:313
  43.0 4.8 %collective-permute-start.19 = (bf16[64,512]{1,0:T(8,128)(2,1)S(1)}, bf16[64,512]{1,0:T(8,128)(2,1)S(1)}, u32[]{:S(2)}, u32[]{:S(2)}) collective-permute-start(bf16[64,512]{1,0:T(8,128)(2,1)S(1)} %mean_of_both_cores.1.refs_0_), channel_id=1, source_target_pairs={{0,20},{1,21},{2,22},{3,23},{4,16},{5,17},{6,18},{7,19},{8,28},{9,... | collective-permute-start | bytes 196616 | tf_op jit(solution)/shard_map/ppermute | solution.py:313
  43.4 4.5 %collective-permute-start.18 = (bf16[64,512]{1,0:T(8,128)(2,1)S(1)}, bf16[64,512]{1,0:T(8,128)(2,1)S(1)}, u32[]{:S(2)}, u32[]{:S(2)}) collective-permute-start(bf16[64,512]{1,0:T(8,128)(2,1)S(1)} %mean_of_both_cores.1.refs_0_), channel_id=1, source_target_pairs={{0,12},{1,13},{2,14},{3,15},{4,8},{5,9},{6,10},{7,11},{8,4},{9,5},... | collective-permute-start | bytes 196616 | tf_op jit(solution)/shard_map/ppermute | solution.py:313

commit v6 on v4

--- a/solution.py
+++ b/solution.py
@@ -69,7 +69,7 @@
     copy.wait()
 
 
-def prepare_kernel(slots, _, lengths_ref, sibling_ref, *refs):
+def prepare_kernel(slots, lengths_ref, sibling_ref, *refs):
     inputs, held = refs[:6], refs[6:11]
     (events_t_ref, key_t_ref, value_t_ref, weight_ref, gated_ref, first_ref,
      gate_ref, own_lengths_ref, sems) = refs[11:]
@@ -192,48 +192,42 @@
             grad_key_ref[places[s], columns[h]] = grad_key.astype(jnp.bfloat16)
 
 
-def add_gradient(picks, events_ref, both_ref, columns, picked_ref, outs, at):
+def summing_half(k, z):
+    return lax.rem(lax.axis_index("dp"), CORES) ^ (1 if k else 0) ^ (1 if z else 0)
+
+
+def gradient_kernel(shard_flips, events_ref, both_ref, outs, picked_ref):
     part_rows = outs[0].shape[0]
+    half = both_ref.shape[1] // CORES
     shard_rows = events_ref.shape[0] // lax.axis_size("fsdp")
-    chip = lax.div(lax.axis_index("dp"), CORES)
-    for i, (k, shard) in enumerate(picks):
-        start = pl.multiple_of(shard * shard_rows + (chip ^ k) * part_rows, part_rows)
-        picked_ref[i * part_rows : (i + 1) * part_rows] = events_ref[pl.ds(start, part_rows)]
-    total = dot(picked_ref[: len(picks) * part_rows], both_ref[:, columns])
-    for i, (k, _) in enumerate(picks):
-        block = total[i * part_rows : (i + 1) * part_rows]
-        outs[k][:, at(i) : at(i) + total.shape[1]] = block.astype(outs[k].dtype)
-
-
-def summing_core(k):
-    return lax.rem(lax.axis_index("dp"), CORES) ^ (1 if k else 0)
-
-
-def whole_gradient_kernel(pairs, events_ref, own_ref, got_ref, both_ref, *refs):
-    outs, picked_ref = refs[:-1], refs[-1]
-    rows, width = own_ref.shape
+    chip, here = lax.div(lax.axis_index("dp"), CORES), lax.axis_index("fsdp")
+    for other in range(CORES):
+        picks = [
+            (k, i, z)
+            for k in range(len(outs))
+            for i, z in enumerate(shard_flips)
+            if (k != 0) ^ (z != 0) == bool(other)
+        ]
+        for p, (k, _, z) in enumerate(picks):
+            start = pl.multiple_of((here ^ z) * shard_rows + (chip ^ k) * part_rows, part_rows)
+            picked_ref[p * part_rows : (p + 1) * part_rows] = events_ref[pl.ds(start, part_rows)]
+        core = summing_half(other, 0)
+        columns = pl.ds(pl.multiple_of(core * half, half), half)
+        total = dot(picked_ref[: len(picks) * part_rows], both_ref[:, columns])
+        for p, (k, i, _) in enumerate(picks):
+            block = total[p * part_rows : (p + 1) * part_rows]
+            outs[k][:, i * half : (i + 1) * half] = block.astype(outs[k].dtype)
+
+
+def far_gradient_kernel(shard_flips, events_ref, own_ref, got_ref, both_ref, *refs):
+    rows = own_ref.shape[0]
     both_ref[:rows] = own_ref[...]
     both_ref[rows:] = got_ref[...]
-    here = lax.axis_index("fsdp")
-    for p, flips in enumerate(pairs):
-        picks = [
-            (k, here ^ jnp.where(summing_core(k) == 0, flips[0], flips[1]))
-            for k in range(len(outs))
-        ]
-        add_gradient(picks, events_ref, both_ref, slice(None), picked_ref, outs,
-                     lambda i: p * width)
-
-
-def half_gradient_kernel(events_ref, both_ref, *refs):
-    outs, picked_ref = refs[:-1], refs[-1]
-    half = both_ref.shape[1] // CORES
-    here = lax.axis_index("fsdp")
-    chips = range(len(outs))
-    for group in (chips[:1], chips[1:]):
-        columns = pl.ds(pl.multiple_of(summing_core(group[0]) * half, half), half)
-        picks = [(k, here ^ z) for k in group for z in (0, lax.axis_size("fsdp") // 2)]
-        add_gradient(picks, events_ref, both_ref, columns, picked_ref, outs,
-                     lambda i: i % 2 * half)
+    gradient_kernel(shard_flips, events_ref, both_ref, refs[:-1], refs[-1])
+
+
+def near_gradient_kernel(shard_flips, events_ref, both_ref, *refs):
+    gradient_kernel(shard_flips, events_ref, both_ref, refs[:-1], refs[-1])
 
 
 def chip_sum_kernel(term_count, _, *refs):
@@ -248,34 +242,23 @@
         at += out.shape[1]
 
 
-def shard_sum_kernel(own_ref, middle_ref, *refs):
-    wholes, out_ref, total_ref = refs[:-2], refs[-2], refs[-1]
-    total = wholes[0][...].astype(jnp.float32)
-    for whole in wholes[1:]:
-        total = total + whole[...].astype(jnp.float32)
-    total_ref[...] = total
-    half = own_ref.shape[1]
-    core = lax.rem(lax.axis_index("dp"), CORES)
-    columns = pl.ds(pl.multiple_of(core * half, half), half)
-    total_ref[:, columns] += own_ref[...]
-    columns = pl.ds(pl.multiple_of((1 - core) * half, half), half)
-    total_ref[:, columns] += middle_ref[...].astype(jnp.float32)
-    out_ref[...] = total_ref[...].astype(out_ref.dtype)
-
-
-def mean_kernel(count, own_ref, sibling_ref, out_ref):
-    total = own_ref[...].astype(jnp.float32) + sibling_ref[...].astype(jnp.float32)
-    out_ref[...] = (total / count).astype(out_ref.dtype)
-
-
-def place_kernel(*refs):
-    blocks, (out_ref, held_ref, sems) = refs[:-3], refs[-3:]
-    rows = blocks[0].shape[0]
-    chip = lax.div(lax.axis_index("dp"), CORES)
+def mean_kernel(count, _, *refs):
+    total = refs[0][...].astype(jnp.float32)
+    for term in refs[1:-1]:
+        total = total + term[...].astype(jnp.float32)
+    refs[-1][...] = (total / count).astype(refs[-1].dtype)
+
+
+def place_kernel(chips, own_ref, sibling_ref, out_ref, held_ref, sems):
+    rows, half = own_ref.shape[0] // chips, own_ref.shape[1]
+    core, chip = lax.rem(lax.axis_index("dp"), CORES), lax.div(lax.axis_index("dp"), CORES)
     copies = []
-    for k, block_ref in enumerate(blocks):
+    for k in range(chips):
         place = pl.ds(pl.multiple_of((chip ^ k) * rows, rows), rows)
-        held_ref[place] = block_ref[...].astype(held_ref.dtype)
+        for block_ref, side in ((own_ref, core), (sibling_ref, 1 - core)):
+            columns = pl.ds(pl.multiple_of((side ^ (1 if k else 0)) * half, half), half)
+            block = block_ref[k * rows : (k + 1) * rows]
+            held_ref[place, columns] = block.astype(held_ref.dtype)
         copies.append(pltpu.make_async_copy(held_ref.at[place], out_ref.at[place], sems.at[k]))
         copies[k].start()
     for copy in copies:
@@ -337,6 +320,7 @@
 
 def share(group, part, wholes, ready, dp_count, fsdp_count):
     alike = (0,) * CORES
+    part, ready = lax.optimization_barrier((part, ready))
     parts, members = [part], [1]
     for chip_bits in range(1, group // CORES):
         parts.append(cross(part, dp_count, fsdp_count, chip_bits, alike))
@@ -352,7 +336,7 @@
         )
     held = [(part, (fsdp_count // 2,) * CORES, members)]
     for block, flips in wholes:
-        held.append((lax.optimization_barrier((block, part, ready))[0], flips, [None]))
+        held.append((lax.optimization_barrier((block, part))[0], flips, [None]))
     found = []
     for block, flips, members in held:
         moved = [m if m is None else m ^ 1 for m in members]
@@ -384,9 +368,9 @@
     prepared = call(
         functools.partial(prepare_kernel, slots),
         "prepared_operands",
-        [part, lengths, sibling_events]
+        [lengths, sibling_events]
         + [flat_events, keys, values, cotangent, query_weight, gates],
-        [ANYWHERE, FAR, NEAR] + [FAR] * 6,
+        [FAR, NEAR] + [FAR] * 6,
         (
             shape(rows, model_width),
             shape(rows, width),
@@ -405,7 +389,7 @@
             pltpu.SMEM(lengths.shape, jnp.int32),
             pltpu.SemaphoreType.DMA((7,)),
         ],
-        flops=22 * 10**8,
+        flops=5 * 10**9,
     )
     near_events, near_keys, near_values, near_cotangent, near_weight = prepared[:5]
     events_t, keys_t, values_t, weight, gated, first = prepared[5:]
@@ -438,33 +422,63 @@
     staged = part_rows % 16 == 0 and fsdp_count % 4 == 0
     terms = [grad_query]
     if staged:
-        pairs = shard_pairs(fsdp_count)
+        alike = (0,) * CORES
+
+        def to_chip(block, k):
+            return cross(block, dp_count, fsdp_count, k, alike)
+
+        def summed_over_chips(terms, name, flips, after):
+            terms = [terms[0]] + far_first(chips, lambda k: to_chip(terms[k], k))
+            return call(
+                functools.partial(chip_sum_kernel, chips),
+                name,
+                [after] + terms,
+                [ANYWHERE] + [NEAR] * chips,
+                tuple(shape(part_rows, half_width, dtype=bf16 if z else f32) for z in flips),
+            )
+
+        def for_chips(flips):
+            columns = len(flips) * half_width
+            return tuple(shape(part_rows, columns, dtype=bf16 if k else f32) for k in range(chips))
+
+        def work(flips):
+            return dict(
+                flops=4 * rows * len(flips) * shard_rows * half_width,
+                moved=2 * (len(flips) * shard_rows + width) * CORES * rows,
+            )
+
+        far_flips, near_flips = tuple(range(2, fsdp_count)), (0, 1)
         got = flip(grad_query, "dp", dp_count, 1)
-        picked = pltpu.VMEM((2 * chips * part_rows, CORES * rows), bf16)
-
-        def for_chips(columns):
-            return tuple(shape(part_rows, columns, dtype=bf16 if k else f32) for k in range(chips))
-
-        both, *whole_terms = call(
-            functools.partial(whole_gradient_kernel, pairs),
-            "weight_gradient_of_whole_shards",
+        picked_rows = (chips - 1) * part_rows * len(far_flips)
+        both, *far_terms = call(
+            functools.partial(far_gradient_kernel, far_flips),
+            "weight_gradient_of_far_shards",
             [events_t, grad_query, got],
             [NEAR] * 3,
-            (shape(CORES * rows, width),) + for_chips(len(pairs) * width),
-            [picked],
-            flops=4 * rows * shard_rows * len(pairs) * width,
-            moved=2 * model_width * (rows + width),
+            (shape(CORES * rows, width),) + for_chips(far_flips),
+            [pltpu.VMEM((picked_rows, CORES * rows), bf16)],
+            **work(far_flips),
         )
         terms = call(
-            half_gradient_kernel,
-            "weight_gradient_of_halves",
+            functools.partial(near_gradient_kernel, near_flips),
+            "weight_gradient_of_near_shards",
             [events_t, both],
             [NEAR] * 2,
-            for_chips(2 * half_width),
-            [picked],
-            flops=4 * rows * shard_rows * width,
-            moved=2 * model_width * (rows + width),
-        )
+            for_chips(near_flips),
+            [pltpu.VMEM((chips * part_rows, CORES * rows), bf16)],
+            **work(near_flips),
+        )
+
+        def to_shard(block, z):
+            return cross(block, dp_count, fsdp_count, 0, (z,) * CORES)
+
+        far_sums = summed_over_chips(far_terms, "far_shards_over_chips", far_flips, both)
+        own_sum, next_sum = summed_over_chips(
+            terms, "near_shards_over_chips", near_flips, far_sums[0]
+        )
+        far_sums = [to_shard(a, z) for a, z in reversed(list(zip(far_sums, far_flips)))]
+        terms = [next_sum]
+        next_sum = to_shard(next_sum, 1)
     grad_keys, grad_values, grad_gates = call(
         functools.partial(outputs_kernel, slots),
         "key_value_gate_gradients",
@@ -475,50 +489,25 @@
         moved=12 * rows * width,
     )
     if staged:
-        alike = (0,) * CORES
-
-        def to_chip(block, k):
-            return cross(block, dp_count, fsdp_count, k, alike)
-
-        whole_terms[1:] = far_first(chips, lambda k: to_chip(whole_terms[k], k))
-        wholes = call(
-            functools.partial(chip_sum_kernel, chips),
-            "sum_of_whole_shards_over_chips",
-            [both] + whole_terms,
-            [ANYWHERE] + [NEAR] * chips,
-            (shape(part_rows, width),) * len(pairs),
-        )
-        wholes = [cross(a, dp_count, fsdp_count, 0, p) for a, p in zip(wholes, pairs)]
-        terms = [terms[0]] + far_first(chips, lambda k: to_chip(terms[k], k))
-        own_half, middle = call(
-            functools.partial(chip_sum_kernel, chips),
-            "sum_of_halves_over_chips",
-            [grad_keys] + terms,
-            [FAR] + [NEAR] * chips,
-            (shape(part_rows, half_width, dtype=f32), shape(part_rows, half_width)),
-        )
-        middle = cross(middle, dp_count, fsdp_count, 0, (fsdp_count // 2,) * CORES)
-        total = call(
-            shard_sum_kernel,
-            "sum_over_shards",
-            [own_half, middle] + wholes,
-            [NEAR] * (2 + len(wholes)),
-            shape(part_rows, width),
-            [pltpu.VMEM((part_rows, width), f32)],
-        )
         mean = call(
             functools.partial(mean_kernel, total_seqs),
-            "mean_of_both_cores",
-            [total, flip(total, "dp", dp_count, 1)],
+            "mean_over_shards",
+            [grad_keys, own_sum, next_sum] + far_sums,
+            [FAR] + [NEAR] * fsdp_count,
+            shape(part_rows, half_width),
+        )
+        blocks = call(
+            stack_kernel,
+            "blocks_of_chips",
+            [mean] + far_first(chips, lambda k: to_chip(mean, k)),
+            [NEAR] * chips,
+            shape(shard_rows, half_width),
+        )
+        grad_weight = call(
+            functools.partial(place_kernel, chips),
+            "blocks_in_place",
+            [blocks, flip(blocks, "dp", dp_count, 1)],
             [NEAR] * 2,
-            shape(part_rows, width),
-        )
-        found = [mean] + far_first(chips, lambda k: to_chip(mean, k))
-        grad_weight = call(
-            place_kernel,
-            "blocks_in_place",
-            found,
-            [NEAR] * chips,
             shape(shard_rows, width, dtype=f32),
             [pltpu.VMEM((shard_rows, width), f32), pltpu.SemaphoreType.DMA((chips,))],
             out_specs=FAR,

time: 48.2 us -> 45 us (0.934)
  starting transfers between devices: 25.6 us -> 22.9 us
  waiting for transfers between devices: 13.1 us -> 12.5 us
    ppermute x5, starting transfers between devices: 4.18 us -> 1.59 us  [flip(): return lax.ppermute(block, axis, [(i, i ^ bits) for i in range(count)])]
    ppermute x16 -> x17, waiting for transfers between devices: 9.54 us -> 8.56 us  [cross(): return lax.ppermute(block, BOTH, pairs)]
    ppermute x16 -> x17, starting transfers between devices: 21.4 us -> 21.3 us  [cross(): return lax.ppermute(block, BOTH, pairs)]
  transfers between devices with their start and end apart: 21 -> 22, of which waited for: 11 -> 13; matrix products, arithmetic and copies ran while one was open for 0% -> 0% of each run, Pallas kernels for 10% -> 11%
where the time goes in v6:
time: 45 us; the launch traced here: 44.7 us
  starting transfers between devices  22.9 us (51%)
  waiting for transfers between devices  12.5 us (28%)
  Pallas kernels  8.6 us (19%)
  between operations  0.72 us (2%)
    ppermute x17, starting transfers between devices, cross(): return lax.ppermute(block, BOTH, pairs)  21.3 us
    pallas_call x12, Pallas kernels, call(): pl.pallas_call(kernel, out_shape=out_shape, in_specs=in_specs, out_specs=...  8.6 us
    ppermute x17, waiting for transfers between devices, cross(): return lax.ppermute(block, BOTH, pairs)  8.56 us
    ppermute x5, waiting for transfers between devices, flip(): return lax.ppermute(block, axis, [(i, i ^ bits) for i in range(count)])  3.93 us
    ppermute x5, starting transfers between devices, flip(): return lax.ppermute(block, axis, [(i, i ^ bits) for i in range(count)])  1.59 us
  transfers between devices with their start and end apart: 22, of which 13 were waited for; matrix products, arithmetic and copies ran while one was open for 0% of the time, Pallas kernels for 11%

profile of v6, /device:TPU:0, one launch (start us, length us, event | category | flops | bytes accessed | tf_op | source)
XLA Modules:
  0.0 44.7 jit_solution(12472496339600634501)
XLA Ops:
  0.6 0.5 %collective-permute-start = (bf16[384,1024]{1,0:T(8,128)(2,1)}, bf16[384,1024]{1,0:T(8,128)(2,1)S(1)}, u32[]{:S(2)}, u32[]{:S(2)}) collective-permute-start(bf16[384,1024]{1,0:T(8,128)(2,1)} %bitcast.9), channel_id=1, source_target_pairs={{0,4},{4,0},{8,12},{12,8},{16,20},{20,16},{24,28},{28,24},{1,5},{5... | collective-permute-start | bytes 2359304 | tf_op jit(solution)/shard_map/ppermute | solution.py:269
  1.1 0.8 %own_part_of_weight.1 = bf16[32,512]{1,0:T(8,128)(2,1)S(1)} custom-call(bf16[256,512]{1,0:T(8,128)(2,1)} %block_ref.1), custom_call_target="tpu_custom_call" | custom-call | tf_op jit(solution)/shard_map/own_part_of_weight/pallas_call | solution.py:33
  1.9 3.8 %collective-permute-start.1 = (bf16[32,512]{1,0:T(8,128)(2,1)S(1)}, bf16[32,512]{1,0:T(8,128)(2,1)S(1)}, u32[]{:S(2)}, u32[]{:S(2)}) collective-permute-start(bf16[32,512]{1,0:T(8,128)(2,1)S(1)} %own_part_of_weight.1), channel_id=1, source_target_pairs={{0,6},{1,7},{2,4},{3,5},{4,2},{5,3},{6,0},{7,1},{8,14},{9,15},{10,... | collective-permute-start | bytes 98312 | tf_op jit(solution)/shard_map/ppermute | solution.py:281
  5.7 1.2 %collective-permute-start.6 = (bf16[256,512]{1,0:T(8,128)(2,1)}, bf16[256,512]{1,0:T(8,128)(2,1)S(1)}, u32[]{:S(2)}, u32[]{:S(2)}) collective-permute-start(bf16[256,512]{1,0:T(8,128)(2,1)} %block_ref.1), channel_id=1, source_target_pairs={{0,5},{1,4},{2,7},{3,6},{4,3},{5,2},{6,1},{7,0},{8,13},{9,12},{10,... | collective-permute-start | bytes 786440 | tf_op jit(solution)/shard_map/ppermute | solution.py:281
  6.9 2.3 %prepared_operands.1 = (bf16[384,1024]{1,0:T(8,128)(2,1)S(1)}, bf16[384,512]{1,0:T(8,128)(2,1)S(1)}, bf16[384,512]{1,0:T(8,128)(2,1)S(1)}, bf16[384,512]{1,0:T(8...) custom-call(s32[96]{0:T(128)} %lengths_ref.1, ...), custom_call_target="tpu_custom_call" | custom-call | flops 5000000000 | tf_op jit(solution)/shard_map/prepared_operands/pallas_call | solution.py:33
  9.2 2.4 %collective-permute-start.4 = (bf16[32,512]{1,0:T(8,128)(2,1)S(1)}, bf16[32,512]{1,0:T(8,128)(2,1)S(1)}, u32[]{:S(2)}, u32[]{:S(2)}) collective-permute-start(bf16[32,512]{1,0:T(8,128)(2,1)S(1)} %collective-permute-done.1.refs_0_), channel_id=1, source_target_pairs={{0,28},{1,29},{2,30},{3,31},{4,24},{5,25},{6,26},{7,27},{8,20},{9,... | collective-permute-start | bytes 98312 | tf_op jit(solution)/shard_map/ppermute | solution.py:281
  12.0 0.4 collective-permute-start.2
  12.4 1.2 %collective-permute-done.4.refs_3_ = bf16[32,512]{1,0:T(8,128)(2,1)S(1)} collective-permute-done((bf16[32,512]{1,0:T(8,128)(2,1)S(1)}, bf16[32,512]{1,0:T(8,128)(2,1)S(1)}, u32[]{:S(2)}, u32[]{:S(2)}) %collective-permute-start.4) | collective-permute-done | bytes 32800 | tf_op jit(solution)/shard_map/ppermute | solution.py:281
  13.5 1.4 %collective-permute-done.3.refs_2_ = bf16[32,512]{1,0:T(8,128)(2,1)S(1)} collective-permute-done((bf16[32,512]{1,0:T(8,128)(2,1)S(1)}, bf16[32,512]{1,0:T(8,128)(2,1)S(1)}, u32[]{:S(2)}, u32[]{:S(2)}) %collective-permute-start.3) | collective-permute-done | bytes 32800 | tf_op jit(solution)/shard_map/ppermute | solution.py:281
  15.9 1.2 %collective-permute-done.5.refs_2_ = bf16[128,512]{1,0:T(8,128)(2,1)S(1)} collective-permute-done((bf16[128,512]{1,0:T(8,128)(2,1)S(1)}, bf16[128,512]{1,0:T(8,128)(2,1)S(1)}, u32[]{:S(2)}, u32[]{:S(2)}) %collective-permute-start.5) | collective-permute-done | bytes 131104 | tf_op jit(solution)/shard_map/ppermute | solution.py:269
  17.1 2.4 %attention_to_grad_query.1 = (bf16[384,512]{1,0:T(8,128)(2,1)S(1)}, bf16[384,512]{1,0:T(8,128)(2,1)S(1)}, f32[384,512]{1,0:T(8,128)S(1)}, bf16[384,512]{1,0:T(8,...) custom-call(bf16[256,512]{1,0:T(8,128)(2,1)S(1)} %get-tuple-element.42.refs_0_, ...), custom_call_target="tpu_custom_call" | custom-call | flops 603979776 | bytes 4718592 | tf_op jit(solution)/shard_map/attention_to_grad_query/pallas_call | solution.py:33
  19.8 1.5 %collective-permute-done.8.got_ref = bf16[384,512]{1,0:T(8,128)(2,1)S(1)} collective-permute-done((bf16[384,512]{1,0:T(8,128)(2,1)S(1)}, bf16[384,512]{1,0:T(8,128)(2,1)S(1)}, u32[]{:S(2)}, u32[]{:S(2)}) %collective-permute-start.8) | collective-permute-done | bytes 393248 | tf_op jit(solution)/shard_map/ppermute | solution.py:269
  21.3 0.4 weight_gradient_of_far_shards.1
  21.7 0.6 %collective-permute-start.9 = (bf16[64,512]{1,0:T(8,128)(2,1)S(1)}, bf16[64,512]{1,0:T(8,128)(2,1)S(1)}, u32[]{:S(2)}, u32[]{:S(2)}) collective-permute-start(bf16[64,512]{1,0:T(8,128)(2,1)S(1)} %get-tuple-element.58), channel_id=1, source_target_pairs={{0,12},{1,13},{2,14},{3,15},{4,8},{5,9},{6,10},{7,11},{8,4},{9,5},... | collective-permute-start | bytes 196616 | tf_op jit(solution)/shard_map/ppermute | solution.py:281
  22.3 1.5 %collective-permute-start.10 = (bf16[64,512]{1,0:T(8,128)(2,1)S(1)}, bf16[64,512]{1,0:T(8,128)(2,1)S(1)}, u32[]{:S(2)}, u32[]{:S(2)}) collective-permute-start(bf16[64,512]{1,0:T(8,128)(2,1)S(1)} %get-tuple-element.59), channel_id=1, source_target_pairs={{0,20},{1,21},{2,22},{3,23},{4,16},{5,17},{6,18},{7,19},{8,28},{9,... | collective-permute-start | bytes 196616 | tf_op jit(solution)/shard_map/ppermute | solution.py:281
  23.8 1.0 %collective-permute-start.11 = (bf16[64,512]{1,0:T(8,128)(2,1)S(1)}, bf16[64,512]{1,0:T(8,128)(2,1)S(1)}, u32[]{:S(2)}, u32[]{:S(2)}) collective-permute-start(bf16[64,512]{1,0:T(8,128)(2,1)S(1)} %get-tuple-element.60), channel_id=1, source_target_pairs={{0,28},{1,29},{2,30},{3,31},{4,24},{5,25},{6,26},{7,27},{8,20},{9,... | collective-permute-start | bytes 196616 | tf_op jit(solution)/shard_map/ppermute | solution.py:281
  25.2 0.7 %collective-permute-start.12 = (bf16[64,512]{1,0:T(8,128)(2,1)S(1)}, bf16[64,512]{1,0:T(8,128)(2,1)S(1)}, u32[]{:S(2)}, u32[]{:S(2)}) collective-permute-start(bf16[64,512]{1,0:T(8,128)(2,1)S(1)} %get-tuple-element.63), channel_id=1, source_target_pairs={{0,12},{1,13},{2,14},{3,15},{4,8},{5,9},{6,10},{7,11},{8,4},{9,5},... | collective-permute-start | bytes 196616 | tf_op jit(solution)/shard_map/ppermute | solution.py:281
  25.9 1.3 %collective-permute-start.13 = (bf16[64,512]{1,0:T(8,128)(2,1)S(1)}, bf16[64,512]{1,0:T(8,128)(2,1)S(1)}, u32[]{:S(2)}, u32[]{:S(2)}) collective-permute-start(bf16[64,512]{1,0:T(8,128)(2,1)S(1)} %get-tuple-element.64), channel_id=1, source_target_pairs={{0,20},{1,21},{2,22},{3,23},{4,16},{5,17},{6,18},{7,19},{8,28},{9,... | collective-permute-start | bytes 196616 | tf_op jit(solution)/shard_map/ppermute | solution.py:281
  27.2 1.1 %collective-permute-start.14 = (bf16[64,512]{1,0:T(8,128)(2,1)S(1)}, bf16[64,512]{1,0:T(8,128)(2,1)S(1)}, u32[]{:S(2)}, u32[]{:S(2)}) collective-permute-start(bf16[64,512]{1,0:T(8,128)(2,1)S(1)} %get-tuple-element.65), channel_id=1, source_target_pairs={{0,28},{1,29},{2,30},{3,31},{4,24},{5,25},{6,26},{7,27},{8,20},{9,... | collective-permute-start | bytes 196616 | tf_op jit(solution)/shard_map/ppermute | solution.py:281
  28.8 2.4 %collective-permute-start.16 = (bf16[64,256]{1,0:T(8,128)(2,1)S(1)}, bf16[64,256]{1,0:T(8,128)(2,1)S(1)}, u32[]{:S(2)}, u32[]{:S(2)}) collective-permute-start(bf16[64,256]{1,0:T(8,128)(2,1)S(1)} %get-tuple-element.77), channel_id=1, source_target_pairs={{0,7},{1,6},{2,5},{3,4},{4,3},{5,2},{6,1},{7,0},{8,15},{9,14},{10,... | collective-permute-start | bytes 98312 | tf_op jit(solution)/shard_map/ppermute | solution.py:281
  31.4 0.6 %collective-permute-done.14.refs_3_ = bf16[64,512]{1,0:T(8,128)(2,1)S(1)} collective-permute-done((bf16[64,512]{1,0:T(8,128)(2,1)S(1)}, bf16[64,512]{1,0:T(8,128)(2,1)S(1)}, u32[]{:S(2)}, u32[]{:S(2)}) %collective-permute-start.14) | collective-permute-done | bytes 65568 | tf_op jit(solution)/shard_map/ppermute | solution.py:281
  32.1 1.3 %collective-permute-start.15 = (bf16[64,256]{1,0:T(8,128)(2,1)S(1)}, bf16[64,256]{1,0:T(8,128)(2,1)S(1)}, u32[]{:S(2)}, u32[]{:S(2)}) collective-permute-start(bf16[64,256]{1,0:T(8,128)(2,1)S(1)} %get-tuple-element.66._), channel_id=1, source_target_pairs={{0,5},{1,4},{2,7},{3,6},{4,1},{5,0},{6,3},{7,2},{8,13},{9,12},{10,... | collective-permute-start | bytes 98312 | tf_op jit(solution)/shard_map/ppermute | solution.py:281
  33.4 1.4 %key_value_gate_gradients.1 = (bf16[384,512]{1,0:T(8,128)(2,1)}, bf16[384,512]{1,0:T(8,128)(2,1)}, bf16[384,512]{1,0:T(8,128)(2,1)}) custom-call(bf16[64,256]{1,0:T(8,128)(2,1)S(1)} %get-tuple-element.66._, bf16[384,512]{1,0:T(8,128)(2,1)S(1)} %get-tuple-element.67.query_ref, f32[384,512]{1,0:T(8,128)S(1)} %get-tuple-element.68.normed_ref, ...), custom_call_target="tpu_custom_call" | custom-call | flops 100663296 | bytes 2359296 | tf_op jit(solution)/shard_map/key_value_gate_gradients/pallas_call | solution.py:33
  34.9 0.9 %collective-permute-done.17.refs_3_ = bf16[64,256]{1,0:T(8,128)(2,1)S(1)} collective-permute-done((bf16[64,256]{1,0:T(8,128)(2,1)S(1)}, bf16[64,256]{1,0:T(8,128)(2,1)S(1)}, u32[]{:S(2)}, u32[]{:S(2)}) %collective-permute-start.17) | collective-permute-done | bytes 32800 | tf_op jit(solution)/shard_map/ppermute | solution.py:281
  35.8 0.5 %collective-permute-done.15.refs_1_ = bf16[64,256]{1,0:T(8,128)(2,1)S(1)} collective-permute-done((bf16[64,256]{1,0:T(8,128)(2,1)S(1)}, bf16[64,256]{1,0:T(8,128)(2,1)S(1)}, u32[]{:S(2)}, u32[]{:S(2)}) %collective-permute-start.15) | collective-permute-done | bytes 32800 | tf_op jit(solution)/shard_map/ppermute | solution.py:281
  36.3 1.3 %collective-permute-start.20 = (bf16[64,256]{1,0:T(8,128)(2,1)S(1)}, bf16[64,256]{1,0:T(8,128)(2,1)S(1)}, u32[]{:S(2)}, u32[]{:S(2)}) collective-permute-start(bf16[64,256]{1,0:T(8,128)(2,1)S(1)} %mean_over_shards.1.refs_0_), channel_id=1, source_target_pairs={{0,28},{1,29},{2,30},{3,31},{4,24},{5,25},{6,26},{7,27},{8,20},{9,... | collective-permute-start | bytes 98312 | tf_op jit(solution)/shard_map/ppermute | solution.py:281
  37.6 1.4 %collective-permute-start.19 = (bf16[64,256]{1,0:T(8,128)(2,1)S(1)}, bf16[64,256]{1,0:T(8,128)(2,1)S(1)}, u32[]{:S(2)}, u32[]{:S(2)}) collective-permute-start(bf16[64,256]{1,0:T(8,128)(2,1)S(1)} %mean_over_shards.1.refs_0_), channel_id=1, source_target_pairs={{0,20},{1,21},{2,22},{3,23},{4,16},{5,17},{6,18},{7,19},{8,28},{9,... | collective-permute-start | bytes 98312 | tf_op jit(solution)/shard_map/ppermute | solution.py:281
  39.3 1.4 %collective-permute-done.20.refs_3_ = bf16[64,256]{1,0:T(8,128)(2,1)S(1)} collective-permute-done((bf16[64,256]{1,0:T(8,128)(2,1)S(1)}, bf16[64,256]{1,0:T(8,128)(2,1)S(1)}, u32[]{:S(2)}, u32[]{:S(2)}) %collective-permute-start.20) | collective-permute-done | bytes 32800 | tf_op jit(solution)/shard_map/ppermute | solution.py:281
  40.7 0.7 %collective-permute-done.19.refs_2_ = bf16[64,256]{1,0:T(8,128)(2,1)S(1)} collective-permute-done((bf16[64,256]{1,0:T(8,128)(2,1)S(1)}, bf16[64,256]{1,0:T(8,128)(2,1)S(1)}, u32[]{:S(2)}, u32[]{:S(2)}) %collective-permute-start.19) | collective-permute-done | bytes 32800 | tf_op jit(solution)/shard_map/ppermute | solution.py:281
  41.4 1.1 %collective-permute-done.18.refs_1_ = bf16[64,256]{1,0:T(8,128)(2,1)S(1)} collective-permute-done((bf16[64,256]{1,0:T(8,128)(2,1)S(1)}, bf16[64,256]{1,0:T(8,128)(2,1)S(1)}, u32[]{:S(2)}, u32[]{:S(2)}) %collective-permute-start.18) | collective-permute-done | bytes 32800 | tf_op jit(solution)/shard_map/ppermute | solution.py:281
  42.7 1.2 %collective-permute-done.21.sibling_ref = bf16[256,256]{1,0:T(8,128)(2,1)S(1)} collective-permute-done((bf16[256,256]{1,0:T(8,128)(2,1)S(1)}, bf16[256,256]{1,0:T(8,128)(2,1)S(1)}, u32[]{:S(2)}, u32[]{:S(2)}) %collective-permute-start.21) | collective-permute-done | bytes 131104 | tf_op jit(solution)/shard_map/ppermute | solution.py:269
  43.9 0.8 %blocks_in_place.1 = f32[256,512]{1,0:T(8,128)} custom-call(bf16[256,256]{1,0:T(8,128)(2,1)S(1)} %blocks_of_chips.1.own_ref, bf16[256,256]{1,0:T(8,128)(2,1)S(1)} %collective-permute-done.21.sibling_ref), custom_call_target="tpu_custom_call" | custom-call | tf_op jit(solution)/shard_map/blocks_in_place/pallas_call | solution.py:33
  (24 shorter events, 3.2 us)
Async XLA Ops:
  0.6 6.3 %collective-permute-start = (bf16[384,1024]{1,0:T(8,128)(2,1)}, bf16[384,1024]{1,0:T(8,128)(2,1)S(1)}, u32[]{:S(2)}, u32[]{:S(2)}) collective-permute-start(bf16[384,1024]{1,0:T(8,128)(2,1)} %bitcast.9), channel_id=1, source_target_pairs={{0,4},{4,0},{8,12},{12,8},{16,20},{20,16},{24,28},{28,24},{1,5},{5... | collective-permute-start | bytes 2359304 | tf_op jit(solution)/shard_map/ppermute | solution.py:269
  1.9 7.3 %collective-permute-start.1 = (bf16[32,512]{1,0:T(8,128)(2,1)S(1)}, bf16[32,512]{1,0:T(8,128)(2,1)S(1)}, u32[]{:S(2)}, u32[]{:S(2)}) collective-permute-start(bf16[32,512]{1,0:T(8,128)(2,1)S(1)} %own_part_of_weight.1), channel_id=1, source_target_pairs={{0,6},{1,7},{2,4},{3,5},{4,2},{5,3},{6,0},{7,1},{8,14},{9,15},{10,... | collective-permute-start | bytes 98312 | tf_op jit(solution)/shard_map/ppermute | solution.py:281
  5.7 9.7 %collective-permute-start.6 = (bf16[256,512]{1,0:T(8,128)(2,1)}, bf16[256,512]{1,0:T(8,128)(2,1)S(1)}, u32[]{:S(2)}, u32[]{:S(2)}) collective-permute-start(bf16[256,512]{1,0:T(8,128)(2,1)} %block_ref.1), channel_id=1, source_target_pairs={{0,5},{1,4},{2,7},{3,6},{4,3},{5,2},{6,1},{7,0},{8,13},{9,12},{10,... | collective-permute-start | bytes 786440 | tf_op jit(solution)/shard_map/ppermute | solution.py:281
  9.2 4.3 %collective-permute-start.4 = (bf16[32,512]{1,0:T(8,128)(2,1)S(1)}, bf16[32,512]{1,0:T(8,128)(2,1)S(1)}, u32[]{:S(2)}, u32[]{:S(2)}) collective-permute-start(bf16[32,512]{1,0:T(8,128)(2,1)S(1)} %collective-permute-done.1.refs_0_), channel_id=1, source_target_pairs={{0,28},{1,29},{2,30},{3,31},{4,24},{5,25},{6,26},{7,27},{8,20},{9,... | collective-permute-start | bytes 98312 | tf_op jit(solution)/shard_map/ppermute | solution.py:281
  11.6 3.3 %collective-permute-start.3 = (bf16[32,512]{1,0:T(8,128)(2,1)S(1)}, bf16[32,512]{1,0:T(8,128)(2,1)S(1)}, u32[]{:S(2)}, u32[]{:S(2)}) collective-permute-start(bf16[32,512]{1,0:T(8,128)(2,1)S(1)} %collective-permute-done.1.refs_0_), channel_id=1, source_target_pairs={{0,20},{1,21},{2,22},{3,23},{4,16},{5,17},{6,18},{7,19},{8,28},{9,... | collective-permute-start | bytes 98312 | tf_op jit(solution)/shard_map/ppermute | solution.py:281
  12.0 3.3 %collective-permute-start.2 = (bf16[32,512]{1,0:T(8,128)(2,1)S(1)}, bf16[32,512]{1,0:T(8,128)(2,1)S(1)}, u32[]{:S(2)}, u32[]{:S(2)}) collective-permute-start(bf16[32,512]{1,0:T(8,128)(2,1)S(1)} %collective-permute-done.1.refs_0_), channel_id=1, source_target_pairs={{0,12},{1,13},{2,14},{3,15},{4,8},{5,9},{6,10},{7,11},{8,4},{9,5},... | collective-permute-start | bytes 98312 | tf_op jit(solution)/shard_map/ppermute | solution.py:281
  15.3 1.8 %collective-permute-start.7 = (bf16[256,512]{1,0:T(8,128)(2,1)S(1)}, bf16[256,512]{1,0:T(8,128)(2,1)S(1)}, u32[]{:S(2)}, u32[]{:S(2)}) collective-permute-start(bf16[256,512]{1,0:T(8,128)(2,1)S(1)} %collective-permute-done.6.refs_3_), channel_id=1, source_target_pairs={{0,4},{4,0},{8,12},{12,8},{16,20},{20,16},{24,28},{28,24},{1,5},{5... | collective-permute-start | bytes 786440 | tf_op jit(solution)/shard_map/ppermute | solution.py:269
  15.7 1.5 %collective-permute-start.5 = (bf16[128,512]{1,0:T(8,128)(2,1)S(1)}, bf16[128,512]{1,0:T(8,128)(2,1)S(1)}, u32[]{:S(2)}, u32[]{:S(2)}) collective-permute-start(bf16[128,512]{1,0:T(8,128)(2,1)S(1)} %parts_of_weight.1.refs_1_), channel_id=1, source_target_pairs={{0,4},{4,0},{8,12},{12,8},{16,20},{20,16},{24,28},{28,24},{1,5},{5... | collective-permute-start | bytes 393224 | tf_op jit(solution)/shard_map/ppermute | solution.py:269
  19.5 1.8 %collective-permute-start.8 = (bf16[384,512]{1,0:T(8,128)(2,1)S(1)}, bf16[384,512]{1,0:T(8,128)(2,1)S(1)}, u32[]{:S(2)}, u32[]{:S(2)}) collective-permute-start(bf16[384,512]{1,0:T(8,128)(2,1)S(1)} %get-tuple-element.55.own_ref), channel_id=1, source_target_pairs={{0,4},{4,0},{8,12},{12,8},{16,20},{20,16},{24,28},{28,24},{1,5},{5... | collective-permute-start | bytes 1179656 | tf_op jit(solution)/shard_map/ppermute | solution.py:269
  21.7 5.5 %collective-permute-start.9 = (bf16[64,512]{1,0:T(8,128)(2,1)S(1)}, bf16[64,512]{1,0:T(8,128)(2,1)S(1)}, u32[]{:S(2)}, u32[]{:S(2)}) collective-permute-start(bf16[64,512]{1,0:T(8,128)(2,1)S(1)} %get-tuple-element.58), channel_id=1, source_target_pairs={{0,12},{1,13},{2,14},{3,15},{4,8},{5,9},{6,10},{7,11},{8,4},{9,5},... | collective-permute-start | bytes 196616 | tf_op jit(solution)/shard_map/ppermute | solution.py:281
  22.3 6.1 %collective-permute-start.10 = (bf16[64,512]{1,0:T(8,128)(2,1)S(1)}, bf16[64,512]{1,0:T(8,128)(2,1)S(1)}, u32[]{:S(2)}, u32[]{:S(2)}) collective-permute-start(bf16[64,512]{1,0:T(8,128)(2,1)S(1)} %get-tuple-element.59), channel_id=1, source_target_pairs={{0,20},{1,21},{2,22},{3,23},{4,16},{5,17},{6,18},{7,19},{8,28},{9,... | collective-permute-start | bytes 196616 | tf_op jit(solution)/shard_map/ppermute | solution.py:281
  23.8 5.0 %collective-permute-start.11 = (bf16[64,512]{1,0:T(8,128)(2,1)S(1)}, bf16[64,512]{1,0:T(8,128)(2,1)S(1)}, u32[]{:S(2)}, u32[]{:S(2)}) collective-permute-start(bf16[64,512]{1,0:T(8,128)(2,1)S(1)} %get-tuple-element.60), channel_id=1, source_target_pairs={{0,28},{1,29},{2,30},{3,31},{4,24},{5,25},{6,26},{7,27},{8,20},{9,... | collective-permute-start | bytes 196616 | tf_op jit(solution)/shard_map/ppermute | solution.py:281
  25.2 6.2 %collective-permute-start.12 = (bf16[64,512]{1,0:T(8,128)(2,1)S(1)}, bf16[64,512]{1,0:T(8,128)(2,1)S(1)}, u32[]{:S(2)}, u32[]{:S(2)}) collective-permute-start(bf16[64,512]{1,0:T(8,128)(2,1)S(1)} %get-tuple-element.63), channel_id=1, source_target_pairs={{0,12},{1,13},{2,14},{3,15},{4,8},{5,9},{6,10},{7,11},{8,4},{9,5},... | collective-permute-start | bytes 196616 | tf_op jit(solution)/shard_map/ppermute | solution.py:281
  25.9 5.5 %collective-permute-start.13 = (bf16[64,512]{1,0:T(8,128)(2,1)S(1)}, bf16[64,512]{1,0:T(8,128)(2,1)S(1)}, u32[]{:S(2)}, u32[]{:S(2)}) collective-permute-start(bf16[64,512]{1,0:T(8,128)(2,1)S(1)} %get-tuple-element.64), channel_id=1, source_target_pairs={{0,20},{1,21},{2,22},{3,23},{4,16},{5,17},{6,18},{7,19},{8,28},{9,... | collective-permute-start | bytes 196616 | tf_op jit(solution)/shard_map/ppermute | solution.py:281
  27.2 4.8 %collective-permute-start.14 = (bf16[64,512]{1,0:T(8,128)(2,1)S(1)}, bf16[64,512]{1,0:T(8,128)(2,1)S(1)}, u32[]{:S(2)}, u32[]{:S(2)}) collective-permute-start(bf16[64,512]{1,0:T(8,128)(2,1)S(1)} %get-tuple-element.65), channel_id=1, source_target_pairs={{0,28},{1,29},{2,30},{3,31},{4,24},{5,25},{6,26},{7,27},{8,20},{9,... | collective-permute-start | bytes 196616 | tf_op jit(solution)/shard_map/ppermute | solution.py:281
  28.8 6.1 %collective-permute-start.16 = (bf16[64,256]{1,0:T(8,128)(2,1)S(1)}, bf16[64,256]{1,0:T(8,128)(2,1)S(1)}, u32[]{:S(2)}, u32[]{:S(2)}) collective-permute-start(bf16[64,256]{1,0:T(8,128)(2,1)S(1)} %get-tuple-element.77), channel_id=1, source_target_pairs={{0,7},{1,6},{2,5},{3,4},{4,3},{5,2},{6,1},{7,0},{8,15},{9,14},{10,... | collective-permute-start | bytes 98312 | tf_op jit(solution)/shard_map/ppermute | solution.py:281
  31.2 4.5 %collective-permute-start.17 = (bf16[64,256]{1,0:T(8,128)(2,1)S(1)}, bf16[64,256]{1,0:T(8,128)(2,1)S(1)}, u32[]{:S(2)}, u32[]{:S(2)}) collective-permute-start(bf16[64,256]{1,0:T(8,128)(2,1)S(1)} %get-tuple-element.61._), channel_id=1, source_target_pairs={{0,6},{1,7},{2,4},{3,5},{4,2},{5,3},{6,0},{7,1},{8,14},{9,15},{10,... | collective-permute-start | bytes 98312 | tf_op jit(solution)/shard_map/ppermute | solution.py:281
  32.1 4.2 %collective-permute-start.15 = (bf16[64,256]{1,0:T(8,128)(2,1)S(1)}, bf16[64,256]{1,0:T(8,128)(2,1)S(1)}, u32[]{:S(2)}, u32[]{:S(2)}) collective-permute-start(bf16[64,256]{1,0:T(8,128)(2,1)S(1)} %get-tuple-element.66._), channel_id=1, source_target_pairs={{0,5},{1,4},{2,7},{3,6},{4,1},{5,0},{6,3},{7,2},{8,13},{9,12},{10,... | collective-permute-start | bytes 98312 | tf_op jit(solution)/shard_map/ppermute | solution.py:281
  36.3 4.4 %collective-permute-start.20 = (bf16[64,256]{1,0:T(8,128)(2,1)S(1)}, bf16[64,256]{1,0:T(8,128)(2,1)S(1)}, u32[]{:S(2)}, u32[]{:S(2)}) collective-permute-start(bf16[64,256]{1,0:T(8,128)(2,1)S(1)} %mean_over_shards.1.refs_0_), channel_id=1, source_target_pairs={{0,28},{1,29},{2,30},{3,31},{4,24},{5,25},{6,26},{7,27},{8,20},{9,... | collective-permute-start | bytes 98312 | tf_op jit(solution)/shard_map/ppermute | solution.py:281
  37.6 3.8 %collective-permute-start.19 = (bf16[64,256]{1,0:T(8,128)(2,1)S(1)}, bf16[64,256]{1,0:T(8,128)(2,1)S(1)}, u32[]{:S(2)}, u32[]{:S(2)}) collective-permute-start(bf16[64,256]{1,0:T(8,128)(2,1)S(1)} %mean_over_shards.1.refs_0_), channel_id=1, source_target_pairs={{0,20},{1,21},{2,22},{3,23},{4,16},{5,17},{6,18},{7,19},{8,28},{9,... | collective-permute-start | bytes 98312 | tf_op jit(solution)/shard_map/ppermute | solution.py:281
  39.0 3.4 %collective-permute-start.18 = (bf16[64,256]{1,0:T(8,128)(2,1)S(1)}, bf16[64,256]{1,0:T(8,128)(2,1)S(1)}, u32[]{:S(2)}, u32[]{:S(2)}) collective-permute-start(bf16[64,256]{1,0:T(8,128)(2,1)S(1)} %mean_over_shards.1.refs_0_), channel_id=1, source_target_pairs={{0,12},{1,13},{2,14},{3,15},{4,8},{5,9},{6,10},{7,11},{8,4},{9,5},... | collective-permute-start | bytes 98312 | tf_op jit(solution)/shard_map/ppermute | solution.py:281
  42.5 1.4 %collective-permute-start.21 = (bf16[256,256]{1,0:T(8,128)(2,1)S(1)}, bf16[256,256]{1,0:T(8,128)(2,1)S(1)}, u32[]{:S(2)}, u32[]{:S(2)}) collective-permute-start(bf16[256,256]{1,0:T(8,128)(2,1)S(1)} %blocks_of_chips.1.own_ref), channel_id=1, source_target_pairs={{0,4},{4,0},{8,12},{12,8},{16,20},{20,16},{24,28},{28,24},{1,5},{5... | collective-permute-start | bytes 393224 | tf_op jit(solution)/shard_map/ppermute | solution.py:269

commit v7 on v6

--- a/solution.py
+++ b/solution.py
@@ -196,38 +196,51 @@
     return lax.rem(lax.axis_index("dp"), CORES) ^ (1 if k else 0) ^ (1 if z else 0)
 
 
-def gradient_kernel(shard_flips, events_ref, both_ref, outs, picked_ref):
+def chip_flips(chips):
+    return (0,) + tuple(range(chips - 1, 0, -1))
+
+
+def gradient_picks(chips, shard_flips):
+    every = [(k, i, z) for k in chip_flips(chips) for i, z in enumerate(shard_flips)]
+    return [[p for p in every if (p[0] != 0) ^ (p[2] != 0) == bool(side)] for side in range(CORES)]
+
+
+def half_columns(side, half):
+    return pl.ds(pl.multiple_of(summing_half(side, 0) * half, half), half)
+
+
+def own_gradient_kernel(chips, sets, events_ref, grad_query_ref, *refs):
+    outs, picked_ref = refs[:-1], refs[-1]
+    rows, half = grad_query_ref.shape[0], grad_query_ref.shape[1] // CORES
+    shard_rows = events_ref.shape[0] // lax.axis_size("fsdp")
+    part_rows = shard_rows // chips
+    chip, here = lax.div(lax.axis_index("dp"), CORES), lax.axis_index("fsdp")
+    for flips, term_ref, other_ref in zip(sets, outs[::2], outs[1::2]):
+        at = 0
+        for side, picks in enumerate(gradient_picks(chips, flips)):
+            first = at
+            for k, _, z in picks:
+                start = (here ^ z) * shard_rows + (chip ^ k) * part_rows
+                source = pl.ds(pl.multiple_of(start, part_rows), part_rows)
+                picked_ref[at : at + part_rows] = events_ref[source, :rows]
+                other_ref[at : at + part_rows] = events_ref[source, rows:]
+                at += part_rows
+            columns = half_columns(side, half)
+            term_ref[first:at] = dot(picked_ref[first:at], grad_query_ref[:, columns])
+
+
+def gradient_kernel(chips, flips, _, term_ref, events_ref, grad_query_ref, *outs):
+    half = term_ref.shape[1]
     part_rows = outs[0].shape[0]
-    half = both_ref.shape[1] // CORES
-    shard_rows = events_ref.shape[0] // lax.axis_size("fsdp")
-    chip, here = lax.div(lax.axis_index("dp"), CORES), lax.axis_index("fsdp")
-    for other in range(CORES):
-        picks = [
-            (k, i, z)
-            for k in range(len(outs))
-            for i, z in enumerate(shard_flips)
-            if (k != 0) ^ (z != 0) == bool(other)
-        ]
-        for p, (k, _, z) in enumerate(picks):
-            start = pl.multiple_of((here ^ z) * shard_rows + (chip ^ k) * part_rows, part_rows)
-            picked_ref[p * part_rows : (p + 1) * part_rows] = events_ref[pl.ds(start, part_rows)]
-        core = summing_half(other, 0)
-        columns = pl.ds(pl.multiple_of(core * half, half), half)
-        total = dot(picked_ref[: len(picks) * part_rows], both_ref[:, columns])
+    out_of = dict(zip(chip_flips(chips), outs))
+    at = 0
+    for side, picks in enumerate(gradient_picks(chips, flips)):
+        rows = slice(at, at + len(picks) * part_rows)
+        total = term_ref[rows] + dot(events_ref[rows], grad_query_ref[:, half_columns(side, half)])
         for p, (k, i, _) in enumerate(picks):
             block = total[p * part_rows : (p + 1) * part_rows]
-            outs[k][:, i * half : (i + 1) * half] = block.astype(outs[k].dtype)
-
-
-def far_gradient_kernel(shard_flips, events_ref, own_ref, got_ref, both_ref, *refs):
-    rows = own_ref.shape[0]
-    both_ref[:rows] = own_ref[...]
-    both_ref[rows:] = got_ref[...]
-    gradient_kernel(shard_flips, events_ref, both_ref, refs[:-1], refs[-1])
-
-
-def near_gradient_kernel(shard_flips, events_ref, both_ref, *refs):
-    gradient_kernel(shard_flips, events_ref, both_ref, refs[:-1], refs[-1])
+            out_of[k][:, i * half : (i + 1) * half] = block.astype(out_of[k].dtype)
+        at = rows.stop
 
 
 def chip_sum_kernel(term_count, _, *refs):
@@ -427,8 +440,10 @@
         def to_chip(block, k):
             return cross(block, dp_count, fsdp_count, k, alike)
 
+        order = chip_flips(chips)
+
         def summed_over_chips(terms, name, flips, after):
-            terms = [terms[0]] + far_first(chips, lambda k: to_chip(terms[k], k))
+            terms = [terms[0]] + [to_chip(a, k) for a, k in zip(terms[1:], order[1:])]
             return call(
                 functools.partial(chip_sum_kernel, chips),
                 name,
@@ -437,46 +452,47 @@
                 tuple(shape(part_rows, half_width, dtype=bf16 if z else f32) for z in flips),
             )
 
-        def for_chips(flips):
-            columns = len(flips) * half_width
-            return tuple(shape(part_rows, columns, dtype=bf16 if k else f32) for k in range(chips))
-
-        def work(flips):
-            return dict(
-                flops=4 * rows * len(flips) * shard_rows * half_width,
-                moved=2 * (len(flips) * shard_rows + width) * CORES * rows,
+        sets = (tuple(range(2, fsdp_count)), (0, 1))
+        picked_rows = [len(flips) * shard_rows for flips in sets]
+        got = flip(grad_query, "dp", dp_count, 1)
+        own_terms = call(
+            functools.partial(own_gradient_kernel, chips, sets),
+            "weight_gradient_of_own_events",
+            [events_t, grad_query],
+            [NEAR] * 2,
+            tuple(
+                a
+                for n in picked_rows
+                for a in (shape(n, half_width, dtype=f32), shape(n, rows))
+            ),
+            [pltpu.VMEM((max(picked_rows), rows), bf16)],
+            flops=2 * rows * model_width * half_width,
+            moved=8 * model_width * rows,
+        )
+
+        def gradient(which, name, after):
+            columns = len(sets[which]) * half_width
+            return call(
+                functools.partial(gradient_kernel, chips, sets[which]),
+                name,
+                [after, *own_terms[2 * which : 2 * which + 2], got],
+                [ANYWHERE] + [NEAR] * 3,
+                tuple(shape(part_rows, columns, dtype=bf16 if k else f32) for k in order),
+                flops=2 * rows * picked_rows[which] * half_width,
+                moved=2 * picked_rows[which] * (rows + 2 * half_width),
             )
 
-        far_flips, near_flips = tuple(range(2, fsdp_count)), (0, 1)
-        got = flip(grad_query, "dp", dp_count, 1)
-        picked_rows = (chips - 1) * part_rows * len(far_flips)
-        both, *far_terms = call(
-            functools.partial(far_gradient_kernel, far_flips),
-            "weight_gradient_of_far_shards",
-            [events_t, grad_query, got],
-            [NEAR] * 3,
-            (shape(CORES * rows, width),) + for_chips(far_flips),
-            [pltpu.VMEM((picked_rows, CORES * rows), bf16)],
-            **work(far_flips),
-        )
-        terms = call(
-            functools.partial(near_gradient_kernel, near_flips),
-            "weight_gradient_of_near_shards",
-            [events_t, both],
-            [NEAR] * 2,
-            for_chips(near_flips),
-            [pltpu.VMEM((chips * part_rows, CORES * rows), bf16)],
-            **work(near_flips),
-        )
+        far_terms = gradient(0, "weight_gradient_of_far_shards", got)
+        terms = gradient(1, "weight_gradient_of_near_shards", far_terms[0])
 
         def to_shard(block, z):
             return cross(block, dp_count, fsdp_count, 0, (z,) * CORES)
 
-        far_sums = summed_over_chips(far_terms, "far_shards_over_chips", far_flips, both)
+        far_sums = summed_over_chips(far_terms, "far_shards_over_chips", sets[0], got)
         own_sum, next_sum = summed_over_chips(
-            terms, "near_shards_over_chips", near_flips, far_sums[0]
-        )
-        far_sums = [to_shard(a, z) for a, z in reversed(list(zip(far_sums, far_flips)))]
+            terms, "near_shards_over_chips", sets[1], far_sums[0]
+        )
+        far_sums = [to_shard(a, z) for a, z in reversed(list(zip(far_sums, sets[0])))]
         terms = [next_sum]
         next_sum = to_shard(next_sum, 1)
     grad_keys, grad_values, grad_gates = call(

time: 45 us -> 44.2 us (0.982)
  waiting for transfers between devices: 12.5 us -> 11.8 us
    ppermute x5, waiting for transfers between devices: 3.93 us -> 3.43 us  [flip(): return lax.ppermute(block, axis, [(i, i ^ bits) for i in range(count)])]
    pallas_call x12 -> x13, Pallas kernels: 8.6 us -> 8.89 us  [call(): pl.pallas_call(kernel, out_shape=out_shape, in_specs=in_specs, out_specs=...]
  transfers between devices with their start and end apart: 22 -> 22, of which waited for: 13 -> 13; matrix products, arithmetic and copies ran while one was open for 0% -> 0% of each run, Pallas kernels for 11% -> 12%
where the time goes in v7:
time: 44.2 us; the launch traced here: 44 us
  starting transfers between devices  22.6 us (51%)
  waiting for transfers between devices  11.8 us (27%)
  Pallas kernels  8.89 us (20%)
  between operations  0.73 us (2%)
    ppermute x17, starting transfers between devices, cross(): return lax.ppermute(block, BOTH, pairs)  21 us
    pallas_call x13, Pallas kernels, call(): pl.pallas_call(kernel, out_shape=out_shape, in_specs=in_specs, out_specs=...  8.89 us
    ppermute x17, waiting for transfers between devices, cross(): return lax.ppermute(block, BOTH, pairs)  8.34 us
    ppermute x5, waiting for transfers between devices, flip(): return lax.ppermute(block, axis, [(i, i ^ bits) for i in range(count)])  3.43 us
    ppermute x5, starting transfers between devices, flip(): return lax.ppermute(block, axis, [(i, i ^ bits) for i in range(count)])  1.59 us
  transfers between devices with their start and end apart: 22, of which 13 were waited for; matrix products, arithmetic and copies ran while one was open for 0% of the time, Pallas kernels for 12%

profile of v7, /device:TPU:0, one launch (start us, length us, event | category | flops | bytes accessed | tf_op | source)
XLA Modules:
  0.0 44.0 jit_solution(2021775542863827969)
XLA Ops:
  0.6 0.5 %collective-permute-start = (bf16[384,1024]{1,0:T(8,128)(2,1)}, bf16[384,1024]{1,0:T(8,128)(2,1)S(1)}, u32[]{:S(2)}, u32[]{:S(2)}) collective-permute-start(bf16[384,1024]{1,0:T(8,128)(2,1)} %bitcast.9), channel_id=1, source_target_pairs={{0,4},{4,0},{8,12},{12,8},{16,20},{20,16},{24,28},{28,24},{1,5},{5... | collective-permute-start | bytes 2359304 | tf_op jit(solution)/shard_map/ppermute | solution.py:282
  1.1 0.8 %own_part_of_weight.1 = bf16[32,512]{1,0:T(8,128)(2,1)S(1)} custom-call(bf16[256,512]{1,0:T(8,128)(2,1)} %block_ref.1), custom_call_target="tpu_custom_call" | custom-call | tf_op jit(solution)/shard_map/own_part_of_weight/pallas_call | solution.py:33
  1.9 3.8 %collective-permute-start.1 = (bf16[32,512]{1,0:T(8,128)(2,1)S(1)}, bf16[32,512]{1,0:T(8,128)(2,1)S(1)}, u32[]{:S(2)}, u32[]{:S(2)}) collective-permute-start(bf16[32,512]{1,0:T(8,128)(2,1)S(1)} %own_part_of_weight.1), channel_id=1, source_target_pairs={{0,6},{1,7},{2,4},{3,5},{4,2},{5,3},{6,0},{7,1},{8,14},{9,15},{10,... | collective-permute-start | bytes 98312 | tf_op jit(solution)/shard_map/ppermute | solution.py:294
  5.7 1.2 %collective-permute-start.6 = (bf16[256,512]{1,0:T(8,128)(2,1)}, bf16[256,512]{1,0:T(8,128)(2,1)S(1)}, u32[]{:S(2)}, u32[]{:S(2)}) collective-permute-start(bf16[256,512]{1,0:T(8,128)(2,1)} %block_ref.1), channel_id=1, source_target_pairs={{0,5},{1,4},{2,7},{3,6},{4,3},{5,2},{6,1},{7,0},{8,13},{9,12},{10,... | collective-permute-start | bytes 786440 | tf_op jit(solution)/shard_map/ppermute | solution.py:294
  6.9 2.3 %prepared_operands.1 = (bf16[384,1024]{1,0:T(8,128)(2,1)S(1)}, bf16[384,512]{1,0:T(8,128)(2,1)S(1)}, bf16[384,512]{1,0:T(8,128)(2,1)S(1)}, bf16[384,512]{1,0:T(8...) custom-call(s32[96]{0:T(128)} %lengths_ref.1, ...), custom_call_target="tpu_custom_call" | custom-call | flops 5000000000 | tf_op jit(solution)/shard_map/prepared_operands/pallas_call | solution.py:33
  9.2 2.4 %collective-permute-start.4 = (bf16[32,512]{1,0:T(8,128)(2,1)S(1)}, bf16[32,512]{1,0:T(8,128)(2,1)S(1)}, u32[]{:S(2)}, u32[]{:S(2)}) collective-permute-start(bf16[32,512]{1,0:T(8,128)(2,1)S(1)} %collective-permute-done.1.refs_0_), channel_id=1, source_target_pairs={{0,28},{1,29},{2,30},{3,31},{4,24},{5,25},{6,26},{7,27},{8,20},{9,... | collective-permute-start | bytes 98312 | tf_op jit(solution)/shard_map/ppermute | solution.py:294
  12.0 0.4 collective-permute-start.2
  12.4 1.2 %collective-permute-done.4.refs_3_ = bf16[32,512]{1,0:T(8,128)(2,1)S(1)} collective-permute-done((bf16[32,512]{1,0:T(8,128)(2,1)S(1)}, bf16[32,512]{1,0:T(8,128)(2,1)S(1)}, u32[]{:S(2)}, u32[]{:S(2)}) %collective-permute-start.4) | collective-permute-done | bytes 32800 | tf_op jit(solution)/shard_map/ppermute | solution.py:294
  13.5 1.4 %collective-permute-done.3.refs_2_ = bf16[32,512]{1,0:T(8,128)(2,1)S(1)} collective-permute-done((bf16[32,512]{1,0:T(8,128)(2,1)S(1)}, bf16[32,512]{1,0:T(8,128)(2,1)S(1)}, u32[]{:S(2)}, u32[]{:S(2)}) %collective-permute-start.3) | collective-permute-done | bytes 32800 | tf_op jit(solution)/shard_map/ppermute | solution.py:294
  15.9 1.2 %collective-permute-done.5.refs_2_ = bf16[128,512]{1,0:T(8,128)(2,1)S(1)} collective-permute-done((bf16[128,512]{1,0:T(8,128)(2,1)S(1)}, bf16[128,512]{1,0:T(8,128)(2,1)S(1)}, u32[]{:S(2)}, u32[]{:S(2)}) %collective-permute-start.5) | collective-permute-done | bytes 131104 | tf_op jit(solution)/shard_map/ppermute | solution.py:282
  17.1 2.4 %attention_to_grad_query.1 = (bf16[384,512]{1,0:T(8,128)(2,1)S(1)}, bf16[384,512]{1,0:T(8,128)(2,1)S(1)}, f32[384,512]{1,0:T(8,128)S(1)}, bf16[384,512]{1,0:T(8,...) custom-call(bf16[256,512]{1,0:T(8,128)(2,1)S(1)} %get-tuple-element.44.refs_0_, ...), custom_call_target="tpu_custom_call" | custom-call | flops 603979776 | bytes 4718592 | tf_op jit(solution)/shard_map/attention_to_grad_query/pallas_call | solution.py:33
  19.8 0.5 %weight_gradient_of_own_events.1 = (f32[512,256]{1,0:T(8,128)S(1)}, bf16[512,384]{1,0:T(8,128)(2,1)S(1)}, f32[512,256]{1,0:T(8,128)S(1)}, bf16[512,384]{1,0:T(8,128)(2,1)S(1)}) custom-call(bf16[1024,768]{1,0:T(8,128)(2,1)S(1)} %get-tuple-element.58.events_ref, bf16[384,512]{1,0:T(8,128)(2,1)S(1)} %get-tuple-element.57.grad_query_ref), custom_call_target="tpu_custom_call" | custom-call | flops 201326592 | bytes 3145728 | tf_op jit(solution)/shard_map/weight_gradient_of_own_events/pallas_call | solution.py:33
  20.3 1.0 %collective-permute-done.8._.grad_query_ref = bf16[384,512]{1,0:T(8,128)(2,1)S(1)} collective-permute-done((bf16[384,512]{1,0:T(8,128)(2,1)S(1)}, bf16[384,512]{1,0:T(8,128)(2,1)S(1)}, u32[]{:S(2)}, u32[]{:S(2)}) %collective-permute-start.8) | collective-permute-done | bytes 393248 | tf_op jit(solution)/shard_map/ppermute | solution.py:282
  21.6 1.6 %collective-permute-start.9 = (bf16[64,512]{1,0:T(8,128)(2,1)S(1)}, bf16[64,512]{1,0:T(8,128)(2,1)S(1)}, u32[]{:S(2)}, u32[]{:S(2)}) collective-permute-start(bf16[64,512]{1,0:T(8,128)(2,1)S(1)} %get-tuple-element.62), channel_id=1, source_target_pairs={{0,28},{1,29},{2,30},{3,31},{4,24},{5,25},{6,26},{7,27},{8,20},{9,... | collective-permute-start | bytes 196616 | tf_op jit(solution)/shard_map/ppermute | solution.py:294
  23.1 0.5 %collective-permute-start.10 = (bf16[64,512]{1,0:T(8,128)(2,1)S(1)}, bf16[64,512]{1,0:T(8,128)(2,1)S(1)}, u32[]{:S(2)}, u32[]{:S(2)}) collective-permute-start(bf16[64,512]{1,0:T(8,128)(2,1)S(1)} %get-tuple-element.63), channel_id=1, source_target_pairs={{0,20},{1,21},{2,22},{3,23},{4,16},{5,17},{6,18},{7,19},{8,28},{9,... | collective-permute-start | bytes 196616 | tf_op jit(solution)/shard_map/ppermute | solution.py:294
  23.6 1.1 %collective-permute-start.11 = (bf16[64,512]{1,0:T(8,128)(2,1)S(1)}, bf16[64,512]{1,0:T(8,128)(2,1)S(1)}, u32[]{:S(2)}, u32[]{:S(2)}) collective-permute-start(bf16[64,512]{1,0:T(8,128)(2,1)S(1)} %get-tuple-element.64), channel_id=1, source_target_pairs={{0,12},{1,13},{2,14},{3,15},{4,8},{5,9},{6,10},{7,11},{8,4},{9,5},... | collective-permute-start | bytes 196616 | tf_op jit(solution)/shard_map/ppermute | solution.py:294
  25.0 1.7 %collective-permute-start.12 = (bf16[64,512]{1,0:T(8,128)(2,1)S(1)}, bf16[64,512]{1,0:T(8,128)(2,1)S(1)}, u32[]{:S(2)}, u32[]{:S(2)}) collective-permute-start(bf16[64,512]{1,0:T(8,128)(2,1)S(1)} %get-tuple-element.69), channel_id=1, source_target_pairs={{0,28},{1,29},{2,30},{3,31},{4,24},{5,25},{6,26},{7,27},{8,20},{9,... | collective-permute-start | bytes 196616 | tf_op jit(solution)/shard_map/ppermute | solution.py:294
  27.0 1.2 %collective-permute-start.14 = (bf16[64,512]{1,0:T(8,128)(2,1)S(1)}, bf16[64,512]{1,0:T(8,128)(2,1)S(1)}, u32[]{:S(2)}, u32[]{:S(2)}) collective-permute-start(bf16[64,512]{1,0:T(8,128)(2,1)S(1)} %get-tuple-element.71), channel_id=1, source_target_pairs={{0,12},{1,13},{2,14},{3,15},{4,8},{5,9},{6,10},{7,11},{8,4},{9,5},... | collective-permute-start | bytes 196616 | tf_op jit(solution)/shard_map/ppermute | solution.py:294
  28.3 2.5 %collective-permute-start.16 = (bf16[64,256]{1,0:T(8,128)(2,1)S(1)}, bf16[64,256]{1,0:T(8,128)(2,1)S(1)}, u32[]{:S(2)}, u32[]{:S(2)}) collective-permute-start(bf16[64,256]{1,0:T(8,128)(2,1)S(1)} %get-tuple-element.83), channel_id=1, source_target_pairs={{0,7},{1,6},{2,5},{3,4},{4,3},{5,2},{6,1},{7,0},{8,15},{9,14},{10,... | collective-permute-start | bytes 98312 | tf_op jit(solution)/shard_map/ppermute | solution.py:294
  30.8 0.9 %collective-permute-done.13.refs_2_ = bf16[64,512]{1,0:T(8,128)(2,1)S(1)} collective-permute-done((bf16[64,512]{1,0:T(8,128)(2,1)S(1)}, bf16[64,512]{1,0:T(8,128)(2,1)S(1)}, u32[]{:S(2)}, u32[]{:S(2)}) %collective-permute-start.13) | collective-permute-done | bytes 65568 | tf_op jit(solution)/shard_map/ppermute | solution.py:294
  31.8 1.2 %collective-permute-start.15 = (bf16[64,256]{1,0:T(8,128)(2,1)S(1)}, bf16[64,256]{1,0:T(8,128)(2,1)S(1)}, u32[]{:S(2)}, u32[]{:S(2)}) collective-permute-start(bf16[64,256]{1,0:T(8,128)(2,1)S(1)} %get-tuple-element.72._), channel_id=1, source_target_pairs={{0,5},{1,4},{2,7},{3,6},{4,1},{5,0},{6,3},{7,2},{8,13},{9,12},{10,... | collective-permute-start | bytes 98312 | tf_op jit(solution)/shard_map/ppermute | solution.py:294
  32.9 1.4 %key_value_gate_gradients.1 = (bf16[384,512]{1,0:T(8,128)(2,1)}, bf16[384,512]{1,0:T(8,128)(2,1)}, bf16[384,512]{1,0:T(8,128)(2,1)}) custom-call(bf16[64,256]{1,0:T(8,128)(2,1)S(1)} %get-tuple-element.72._, bf16[384,512]{1,0:T(8,128)(2,1)S(1)} %get-tuple-element.73.query_ref, f32[384,512]{1,0:T(8,128)S(1)} %get-tuple-element.74.normed_ref, ...), custom_call_target="tpu_custom_call" | custom-call | flops 100663296 | bytes 2359296 | tf_op jit(solution)/shard_map/key_value_gate_gradients/pallas_call | solution.py:33
  34.4 0.7 %collective-permute-done.17.refs_3_ = bf16[64,256]{1,0:T(8,128)(2,1)S(1)} collective-permute-done((bf16[64,256]{1,0:T(8,128)(2,1)S(1)}, bf16[64,256]{1,0:T(8,128)(2,1)S(1)}, u32[]{:S(2)}, u32[]{:S(2)}) %collective-permute-start.17) | collective-permute-done | bytes 32800 | tf_op jit(solution)/shard_map/ppermute | solution.py:294
  35.0 0.9 %collective-permute-done.15.refs_1_ = bf16[64,256]{1,0:T(8,128)(2,1)S(1)} collective-permute-done((bf16[64,256]{1,0:T(8,128)(2,1)S(1)}, bf16[64,256]{1,0:T(8,128)(2,1)S(1)}, u32[]{:S(2)}, u32[]{:S(2)}) %collective-permute-start.15) | collective-permute-done | bytes 32800 | tf_op jit(solution)/shard_map/ppermute | solution.py:294
  36.0 1.5 %collective-permute-start.20 = (bf16[64,256]{1,0:T(8,128)(2,1)S(1)}, bf16[64,256]{1,0:T(8,128)(2,1)S(1)}, u32[]{:S(2)}, u32[]{:S(2)}) collective-permute-start(bf16[64,256]{1,0:T(8,128)(2,1)S(1)} %mean_over_shards.1.refs_0_), channel_id=1, source_target_pairs={{0,28},{1,29},{2,30},{3,31},{4,24},{5,25},{6,26},{7,27},{8,20},{9,... | collective-permute-start | bytes 98312 | tf_op jit(solution)/shard_map/ppermute | solution.py:294
  37.5 0.8 %collective-permute-start.19 = (bf16[64,256]{1,0:T(8,128)(2,1)S(1)}, bf16[64,256]{1,0:T(8,128)(2,1)S(1)}, u32[]{:S(2)}, u32[]{:S(2)}) collective-permute-start(bf16[64,256]{1,0:T(8,128)(2,1)S(1)} %mean_over_shards.1.refs_0_), channel_id=1, source_target_pairs={{0,20},{1,21},{2,22},{3,23},{4,16},{5,17},{6,18},{7,19},{8,28},{9,... | collective-permute-start | bytes 98312 | tf_op jit(solution)/shard_map/ppermute | solution.py:294
  38.3 0.7 %collective-permute-start.18 = (bf16[64,256]{1,0:T(8,128)(2,1)S(1)}, bf16[64,256]{1,0:T(8,128)(2,1)S(1)}, u32[]{:S(2)}, u32[]{:S(2)}) collective-permute-start(bf16[64,256]{1,0:T(8,128)(2,1)S(1)} %mean_over_shards.1.refs_0_), channel_id=1, source_target_pairs={{0,12},{1,13},{2,14},{3,15},{4,8},{5,9},{6,10},{7,11},{8,4},{9,5},... | collective-permute-start | bytes 98312 | tf_op jit(solution)/shard_map/ppermute | solution.py:294
  39.0 1.4 %collective-permute-done.20.refs_3_ = bf16[64,256]{1,0:T(8,128)(2,1)S(1)} collective-permute-done((bf16[64,256]{1,0:T(8,128)(2,1)S(1)}, bf16[64,256]{1,0:T(8,128)(2,1)S(1)}, u32[]{:S(2)}, u32[]{:S(2)}) %collective-permute-start.20) | collective-permute-done | bytes 32800 | tf_op jit(solution)/shard_map/ppermute | solution.py:294
  40.4 0.6 %collective-permute-done.19.refs_2_ = bf16[64,256]{1,0:T(8,128)(2,1)S(1)} collective-permute-done((bf16[64,256]{1,0:T(8,128)(2,1)S(1)}, bf16[64,256]{1,0:T(8,128)(2,1)S(1)}, u32[]{:S(2)}, u32[]{:S(2)}) %collective-permute-start.19) | collective-permute-done | bytes 32800 | tf_op jit(solution)/shard_map/ppermute | solution.py:294
  41.0 0.7 %collective-permute-done.18.refs_1_ = bf16[64,256]{1,0:T(8,128)(2,1)S(1)} collective-permute-done((bf16[64,256]{1,0:T(8,128)(2,1)S(1)}, bf16[64,256]{1,0:T(8,128)(2,1)S(1)}, u32[]{:S(2)}, u32[]{:S(2)}) %collective-permute-start.18) | collective-permute-done | bytes 32800 | tf_op jit(solution)/shard_map/ppermute | solution.py:294
  41.9 1.2 %collective-permute-done.21.sibling_ref = bf16[256,256]{1,0:T(8,128)(2,1)S(1)} collective-permute-done((bf16[256,256]{1,0:T(8,128)(2,1)S(1)}, bf16[256,256]{1,0:T(8,128)(2,1)S(1)}, u32[]{:S(2)}, u32[]{:S(2)}) %collective-permute-start.21) | collective-permute-done | bytes 131104 | tf_op jit(solution)/shard_map/ppermute | solution.py:282
  43.1 0.8 %blocks_in_place.1 = f32[256,512]{1,0:T(8,128)} custom-call(bf16[256,256]{1,0:T(8,128)(2,1)S(1)} %blocks_of_chips.1.own_ref, bf16[256,256]{1,0:T(8,128)(2,1)S(1)} %collective-permute-done.21.sibling_ref), custom_call_target="tpu_custom_call" | custom-call | tf_op jit(solution)/shard_map/blocks_in_place/pallas_call | solution.py:33
  (25 shorter events, 2.9 us)
Async XLA Ops:
  0.6 6.3 %collective-permute-start = (bf16[384,1024]{1,0:T(8,128)(2,1)}, bf16[384,1024]{1,0:T(8,128)(2,1)S(1)}, u32[]{:S(2)}, u32[]{:S(2)}) collective-permute-start(bf16[384,1024]{1,0:T(8,128)(2,1)} %bitcast.9), channel_id=1, source_target_pairs={{0,4},{4,0},{8,12},{12,8},{16,20},{20,16},{24,28},{28,24},{1,5},{5... | collective-permute-start | bytes 2359304 | tf_op jit(solution)/shard_map/ppermute | solution.py:282
  1.9 7.3 %collective-permute-start.1 = (bf16[32,512]{1,0:T(8,128)(2,1)S(1)}, bf16[32,512]{1,0:T(8,128)(2,1)S(1)}, u32[]{:S(2)}, u32[]{:S(2)}) collective-permute-start(bf16[32,512]{1,0:T(8,128)(2,1)S(1)} %own_part_of_weight.1), channel_id=1, source_target_pairs={{0,6},{1,7},{2,4},{3,5},{4,2},{5,3},{6,0},{7,1},{8,14},{9,15},{10,... | collective-permute-start | bytes 98312 | tf_op jit(solution)/shard_map/ppermute | solution.py:294
  5.7 9.7 %collective-permute-start.6 = (bf16[256,512]{1,0:T(8,128)(2,1)}, bf16[256,512]{1,0:T(8,128)(2,1)S(1)}, u32[]{:S(2)}, u32[]{:S(2)}) collective-permute-start(bf16[256,512]{1,0:T(8,128)(2,1)} %block_ref.1), channel_id=1, source_target_pairs={{0,5},{1,4},{2,7},{3,6},{4,3},{5,2},{6,1},{7,0},{8,13},{9,12},{10,... | collective-permute-start | bytes 786440 | tf_op jit(solution)/shard_map/ppermute | solution.py:294
  9.2 4.3 %collective-permute-start.4 = (bf16[32,512]{1,0:T(8,128)(2,1)S(1)}, bf16[32,512]{1,0:T(8,128)(2,1)S(1)}, u32[]{:S(2)}, u32[]{:S(2)}) collective-permute-start(bf16[32,512]{1,0:T(8,128)(2,1)S(1)} %collective-permute-done.1.refs_0_), channel_id=1, source_target_pairs={{0,28},{1,29},{2,30},{3,31},{4,24},{5,25},{6,26},{7,27},{8,20},{9,... | collective-permute-start | bytes 98312 | tf_op jit(solution)/shard_map/ppermute | solution.py:294
  11.6 3.3 %collective-permute-start.3 = (bf16[32,512]{1,0:T(8,128)(2,1)S(1)}, bf16[32,512]{1,0:T(8,128)(2,1)S(1)}, u32[]{:S(2)}, u32[]{:S(2)}) collective-permute-start(bf16[32,512]{1,0:T(8,128)(2,1)S(1)} %collective-permute-done.1.refs_0_), channel_id=1, source_target_pairs={{0,20},{1,21},{2,22},{3,23},{4,16},{5,17},{6,18},{7,19},{8,28},{9,... | collective-permute-start | bytes 98312 | tf_op jit(solution)/shard_map/ppermute | solution.py:294
  12.0 3.3 %collective-permute-start.2 = (bf16[32,512]{1,0:T(8,128)(2,1)S(1)}, bf16[32,512]{1,0:T(8,128)(2,1)S(1)}, u32[]{:S(2)}, u32[]{:S(2)}) collective-permute-start(bf16[32,512]{1,0:T(8,128)(2,1)S(1)} %collective-permute-done.1.refs_0_), channel_id=1, source_target_pairs={{0,12},{1,13},{2,14},{3,15},{4,8},{5,9},{6,10},{7,11},{8,4},{9,5},... | collective-permute-start | bytes 98312 | tf_op jit(solution)/shard_map/ppermute | solution.py:294
  15.3 1.8 %collective-permute-start.7 = (bf16[256,512]{1,0:T(8,128)(2,1)S(1)}, bf16[256,512]{1,0:T(8,128)(2,1)S(1)}, u32[]{:S(2)}, u32[]{:S(2)}) collective-permute-start(bf16[256,512]{1,0:T(8,128)(2,1)S(1)} %collective-permute-done.6.refs_3_), channel_id=1, source_target_pairs={{0,4},{4,0},{8,12},{12,8},{16,20},{20,16},{24,28},{28,24},{1,5},{5... | collective-permute-start | bytes 786440 | tf_op jit(solution)/shard_map/ppermute | solution.py:282
  15.7 1.5 %collective-permute-start.5 = (bf16[128,512]{1,0:T(8,128)(2,1)S(1)}, bf16[128,512]{1,0:T(8,128)(2,1)S(1)}, u32[]{:S(2)}, u32[]{:S(2)}) collective-permute-start(bf16[128,512]{1,0:T(8,128)(2,1)S(1)} %parts_of_weight.1.refs_1_), channel_id=1, source_target_pairs={{0,4},{4,0},{8,12},{12,8},{16,20},{20,16},{24,28},{28,24},{1,5},{5... | collective-permute-start | bytes 393224 | tf_op jit(solution)/shard_map/ppermute | solution.py:282
  19.5 1.8 %collective-permute-start.8 = (bf16[384,512]{1,0:T(8,128)(2,1)S(1)}, bf16[384,512]{1,0:T(8,128)(2,1)S(1)}, u32[]{:S(2)}, u32[]{:S(2)}) collective-permute-start(bf16[384,512]{1,0:T(8,128)(2,1)S(1)} %get-tuple-element.57.grad_query_ref), channel_id=1, source_target_pairs={{0,4},{4,0},{8,12},{12,8},{16,20},{20,16},{24,28},{28,24},{1,5},{5... | collective-permute-start | bytes 1179656 | tf_op jit(solution)/shard_map/ppermute | solution.py:282
  21.6 5.4 %collective-permute-start.9 = (bf16[64,512]{1,0:T(8,128)(2,1)S(1)}, bf16[64,512]{1,0:T(8,128)(2,1)S(1)}, u32[]{:S(2)}, u32[]{:S(2)}) collective-permute-start(bf16[64,512]{1,0:T(8,128)(2,1)S(1)} %get-tuple-element.62), channel_id=1, source_target_pairs={{0,28},{1,29},{2,30},{3,31},{4,24},{5,25},{6,26},{7,27},{8,20},{9,... | collective-permute-start | bytes 196616 | tf_op jit(solution)/shard_map/ppermute | solution.py:294
  23.1 5.2 %collective-permute-start.10 = (bf16[64,512]{1,0:T(8,128)(2,1)S(1)}, bf16[64,512]{1,0:T(8,128)(2,1)S(1)}, u32[]{:S(2)}, u32[]{:S(2)}) collective-permute-start(bf16[64,512]{1,0:T(8,128)(2,1)S(1)} %get-tuple-element.63), channel_id=1, source_target_pairs={{0,20},{1,21},{2,22},{3,23},{4,16},{5,17},{6,18},{7,19},{8,28},{9,... | collective-permute-start | bytes 196616 | tf_op jit(solution)/shard_map/ppermute | solution.py:294
  23.6 4.7 %collective-permute-start.11 = (bf16[64,512]{1,0:T(8,128)(2,1)S(1)}, bf16[64,512]{1,0:T(8,128)(2,1)S(1)}, u32[]{:S(2)}, u32[]{:S(2)}) collective-permute-start(bf16[64,512]{1,0:T(8,128)(2,1)S(1)} %get-tuple-element.64), channel_id=1, source_target_pairs={{0,12},{1,13},{2,14},{3,15},{4,8},{5,9},{6,10},{7,11},{8,4},{9,5},... | collective-permute-start | bytes 196616 | tf_op jit(solution)/shard_map/ppermute | solution.py:294
  25.0 5.8 %collective-permute-start.12 = (bf16[64,512]{1,0:T(8,128)(2,1)S(1)}, bf16[64,512]{1,0:T(8,128)(2,1)S(1)}, u32[]{:S(2)}, u32[]{:S(2)}) collective-permute-start(bf16[64,512]{1,0:T(8,128)(2,1)S(1)} %get-tuple-element.69), channel_id=1, source_target_pairs={{0,28},{1,29},{2,30},{3,31},{4,24},{5,25},{6,26},{7,27},{8,20},{9,... | collective-permute-start | bytes 196616 | tf_op jit(solution)/shard_map/ppermute | solution.py:294
  26.7 5.0 %collective-permute-start.13 = (bf16[64,512]{1,0:T(8,128)(2,1)S(1)}, bf16[64,512]{1,0:T(8,128)(2,1)S(1)}, u32[]{:S(2)}, u32[]{:S(2)}) collective-permute-start(bf16[64,512]{1,0:T(8,128)(2,1)S(1)} %get-tuple-element.70), channel_id=1, source_target_pairs={{0,20},{1,21},{2,22},{3,23},{4,16},{5,17},{6,18},{7,19},{8,28},{9,... | collective-permute-start | bytes 196616 | tf_op jit(solution)/shard_map/ppermute | solution.py:294
  27.0 4.8 %collective-permute-start.14 = (bf16[64,512]{1,0:T(8,128)(2,1)S(1)}, bf16[64,512]{1,0:T(8,128)(2,1)S(1)}, u32[]{:S(2)}, u32[]{:S(2)}) collective-permute-start(bf16[64,512]{1,0:T(8,128)(2,1)S(1)} %get-tuple-element.71), channel_id=1, source_target_pairs={{0,12},{1,13},{2,14},{3,15},{4,8},{5,9},{6,10},{7,11},{8,4},{9,5},... | collective-permute-start | bytes 196616 | tf_op jit(solution)/shard_map/ppermute | solution.py:294
  28.3 6.0 %collective-permute-start.16 = (bf16[64,256]{1,0:T(8,128)(2,1)S(1)}, bf16[64,256]{1,0:T(8,128)(2,1)S(1)}, u32[]{:S(2)}, u32[]{:S(2)}) collective-permute-start(bf16[64,256]{1,0:T(8,128)(2,1)S(1)} %get-tuple-element.83), channel_id=1, source_target_pairs={{0,7},{1,6},{2,5},{3,4},{4,3},{5,2},{6,1},{7,0},{8,15},{9,14},{10,... | collective-permute-start | bytes 98312 | tf_op jit(solution)/shard_map/ppermute | solution.py:294
  30.8 4.3 %collective-permute-start.17 = (bf16[64,256]{1,0:T(8,128)(2,1)S(1)}, bf16[64,256]{1,0:T(8,128)(2,1)S(1)}, u32[]{:S(2)}, u32[]{:S(2)}) collective-permute-start(bf16[64,256]{1,0:T(8,128)(2,1)S(1)} %get-tuple-element.65._), channel_id=1, source_target_pairs={{0,6},{1,7},{2,4},{3,5},{4,2},{5,3},{6,0},{7,1},{8,14},{9,15},{10,... | collective-permute-start | bytes 98312 | tf_op jit(solution)/shard_map/ppermute | solution.py:294
  31.8 4.2 %collective-permute-start.15 = (bf16[64,256]{1,0:T(8,128)(2,1)S(1)}, bf16[64,256]{1,0:T(8,128)(2,1)S(1)}, u32[]{:S(2)}, u32[]{:S(2)}) collective-permute-start(bf16[64,256]{1,0:T(8,128)(2,1)S(1)} %get-tuple-element.72._), channel_id=1, source_target_pairs={{0,5},{1,4},{2,7},{3,6},{4,1},{5,0},{6,3},{7,2},{8,13},{9,12},{10,... | collective-permute-start | bytes 98312 | tf_op jit(solution)/shard_map/ppermute | solution.py:294
  36.0 4.4 %collective-permute-start.20 = (bf16[64,256]{1,0:T(8,128)(2,1)S(1)}, bf16[64,256]{1,0:T(8,128)(2,1)S(1)}, u32[]{:S(2)}, u32[]{:S(2)}) collective-permute-start(bf16[64,256]{1,0:T(8,128)(2,1)S(1)} %mean_over_shards.1.refs_0_), channel_id=1, source_target_pairs={{0,28},{1,29},{2,30},{3,31},{4,24},{5,25},{6,26},{7,27},{8,20},{9,... | collective-permute-start | bytes 98312 | tf_op jit(solution)/shard_map/ppermute | solution.py:294
  37.5 3.5 %collective-permute-start.19 = (bf16[64,256]{1,0:T(8,128)(2,1)S(1)}, bf16[64,256]{1,0:T(8,128)(2,1)S(1)}, u32[]{:S(2)}, u32[]{:S(2)}) collective-permute-start(bf16[64,256]{1,0:T(8,128)(2,1)S(1)} %mean_over_shards.1.refs_0_), channel_id=1, source_target_pairs={{0,20},{1,21},{2,22},{3,23},{4,16},{5,17},{6,18},{7,19},{8,28},{9,... | collective-permute-start | bytes 98312 | tf_op jit(solution)/shard_map/ppermute | solution.py:294
  38.3 3.4 %collective-permute-start.18 = (bf16[64,256]{1,0:T(8,128)(2,1)S(1)}, bf16[64,256]{1,0:T(8,128)(2,1)S(1)}, u32[]{:S(2)}, u32[]{:S(2)}) collective-permute-start(bf16[64,256]{1,0:T(8,128)(2,1)S(1)} %mean_over_shards.1.refs_0_), channel_id=1, source_target_pairs={{0,12},{1,13},{2,14},{3,15},{4,8},{5,9},{6,10},{7,11},{8,4},{9,5},... | collective-permute-start | bytes 98312 | tf_op jit(solution)/shard_map/ppermute | solution.py:294
  41.7 1.4 %collective-permute-start.21 = (bf16[256,256]{1,0:T(8,128)(2,1)S(1)}, bf16[256,256]{1,0:T(8,128)(2,1)S(1)}, u32[]{:S(2)}, u32[]{:S(2)}) collective-permute-start(bf16[256,256]{1,0:T(8,128)(2,1)S(1)} %blocks_of_chips.1.own_ref), channel_id=1, source_target_pairs={{0,4},{4,0},{8,12},{12,8},{16,20},{20,16},{24,28},{28,24},{1,5},{5... | collective-permute-start | bytes 393224 | tf_op jit(solution)/shard_map/ppermute | solution.py:282

commit v8 on v7

--- a/solution.py
+++ b/solution.py
@@ -69,7 +69,7 @@
     copy.wait()
 
 
-def prepare_kernel(slots, lengths_ref, sibling_ref, *refs):
+def prepare_kernel(slots, _, lengths_ref, sibling_ref, *refs):
     inputs, held = refs[:6], refs[6:11]
     (events_t_ref, key_t_ref, value_t_ref, weight_ref, gated_ref, first_ref,
      gate_ref, own_lengths_ref, sems) = refs[11:]
@@ -114,28 +114,63 @@
     return pl.multiple_of(start, 16)
 
 
-def attention_kernel(slots, group, origins, *refs):
+def aligned(shard_rows):
+    return shard_rows % 128 == 0
+
+
+def project(events_ref, pieces, origins, group, shard_rows, spare_ref, sems):
+    copies, total = [], None
+    for piece, (flips, members) in zip(pieces, origins):
+        rows = piece.shape[0] // len(members)
+        starts = [piece_start(shard_rows, group, rows, flips, m) for m in members]
+        if not aligned(shard_rows):
+            for i, start in enumerate(starts):
+                copy = pltpu.make_async_copy(
+                    piece.at[pl.ds(i * rows, rows)],
+                    spare_ref.at[pl.ds(start, rows)],
+                    sems.at[len(copies)],
+                )
+                copy.start()
+                copies.append(copy)
+            continue
+        first = piece_start(shard_rows, group, rows, flips, None)
+        if len(members) > 1:
+            spare_ref[...] = jnp.zeros_like(spare_ref)
+            for i, start in enumerate(starts):
+                place = pl.ds(pl.multiple_of(start - first, 16), rows)
+                spare_ref[place] = piece[i * rows : (i + 1) * rows]
+            piece = spare_ref
+        columns = pl.ds(pl.multiple_of(first, 128), shard_rows)
+        term = dot(events_ref[:, columns], piece[...])
+        total = term if total is None else total + term
+    if copies:
+        for copy in copies:
+            copy.wait()
+        total = dot(events_ref[...], spare_ref[...])
+    return total
+
+
+def projection_scratch(shard_rows, model_width, width, origins):
+    count = sum(len(members) for _, members in origins)
+    spare_rows = shard_rows if aligned(shard_rows) else model_width
+    return [pltpu.VMEM((spare_rows, width), jnp.bfloat16), pltpu.SemaphoreType.DMA((count,))]
+
+
+def held_projection_kernel(group, shard_rows, origins, *refs):
+    pieces, (events_ref, out_ref, spare_ref, sems) = refs[: len(origins)], refs[len(origins) :]
+    out_ref[...] = project(events_ref, pieces, origins, group, shard_rows, spare_ref, sems)
+
+
+def attention_kernel(slots, group, shard_rows, origins, *refs):
     pieces = refs[: len(origins)]
+    terms, refs = refs[len(origins) : -16], refs[-16:]
     (events_ref, key_ref, value_ref, key_t_ref, value_t_ref, weight_ref, gated_ref, first_ref,
      grad_query_ref, query_ref, normed_ref, mixed_grad_ref, attention_ref, scores_grad_ref,
-     projection_ref, sems) = refs[len(origins) :]
-    copies = []
-    for piece, (flips, members) in zip(pieces, origins):
-        rows = piece.shape[0] // len(members)
-        for i, member in enumerate(members):
-            start = piece_start(pieces[0].shape[0], group, rows, flips, member)
-            copies.append(
-                pltpu.make_async_copy(
-                    piece.at[pl.ds(i * rows, rows)],
-                    projection_ref.at[pl.ds(start, rows)],
-                    sems.at[len(copies)],
-                )
-            )
-    for copy in copies:
-        copy.start()
-    for copy in copies:
-        copy.wait()
-    query_ref[...] = dot(events_ref[...], projection_ref[...]).astype(jnp.bfloat16)
+     spare_ref, sems) = refs
+    query = project(events_ref, pieces, origins, group, shard_rows, spare_ref, sems)
+    for term in terms:
+        query = query + term[...]
+    query_ref[...] = query.astype(jnp.bfloat16)
 
     rows, width = key_ref.shape
     scale = 1.0 / math.sqrt(width // HEADS)
@@ -324,7 +359,7 @@
     return group, part, wholes
 
 
-def stack_kernel(*refs):
+def stack_kernel(_, *refs):
     out_ref = refs[-1]
     rows = refs[0].shape[0]
     for i, block_ref in enumerate(refs[:-1]):
@@ -333,7 +368,6 @@
 
 def share(group, part, wholes, ready, dp_count, fsdp_count):
     alike = (0,) * CORES
-    part, ready = lax.optimization_barrier((part, ready))
     parts, members = [part], [1]
     for chip_bits in range(1, group // CORES):
         parts.append(cross(part, dp_count, fsdp_count, chip_bits, alike))
@@ -343,19 +377,18 @@
         part = call(
             stack_kernel,
             "parts_of_weight",
-            parts,
-            [NEAR] * len(parts),
+            [ready] + parts,
+            [ANYWHERE] + [NEAR] * len(parts),
             jax.ShapeDtypeStruct((len(parts) * rows, columns), part.dtype),
         )
     held = [(part, (fsdp_count // 2,) * CORES, members)]
     for block, flips in wholes:
         held.append((lax.optimization_barrier((block, part))[0], flips, [None]))
-    found = []
+    moved = []
     for block, flips, members in held:
-        moved = [m if m is None else m ^ 1 for m in members]
-        found.append((block, (flips, members)))
-        found.append((flip(block, "dp", dp_count, 1), (flips[::-1], moved)))
-    return found
+        places = [m if m is None else m ^ 1 for m in members]
+        moved.append((flip(block, "dp", dp_count, 1), flips[::-1], places))
+    return held, moved
 
 
 def shards(events, query_weight, keys, values, gates, cotangent, lengths):
@@ -381,9 +414,9 @@
     prepared = call(
         functools.partial(prepare_kernel, slots),
         "prepared_operands",
-        [lengths, sibling_events]
+        [part, lengths, sibling_events]
         + [flat_events, keys, values, cotangent, query_weight, gates],
-        [FAR, NEAR] + [FAR] * 6,
+        [ANYWHERE, FAR, NEAR] + [FAR] * 6,
         (
             shape(rows, model_width),
             shape(rows, width),
@@ -406,16 +439,38 @@
     )
     near_events, near_keys, near_values, near_cotangent, near_weight = prepared[:5]
     events_t, keys_t, values_t, weight, gated, first = prepared[5:]
-    found = [(near_weight, ((0, 0), [None]))]
-    found += share(group, part, wholes, first, dp_count, fsdp_count)
-    pieces, origins = zip(*found)
+    held, moved = share(group, part, wholes, first, dp_count, fsdp_count)
+    held = [(near_weight, (0, 0), [None])] + held
+    if not aligned(shard_rows):
+        held, moved = [], held + moved
+
+    def split(found):
+        return [f[0] for f in found], [f[1:] for f in found]
+
+    terms = []
+    if held:
+        pieces, origins = split(held)
+        terms = [
+            call(
+                functools.partial(held_projection_kernel, group, shard_rows, origins),
+                "projection_by_held_rows",
+                pieces + [near_events],
+                [NEAR] * (len(pieces) + 1),
+                shape(rows, width, dtype=f32),
+                projection_scratch(shard_rows, model_width, width, origins),
+                flops=2 * rows * width * shard_rows * len(pieces),
+                moved=4 * rows * width,
+            )
+        ]
+    pieces, origins = split(moved)
     blocks = shape(slots * HEADS, span, span)
     grad_query, query, normed, grad_mixed, attention, grad_scores = call(
-        functools.partial(attention_kernel, slots, group, origins),
+        functools.partial(attention_kernel, slots, group, shard_rows, origins),
         "attention_to_grad_query",
-        list(pieces)
+        pieces
+        + terms
         + [near_events, near_keys, near_values, keys_t, values_t, weight, gated, first],
-        [ANYWHERE] * len(pieces) + [NEAR] * 8,
+        [NEAR] * (len(pieces) + len(terms) + 8),
         (
             shape(rows, width),
             shape(rows, width),
@@ -424,10 +479,7 @@
             blocks,
             blocks,
         ),
-        [
-            pltpu.VMEM((model_width, width), bf16),
-            pltpu.SemaphoreType.DMA((sum(len(members) for _, members in origins),)),
-        ],
+        projection_scratch(shard_rows, model_width, width, origins),
         flops=2 * rows * width * (model_width + 4 * span),
         moved=24 * rows * width,
     )
@@ -515,8 +567,8 @@
         blocks = call(
             stack_kernel,
             "blocks_of_chips",
-            [mean] + far_first(chips, lambda k: to_chip(mean, k)),
-            [NEAR] * chips,
+            [mean, mean] + far_first(chips, lambda k: to_chip(mean, k)),
+            [ANYWHERE] + [NEAR] * chips,
             shape(shard_rows, half_width),
         )
         grad_weight = call(

time: 44.2 us -> 43.3 us (0.980)
  waiting for transfers between devices: 11.8 us -> 10.8 us
    ppermute x17, waiting for transfers between devices: 8.34 us -> 7.86 us  [cross(): return lax.ppermute(block, BOTH, pairs)]
    ppermute x5, waiting for transfers between devices: 3.43 us -> 2.98 us  [flip(): return lax.ppermute(block, axis, [(i, i ^ bits) for i in range(count)])]
    pallas_call x13 -> x14, Pallas kernels: 8.89 us -> 8.72 us  [call(): pl.pallas_call(kernel, out_shape=out_shape, in_specs=in_specs, out_specs=...]
  transfers between devices with their start and end apart: 22 -> 22, of which waited for: 13 -> 14; matrix products, arithmetic and copies ran while one was open for 0% -> 0% of each run, Pallas kernels for 12% -> 14%
where the time goes in v8:
time: 43.3 us; the launch traced here: 43.1 us
  starting transfers between devices  22.8 us (53%)
  waiting for transfers between devices  10.8 us (25%)
  Pallas kernels  8.72 us (20%)
  between operations  0.73 us (2%)
    ppermute x17, starting transfers between devices, cross(): return lax.ppermute(block, BOTH, pairs)  21.4 us
    pallas_call x14, Pallas kernels, call(): pl.pallas_call(kernel, out_shape=out_shape, in_specs=in_specs, out_specs=...  8.72 us
    ppermute x17, waiting for transfers between devices, cross(): return lax.ppermute(block, BOTH, pairs)  7.86 us
    ppermute x5, waiting for transfers between devices, flip(): return lax.ppermute(block, axis, [(i, i ^ bits) for i in range(count)])  2.98 us
    ppermute x5, starting transfers between devices, flip(): return lax.ppermute(block, axis, [(i, i ^ bits) for i in range(count)])  1.41 us
  transfers between devices with their start and end apart: 22, of which 14 were waited for; matrix products, arithmetic and copies ran while one was open for 0% of the time, Pallas kernels for 14%

profile of v8, /device:TPU:0, one launch (start us, length us, event | category | flops | bytes accessed | tf_op | source)
XLA Modules:
  0.0 43.1 jit_solution(8712263671997241413)
XLA Ops:
  0.6 0.5 %collective-permute-start.1 = (bf16[384,1024]{1,0:T(8,128)(2,1)}, bf16[384,1024]{1,0:T(8,128)(2,1)S(1)}, u32[]{:S(2)}, u32[]{:S(2)}) collective-permute-start(bf16[384,1024]{1,0:T(8,128)(2,1)} %bitcast.9), channel_id=1, source_target_pairs={{0,4},{4,0},{8,12},{12,8},{16,20},{20,16},{24,28},{28,24},{1,5},{5... | collective-permute-start | bytes 2359304 | tf_op jit(solution)/shard_map/ppermute | solution.py:317
  1.1 0.8 %own_part_of_weight.1 = bf16[32,512]{1,0:T(8,128)(2,1)S(1)} custom-call(bf16[256,512]{1,0:T(8,128)(2,1)} %refs_4_.1), custom_call_target="tpu_custom_call" | custom-call | tf_op jit(solution)/shard_map/own_part_of_weight/pallas_call | solution.py:33
  1.9 3.8 %collective-permute-start = (bf16[32,512]{1,0:T(8,128)(2,1)S(1)}, bf16[32,512]{1,0:T(8,128)(2,1)S(1)}, u32[]{:S(2)}, u32[]{:S(2)}) collective-permute-start(bf16[32,512]{1,0:T(8,128)(2,1)S(1)} %own_part_of_weight.1), channel_id=1, source_target_pairs={{0,6},{1,7},{2,4},{3,5},{4,2},{5,3},{6,0},{7,1},{8,14},{9,15},{10,... | collective-permute-start | bytes 98312 | tf_op jit(solution)/shard_map/ppermute | solution.py:329
  5.7 1.2 %collective-permute-start.6 = (bf16[256,512]{1,0:T(8,128)(2,1)}, bf16[256,512]{1,0:T(8,128)(2,1)S(1)}, u32[]{:S(2)}, u32[]{:S(2)}) collective-permute-start(bf16[256,512]{1,0:T(8,128)(2,1)} %refs_4_.1), channel_id=1, source_target_pairs={{0,5},{1,4},{2,7},{3,6},{4,3},{5,2},{6,1},{7,0},{8,13},{9,12},{10,... | collective-permute-start | bytes 786440 | tf_op jit(solution)/shard_map/ppermute | solution.py:329
  6.9 0.5 %collective-permute-done._.refs_0_ = bf16[32,512]{1,0:T(8,128)(2,1)S(1)} collective-permute-done((bf16[32,512]{1,0:T(8,128)(2,1)S(1)}, bf16[32,512]{1,0:T(8,128)(2,1)S(1)}, u32[]{:S(2)}, u32[]{:S(2)}) %collective-permute-start) | collective-permute-done | bytes 32800 | tf_op jit(solution)/shard_map/ppermute | solution.py:329
  7.4 2.4 %collective-permute-start.4 = (bf16[32,512]{1,0:T(8,128)(2,1)S(1)}, bf16[32,512]{1,0:T(8,128)(2,1)S(1)}, u32[]{:S(2)}, u32[]{:S(2)}) collective-permute-start(bf16[32,512]{1,0:T(8,128)(2,1)S(1)} %collective-permute-done._.refs_0_), channel_id=1, source_target_pairs={{0,28},{1,29},{2,30},{3,31},{4,24},{5,25},{6,26},{7,27},{8,20},{9,... | collective-permute-start | bytes 98312 | tf_op jit(solution)/shard_map/ppermute | solution.py:329
  10.4 2.3 %prepared_operands.1 = (bf16[384,1024]{1,0:T(8,128)(2,1)S(1)}, bf16[384,512]{1,0:T(8,128)(2,1)S(1)}, bf16[384,512]{1,0:T(8,128)(2,1)S(1)}, bf16[384,512]{1,0:T(8...) custom-call(bf16[32,512]{1,0:T(8,128)(2,1)S(1)} %collective-permute-, ...), custom_call_target="tpu_custom_call" | custom-call | flops 5000000000 | tf_op jit(solution)/shard_map/prepared_operands/pallas_call | solution.py:33
  12.7 0.5 %collective-permute-done.3.refs_2_ = bf16[32,512]{1,0:T(8,128)(2,1)S(1)} collective-permute-done((bf16[32,512]{1,0:T(8,128)(2,1)S(1)}, bf16[32,512]{1,0:T(8,128)(2,1)S(1)}, u32[]{:S(2)}, u32[]{:S(2)}) %collective-permute-start.3) | collective-permute-done | bytes 32800 | tf_op jit(solution)/shard_map/ppermute | solution.py:329
  13.3 1.4 %collective-permute-done.6.refs_2_ = bf16[256,512]{1,0:T(8,128)(2,1)S(1)} collective-permute-done((bf16[256,512]{1,0:T(8,128)(2,1)}, bf16[256,512]{1,0:T(8,128)(2,1)S(1)}, u32[]{:S(2)}, u32[]{:S(2)}) %collective-permute-start.6) | collective-permute-done | bytes 262176 | tf_op jit(solution)/shard_map/ppermute | solution.py:329
  14.7 0.5 %collective-permute-start.5 = (bf16[128,512]{1,0:T(8,128)(2,1)S(1)}, bf16[128,512]{1,0:T(8,128)(2,1)S(1)}, u32[]{:S(2)}, u32[]{:S(2)}) collective-permute-start(bf16[128,512]{1,0:T(8,128)(2,1)S(1)} %parts_of_weight.1.refs_1_), channel_id=1, source_target_pairs={{0,4},{4,0},{8,12},{12,8},{16,20},{20,16},{24,28},{28,24},{1,5},{5... | collective-permute-start | bytes 393224 | tf_op jit(solution)/shard_map/ppermute | solution.py:317
  15.2 0.5 %projection_by_held_rows.1.refs_2_ = f32[384,512]{1,0:T(8,128)S(1)} custom-call(bf16[256,512]{1,0:T(8,128)(2,1)S(1)} %get-tuple-element.47.refs_0_, bf16[128,512]{1,0:T(8,128)(2,1)S(1)} %parts_of_weight.1.refs_1_, bf16[256,512]{1,0:T(8,128)(2,1)S(1)} %collective-permute-done.6.refs_2_, bf16[384,1024]{1,0:T(8,128)(2,1)S(1)} %get-tuple-element.48.refs_3_), custom_call_target="tpu_custom_call" | custom-call | flops 301989888 | bytes 786432 | tf_op jit(solution)/shard_map/projection_by_held_rows/pallas_call | solution.py:33
  15.8 0.7 %collective-permute-done.5.refs_0_ = bf16[128,512]{1,0:T(8,128)(2,1)S(1)} collective-permute-done((bf16[128,512]{1,0:T(8,128)(2,1)S(1)}, bf16[128,512]{1,0:T(8,128)(2,1)S(1)}, u32[]{:S(2)}, u32[]{:S(2)}) %collective-permute-start.5) | collective-permute-done | bytes 131104 | tf_op jit(solution)/shard_map/ppermute | solution.py:317
  16.4 1.6 %attention_to_grad_query.1 = (bf16[384,512]{1,0:T(8,128)(2,1)S(1)}, bf16[384,512]{1,0:T(8,128)(2,1)S(1)}, f32[384,512]{1,0:T(8,128)S(1)}, bf16[384,512]{1,0:T(8,...) custom-call(bf16[128,512]{1,0:T(8,128)(2,1)S(1)} %collective-permute-done.5.refs_0_, ...), custom_call_target="tpu_custom_call" | custom-call | flops 603979776 | bytes 4718592 | tf_op jit(solution)/shard_map/attention_to_grad_query/pallas_call | solution.py:33
  18.3 0.5 %weight_gradient_of_own_events.1 = (f32[512,256]{1,0:T(8,128)S(1)}, bf16[512,384]{1,0:T(8,128)(2,1)S(1)}, f32[512,256]{1,0:T(8,128)S(1)}, bf16[512,384]{1,0:T(8,128)(2,1)S(1)}) custom-call(bf16[1024,768]{1,0:T(8,128)(2,1)S(1)} %get-tuple-element.56.events_ref, bf16[384,512]{1,0:T(8,128)(2,1)S(1)} %get-tuple-element.55.grad_query_ref), custom_call_target="tpu_custom_call" | custom-call | flops 201326592 | bytes 3145728 | tf_op jit(solution)/shard_map/weight_gradient_of_own_events/pallas_call | solution.py:33
  18.8 1.1 %collective-permute-done.8._.grad_query_ref = bf16[384,512]{1,0:T(8,128)(2,1)S(1)} collective-permute-done((bf16[384,512]{1,0:T(8,128)(2,1)S(1)}, bf16[384,512]{1,0:T(8,128)(2,1)S(1)}, u32[]{:S(2)}, u32[]{:S(2)}) %collective-permute-start.8) | collective-permute-done | bytes 393248 | tf_op jit(solution)/shard_map/ppermute | solution.py:317
  20.1 2.3 %collective-permute-start.9 = (bf16[64,512]{1,0:T(8,128)(2,1)S(1)}, bf16[64,512]{1,0:T(8,128)(2,1)S(1)}, u32[]{:S(2)}, u32[]{:S(2)}) collective-permute-start(bf16[64,512]{1,0:T(8,128)(2,1)S(1)} %get-tuple-element.60), channel_id=1, source_target_pairs={{0,28},{1,29},{2,30},{3,31},{4,24},{5,25},{6,26},{7,27},{8,20},{9,... | collective-permute-start | bytes 196616 | tf_op jit(solution)/shard_map/ppermute | solution.py:329
  22.4 0.5 %collective-permute-start.10 = (bf16[64,512]{1,0:T(8,128)(2,1)S(1)}, bf16[64,512]{1,0:T(8,128)(2,1)S(1)}, u32[]{:S(2)}, u32[]{:S(2)}) collective-permute-start(bf16[64,512]{1,0:T(8,128)(2,1)S(1)} %get-tuple-element.61), channel_id=1, source_target_pairs={{0,20},{1,21},{2,22},{3,23},{4,16},{5,17},{6,18},{7,19},{8,28},{9,... | collective-permute-start | bytes 196616 | tf_op jit(solution)/shard_map/ppermute | solution.py:329
  23.5 2.5 %collective-permute-start.12 = (bf16[64,512]{1,0:T(8,128)(2,1)S(1)}, bf16[64,512]{1,0:T(8,128)(2,1)S(1)}, u32[]{:S(2)}, u32[]{:S(2)}) collective-permute-start(bf16[64,512]{1,0:T(8,128)(2,1)S(1)} %get-tuple-element.67), channel_id=1, source_target_pairs={{0,28},{1,29},{2,30},{3,31},{4,24},{5,25},{6,26},{7,27},{8,20},{9,... | collective-permute-start | bytes 196616 | tf_op jit(solution)/shard_map/ppermute | solution.py:329
  26.2 0.5 %collective-permute-start.14 = (bf16[64,512]{1,0:T(8,128)(2,1)S(1)}, bf16[64,512]{1,0:T(8,128)(2,1)S(1)}, u32[]{:S(2)}, u32[]{:S(2)}) collective-permute-start(bf16[64,512]{1,0:T(8,128)(2,1)S(1)} %get-tuple-element.69), channel_id=1, source_target_pairs={{0,12},{1,13},{2,14},{3,15},{4,8},{5,9},{6,10},{7,11},{8,4},{9,5},... | collective-permute-start | bytes 196616 | tf_op jit(solution)/shard_map/ppermute | solution.py:329
  27.0 3.1 %collective-permute-start.16 = (bf16[64,256]{1,0:T(8,128)(2,1)S(1)}, bf16[64,256]{1,0:T(8,128)(2,1)S(1)}, u32[]{:S(2)}, u32[]{:S(2)}) collective-permute-start(bf16[64,256]{1,0:T(8,128)(2,1)S(1)} %get-tuple-element.81), channel_id=1, source_target_pairs={{0,7},{1,6},{2,5},{3,4},{4,3},{5,2},{6,1},{7,0},{8,15},{9,14},{10,... | collective-permute-start | bytes 98312 | tf_op jit(solution)/shard_map/ppermute | solution.py:329
  30.1 1.0 %collective-permute-done.13.refs_2_ = bf16[64,512]{1,0:T(8,128)(2,1)S(1)} collective-permute-done((bf16[64,512]{1,0:T(8,128)(2,1)S(1)}, bf16[64,512]{1,0:T(8,128)(2,1)S(1)}, u32[]{:S(2)}, u32[]{:S(2)}) %collective-permute-start.13) | collective-permute-done | bytes 65568 | tf_op jit(solution)/shard_map/ppermute | solution.py:329
  31.0 1.1 %collective-permute-start.15 = (bf16[64,256]{1,0:T(8,128)(2,1)S(1)}, bf16[64,256]{1,0:T(8,128)(2,1)S(1)}, u32[]{:S(2)}, u32[]{:S(2)}) collective-permute-start(bf16[64,256]{1,0:T(8,128)(2,1)S(1)} %get-tuple-element.70._), channel_id=1, source_target_pairs={{0,5},{1,4},{2,7},{3,6},{4,1},{5,0},{6,3},{7,2},{8,13},{9,12},{10,... | collective-permute-start | bytes 98312 | tf_op jit(solution)/shard_map/ppermute | solution.py:329
  32.2 1.4 %key_value_gate_gradients.1 = (bf16[384,512]{1,0:T(8,128)(2,1)}, bf16[384,512]{1,0:T(8,128)(2,1)}, bf16[384,512]{1,0:T(8,128)(2,1)}) custom-call(bf16[64,256]{1,0:T(8,128)(2,1)S(1)} %get-tuple-element.70._, bf16[384,512]{1,0:T(8,128)(2,1)S(1)} %get-tuple-element.71.query_ref, f32[384,512]{1,0:T(8,128)S(1)} %get-tuple-element.72.normed_ref, ...), custom_call_target="tpu_custom_call" | custom-call | flops 100663296 | bytes 2359296 | tf_op jit(solution)/shard_map/key_value_gate_gradients/pallas_call | solution.py:33
  33.6 0.7 %collective-permute-done.17.refs_3_ = bf16[64,256]{1,0:T(8,128)(2,1)S(1)} collective-permute-done((bf16[64,256]{1,0:T(8,128)(2,1)S(1)}, bf16[64,256]{1,0:T(8,128)(2,1)S(1)}, u32[]{:S(2)}, u32[]{:S(2)}) %collective-permute-start.17) | collective-permute-done | bytes 32800 | tf_op jit(solution)/shard_map/ppermute | solution.py:329
  34.3 0.9 %collective-permute-done.15.refs_1_ = bf16[64,256]{1,0:T(8,128)(2,1)S(1)} collective-permute-done((bf16[64,256]{1,0:T(8,128)(2,1)S(1)}, bf16[64,256]{1,0:T(8,128)(2,1)S(1)}, u32[]{:S(2)}, u32[]{:S(2)}) %collective-permute-start.15) | collective-permute-done | bytes 32800 | tf_op jit(solution)/shard_map/ppermute | solution.py:329
  35.3 1.0 %collective-permute-start.20 = (bf16[64,256]{1,0:T(8,128)(2,1)S(1)}, bf16[64,256]{1,0:T(8,128)(2,1)S(1)}, u32[]{:S(2)}, u32[]{:S(2)}) collective-permute-start(bf16[64,256]{1,0:T(8,128)(2,1)S(1)} %mean_over_shards.1._.refs_0_), channel_id=1, source_target_pairs={{0,28},{1,29},{2,30},{3,31},{4,24},{5,25},{6,26},{7,27},{8,20},{9,... | collective-permute-start | bytes 98312 | tf_op jit(solution)/shard_map/ppermute | solution.py:329
  36.3 1.1 %collective-permute-start.19 = (bf16[64,256]{1,0:T(8,128)(2,1)S(1)}, bf16[64,256]{1,0:T(8,128)(2,1)S(1)}, u32[]{:S(2)}, u32[]{:S(2)}) collective-permute-start(bf16[64,256]{1,0:T(8,128)(2,1)S(1)} %mean_over_shards.1._.refs_0_), channel_id=1, source_target_pairs={{0,20},{1,21},{2,22},{3,23},{4,16},{5,17},{6,18},{7,19},{8,28},{9,... | collective-permute-start | bytes 98312 | tf_op jit(solution)/shard_map/ppermute | solution.py:329
  37.4 0.9 %collective-permute-start.18 = (bf16[64,256]{1,0:T(8,128)(2,1)S(1)}, bf16[64,256]{1,0:T(8,128)(2,1)S(1)}, u32[]{:S(2)}, u32[]{:S(2)}) collective-permute-start(bf16[64,256]{1,0:T(8,128)(2,1)S(1)} %mean_over_shards.1._.refs_0_), channel_id=1, source_target_pairs={{0,12},{1,13},{2,14},{3,15},{4,8},{5,9},{6,10},{7,11},{8,4},{9,5},... | collective-permute-start | bytes 98312 | tf_op jit(solution)/shard_map/ppermute | solution.py:329
  38.3 1.4 %collective-permute-done.20.refs_3_ = bf16[64,256]{1,0:T(8,128)(2,1)S(1)} collective-permute-done((bf16[64,256]{1,0:T(8,128)(2,1)S(1)}, bf16[64,256]{1,0:T(8,128)(2,1)S(1)}, u32[]{:S(2)}, u32[]{:S(2)}) %collective-permute-start.20) | collective-permute-done | bytes 32800 | tf_op jit(solution)/shard_map/ppermute | solution.py:329
  39.6 0.9 %collective-permute-done.19.refs_2_ = bf16[64,256]{1,0:T(8,128)(2,1)S(1)} collective-permute-done((bf16[64,256]{1,0:T(8,128)(2,1)S(1)}, bf16[64,256]{1,0:T(8,128)(2,1)S(1)}, u32[]{:S(2)}, u32[]{:S(2)}) %collective-permute-start.19) | collective-permute-done | bytes 32800 | tf_op jit(solution)/shard_map/ppermute | solution.py:329
  41.0 1.2 %collective-permute-done.21.sibling_ref = bf16[256,256]{1,0:T(8,128)(2,1)S(1)} collective-permute-done((bf16[256,256]{1,0:T(8,128)(2,1)S(1)}, bf16[256,256]{1,0:T(8,128)(2,1)S(1)}, u32[]{:S(2)}, u32[]{:S(2)}) %collective-permute-start.21) | collective-permute-done | bytes 131104 | tf_op jit(solution)/shard_map/ppermute | solution.py:317
  42.2 0.8 %blocks_in_place.1 = f32[256,512]{1,0:T(8,128)} custom-call(bf16[256,256]{1,0:T(8,128)(2,1)S(1)} %blocks_of_chips.1.own_ref, bf16[256,256]{1,0:T(8,128)(2,1)S(1)} %collective-permute-done.21.sibling_ref), custom_call_target="tpu_custom_call" | custom-call | tf_op jit(solution)/shard_map/blocks_in_place/pallas_call | solution.py:33
  (26 shorter events, 2.8 us)
Async XLA Ops:
  0.6 9.7 %collective-permute-start.1 = (bf16[384,1024]{1,0:T(8,128)(2,1)}, bf16[384,1024]{1,0:T(8,128)(2,1)S(1)}, u32[]{:S(2)}, u32[]{:S(2)}) collective-permute-start(bf16[384,1024]{1,0:T(8,128)(2,1)} %bitcast.9), channel_id=1, source_target_pairs={{0,4},{4,0},{8,12},{12,8},{16,20},{20,16},{24,28},{28,24},{1,5},{5... | collective-permute-start | bytes 2359304 | tf_op jit(solution)/shard_map/ppermute | solution.py:317
  1.9 5.5 %collective-permute-start = (bf16[32,512]{1,0:T(8,128)(2,1)S(1)}, bf16[32,512]{1,0:T(8,128)(2,1)S(1)}, u32[]{:S(2)}, u32[]{:S(2)}) collective-permute-start(bf16[32,512]{1,0:T(8,128)(2,1)S(1)} %own_part_of_weight.1), channel_id=1, source_target_pairs={{0,6},{1,7},{2,4},{3,5},{4,2},{5,3},{6,0},{7,1},{8,14},{9,15},{10,... | collective-permute-start | bytes 98312 | tf_op jit(solution)/shard_map/ppermute | solution.py:329
  5.7 9.0 %collective-permute-start.6 = (bf16[256,512]{1,0:T(8,128)(2,1)}, bf16[256,512]{1,0:T(8,128)(2,1)S(1)}, u32[]{:S(2)}, u32[]{:S(2)}) collective-permute-start(bf16[256,512]{1,0:T(8,128)(2,1)} %refs_4_.1), channel_id=1, source_target_pairs={{0,5},{1,4},{2,7},{3,6},{4,3},{5,2},{6,1},{7,0},{8,13},{9,12},{10,... | collective-permute-start | bytes 786440 | tf_op jit(solution)/shard_map/ppermute | solution.py:329
  7.4 5.3 %collective-permute-start.4 = (bf16[32,512]{1,0:T(8,128)(2,1)S(1)}, bf16[32,512]{1,0:T(8,128)(2,1)S(1)}, u32[]{:S(2)}, u32[]{:S(2)}) collective-permute-start(bf16[32,512]{1,0:T(8,128)(2,1)S(1)} %collective-permute-done._.refs_0_), channel_id=1, source_target_pairs={{0,28},{1,29},{2,30},{3,31},{4,24},{5,25},{6,26},{7,27},{8,20},{9,... | collective-permute-start | bytes 98312 | tf_op jit(solution)/shard_map/ppermute | solution.py:329
  9.8 3.4 %collective-permute-start.3 = (bf16[32,512]{1,0:T(8,128)(2,1)S(1)}, bf16[32,512]{1,0:T(8,128)(2,1)S(1)}, u32[]{:S(2)}, u32[]{:S(2)}) collective-permute-start(bf16[32,512]{1,0:T(8,128)(2,1)S(1)} %collective-permute-done._.refs_0_), channel_id=1, source_target_pairs={{0,20},{1,21},{2,22},{3,23},{4,16},{5,17},{6,18},{7,19},{8,28},{9,... | collective-permute-start | bytes 98312 | tf_op jit(solution)/shard_map/ppermute | solution.py:329
  10.0 3.3 %collective-permute-start.2 = (bf16[32,512]{1,0:T(8,128)(2,1)S(1)}, bf16[32,512]{1,0:T(8,128)(2,1)S(1)}, u32[]{:S(2)}, u32[]{:S(2)}) collective-permute-start(bf16[32,512]{1,0:T(8,128)(2,1)S(1)} %collective-permute-done._.refs_0_), channel_id=1, source_target_pairs={{0,12},{1,13},{2,14},{3,15},{4,8},{5,9},{6,10},{7,11},{8,4},{9,5},... | collective-permute-start | bytes 98312 | tf_op jit(solution)/shard_map/ppermute | solution.py:329
  14.7 1.7 %collective-permute-start.7 = (bf16[256,512]{1,0:T(8,128)(2,1)S(1)}, bf16[256,512]{1,0:T(8,128)(2,1)S(1)}, u32[]{:S(2)}, u32[]{:S(2)}) collective-permute-start(bf16[256,512]{1,0:T(8,128)(2,1)S(1)} %collective-permute-done.6.refs_2_), channel_id=1, source_target_pairs={{0,4},{4,0},{8,12},{12,8},{16,20},{20,16},{24,28},{28,24},{1,5},{5... | collective-permute-start | bytes 786440 | tf_op jit(solution)/shard_map/ppermute | solution.py:317
  14.7 1.7 %collective-permute-start.5 = (bf16[128,512]{1,0:T(8,128)(2,1)S(1)}, bf16[128,512]{1,0:T(8,128)(2,1)S(1)}, u32[]{:S(2)}, u32[]{:S(2)}) collective-permute-start(bf16[128,512]{1,0:T(8,128)(2,1)S(1)} %parts_of_weight.1.refs_1_), channel_id=1, source_target_pairs={{0,4},{4,0},{8,12},{12,8},{16,20},{20,16},{24,28},{28,24},{1,5},{5... | collective-permute-start | bytes 393224 | tf_op jit(solution)/shard_map/ppermute | solution.py:317
  18.1 1.8 %collective-permute-start.8 = (bf16[384,512]{1,0:T(8,128)(2,1)S(1)}, bf16[384,512]{1,0:T(8,128)(2,1)S(1)}, u32[]{:S(2)}, u32[]{:S(2)}) collective-permute-start(bf16[384,512]{1,0:T(8,128)(2,1)S(1)} %get-tuple-element.55.grad_query_ref), channel_id=1, source_target_pairs={{0,4},{4,0},{8,12},{12,8},{16,20},{20,16},{24,28},{28,24},{1,5},{5... | collective-permute-start | bytes 1179656 | tf_op jit(solution)/shard_map/ppermute | solution.py:317
  20.1 6.1 %collective-permute-start.9 = (bf16[64,512]{1,0:T(8,128)(2,1)S(1)}, bf16[64,512]{1,0:T(8,128)(2,1)S(1)}, u32[]{:S(2)}, u32[]{:S(2)}) collective-permute-start(bf16[64,512]{1,0:T(8,128)(2,1)S(1)} %get-tuple-element.60), channel_id=1, source_target_pairs={{0,28},{1,29},{2,30},{3,31},{4,24},{5,25},{6,26},{7,27},{8,20},{9,... | collective-permute-start | bytes 196616 | tf_op jit(solution)/shard_map/ppermute | solution.py:329
  22.4 4.3 %collective-permute-start.10 = (bf16[64,512]{1,0:T(8,128)(2,1)S(1)}, bf16[64,512]{1,0:T(8,128)(2,1)S(1)}, u32[]{:S(2)}, u32[]{:S(2)}) collective-permute-start(bf16[64,512]{1,0:T(8,128)(2,1)S(1)} %get-tuple-element.61), channel_id=1, source_target_pairs={{0,20},{1,21},{2,22},{3,23},{4,16},{5,17},{6,18},{7,19},{8,28},{9,... | collective-permute-start | bytes 196616 | tf_op jit(solution)/shard_map/ppermute | solution.py:329
  22.9 4.1 %collective-permute-start.11 = (bf16[64,512]{1,0:T(8,128)(2,1)S(1)}, bf16[64,512]{1,0:T(8,128)(2,1)S(1)}, u32[]{:S(2)}, u32[]{:S(2)}) collective-permute-start(bf16[64,512]{1,0:T(8,128)(2,1)S(1)} %get-tuple-element.62), channel_id=1, source_target_pairs={{0,12},{1,13},{2,14},{3,15},{4,8},{5,9},{6,10},{7,11},{8,4},{9,5},... | collective-permute-start | bytes 196616 | tf_op jit(solution)/shard_map/ppermute | solution.py:329
  23.5 6.6 %collective-permute-start.12 = (bf16[64,512]{1,0:T(8,128)(2,1)S(1)}, bf16[64,512]{1,0:T(8,128)(2,1)S(1)}, u32[]{:S(2)}, u32[]{:S(2)}) collective-permute-start(bf16[64,512]{1,0:T(8,128)(2,1)S(1)} %get-tuple-element.67), channel_id=1, source_target_pairs={{0,28},{1,29},{2,30},{3,31},{4,24},{5,25},{6,26},{7,27},{8,20},{9,... | collective-permute-start | bytes 196616 | tf_op jit(solution)/shard_map/ppermute | solution.py:329
  26.0 5.0 %collective-permute-start.13 = (bf16[64,512]{1,0:T(8,128)(2,1)S(1)}, bf16[64,512]{1,0:T(8,128)(2,1)S(1)}, u32[]{:S(2)}, u32[]{:S(2)}) collective-permute-start(bf16[64,512]{1,0:T(8,128)(2,1)S(1)} %get-tuple-element.68), channel_id=1, source_target_pairs={{0,20},{1,21},{2,22},{3,23},{4,16},{5,17},{6,18},{7,19},{8,28},{9,... | collective-permute-start | bytes 196616 | tf_op jit(solution)/shard_map/ppermute | solution.py:329
  26.2 4.8 %collective-permute-start.14 = (bf16[64,512]{1,0:T(8,128)(2,1)S(1)}, bf16[64,512]{1,0:T(8,128)(2,1)S(1)}, u32[]{:S(2)}, u32[]{:S(2)}) collective-permute-start(bf16[64,512]{1,0:T(8,128)(2,1)S(1)} %get-tuple-element.69), channel_id=1, source_target_pairs={{0,12},{1,13},{2,14},{3,15},{4,8},{5,9},{6,10},{7,11},{8,4},{9,5},... | collective-permute-start | bytes 196616 | tf_op jit(solution)/shard_map/ppermute | solution.py:329
  27.0 6.7 %collective-permute-start.16 = (bf16[64,256]{1,0:T(8,128)(2,1)S(1)}, bf16[64,256]{1,0:T(8,128)(2,1)S(1)}, u32[]{:S(2)}, u32[]{:S(2)}) collective-permute-start(bf16[64,256]{1,0:T(8,128)(2,1)S(1)} %get-tuple-element.81), channel_id=1, source_target_pairs={{0,7},{1,6},{2,5},{3,4},{4,3},{5,2},{6,1},{7,0},{8,15},{9,14},{10,... | collective-permute-start | bytes 98312 | tf_op jit(solution)/shard_map/ppermute | solution.py:329
  30.1 4.3 %collective-permute-start.17 = (bf16[64,256]{1,0:T(8,128)(2,1)S(1)}, bf16[64,256]{1,0:T(8,128)(2,1)S(1)}, u32[]{:S(2)}, u32[]{:S(2)}) collective-permute-start(bf16[64,256]{1,0:T(8,128)(2,1)S(1)} %get-tuple-element.63._), channel_id=1, source_target_pairs={{0,6},{1,7},{2,4},{3,5},{4,2},{5,3},{6,0},{7,1},{8,14},{9,15},{10,... | collective-permute-start | bytes 98312 | tf_op jit(solution)/shard_map/ppermute | solution.py:329
  31.0 4.2 %collective-permute-start.15 = (bf16[64,256]{1,0:T(8,128)(2,1)S(1)}, bf16[64,256]{1,0:T(8,128)(2,1)S(1)}, u32[]{:S(2)}, u32[]{:S(2)}) collective-permute-start(bf16[64,256]{1,0:T(8,128)(2,1)S(1)} %get-tuple-element.70._), channel_id=1, source_target_pairs={{0,5},{1,4},{2,7},{3,6},{4,1},{5,0},{6,3},{7,2},{8,13},{9,12},{10,... | collective-permute-start | bytes 98312 | tf_op jit(solution)/shard_map/ppermute | solution.py:329
  35.3 4.4 %collective-permute-start.20 = (bf16[64,256]{1,0:T(8,128)(2,1)S(1)}, bf16[64,256]{1,0:T(8,128)(2,1)S(1)}, u32[]{:S(2)}, u32[]{:S(2)}) collective-permute-start(bf16[64,256]{1,0:T(8,128)(2,1)S(1)} %mean_over_shards.1._.refs_0_), channel_id=1, source_target_pairs={{0,28},{1,29},{2,30},{3,31},{4,24},{5,25},{6,26},{7,27},{8,20},{9,... | collective-permute-start | bytes 98312 | tf_op jit(solution)/shard_map/ppermute | solution.py:329
  36.3 4.3 %collective-permute-start.19 = (bf16[64,256]{1,0:T(8,128)(2,1)S(1)}, bf16[64,256]{1,0:T(8,128)(2,1)S(1)}, u32[]{:S(2)}, u32[]{:S(2)}) collective-permute-start(bf16[64,256]{1,0:T(8,128)(2,1)S(1)} %mean_over_shards.1._.refs_0_), channel_id=1, source_target_pairs={{0,20},{1,21},{2,22},{3,23},{4,16},{5,17},{6,18},{7,19},{8,28},{9,... | collective-permute-start | bytes 98312 | tf_op jit(solution)/shard_map/ppermute | solution.py:329
  37.4 3.4 %collective-permute-start.18 = (bf16[64,256]{1,0:T(8,128)(2,1)S(1)}, bf16[64,256]{1,0:T(8,128)(2,1)S(1)}, u32[]{:S(2)}, u32[]{:S(2)}) collective-permute-start(bf16[64,256]{1,0:T(8,128)(2,1)S(1)} %mean_over_shards.1._.refs_0_), channel_id=1, source_target_pairs={{0,12},{1,13},{2,14},{3,15},{4,8},{5,9},{6,10},{7,11},{8,4},{9,5},... | collective-permute-start | bytes 98312 | tf_op jit(solution)/shard_map/ppermute | solution.py:329
  40.8 1.4 %collective-permute-start.21 = (bf16[256,256]{1,0:T(8,128)(2,1)S(1)}, bf16[256,256]{1,0:T(8,128)(2,1)S(1)}, u32[]{:S(2)}, u32[]{:S(2)}) collective-permute-start(bf16[256,256]{1,0:T(8,128)(2,1)S(1)} %blocks_of_chips.1.own_ref), channel_id=1, source_target_pairs={{0,4},{4,0},{8,12},{12,8},{16,20},{20,16},{24,28},{28,24},{1,5},{5... | collective-permute-start | bytes 393224 | tf_op jit(solution)/shard_map/ppermute | solution.py:317

commit v9 on v8

--- a/solution.py
+++ b/solution.py
@@ -180,7 +180,7 @@
     slopes, mixed, grad_mixed = [], [], []
     for s, h, i in each:
         scores = dot(query_ref[places[s], columns[h]], key_t_ref[columns[h], places[s]]) * scale
-        sigmoid = 0.5 * jnp.tanh(0.5 * scores) + 0.5
+        sigmoid = 1.0 / (1.0 + jnp.exp(-scores))
         silu = scores * sigmoid
         attention_ref[i] = (silu * weight_ref[s]).astype(jnp.bfloat16)
         slopes.append((sigmoid + silu * (1.0 - sigmoid)) * weight_ref[s])
@@ -231,12 +231,8 @@
     return lax.rem(lax.axis_index("dp"), CORES) ^ (1 if k else 0) ^ (1 if z else 0)
 
 
-def chip_flips(chips):
-    return (0,) + tuple(range(chips - 1, 0, -1))
-
-
 def gradient_picks(chips, shard_flips):
-    every = [(k, i, z) for k in chip_flips(chips) for i, z in enumerate(shard_flips)]
+    every = [(k, i, z) for k in range(chips) for i, z in enumerate(shard_flips)]
     return [[p for p in every if (p[0] != 0) ^ (p[2] != 0) == bool(side)] for side in range(CORES)]
 
 
@@ -264,12 +260,12 @@
             term_ref[first:at] = dot(picked_ref[first:at], grad_query_ref[:, columns])
 
 
-def gradient_kernel(chips, flips, _, term_ref, events_ref, grad_query_ref, *outs):
+def gradient_kernel(order, flips, _, term_ref, events_ref, grad_query_ref, *outs):
     half = term_ref.shape[1]
     part_rows = outs[0].shape[0]
-    out_of = dict(zip(chip_flips(chips), outs))
+    out_of = dict(zip(order, outs))
     at = 0
-    for side, picks in enumerate(gradient_picks(chips, flips)):
+    for side, picks in enumerate(gradient_picks(len(order), flips)):
         rows = slice(at, at + len(picks) * part_rows)
         total = term_ref[rows] + dot(events_ref[rows], grad_query_ref[:, half_columns(side, half)])
         for p, (k, i, _) in enumerate(picks):
@@ -492,10 +488,11 @@
         def to_chip(block, k):
             return cross(block, dp_count, fsdp_count, k, alike)
 
-        order = chip_flips(chips)
-
-        def summed_over_chips(terms, name, flips, after):
-            terms = [terms[0]] + [to_chip(a, k) for a, k in zip(terms[1:], order[1:])]
+        orders = (tuple(range(chips)), (0,) + tuple(range(chips - 1, 0, -1)))
+
+        def summed_over_chips(terms, name, which, after):
+            flips = sets[which]
+            terms = [terms[0]] + [to_chip(a, k) for a, k in zip(terms[1:], orders[which][1:])]
             return call(
                 functools.partial(chip_sum_kernel, chips),
                 name,
@@ -525,11 +522,11 @@
         def gradient(which, name, after):
             columns = len(sets[which]) * half_width
             return call(
-                functools.partial(gradient_kernel, chips, sets[which]),
+                functools.partial(gradient_kernel, orders[which], sets[which]),
                 name,
                 [after, *own_terms[2 * which : 2 * which + 2], got],
                 [ANYWHERE] + [NEAR] * 3,
-                tuple(shape(part_rows, columns, dtype=bf16 if k else f32) for k in order),
+                tuple(shape(part_rows, columns, dtype=bf16 if k else f32) for k in orders[which]),
                 flops=2 * rows * picked_rows[which] * half_width,
                 moved=2 * picked_rows[which] * (rows + 2 * half_width),
             )
@@ -540,9 +537,9 @@
         def to_shard(block, z):
             return cross(block, dp_count, fsdp_count, 0, (z,) * CORES)
 
-        far_sums = summed_over_chips(far_terms, "far_shards_over_chips", sets[0], got)
+        far_sums = summed_over_chips(far_terms, "far_shards_over_chips", 0, got)
         own_sum, next_sum = summed_over_chips(
-            terms, "near_shards_over_chips", sets[1], far_sums[0]
+            terms, "near_shards_over_chips", 1, far_sums[0]
         )
         far_sums = [to_shard(a, z) for a, z in reversed(list(zip(far_sums, sets[0])))]
         terms = [next_sum]

time: 43.3 us -> 44 us (1.016)
  waiting for transfers between devices: 10.8 us -> 11.3 us
  transfers between devices with their start and end apart: 22 -> 22, of which waited for: 14 -> 11; matrix products, arithmetic and copies ran while one was open for 0% -> 0% of each run, Pallas kernels for 14% -> 14%
where the time goes in v9:
time: 44 us; the launch traced here: 43.8 us
  starting transfers between devices  23.1 us (52%)
  waiting for transfers between devices  11.3 us (26%)
  Pallas kernels  8.72 us (20%)
  between operations  0.73 us (2%)
    ppermute x17, starting transfers between devices, cross(): return lax.ppermute(block, BOTH, pairs)  21.7 us
    pallas_call x14, Pallas kernels, call(): pl.pallas_call(kernel, out_shape=out_shape, in_specs=in_specs, out_specs=...  8.72 us
    ppermute x17, waiting for transfers between devices, cross(): return lax.ppermute(block, BOTH, pairs)  8.27 us
    ppermute x5, waiting for transfers between devices, flip(): return lax.ppermute(block, axis, [(i, i ^ bits) for i in range(count)])  2.98 us
    ppermute x5, starting transfers between devices, flip(): return lax.ppermute(block, axis, [(i, i ^ bits) for i in range(count)])  1.41 us
  transfers between devices with their start and end apart: 22, of which 11 were waited for; matrix products, arithmetic and copies ran while one was open for 0% of the time, Pallas kernels for 14%

profile of v9, /device:TPU:0, one launch (start us, length us, event | category | flops | bytes accessed | tf_op | source)
XLA Modules:
  0.0 43.8 jit_solution(374074497840508867)
XLA Ops:
  0.6 0.5 %collective-permute-start.1 = (bf16[384,1024]{1,0:T(8,128)(2,1)}, bf16[384,1024]{1,0:T(8,128)(2,1)S(1)}, u32[]{:S(2)}, u32[]{:S(2)}) collective-permute-start(bf16[384,1024]{1,0:T(8,128)(2,1)} %bitcast.9), channel_id=1, source_target_pairs={{0,4},{4,0},{8,12},{12,8},{16,20},{20,16},{24,28},{28,24},{1,5},{5... | collective-permute-start | bytes 2359304 | tf_op jit(solution)/shard_map/ppermute | solution.py:313
  1.1 0.8 %own_part_of_weight.1 = bf16[32,512]{1,0:T(8,128)(2,1)S(1)} custom-call(bf16[256,512]{1,0:T(8,128)(2,1)} %refs_4_.1), custom_call_target="tpu_custom_call" | custom-call | tf_op jit(solution)/shard_map/own_part_of_weight/pallas_call | solution.py:33
  1.9 3.8 %collective-permute-start = (bf16[32,512]{1,0:T(8,128)(2,1)S(1)}, bf16[32,512]{1,0:T(8,128)(2,1)S(1)}, u32[]{:S(2)}, u32[]{:S(2)}) collective-permute-start(bf16[32,512]{1,0:T(8,128)(2,1)S(1)} %own_part_of_weight.1), channel_id=1, source_target_pairs={{0,6},{1,7},{2,4},{3,5},{4,2},{5,3},{6,0},{7,1},{8,14},{9,15},{10,... | collective-permute-start | bytes 98312 | tf_op jit(solution)/shard_map/ppermute | solution.py:325
  5.7 1.2 %collective-permute-start.6 = (bf16[256,512]{1,0:T(8,128)(2,1)}, bf16[256,512]{1,0:T(8,128)(2,1)S(1)}, u32[]{:S(2)}, u32[]{:S(2)}) collective-permute-start(bf16[256,512]{1,0:T(8,128)(2,1)} %refs_4_.1), channel_id=1, source_target_pairs={{0,5},{1,4},{2,7},{3,6},{4,3},{5,2},{6,1},{7,0},{8,13},{9,12},{10,... | collective-permute-start | bytes 786440 | tf_op jit(solution)/shard_map/ppermute | solution.py:325
  6.9 0.5 %collective-permute-done._.refs_0_ = bf16[32,512]{1,0:T(8,128)(2,1)S(1)} collective-permute-done((bf16[32,512]{1,0:T(8,128)(2,1)S(1)}, bf16[32,512]{1,0:T(8,128)(2,1)S(1)}, u32[]{:S(2)}, u32[]{:S(2)}) %collective-permute-start) | collective-permute-done | bytes 32800 | tf_op jit(solution)/shard_map/ppermute | solution.py:325
  7.4 2.4 %collective-permute-start.4 = (bf16[32,512]{1,0:T(8,128)(2,1)S(1)}, bf16[32,512]{1,0:T(8,128)(2,1)S(1)}, u32[]{:S(2)}, u32[]{:S(2)}) collective-permute-start(bf16[32,512]{1,0:T(8,128)(2,1)S(1)} %collective-permute-done._.refs_0_), channel_id=1, source_target_pairs={{0,28},{1,29},{2,30},{3,31},{4,24},{5,25},{6,26},{7,27},{8,20},{9,... | collective-permute-start | bytes 98312 | tf_op jit(solution)/shard_map/ppermute | solution.py:325
  10.0 0.4 collective-permute-start.2
  10.4 2.3 %prepared_operands.1 = (bf16[384,1024]{1,0:T(8,128)(2,1)S(1)}, bf16[384,512]{1,0:T(8,128)(2,1)S(1)}, bf16[384,512]{1,0:T(8,128)(2,1)S(1)}, bf16[384,512]{1,0:T(8...) custom-call(bf16[32,512]{1,0:T(8,128)(2,1)S(1)} %collective-permute-, ...), custom_call_target="tpu_custom_call" | custom-call | flops 5000000000 | tf_op jit(solution)/shard_map/prepared_operands/pallas_call | solution.py:33
  12.7 0.5 %collective-permute-done.3.refs_2_ = bf16[32,512]{1,0:T(8,128)(2,1)S(1)} collective-permute-done((bf16[32,512]{1,0:T(8,128)(2,1)S(1)}, bf16[32,512]{1,0:T(8,128)(2,1)S(1)}, u32[]{:S(2)}, u32[]{:S(2)}) %collective-permute-start.3) | collective-permute-done | bytes 32800 | tf_op jit(solution)/shard_map/ppermute | solution.py:325
  13.3 1.4 %collective-permute-done.6.refs_2_ = bf16[256,512]{1,0:T(8,128)(2,1)S(1)} collective-permute-done((bf16[256,512]{1,0:T(8,128)(2,1)}, bf16[256,512]{1,0:T(8,128)(2,1)S(1)}, u32[]{:S(2)}, u32[]{:S(2)}) %collective-permute-start.6) | collective-permute-done | bytes 262176 | tf_op jit(solution)/shard_map/ppermute | solution.py:325
  14.7 0.5 %collective-permute-start.5 = (bf16[128,512]{1,0:T(8,128)(2,1)S(1)}, bf16[128,512]{1,0:T(8,128)(2,1)S(1)}, u32[]{:S(2)}, u32[]{:S(2)}) collective-permute-start(bf16[128,512]{1,0:T(8,128)(2,1)S(1)} %parts_of_weight.1.refs_1_), channel_id=1, source_target_pairs={{0,4},{4,0},{8,12},{12,8},{16,20},{20,16},{24,28},{28,24},{1,5},{5... | collective-permute-start | bytes 393224 | tf_op jit(solution)/shard_map/ppermute | solution.py:313
  15.2 0.5 %projection_by_held_rows.1.refs_2_ = f32[384,512]{1,0:T(8,128)S(1)} custom-call(bf16[256,512]{1,0:T(8,128)(2,1)S(1)} %get-tuple-element.47.refs_0_, bf16[128,512]{1,0:T(8,128)(2,1)S(1)} %parts_of_weight.1.refs_1_, bf16[256,512]{1,0:T(8,128)(2,1)S(1)} %collective-permute-done.6.refs_2_, bf16[384,1024]{1,0:T(8,128)(2,1)S(1)} %get-tuple-element.48.refs_3_), custom_call_target="tpu_custom_call" | custom-call | flops 301989888 | bytes 786432 | tf_op jit(solution)/shard_map/projection_by_held_rows/pallas_call | solution.py:33
  15.8 0.7 %collective-permute-done.5.refs_0_ = bf16[128,512]{1,0:T(8,128)(2,1)S(1)} collective-permute-done((bf16[128,512]{1,0:T(8,128)(2,1)S(1)}, bf16[128,512]{1,0:T(8,128)(2,1)S(1)}, u32[]{:S(2)}, u32[]{:S(2)}) %collective-permute-start.5) | collective-permute-done | bytes 131104 | tf_op jit(solution)/shard_map/ppermute | solution.py:313
  16.4 1.6 %attention_to_grad_query.1 = (bf16[384,512]{1,0:T(8,128)(2,1)S(1)}, bf16[384,512]{1,0:T(8,128)(2,1)S(1)}, f32[384,512]{1,0:T(8,128)S(1)}, bf16[384,512]{1,0:T(8,...) custom-call(bf16[128,512]{1,0:T(8,128)(2,1)S(1)} %collective-permute-done.5.refs_0_, ...), custom_call_target="tpu_custom_call" | custom-call | flops 603979776 | bytes 4718592 | tf_op jit(solution)/shard_map/attention_to_grad_query/pallas_call | solution.py:33
  18.3 0.5 %weight_gradient_of_own_events.1 = (f32[512,256]{1,0:T(8,128)S(1)}, bf16[512,384]{1,0:T(8,128)(2,1)S(1)}, f32[512,256]{1,0:T(8,128)S(1)}, bf16[512,384]{1,0:T(8,128)(2,1)S(1)}) custom-call(bf16[1024,768]{1,0:T(8,128)(2,1)S(1)} %get-tuple-element.56.events_ref, bf16[384,512]{1,0:T(8,128)(2,1)S(1)} %get-tuple-element.55.grad_query_ref), custom_call_target="tpu_custom_call" | custom-call | flops 201326592 | bytes 3145728 | tf_op jit(solution)/shard_map/weight_gradient_of_own_events/pallas_call | solution.py:33
  18.8 1.1 %collective-permute-done.8._.grad_query_ref = bf16[384,512]{1,0:T(8,128)(2,1)S(1)} collective-permute-done((bf16[384,512]{1,0:T(8,128)(2,1)S(1)}, bf16[384,512]{1,0:T(8,128)(2,1)S(1)}, u32[]{:S(2)}, u32[]{:S(2)}) %collective-permute-start.8) | collective-permute-done | bytes 393248 | tf_op jit(solution)/shard_map/ppermute | solution.py:313
  20.2 1.3 %collective-permute-start.9 = (bf16[64,512]{1,0:T(8,128)(2,1)S(1)}, bf16[64,512]{1,0:T(8,128)(2,1)S(1)}, u32[]{:S(2)}, u32[]{:S(2)}) collective-permute-start(bf16[64,512]{1,0:T(8,128)(2,1)S(1)} %get-tuple-element.60), channel_id=1, source_target_pairs={{0,12},{1,13},{2,14},{3,15},{4,8},{5,9},{6,10},{7,11},{8,4},{9,5},... | collective-permute-start | bytes 196616 | tf_op jit(solution)/shard_map/ppermute | solution.py:325
  21.5 1.5 %collective-permute-start.10 = (bf16[64,512]{1,0:T(8,128)(2,1)S(1)}, bf16[64,512]{1,0:T(8,128)(2,1)S(1)}, u32[]{:S(2)}, u32[]{:S(2)}) collective-permute-start(bf16[64,512]{1,0:T(8,128)(2,1)S(1)} %get-tuple-element.61), channel_id=1, source_target_pairs={{0,20},{1,21},{2,22},{3,23},{4,16},{5,17},{6,18},{7,19},{8,28},{9,... | collective-permute-start | bytes 196616 | tf_op jit(solution)/shard_map/ppermute | solution.py:325
  23.5 2.5 %collective-permute-start.12 = (bf16[64,512]{1,0:T(8,128)(2,1)S(1)}, bf16[64,512]{1,0:T(8,128)(2,1)S(1)}, u32[]{:S(2)}, u32[]{:S(2)}) collective-permute-start(bf16[64,512]{1,0:T(8,128)(2,1)S(1)} %get-tuple-element.67), channel_id=1, source_target_pairs={{0,28},{1,29},{2,30},{3,31},{4,24},{5,25},{6,26},{7,27},{8,20},{9,... | collective-permute-start | bytes 196616 | tf_op jit(solution)/shard_map/ppermute | solution.py:325
  26.3 0.5 %collective-permute-start.14 = (bf16[64,512]{1,0:T(8,128)(2,1)S(1)}, bf16[64,512]{1,0:T(8,128)(2,1)S(1)}, u32[]{:S(2)}, u32[]{:S(2)}) collective-permute-start(bf16[64,512]{1,0:T(8,128)(2,1)S(1)} %get-tuple-element.69), channel_id=1, source_target_pairs={{0,12},{1,13},{2,14},{3,15},{4,8},{5,9},{6,10},{7,11},{8,4},{9,5},... | collective-permute-start | bytes 196616 | tf_op jit(solution)/shard_map/ppermute | solution.py:325
  26.8 1.2 %collective-permute-done.11.refs_3_ = bf16[64,512]{1,0:T(8,128)(2,1)S(1)} collective-permute-done((bf16[64,512]{1,0:T(8,128)(2,1)S(1)}, bf16[64,512]{1,0:T(8,128)(2,1)S(1)}, u32[]{:S(2)}, u32[]{:S(2)}) %collective-permute-start.11) | collective-permute-done | bytes 65568 | tf_op jit(solution)/shard_map/ppermute | solution.py:325
  28.0 3.0 %collective-permute-start.16 = (bf16[64,256]{1,0:T(8,128)(2,1)S(1)}, bf16[64,256]{1,0:T(8,128)(2,1)S(1)}, u32[]{:S(2)}, u32[]{:S(2)}) collective-permute-start(bf16[64,256]{1,0:T(8,128)(2,1)S(1)} %get-tuple-element.81), channel_id=1, source_target_pairs={{0,7},{1,6},{2,5},{3,4},{4,3},{5,2},{6,1},{7,0},{8,15},{9,14},{10,... | collective-permute-start | bytes 98312 | tf_op jit(solution)/shard_map/ppermute | solution.py:325
  31.1 1.6 %collective-permute-start.15 = (bf16[64,256]{1,0:T(8,128)(2,1)S(1)}, bf16[64,256]{1,0:T(8,128)(2,1)S(1)}, u32[]{:S(2)}, u32[]{:S(2)}) collective-permute-start(bf16[64,256]{1,0:T(8,128)(2,1)S(1)} %get-tuple-element.70._), channel_id=1, source_target_pairs={{0,5},{1,4},{2,7},{3,6},{4,1},{5,0},{6,3},{7,2},{8,13},{9,12},{10,... | collective-permute-start | bytes 98312 | tf_op jit(solution)/shard_map/ppermute | solution.py:325
  32.6 1.4 %key_value_gate_gradients.1 = (bf16[384,512]{1,0:T(8,128)(2,1)}, bf16[384,512]{1,0:T(8,128)(2,1)}, bf16[384,512]{1,0:T(8,128)(2,1)}) custom-call(bf16[64,256]{1,0:T(8,128)(2,1)S(1)} %get-tuple-element.70._, bf16[384,512]{1,0:T(8,128)(2,1)S(1)} %get-tuple-element.71.query_ref, f32[384,512]{1,0:T(8,128)S(1)} %get-tuple-element.72.normed_ref, ...), custom_call_target="tpu_custom_call" | custom-call | flops 100663296 | bytes 2359296 | tf_op jit(solution)/shard_map/key_value_gate_gradients/pallas_call | solution.py:33
  34.1 1.5 %collective-permute-done.17.refs_3_ = bf16[64,256]{1,0:T(8,128)(2,1)S(1)} collective-permute-done((bf16[64,256]{1,0:T(8,128)(2,1)S(1)}, bf16[64,256]{1,0:T(8,128)(2,1)S(1)}, u32[]{:S(2)}, u32[]{:S(2)}) %collective-permute-start.17) | collective-permute-done | bytes 32800 | tf_op jit(solution)/shard_map/ppermute | solution.py:325
  35.6 0.5 %collective-permute-start.20 = (bf16[64,256]{1,0:T(8,128)(2,1)S(1)}, bf16[64,256]{1,0:T(8,128)(2,1)S(1)}, u32[]{:S(2)}, u32[]{:S(2)}) collective-permute-start(bf16[64,256]{1,0:T(8,128)(2,1)S(1)} %mean_over_shards.1._.refs_0_), channel_id=1, source_target_pairs={{0,28},{1,29},{2,30},{3,31},{4,24},{5,25},{6,26},{7,27},{8,20},{9,... | collective-permute-start | bytes 98312 | tf_op jit(solution)/shard_map/ppermute | solution.py:325
  36.1 1.7 %collective-permute-start.19 = (bf16[64,256]{1,0:T(8,128)(2,1)S(1)}, bf16[64,256]{1,0:T(8,128)(2,1)S(1)}, u32[]{:S(2)}, u32[]{:S(2)}) collective-permute-start(bf16[64,256]{1,0:T(8,128)(2,1)S(1)} %mean_over_shards.1._.refs_0_), channel_id=1, source_target_pairs={{0,20},{1,21},{2,22},{3,23},{4,16},{5,17},{6,18},{7,19},{8,28},{9,... | collective-permute-start | bytes 98312 | tf_op jit(solution)/shard_map/ppermute | solution.py:325
  37.8 0.6 %collective-permute-start.18 = (bf16[64,256]{1,0:T(8,128)(2,1)S(1)}, bf16[64,256]{1,0:T(8,128)(2,1)S(1)}, u32[]{:S(2)}, u32[]{:S(2)}) collective-permute-start(bf16[64,256]{1,0:T(8,128)(2,1)S(1)} %mean_over_shards.1._.refs_0_), channel_id=1, source_target_pairs={{0,12},{1,13},{2,14},{3,15},{4,8},{5,9},{6,10},{7,11},{8,4},{9,5},... | collective-permute-start | bytes 98312 | tf_op jit(solution)/shard_map/ppermute | solution.py:325
  38.5 1.6 %collective-permute-done.20.refs_3_ = bf16[64,256]{1,0:T(8,128)(2,1)S(1)} collective-permute-done((bf16[64,256]{1,0:T(8,128)(2,1)S(1)}, bf16[64,256]{1,0:T(8,128)(2,1)S(1)}, u32[]{:S(2)}, u32[]{:S(2)}) %collective-permute-start.20) | collective-permute-done | bytes 32800 | tf_op jit(solution)/shard_map/ppermute | solution.py:325
  40.1 1.4 %collective-permute-done.18.refs_1_ = bf16[64,256]{1,0:T(8,128)(2,1)S(1)} collective-permute-done((bf16[64,256]{1,0:T(8,128)(2,1)S(1)}, bf16[64,256]{1,0:T(8,128)(2,1)S(1)}, u32[]{:S(2)}, u32[]{:S(2)}) %collective-permute-start.18) | collective-permute-done | bytes 32800 | tf_op jit(solution)/shard_map/ppermute | solution.py:325
  41.7 1.2 %collective-permute-done.21.sibling_ref = bf16[256,256]{1,0:T(8,128)(2,1)S(1)} collective-permute-done((bf16[256,256]{1,0:T(8,128)(2,1)S(1)}, bf16[256,256]{1,0:T(8,128)(2,1)S(1)}, u32[]{:S(2)}, u32[]{:S(2)}) %collective-permute-start.21) | collective-permute-done | bytes 131104 | tf_op jit(solution)/shard_map/ppermute | solution.py:313
  42.9 0.8 %blocks_in_place.1 = f32[256,512]{1,0:T(8,128)} custom-call(bf16[256,256]{1,0:T(8,128)(2,1)S(1)} %blocks_of_chips.1.own_ref, bf16[256,256]{1,0:T(8,128)(2,1)S(1)} %collective-permute-done.21.sibling_ref), custom_call_target="tpu_custom_call" | custom-call | tf_op jit(solution)/shard_map/blocks_in_place/pallas_call | solution.py:33
  (26 shorter events, 1.9 us)
Async XLA Ops:
  0.6 9.7 %collective-permute-start.1 = (bf16[384,1024]{1,0:T(8,128)(2,1)}, bf16[384,1024]{1,0:T(8,128)(2,1)S(1)}, u32[]{:S(2)}, u32[]{:S(2)}) collective-permute-start(bf16[384,1024]{1,0:T(8,128)(2,1)} %bitcast.9), channel_id=1, source_target_pairs={{0,4},{4,0},{8,12},{12,8},{16,20},{20,16},{24,28},{28,24},{1,5},{5... | collective-permute-start | bytes 2359304 | tf_op jit(solution)/shard_map/ppermute | solution.py:313
  1.9 5.5 %collective-permute-start = (bf16[32,512]{1,0:T(8,128)(2,1)S(1)}, bf16[32,512]{1,0:T(8,128)(2,1)S(1)}, u32[]{:S(2)}, u32[]{:S(2)}) collective-permute-start(bf16[32,512]{1,0:T(8,128)(2,1)S(1)} %own_part_of_weight.1), channel_id=1, source_target_pairs={{0,6},{1,7},{2,4},{3,5},{4,2},{5,3},{6,0},{7,1},{8,14},{9,15},{10,... | collective-permute-start | bytes 98312 | tf_op jit(solution)/shard_map/ppermute | solution.py:325
  5.7 9.0 %collective-permute-start.6 = (bf16[256,512]{1,0:T(8,128)(2,1)}, bf16[256,512]{1,0:T(8,128)(2,1)S(1)}, u32[]{:S(2)}, u32[]{:S(2)}) collective-permute-start(bf16[256,512]{1,0:T(8,128)(2,1)} %refs_4_.1), channel_id=1, source_target_pairs={{0,5},{1,4},{2,7},{3,6},{4,3},{5,2},{6,1},{7,0},{8,13},{9,12},{10,... | collective-permute-start | bytes 786440 | tf_op jit(solution)/shard_map/ppermute | solution.py:325
  7.4 5.3 %collective-permute-start.4 = (bf16[32,512]{1,0:T(8,128)(2,1)S(1)}, bf16[32,512]{1,0:T(8,128)(2,1)S(1)}, u32[]{:S(2)}, u32[]{:S(2)}) collective-permute-start(bf16[32,512]{1,0:T(8,128)(2,1)S(1)} %collective-permute-done._.refs_0_), channel_id=1, source_target_pairs={{0,28},{1,29},{2,30},{3,31},{4,24},{5,25},{6,26},{7,27},{8,20},{9,... | collective-permute-start | bytes 98312 | tf_op jit(solution)/shard_map/ppermute | solution.py:325
  9.8 3.4 %collective-permute-start.3 = (bf16[32,512]{1,0:T(8,128)(2,1)S(1)}, bf16[32,512]{1,0:T(8,128)(2,1)S(1)}, u32[]{:S(2)}, u32[]{:S(2)}) collective-permute-start(bf16[32,512]{1,0:T(8,128)(2,1)S(1)} %collective-permute-done._.refs_0_), channel_id=1, source_target_pairs={{0,20},{1,21},{2,22},{3,23},{4,16},{5,17},{6,18},{7,19},{8,28},{9,... | collective-permute-start | bytes 98312 | tf_op jit(solution)/shard_map/ppermute | solution.py:325
  10.0 3.3 %collective-permute-start.2 = (bf16[32,512]{1,0:T(8,128)(2,1)S(1)}, bf16[32,512]{1,0:T(8,128)(2,1)S(1)}, u32[]{:S(2)}, u32[]{:S(2)}) collective-permute-start(bf16[32,512]{1,0:T(8,128)(2,1)S(1)} %collective-permute-done._.refs_0_), channel_id=1, source_target_pairs={{0,12},{1,13},{2,14},{3,15},{4,8},{5,9},{6,10},{7,11},{8,4},{9,5},... | collective-permute-start | bytes 98312 | tf_op jit(solution)/shard_map/ppermute | solution.py:325
  14.7 1.7 %collective-permute-start.7 = (bf16[256,512]{1,0:T(8,128)(2,1)S(1)}, bf16[256,512]{1,0:T(8,128)(2,1)S(1)}, u32[]{:S(2)}, u32[]{:S(2)}) collective-permute-start(bf16[256,512]{1,0:T(8,128)(2,1)S(1)} %collective-permute-done.6.refs_2_), channel_id=1, source_target_pairs={{0,4},{4,0},{8,12},{12,8},{16,20},{20,16},{24,28},{28,24},{1,5},{5... | collective-permute-start | bytes 786440 | tf_op jit(solution)/shard_map/ppermute | solution.py:313
  14.7 1.7 %collective-permute-start.5 = (bf16[128,512]{1,0:T(8,128)(2,1)S(1)}, bf16[128,512]{1,0:T(8,128)(2,1)S(1)}, u32[]{:S(2)}, u32[]{:S(2)}) collective-permute-start(bf16[128,512]{1,0:T(8,128)(2,1)S(1)} %parts_of_weight.1.refs_1_), channel_id=1, source_target_pairs={{0,4},{4,0},{8,12},{12,8},{16,20},{20,16},{24,28},{28,24},{1,5},{5... | collective-permute-start | bytes 393224 | tf_op jit(solution)/shard_map/ppermute | solution.py:313
  18.1 1.8 %collective-permute-start.8 = (bf16[384,512]{1,0:T(8,128)(2,1)S(1)}, bf16[384,512]{1,0:T(8,128)(2,1)S(1)}, u32[]{:S(2)}, u32[]{:S(2)}) collective-permute-start(bf16[384,512]{1,0:T(8,128)(2,1)S(1)} %get-tuple-element.55.grad_query_ref), channel_id=1, source_target_pairs={{0,4},{4,0},{8,12},{12,8},{16,20},{20,16},{24,28},{28,24},{1,5},{5... | collective-permute-start | bytes 1179656 | tf_op jit(solution)/shard_map/ppermute | solution.py:313
  20.2 6.1 %collective-permute-start.9 = (bf16[64,512]{1,0:T(8,128)(2,1)S(1)}, bf16[64,512]{1,0:T(8,128)(2,1)S(1)}, u32[]{:S(2)}, u32[]{:S(2)}) collective-permute-start(bf16[64,512]{1,0:T(8,128)(2,1)S(1)} %get-tuple-element.60), channel_id=1, source_target_pairs={{0,12},{1,13},{2,14},{3,15},{4,8},{5,9},{6,10},{7,11},{8,4},{9,5},... | collective-permute-start | bytes 196616 | tf_op jit(solution)/shard_map/ppermute | solution.py:325
  21.5 5.3 %collective-permute-start.10 = (bf16[64,512]{1,0:T(8,128)(2,1)S(1)}, bf16[64,512]{1,0:T(8,128)(2,1)S(1)}, u32[]{:S(2)}, u32[]{:S(2)}) collective-permute-start(bf16[64,512]{1,0:T(8,128)(2,1)S(1)} %get-tuple-element.61), channel_id=1, source_target_pairs={{0,20},{1,21},{2,22},{3,23},{4,16},{5,17},{6,18},{7,19},{8,28},{9,... | collective-permute-start | bytes 196616 | tf_op jit(solution)/shard_map/ppermute | solution.py:325
  23.0 5.0 %collective-permute-start.11 = (bf16[64,512]{1,0:T(8,128)(2,1)S(1)}, bf16[64,512]{1,0:T(8,128)(2,1)S(1)}, u32[]{:S(2)}, u32[]{:S(2)}) collective-permute-start(bf16[64,512]{1,0:T(8,128)(2,1)S(1)} %get-tuple-element.62), channel_id=1, source_target_pairs={{0,28},{1,29},{2,30},{3,31},{4,24},{5,25},{6,26},{7,27},{8,20},{9,... | collective-permute-start | bytes 196616 | tf_op jit(solution)/shard_map/ppermute | solution.py:325
  23.5 7.5 %collective-permute-start.12 = (bf16[64,512]{1,0:T(8,128)(2,1)S(1)}, bf16[64,512]{1,0:T(8,128)(2,1)S(1)}, u32[]{:S(2)}, u32[]{:S(2)}) collective-permute-start(bf16[64,512]{1,0:T(8,128)(2,1)S(1)} %get-tuple-element.67), channel_id=1, source_target_pairs={{0,28},{1,29},{2,30},{3,31},{4,24},{5,25},{6,26},{7,27},{8,20},{9,... | collective-permute-start | bytes 196616 | tf_op jit(solution)/shard_map/ppermute | solution.py:325
  26.0 5.0 %collective-permute-start.13 = (bf16[64,512]{1,0:T(8,128)(2,1)S(1)}, bf16[64,512]{1,0:T(8,128)(2,1)S(1)}, u32[]{:S(2)}, u32[]{:S(2)}) collective-permute-start(bf16[64,512]{1,0:T(8,128)(2,1)S(1)} %get-tuple-element.68), channel_id=1, source_target_pairs={{0,20},{1,21},{2,22},{3,23},{4,16},{5,17},{6,18},{7,19},{8,28},{9,... | collective-permute-start | bytes 196616 | tf_op jit(solution)/shard_map/ppermute | solution.py:325
  26.3 4.8 %collective-permute-start.14 = (bf16[64,512]{1,0:T(8,128)(2,1)S(1)}, bf16[64,512]{1,0:T(8,128)(2,1)S(1)}, u32[]{:S(2)}, u32[]{:S(2)}) collective-permute-start(bf16[64,512]{1,0:T(8,128)(2,1)S(1)} %get-tuple-element.69), channel_id=1, source_target_pairs={{0,12},{1,13},{2,14},{3,15},{4,8},{5,9},{6,10},{7,11},{8,4},{9,5},... | collective-permute-start | bytes 196616 | tf_op jit(solution)/shard_map/ppermute | solution.py:325
  28.0 6.1 %collective-permute-start.16 = (bf16[64,256]{1,0:T(8,128)(2,1)S(1)}, bf16[64,256]{1,0:T(8,128)(2,1)S(1)}, u32[]{:S(2)}, u32[]{:S(2)}) collective-permute-start(bf16[64,256]{1,0:T(8,128)(2,1)S(1)} %get-tuple-element.81), channel_id=1, source_target_pairs={{0,7},{1,6},{2,5},{3,4},{4,3},{5,2},{6,1},{7,0},{8,15},{9,14},{10,... | collective-permute-start | bytes 98312 | tf_op jit(solution)/shard_map/ppermute | solution.py:325
  31.0 4.6 %collective-permute-start.17 = (bf16[64,256]{1,0:T(8,128)(2,1)S(1)}, bf16[64,256]{1,0:T(8,128)(2,1)S(1)}, u32[]{:S(2)}, u32[]{:S(2)}) collective-permute-start(bf16[64,256]{1,0:T(8,128)(2,1)S(1)} %get-tuple-element.63._), channel_id=1, source_target_pairs={{0,6},{1,7},{2,4},{3,5},{4,2},{5,3},{6,0},{7,1},{8,14},{9,15},{10,... | collective-permute-start | bytes 98312 | tf_op jit(solution)/shard_map/ppermute | solution.py:325
  31.1 4.5 %collective-permute-start.15 = (bf16[64,256]{1,0:T(8,128)(2,1)S(1)}, bf16[64,256]{1,0:T(8,128)(2,1)S(1)}, u32[]{:S(2)}, u32[]{:S(2)}) collective-permute-start(bf16[64,256]{1,0:T(8,128)(2,1)S(1)} %get-tuple-element.70._), channel_id=1, source_target_pairs={{0,5},{1,4},{2,7},{3,6},{4,1},{5,0},{6,3},{7,2},{8,13},{9,12},{10,... | collective-permute-start | bytes 98312 | tf_op jit(solution)/shard_map/ppermute | solution.py:325
  35.6 4.5 %collective-permute-start.20 = (bf16[64,256]{1,0:T(8,128)(2,1)S(1)}, bf16[64,256]{1,0:T(8,128)(2,1)S(1)}, u32[]{:S(2)}, u32[]{:S(2)}) collective-permute-start(bf16[64,256]{1,0:T(8,128)(2,1)S(1)} %mean_over_shards.1._.refs_0_), channel_id=1, source_target_pairs={{0,28},{1,29},{2,30},{3,31},{4,24},{5,25},{6,26},{7,27},{8,20},{9,... | collective-permute-start | bytes 98312 | tf_op jit(solution)/shard_map/ppermute | solution.py:325
  36.1 4.0 %collective-permute-start.19 = (bf16[64,256]{1,0:T(8,128)(2,1)S(1)}, bf16[64,256]{1,0:T(8,128)(2,1)S(1)}, u32[]{:S(2)}, u32[]{:S(2)}) collective-permute-start(bf16[64,256]{1,0:T(8,128)(2,1)S(1)} %mean_over_shards.1._.refs_0_), channel_id=1, source_target_pairs={{0,20},{1,21},{2,22},{3,23},{4,16},{5,17},{6,18},{7,19},{8,28},{9,... | collective-permute-start | bytes 98312 | tf_op jit(solution)/shard_map/ppermute | solution.py:325
  37.8 3.7 %collective-permute-start.18 = (bf16[64,256]{1,0:T(8,128)(2,1)S(1)}, bf16[64,256]{1,0:T(8,128)(2,1)S(1)}, u32[]{:S(2)}, u32[]{:S(2)}) collective-permute-start(bf16[64,256]{1,0:T(8,128)(2,1)S(1)} %mean_over_shards.1._.refs_0_), channel_id=1, source_target_pairs={{0,12},{1,13},{2,14},{3,15},{4,8},{5,9},{6,10},{7,11},{8,4},{9,5},... | collective-permute-start | bytes 98312 | tf_op jit(solution)/shard_map/ppermute | solution.py:325
  41.5 1.4 %collective-permute-start.21 = (bf16[256,256]{1,0:T(8,128)(2,1)S(1)}, bf16[256,256]{1,0:T(8,128)(2,1)S(1)}, u32[]{:S(2)}, u32[]{:S(2)}) collective-permute-start(bf16[256,256]{1,0:T(8,128)(2,1)S(1)} %blocks_of_chips.1.own_ref), channel_id=1, source_target_pairs={{0,4},{4,0},{8,12},{12,8},{16,20},{20,16},{24,28},{28,24},{1,5},{5... | collective-permute-start | bytes 393224 | tf_op jit(solution)/shard_map/ppermute | solution.py:313

commit v10 on v9

--- a/solution.py
+++ b/solution.py
@@ -23,7 +23,7 @@
 
 
 def call(kernel, name, operands, in_specs, out_shape, scratch=(), flops=0, moved=0,
-         out_specs=None):
+         out_specs=None, aliases=None):
     vmem = pl.BlockSpec(memory_space=pltpu.VMEM)
     many = isinstance(out_shape, tuple)
     operands = [
@@ -36,6 +36,7 @@
         in_specs=in_specs,
         out_specs=out_specs or ((vmem,) * len(out_shape) if many else vmem),
         scratch_shapes=list(scratch),
+        input_output_aliases=aliases or {},
         compiler_params=pltpu.CompilerParams(vmem_limit_bytes=VMEM_LIMIT),
         cost_estimate=pl.CostEstimate(flops=flops, bytes_accessed=moved, transcendentals=0),
         name=name,
@@ -293,17 +294,17 @@
     refs[-1][...] = (total / count).astype(refs[-1].dtype)
 
 
-def place_kernel(chips, own_ref, sibling_ref, out_ref, held_ref, sems):
-    rows, half = own_ref.shape[0] // chips, own_ref.shape[1]
-    core, chip = lax.rem(lax.axis_index("dp"), CORES), lax.div(lax.axis_index("dp"), CORES)
+def place_kernel(side, chips, blocks_ref, *refs):
+    out_ref, held_ref, sems = refs[-3:]
+    rows, half = blocks_ref.shape[0] // chips, blocks_ref.shape[1]
+    core, chip = lax.rem(lax.axis_index("dp"), CORES) ^ side, lax.div(lax.axis_index("dp"), CORES)
+    held_ref[...] = blocks_ref[...].astype(held_ref.dtype)
     copies = []
     for k in range(chips):
         place = pl.ds(pl.multiple_of((chip ^ k) * rows, rows), rows)
-        for block_ref, side in ((own_ref, core), (sibling_ref, 1 - core)):
-            columns = pl.ds(pl.multiple_of((side ^ (1 if k else 0)) * half, half), half)
-            block = block_ref[k * rows : (k + 1) * rows]
-            held_ref[place, columns] = block.astype(held_ref.dtype)
-        copies.append(pltpu.make_async_copy(held_ref.at[place], out_ref.at[place], sems.at[k]))
+        columns = pl.ds(pl.multiple_of((core ^ (1 if k else 0)) * half, half), half)
+        block = held_ref.at[pl.ds(k * rows, rows)]
+        copies.append(pltpu.make_async_copy(block, out_ref.at[place, columns], sems.at[k]))
         copies[k].start()
     for copy in copies:
         copy.wait()
@@ -488,11 +489,11 @@
         def to_chip(block, k):
             return cross(block, dp_count, fsdp_count, k, alike)
 
-        orders = (tuple(range(chips)), (0,) + tuple(range(chips - 1, 0, -1)))
+        order = (0,) + tuple(range(chips - 1, 0, -1))
 
         def summed_over_chips(terms, name, which, after):
             flips = sets[which]
-            terms = [terms[0]] + [to_chip(a, k) for a, k in zip(terms[1:], orders[which][1:])]
+            terms = [terms[0]] + [to_chip(a, k) for a, k in zip(terms[1:], order[1:])]
             return call(
                 functools.partial(chip_sum_kernel, chips),
                 name,
@@ -522,11 +523,11 @@
         def gradient(which, name, after):
             columns = len(sets[which]) * half_width
             return call(
-                functools.partial(gradient_kernel, orders[which], sets[which]),
+                functools.partial(gradient_kernel, order, sets[which]),
                 name,
                 [after, *own_terms[2 * which : 2 * which + 2], got],
                 [ANYWHERE] + [NEAR] * 3,
-                tuple(shape(part_rows, columns, dtype=bf16 if k else f32) for k in orders[which]),
+                tuple(shape(part_rows, columns, dtype=bf16 if k else f32) for k in order),
                 flops=2 * rows * picked_rows[which] * half_width,
                 moved=2 * picked_rows[which] * (rows + 2 * half_width),
             )
@@ -568,15 +569,22 @@
             [ANYWHERE] + [NEAR] * chips,
             shape(shard_rows, half_width),
         )
-        grad_weight = call(
-            functools.partial(place_kernel, chips),
-            "blocks_in_place",
-            [blocks, flip(blocks, "dp", dp_count, 1)],
-            [NEAR] * 2,
-            shape(shard_rows, width, dtype=f32),
-            [pltpu.VMEM((shard_rows, width), f32), pltpu.SemaphoreType.DMA((chips,))],
-            out_specs=FAR,
-        )
+        grad_weight = ()
+        for side in range(CORES):
+            grad_weight = call(
+                functools.partial(place_kernel, side, chips),
+                f"blocks_of_{'sibling' if side else 'own'}_core_in_place",
+                [flip(blocks, "dp", dp_count, 1) if side else blocks, *grad_weight],
+                [NEAR] + [FAR] * side,
+                shape(shard_rows, width, dtype=f32),
+                [
+                    pltpu.VMEM((shard_rows, half_width), f32),
+                    pltpu.SemaphoreType.DMA((chips,)),
+                ],
+                out_specs=FAR,
+                aliases={1: 0} if side else {},
+            )
+            grad_weight = grad_weight if side else (grad_weight,)
     else:
         whole = lax.dot_general(flat_events, grad_query, FIRST, preferred_element_type=f32)
         mine = lax.psum_scatter(whole, "fsdp", scatter_dimension=0, tiled=True)

time: 44 us -> 43.2 us (0.982)
  waiting for transfers between devices: 11.3 us -> 10.1 us
  Pallas kernels: 8.72 us -> 9.37 us
    ppermute x5, waiting for transfers between devices: 2.98 us -> 2.23 us  [flip(): return lax.ppermute(block, axis, [(i, i ^ bits) for i in range(count)])]
    pallas_call x14 -> x15, Pallas kernels: 8.72 us -> 9.37 us  [call(): pl.pallas_call(kernel, out_shape=out_shape, in_specs=in_specs, out_specs=...]
  transfers between devices with their start and end apart: 22 -> 22, of which waited for: 11 -> 14; matrix products, arithmetic and copies ran while one was open for 0% -> 0% of each run, Pallas kernels for 14% -> 16%
where the time goes in v10:
time: 43.2 us; the launch traced here: 43 us
  starting transfers between devices  22.8 us (53%)
  waiting for transfers between devices  10.1 us (23%)
  Pallas kernels  9.37 us (22%)
  between operations  0.74 us (2%)
    ppermute x17, starting transfers between devices, cross(): return lax.ppermute(block, BOTH, pairs)  21.4 us
    pallas_call x15, Pallas kernels, call(): pl.pallas_call(kernel, out_shape=out_shape, in_specs=in_specs, out_specs=...  9.37 us
    ppermute x17, waiting for transfers between devices, cross(): return lax.ppermute(block, BOTH, pairs)  7.86 us
    ppermute x5, waiting for transfers between devices, flip(): return lax.ppermute(block, axis, [(i, i ^ bits) for i in range(count)])  2.23 us
    ppermute x5, starting transfers between devices, flip(): return lax.ppermute(block, axis, [(i, i ^ bits) for i in range(count)])  1.41 us
  transfers between devices with their start and end apart: 22, of which 14 were waited for; matrix products, arithmetic and copies ran while one was open for 0% of the time, Pallas kernels for 16%

profile of v10, /device:TPU:0, one launch (start us, length us, event | category | flops | bytes accessed | tf_op | source)
XLA Modules:
  0.0 43.0 jit_solution(4536597475541587361)
XLA Ops:
  0.6 0.5 %collective-permute-start.1 = (bf16[384,1024]{1,0:T(8,128)(2,1)}, bf16[384,1024]{1,0:T(8,128)(2,1)S(1)}, u32[]{:S(2)}, u32[]{:S(2)}) collective-permute-start(bf16[384,1024]{1,0:T(8,128)(2,1)} %bitcast.9), channel_id=1, source_target_pairs={{0,4},{4,0},{8,12},{12,8},{16,20},{20,16},{24,28},{28,24},{1,5},{5... | collective-permute-start | bytes 2359304 | tf_op jit(solution)/shard_map/ppermute | solution.py:314
  1.1 0.8 %own_part_of_weight.1 = bf16[32,512]{1,0:T(8,128)(2,1)S(1)} custom-call(bf16[256,512]{1,0:T(8,128)(2,1)} %refs_4_.1), custom_call_target="tpu_custom_call" | custom-call | tf_op jit(solution)/shard_map/own_part_of_weight/pallas_call | solution.py:33
  1.9 3.8 %collective-permute-start = (bf16[32,512]{1,0:T(8,128)(2,1)S(1)}, bf16[32,512]{1,0:T(8,128)(2,1)S(1)}, u32[]{:S(2)}, u32[]{:S(2)}) collective-permute-start(bf16[32,512]{1,0:T(8,128)(2,1)S(1)} %own_part_of_weight.1), channel_id=1, source_target_pairs={{0,6},{1,7},{2,4},{3,5},{4,2},{5,3},{6,0},{7,1},{8,14},{9,15},{10,... | collective-permute-start | bytes 98312 | tf_op jit(solution)/shard_map/ppermute | solution.py:326
  5.7 1.2 %collective-permute-start.6 = (bf16[256,512]{1,0:T(8,128)(2,1)}, bf16[256,512]{1,0:T(8,128)(2,1)S(1)}, u32[]{:S(2)}, u32[]{:S(2)}) collective-permute-start(bf16[256,512]{1,0:T(8,128)(2,1)} %refs_4_.1), channel_id=1, source_target_pairs={{0,5},{1,4},{2,7},{3,6},{4,3},{5,2},{6,1},{7,0},{8,13},{9,12},{10,... | collective-permute-start | bytes 786440 | tf_op jit(solution)/shard_map/ppermute | solution.py:326
  6.9 0.5 %collective-permute-done._.refs_0_ = bf16[32,512]{1,0:T(8,128)(2,1)S(1)} collective-permute-done((bf16[32,512]{1,0:T(8,128)(2,1)S(1)}, bf16[32,512]{1,0:T(8,128)(2,1)S(1)}, u32[]{:S(2)}, u32[]{:S(2)}) %collective-permute-start) | collective-permute-done | bytes 32800 | tf_op jit(solution)/shard_map/ppermute | solution.py:326
  7.4 2.4 %collective-permute-start.4 = (bf16[32,512]{1,0:T(8,128)(2,1)S(1)}, bf16[32,512]{1,0:T(8,128)(2,1)S(1)}, u32[]{:S(2)}, u32[]{:S(2)}) collective-permute-start(bf16[32,512]{1,0:T(8,128)(2,1)S(1)} %collective-permute-done._.refs_0_), channel_id=1, source_target_pairs={{0,28},{1,29},{2,30},{3,31},{4,24},{5,25},{6,26},{7,27},{8,20},{9,... | collective-permute-start | bytes 98312 | tf_op jit(solution)/shard_map/ppermute | solution.py:326
  10.4 2.3 %prepared_operands.1 = (bf16[384,1024]{1,0:T(8,128)(2,1)S(1)}, bf16[384,512]{1,0:T(8,128)(2,1)S(1)}, bf16[384,512]{1,0:T(8,128)(2,1)S(1)}, bf16[384,512]{1,0:T(8...) custom-call(bf16[32,512]{1,0:T(8,128)(2,1)S(1)} %collective-permute-, ...), custom_call_target="tpu_custom_call" | custom-call | flops 5000000000 | tf_op jit(solution)/shard_map/prepared_operands/pallas_call | solution.py:33
  12.7 0.5 %collective-permute-done.3.refs_2_ = bf16[32,512]{1,0:T(8,128)(2,1)S(1)} collective-permute-done((bf16[32,512]{1,0:T(8,128)(2,1)S(1)}, bf16[32,512]{1,0:T(8,128)(2,1)S(1)}, u32[]{:S(2)}, u32[]{:S(2)}) %collective-permute-start.3) | collective-permute-done | bytes 32800 | tf_op jit(solution)/shard_map/ppermute | solution.py:326
  13.3 1.4 %collective-permute-done.6.refs_2_ = bf16[256,512]{1,0:T(8,128)(2,1)S(1)} collective-permute-done((bf16[256,512]{1,0:T(8,128)(2,1)}, bf16[256,512]{1,0:T(8,128)(2,1)S(1)}, u32[]{:S(2)}, u32[]{:S(2)}) %collective-permute-start.6) | collective-permute-done | bytes 262176 | tf_op jit(solution)/shard_map/ppermute | solution.py:326
  14.7 0.5 %collective-permute-start.5 = (bf16[128,512]{1,0:T(8,128)(2,1)S(1)}, bf16[128,512]{1,0:T(8,128)(2,1)S(1)}, u32[]{:S(2)}, u32[]{:S(2)}) collective-permute-start(bf16[128,512]{1,0:T(8,128)(2,1)S(1)} %parts_of_weight.1.refs_1_), channel_id=1, source_target_pairs={{0,4},{4,0},{8,12},{12,8},{16,20},{20,16},{24,28},{28,24},{1,5},{5... | collective-permute-start | bytes 393224 | tf_op jit(solution)/shard_map/ppermute | solution.py:314
  15.2 0.5 %projection_by_held_rows.1.refs_2_ = f32[384,512]{1,0:T(8,128)S(1)} custom-call(bf16[256,512]{1,0:T(8,128)(2,1)S(1)} %get-tuple-element.47.refs_0_, bf16[128,512]{1,0:T(8,128)(2,1)S(1)} %parts_of_weight.1.refs_1_, bf16[256,512]{1,0:T(8,128)(2,1)S(1)} %collective-permute-done.6.refs_2_, bf16[384,1024]{1,0:T(8,128)(2,1)S(1)} %get-tuple-element.48.refs_3_), custom_call_target="tpu_custom_call" | custom-call | flops 301989888 | bytes 786432 | tf_op jit(solution)/shard_map/projection_by_held_rows/pallas_call | solution.py:33
  15.8 0.7 %collective-permute-done.5.refs_0_ = bf16[128,512]{1,0:T(8,128)(2,1)S(1)} collective-permute-done((bf16[128,512]{1,0:T(8,128)(2,1)S(1)}, bf16[128,512]{1,0:T(8,128)(2,1)S(1)}, u32[]{:S(2)}, u32[]{:S(2)}) %collective-permute-start.5) | collective-permute-done | bytes 131104 | tf_op jit(solution)/shard_map/ppermute | solution.py:314
  16.4 1.6 %attention_to_grad_query.1 = (bf16[384,512]{1,0:T(8,128)(2,1)S(1)}, bf16[384,512]{1,0:T(8,128)(2,1)S(1)}, f32[384,512]{1,0:T(8,128)S(1)}, bf16[384,512]{1,0:T(8,...) custom-call(bf16[128,512]{1,0:T(8,128)(2,1)S(1)} %collective-permute-done.5.refs_0_, ...), custom_call_target="tpu_custom_call" | custom-call | flops 603979776 | bytes 4718592 | tf_op jit(solution)/shard_map/attention_to_grad_query/pallas_call | solution.py:33
  18.3 0.5 %weight_gradient_of_own_events.1 = (f32[512,256]{1,0:T(8,128)S(1)}, bf16[512,384]{1,0:T(8,128)(2,1)S(1)}, f32[512,256]{1,0:T(8,128)S(1)}, bf16[512,384]{1,0:T(8,128)(2,1)S(1)}) custom-call(bf16[1024,768]{1,0:T(8,128)(2,1)S(1)} %get-tuple-element.56.events_ref, bf16[384,512]{1,0:T(8,128)(2,1)S(1)} %get-tuple-element.55.grad_query_ref), custom_call_target="tpu_custom_call" | custom-call | flops 201326592 | bytes 3145728 | tf_op jit(solution)/shard_map/weight_gradient_of_own_events/pallas_call | solution.py:33
  18.8 1.1 %collective-permute-done.8._.grad_query_ref = bf16[384,512]{1,0:T(8,128)(2,1)S(1)} collective-permute-done((bf16[384,512]{1,0:T(8,128)(2,1)S(1)}, bf16[384,512]{1,0:T(8,128)(2,1)S(1)}, u32[]{:S(2)}, u32[]{:S(2)}) %collective-permute-start.8) | collective-permute-done | bytes 393248 | tf_op jit(solution)/shard_map/ppermute | solution.py:314
  20.2 2.3 %collective-permute-start.9 = (bf16[64,512]{1,0:T(8,128)(2,1)S(1)}, bf16[64,512]{1,0:T(8,128)(2,1)S(1)}, u32[]{:S(2)}, u32[]{:S(2)}) collective-permute-start(bf16[64,512]{1,0:T(8,128)(2,1)S(1)} %get-tuple-element.60), channel_id=1, source_target_pairs={{0,28},{1,29},{2,30},{3,31},{4,24},{5,25},{6,26},{7,27},{8,20},{9,... | collective-permute-start | bytes 196616 | tf_op jit(solution)/shard_map/ppermute | solution.py:326
  22.4 0.5 %collective-permute-start.10 = (bf16[64,512]{1,0:T(8,128)(2,1)S(1)}, bf16[64,512]{1,0:T(8,128)(2,1)S(1)}, u32[]{:S(2)}, u32[]{:S(2)}) collective-permute-start(bf16[64,512]{1,0:T(8,128)(2,1)S(1)} %get-tuple-element.61), channel_id=1, source_target_pairs={{0,20},{1,21},{2,22},{3,23},{4,16},{5,17},{6,18},{7,19},{8,28},{9,... | collective-permute-start | bytes 196616 | tf_op jit(solution)/shard_map/ppermute | solution.py:326
  23.5 2.5 %collective-permute-start.12 = (bf16[64,512]{1,0:T(8,128)(2,1)S(1)}, bf16[64,512]{1,0:T(8,128)(2,1)S(1)}, u32[]{:S(2)}, u32[]{:S(2)}) collective-permute-start(bf16[64,512]{1,0:T(8,128)(2,1)S(1)} %get-tuple-element.67), channel_id=1, source_target_pairs={{0,28},{1,29},{2,30},{3,31},{4,24},{5,25},{6,26},{7,27},{8,20},{9,... | collective-permute-start | bytes 196616 | tf_op jit(solution)/shard_map/ppermute | solution.py:326
  26.3 0.5 %collective-permute-start.14 = (bf16[64,512]{1,0:T(8,128)(2,1)S(1)}, bf16[64,512]{1,0:T(8,128)(2,1)S(1)}, u32[]{:S(2)}, u32[]{:S(2)}) collective-permute-start(bf16[64,512]{1,0:T(8,128)(2,1)S(1)} %get-tuple-element.69), channel_id=1, source_target_pairs={{0,12},{1,13},{2,14},{3,15},{4,8},{5,9},{6,10},{7,11},{8,4},{9,5},... | collective-permute-start | bytes 196616 | tf_op jit(solution)/shard_map/ppermute | solution.py:326
  27.0 3.1 %collective-permute-start.16 = (bf16[64,256]{1,0:T(8,128)(2,1)S(1)}, bf16[64,256]{1,0:T(8,128)(2,1)S(1)}, u32[]{:S(2)}, u32[]{:S(2)}) collective-permute-start(bf16[64,256]{1,0:T(8,128)(2,1)S(1)} %get-tuple-element.81), channel_id=1, source_target_pairs={{0,7},{1,6},{2,5},{3,4},{4,3},{5,2},{6,1},{7,0},{8,15},{9,14},{10,... | collective-permute-start | bytes 98312 | tf_op jit(solution)/shard_map/ppermute | solution.py:326
  30.1 1.0 %collective-permute-done.13.refs_2_ = bf16[64,512]{1,0:T(8,128)(2,1)S(1)} collective-permute-done((bf16[64,512]{1,0:T(8,128)(2,1)S(1)}, bf16[64,512]{1,0:T(8,128)(2,1)S(1)}, u32[]{:S(2)}, u32[]{:S(2)}) %collective-permute-start.13) | collective-permute-done | bytes 65568 | tf_op jit(solution)/shard_map/ppermute | solution.py:326
  31.1 1.1 %collective-permute-start.15 = (bf16[64,256]{1,0:T(8,128)(2,1)S(1)}, bf16[64,256]{1,0:T(8,128)(2,1)S(1)}, u32[]{:S(2)}, u32[]{:S(2)}) collective-permute-start(bf16[64,256]{1,0:T(8,128)(2,1)S(1)} %get-tuple-element.70._), channel_id=1, source_target_pairs={{0,5},{1,4},{2,7},{3,6},{4,1},{5,0},{6,3},{7,2},{8,13},{9,12},{10,... | collective-permute-start | bytes 98312 | tf_op jit(solution)/shard_map/ppermute | solution.py:326
  32.2 1.4 %key_value_gate_gradients.1 = (bf16[384,512]{1,0:T(8,128)(2,1)}, bf16[384,512]{1,0:T(8,128)(2,1)}, bf16[384,512]{1,0:T(8,128)(2,1)}) custom-call(bf16[64,256]{1,0:T(8,128)(2,1)S(1)} %get-tuple-element.70._, bf16[384,512]{1,0:T(8,128)(2,1)S(1)} %get-tuple-element.71.query_ref, f32[384,512]{1,0:T(8,128)S(1)} %get-tuple-element.72.normed_ref, ...), custom_call_target="tpu_custom_call" | custom-call | flops 100663296 | bytes 2359296 | tf_op jit(solution)/shard_map/key_value_gate_gradients/pallas_call | solution.py:33
  33.7 0.7 %collective-permute-done.17.refs_3_ = bf16[64,256]{1,0:T(8,128)(2,1)S(1)} collective-permute-done((bf16[64,256]{1,0:T(8,128)(2,1)S(1)}, bf16[64,256]{1,0:T(8,128)(2,1)S(1)}, u32[]{:S(2)}, u32[]{:S(2)}) %collective-permute-start.17) | collective-permute-done | bytes 32800 | tf_op jit(solution)/shard_map/ppermute | solution.py:326
  34.3 0.9 %collective-permute-done.15.refs_1_ = bf16[64,256]{1,0:T(8,128)(2,1)S(1)} collective-permute-done((bf16[64,256]{1,0:T(8,128)(2,1)S(1)}, bf16[64,256]{1,0:T(8,128)(2,1)S(1)}, u32[]{:S(2)}, u32[]{:S(2)}) %collective-permute-start.15) | collective-permute-done | bytes 32800 | tf_op jit(solution)/shard_map/ppermute | solution.py:326
  35.3 1.0 %collective-permute-start.20 = (bf16[64,256]{1,0:T(8,128)(2,1)S(1)}, bf16[64,256]{1,0:T(8,128)(2,1)S(1)}, u32[]{:S(2)}, u32[]{:S(2)}) collective-permute-start(bf16[64,256]{1,0:T(8,128)(2,1)S(1)} %mean_over_shards.1._.refs_0_), channel_id=1, source_target_pairs={{0,28},{1,29},{2,30},{3,31},{4,24},{5,25},{6,26},{7,27},{8,20},{9,... | collective-permute-start | bytes 98312 | tf_op jit(solution)/shard_map/ppermute | solution.py:326
  36.3 1.1 %collective-permute-start.19 = (bf16[64,256]{1,0:T(8,128)(2,1)S(1)}, bf16[64,256]{1,0:T(8,128)(2,1)S(1)}, u32[]{:S(2)}, u32[]{:S(2)}) collective-permute-start(bf16[64,256]{1,0:T(8,128)(2,1)S(1)} %mean_over_shards.1._.refs_0_), channel_id=1, source_target_pairs={{0,20},{1,21},{2,22},{3,23},{4,16},{5,17},{6,18},{7,19},{8,28},{9,... | collective-permute-start | bytes 98312 | tf_op jit(solution)/shard_map/ppermute | solution.py:326
  37.4 0.9 %collective-permute-start.18 = (bf16[64,256]{1,0:T(8,128)(2,1)S(1)}, bf16[64,256]{1,0:T(8,128)(2,1)S(1)}, u32[]{:S(2)}, u32[]{:S(2)}) collective-permute-start(bf16[64,256]{1,0:T(8,128)(2,1)S(1)} %mean_over_shards.1._.refs_0_), channel_id=1, source_target_pairs={{0,12},{1,13},{2,14},{3,15},{4,8},{5,9},{6,10},{7,11},{8,4},{9,5},... | collective-permute-start | bytes 98312 | tf_op jit(solution)/shard_map/ppermute | solution.py:326
  38.3 1.4 %collective-permute-done.20.refs_3_ = bf16[64,256]{1,0:T(8,128)(2,1)S(1)} collective-permute-done((bf16[64,256]{1,0:T(8,128)(2,1)S(1)}, bf16[64,256]{1,0:T(8,128)(2,1)S(1)}, u32[]{:S(2)}, u32[]{:S(2)}) %collective-permute-start.20) | collective-permute-done | bytes 32800 | tf_op jit(solution)/shard_map/ppermute | solution.py:326
  39.7 0.9 %collective-permute-done.19.refs_2_ = bf16[64,256]{1,0:T(8,128)(2,1)S(1)} collective-permute-done((bf16[64,256]{1,0:T(8,128)(2,1)S(1)}, bf16[64,256]{1,0:T(8,128)(2,1)S(1)}, u32[]{:S(2)}, u32[]{:S(2)}) %collective-permute-start.19) | collective-permute-done | bytes 32800 | tf_op jit(solution)/shard_map/ppermute | solution.py:326
  41.0 0.7 %blocks_of_own_core_in_place.1.refs_0_ = f32[256,512]{1,0:T(8,128)} custom-call(bf16[256,256]{1,0:T(8,128)(2,1)S(1)} %blocks_of_chips.1.blocks_ref), custom_call_target="tpu_custom_call" | custom-call | tf_op jit(solution)/shard_map/blocks_of_own_core_in_place/pallas_call | solution.py:33
  42.3 0.7 %blocks_of_sibling_core_in_place.1 = f32[256,512]{1,0:T(8,128)} custom-call(bf16[256,256]{1,0:T(8,128)(2,1)S(1)} %collective-permute-done.21.blocks_ref, f32[256,512]{1,0:T(8,128)} %blocks_of_own_core_in_place.1.refs_0_), custom_call_target="tpu_custom_call", output_to_operand_aliasing={{}: (1, {})} | custom-call | tf_op jit(solution)/shard_map/blocks_of_sibling_core_in_place/pallas_call | solution.py:33
  (27 shorter events, 3.2 us)
Async XLA Ops:
  0.6 9.7 %collective-permute-start.1 = (bf16[384,1024]{1,0:T(8,128)(2,1)}, bf16[384,1024]{1,0:T(8,128)(2,1)S(1)}, u32[]{:S(2)}, u32[]{:S(2)}) collective-permute-start(bf16[384,1024]{1,0:T(8,128)(2,1)} %bitcast.9), channel_id=1, source_target_pairs={{0,4},{4,0},{8,12},{12,8},{16,20},{20,16},{24,28},{28,24},{1,5},{5... | collective-permute-start | bytes 2359304 | tf_op jit(solution)/shard_map/ppermute | solution.py:314
  1.9 5.5 %collective-permute-start = (bf16[32,512]{1,0:T(8,128)(2,1)S(1)}, bf16[32,512]{1,0:T(8,128)(2,1)S(1)}, u32[]{:S(2)}, u32[]{:S(2)}) collective-permute-start(bf16[32,512]{1,0:T(8,128)(2,1)S(1)} %own_part_of_weight.1), channel_id=1, source_target_pairs={{0,6},{1,7},{2,4},{3,5},{4,2},{5,3},{6,0},{7,1},{8,14},{9,15},{10,... | collective-permute-start | bytes 98312 | tf_op jit(solution)/shard_map/ppermute | solution.py:326
  5.7 9.0 %collective-permute-start.6 = (bf16[256,512]{1,0:T(8,128)(2,1)}, bf16[256,512]{1,0:T(8,128)(2,1)S(1)}, u32[]{:S(2)}, u32[]{:S(2)}) collective-permute-start(bf16[256,512]{1,0:T(8,128)(2,1)} %refs_4_.1), channel_id=1, source_target_pairs={{0,5},{1,4},{2,7},{3,6},{4,3},{5,2},{6,1},{7,0},{8,13},{9,12},{10,... | collective-permute-start | bytes 786440 | tf_op jit(solution)/shard_map/ppermute | solution.py:326
  7.4 5.3 %collective-permute-start.4 = (bf16[32,512]{1,0:T(8,128)(2,1)S(1)}, bf16[32,512]{1,0:T(8,128)(2,1)S(1)}, u32[]{:S(2)}, u32[]{:S(2)}) collective-permute-start(bf16[32,512]{1,0:T(8,128)(2,1)S(1)} %collective-permute-done._.refs_0_), channel_id=1, source_target_pairs={{0,28},{1,29},{2,30},{3,31},{4,24},{5,25},{6,26},{7,27},{8,20},{9,... | collective-permute-start | bytes 98312 | tf_op jit(solution)/shard_map/ppermute | solution.py:326
  9.8 3.4 %collective-permute-start.3 = (bf16[32,512]{1,0:T(8,128)(2,1)S(1)}, bf16[32,512]{1,0:T(8,128)(2,1)S(1)}, u32[]{:S(2)}, u32[]{:S(2)}) collective-permute-start(bf16[32,512]{1,0:T(8,128)(2,1)S(1)} %collective-permute-done._.refs_0_), channel_id=1, source_target_pairs={{0,20},{1,21},{2,22},{3,23},{4,16},{5,17},{6,18},{7,19},{8,28},{9,... | collective-permute-start | bytes 98312 | tf_op jit(solution)/shard_map/ppermute | solution.py:326
  10.0 3.3 %collective-permute-start.2 = (bf16[32,512]{1,0:T(8,128)(2,1)S(1)}, bf16[32,512]{1,0:T(8,128)(2,1)S(1)}, u32[]{:S(2)}, u32[]{:S(2)}) collective-permute-start(bf16[32,512]{1,0:T(8,128)(2,1)S(1)} %collective-permute-done._.refs_0_), channel_id=1, source_target_pairs={{0,12},{1,13},{2,14},{3,15},{4,8},{5,9},{6,10},{7,11},{8,4},{9,5},... | collective-permute-start | bytes 98312 | tf_op jit(solution)/shard_map/ppermute | solution.py:326
  14.7 1.7 %collective-permute-start.7 = (bf16[256,512]{1,0:T(8,128)(2,1)S(1)}, bf16[256,512]{1,0:T(8,128)(2,1)S(1)}, u32[]{:S(2)}, u32[]{:S(2)}) collective-permute-start(bf16[256,512]{1,0:T(8,128)(2,1)S(1)} %collective-permute-done.6.refs_2_), channel_id=1, source_target_pairs={{0,4},{4,0},{8,12},{12,8},{16,20},{20,16},{24,28},{28,24},{1,5},{5... | collective-permute-start | bytes 786440 | tf_op jit(solution)/shard_map/ppermute | solution.py:314
  14.7 1.7 %collective-permute-start.5 = (bf16[128,512]{1,0:T(8,128)(2,1)S(1)}, bf16[128,512]{1,0:T(8,128)(2,1)S(1)}, u32[]{:S(2)}, u32[]{:S(2)}) collective-permute-start(bf16[128,512]{1,0:T(8,128)(2,1)S(1)} %parts_of_weight.1.refs_1_), channel_id=1, source_target_pairs={{0,4},{4,0},{8,12},{12,8},{16,20},{20,16},{24,28},{28,24},{1,5},{5... | collective-permute-start | bytes 393224 | tf_op jit(solution)/shard_map/ppermute | solution.py:314
  18.1 1.8 %collective-permute-start.8 = (bf16[384,512]{1,0:T(8,128)(2,1)S(1)}, bf16[384,512]{1,0:T(8,128)(2,1)S(1)}, u32[]{:S(2)}, u32[]{:S(2)}) collective-permute-start(bf16[384,512]{1,0:T(8,128)(2,1)S(1)} %get-tuple-element.55.grad_query_ref), channel_id=1, source_target_pairs={{0,4},{4,0},{8,12},{12,8},{16,20},{20,16},{24,28},{28,24},{1,5},{5... | collective-permute-start | bytes 1179656 | tf_op jit(solution)/shard_map/ppermute | solution.py:314
  20.2 6.1 %collective-permute-start.9 = (bf16[64,512]{1,0:T(8,128)(2,1)S(1)}, bf16[64,512]{1,0:T(8,128)(2,1)S(1)}, u32[]{:S(2)}, u32[]{:S(2)}) collective-permute-start(bf16[64,512]{1,0:T(8,128)(2,1)S(1)} %get-tuple-element.60), channel_id=1, source_target_pairs={{0,28},{1,29},{2,30},{3,31},{4,24},{5,25},{6,26},{7,27},{8,20},{9,... | collective-permute-start | bytes 196616 | tf_op jit(solution)/shard_map/ppermute | solution.py:326
  22.4 4.3 %collective-permute-start.10 = (bf16[64,512]{1,0:T(8,128)(2,1)S(1)}, bf16[64,512]{1,0:T(8,128)(2,1)S(1)}, u32[]{:S(2)}, u32[]{:S(2)}) collective-permute-start(bf16[64,512]{1,0:T(8,128)(2,1)S(1)} %get-tuple-element.61), channel_id=1, source_target_pairs={{0,20},{1,21},{2,22},{3,23},{4,16},{5,17},{6,18},{7,19},{8,28},{9,... | collective-permute-start | bytes 196616 | tf_op jit(solution)/shard_map/ppermute | solution.py:326
  22.9 4.1 %collective-permute-start.11 = (bf16[64,512]{1,0:T(8,128)(2,1)S(1)}, bf16[64,512]{1,0:T(8,128)(2,1)S(1)}, u32[]{:S(2)}, u32[]{:S(2)}) collective-permute-start(bf16[64,512]{1,0:T(8,128)(2,1)S(1)} %get-tuple-element.62), channel_id=1, source_target_pairs={{0,12},{1,13},{2,14},{3,15},{4,8},{5,9},{6,10},{7,11},{8,4},{9,5},... | collective-permute-start | bytes 196616 | tf_op jit(solution)/shard_map/ppermute | solution.py:326
  23.5 6.6 %collective-permute-start.12 = (bf16[64,512]{1,0:T(8,128)(2,1)S(1)}, bf16[64,512]{1,0:T(8,128)(2,1)S(1)}, u32[]{:S(2)}, u32[]{:S(2)}) collective-permute-start(bf16[64,512]{1,0:T(8,128)(2,1)S(1)} %get-tuple-element.67), channel_id=1, source_target_pairs={{0,28},{1,29},{2,30},{3,31},{4,24},{5,25},{6,26},{7,27},{8,20},{9,... | collective-permute-start | bytes 196616 | tf_op jit(solution)/shard_map/ppermute | solution.py:326
  26.0 5.0 %collective-permute-start.13 = (bf16[64,512]{1,0:T(8,128)(2,1)S(1)}, bf16[64,512]{1,0:T(8,128)(2,1)S(1)}, u32[]{:S(2)}, u32[]{:S(2)}) collective-permute-start(bf16[64,512]{1,0:T(8,128)(2,1)S(1)} %get-tuple-element.68), channel_id=1, source_target_pairs={{0,20},{1,21},{2,22},{3,23},{4,16},{5,17},{6,18},{7,19},{8,28},{9,... | collective-permute-start | bytes 196616 | tf_op jit(solution)/shard_map/ppermute | solution.py:326
  26.3 4.8 %collective-permute-start.14 = (bf16[64,512]{1,0:T(8,128)(2,1)S(1)}, bf16[64,512]{1,0:T(8,128)(2,1)S(1)}, u32[]{:S(2)}, u32[]{:S(2)}) collective-permute-start(bf16[64,512]{1,0:T(8,128)(2,1)S(1)} %get-tuple-element.69), channel_id=1, source_target_pairs={{0,12},{1,13},{2,14},{3,15},{4,8},{5,9},{6,10},{7,11},{8,4},{9,5},... | collective-permute-start | bytes 196616 | tf_op jit(solution)/shard_map/ppermute | solution.py:326
  27.0 6.7 %collective-permute-start.16 = (bf16[64,256]{1,0:T(8,128)(2,1)S(1)}, bf16[64,256]{1,0:T(8,128)(2,1)S(1)}, u32[]{:S(2)}, u32[]{:S(2)}) collective-permute-start(bf16[64,256]{1,0:T(8,128)(2,1)S(1)} %get-tuple-element.81), channel_id=1, source_target_pairs={{0,7},{1,6},{2,5},{3,4},{4,3},{5,2},{6,1},{7,0},{8,15},{9,14},{10,... | collective-permute-start | bytes 98312 | tf_op jit(solution)/shard_map/ppermute | solution.py:326
  30.1 4.3 %collective-permute-start.17 = (bf16[64,256]{1,0:T(8,128)(2,1)S(1)}, bf16[64,256]{1,0:T(8,128)(2,1)S(1)}, u32[]{:S(2)}, u32[]{:S(2)}) collective-permute-start(bf16[64,256]{1,0:T(8,128)(2,1)S(1)} %get-tuple-element.63._), channel_id=1, source_target_pairs={{0,6},{1,7},{2,4},{3,5},{4,2},{5,3},{6,0},{7,1},{8,14},{9,15},{10,... | collective-permute-start | bytes 98312 | tf_op jit(solution)/shard_map/ppermute | solution.py:326
  31.1 4.2 %collective-permute-start.15 = (bf16[64,256]{1,0:T(8,128)(2,1)S(1)}, bf16[64,256]{1,0:T(8,128)(2,1)S(1)}, u32[]{:S(2)}, u32[]{:S(2)}) collective-permute-start(bf16[64,256]{1,0:T(8,128)(2,1)S(1)} %get-tuple-element.70._), channel_id=1, source_target_pairs={{0,5},{1,4},{2,7},{3,6},{4,1},{5,0},{6,3},{7,2},{8,13},{9,12},{10,... | collective-permute-start | bytes 98312 | tf_op jit(solution)/shard_map/ppermute | solution.py:326
  35.3 4.4 %collective-permute-start.20 = (bf16[64,256]{1,0:T(8,128)(2,1)S(1)}, bf16[64,256]{1,0:T(8,128)(2,1)S(1)}, u32[]{:S(2)}, u32[]{:S(2)}) collective-permute-start(bf16[64,256]{1,0:T(8,128)(2,1)S(1)} %mean_over_shards.1._.refs_0_), channel_id=1, source_target_pairs={{0,28},{1,29},{2,30},{3,31},{4,24},{5,25},{6,26},{7,27},{8,20},{9,... | collective-permute-start | bytes 98312 | tf_op jit(solution)/shard_map/ppermute | solution.py:326
  36.3 4.3 %collective-permute-start.19 = (bf16[64,256]{1,0:T(8,128)(2,1)S(1)}, bf16[64,256]{1,0:T(8,128)(2,1)S(1)}, u32[]{:S(2)}, u32[]{:S(2)}) collective-permute-start(bf16[64,256]{1,0:T(8,128)(2,1)S(1)} %mean_over_shards.1._.refs_0_), channel_id=1, source_target_pairs={{0,20},{1,21},{2,22},{3,23},{4,16},{5,17},{6,18},{7,19},{8,28},{9,... | collective-permute-start | bytes 98312 | tf_op jit(solution)/shard_map/ppermute | solution.py:326
  37.4 3.4 %collective-permute-start.18 = (bf16[64,256]{1,0:T(8,128)(2,1)S(1)}, bf16[64,256]{1,0:T(8,128)(2,1)S(1)}, u32[]{:S(2)}, u32[]{:S(2)}) collective-permute-start(bf16[64,256]{1,0:T(8,128)(2,1)S(1)} %mean_over_shards.1._.refs_0_), channel_id=1, source_target_pairs={{0,12},{1,13},{2,14},{3,15},{4,8},{5,9},{6,10},{7,11},{8,4},{9,5},... | collective-permute-start | bytes 98312 | tf_op jit(solution)/shard_map/ppermute | solution.py:326
  40.8 1.4 %collective-permute-start.21 = (bf16[256,256]{1,0:T(8,128)(2,1)S(1)}, bf16[256,256]{1,0:T(8,128)(2,1)S(1)}, u32[]{:S(2)}, u32[]{:S(2)}) collective-permute-start(bf16[256,256]{1,0:T(8,128)(2,1)S(1)} %blocks_of_chips.1.blocks_ref), channel_id=1, source_target_pairs={{0,4},{4,0},{8,12},{12,8},{16,20},{20,16},{24,28},{28,24},{1,5},{5... | collective-permute-start | bytes 393224 | tf_op jit(solution)/shard_map/ppermute | solution.py:314

commit v11 on v10

--- a/solution.py
+++ b/solution.py
@@ -331,7 +331,7 @@
 
 
 def shard_pairs(fsdp_count):
-    others = [d for d in range(1, fsdp_count) if d != fsdp_count // 2]
+    others = range(1, fsdp_count - 1)
     return list(zip(others[::2], others[1::2]))
 
 
@@ -347,8 +347,7 @@
         [pltpu.SemaphoreType.DMA],
     )
     weight, part = lax.optimization_barrier((weight, part))
-    middle = (fsdp_count // 2,) * CORES
-    part = cross(part, dp_count, fsdp_count, 0, middle)
+    part = cross(part, dp_count, fsdp_count, 0, (fsdp_count - 1,) * CORES)
     wholes = [
         (cross(weight, dp_count, fsdp_count, 0, flips), flips[::-1])
         for flips in shard_pairs(fsdp_count)
@@ -378,7 +377,7 @@
             [ANYWHERE] + [NEAR] * len(parts),
             jax.ShapeDtypeStruct((len(parts) * rows, columns), part.dtype),
         )
-    held = [(part, (fsdp_count // 2,) * CORES, members)]
+    held = [(part, (fsdp_count - 1,) * CORES, members)]
     for block, flips in wholes:
         held.append((lax.optimization_barrier((block, part))[0], flips, [None]))
     moved = []

time: 43.2 us -> 44.3 us (1.025)
  waiting for transfers between devices: 10.1 us -> 13.3 us
  starting transfers between devices: 22.8 us -> 20.7 us
    ppermute x17, waiting for transfers between devices: 7.86 us -> 11.1 us  [cross(): return lax.ppermute(block, BOTH, pairs)]
    ppermute x17, starting transfers between devices: 21.4 us -> 19.3 us  [cross(): return lax.ppermute(block, BOTH, pairs)]
  transfers between devices with their start and end apart: 22 -> 22, of which waited for: 14 -> 15; matrix products, arithmetic and copies ran while one was open for 0% -> 0% of each run, Pallas kernels for 16% -> 15%
where the time goes in v11:
time: 44.3 us; the launch traced here: 44.1 us
  starting transfers between devices  20.7 us (47%)
  waiting for transfers between devices  13.3 us (30%)
  Pallas kernels  9.39 us (21%)
  between operations  0.75 us (2%)
    ppermute x17, starting transfers between devices, cross(): return lax.ppermute(block, BOTH, pairs)  19.3 us
    ppermute x17, waiting for transfers between devices, cross(): return lax.ppermute(block, BOTH, pairs)  11.1 us
    pallas_call x15, Pallas kernels, call(): pl.pallas_call(kernel, out_shape=out_shape, in_specs=in_specs, out_specs=...  9.39 us
    ppermute x5, waiting for transfers between devices, flip(): return lax.ppermute(block, axis, [(i, i ^ bits) for i in range(count)])  2.23 us
    ppermute x5, starting transfers between devices, flip(): return lax.ppermute(block, axis, [(i, i ^ bits) for i in range(count)])  1.4 us
  transfers between devices with their start and end apart: 22, of which 15 were waited for; matrix products, arithmetic and copies ran while one was open for 0% of the time, Pallas kernels for 15%

profile of v11, /device:TPU:0, one launch (start us, length us, event | category | flops | bytes accessed | tf_op | source)
XLA Modules:
  0.0 44.1 jit_solution(3679269960852100457)
XLA Ops:
  0.6 0.5 %collective-permute-start.1 = (bf16[384,1024]{1,0:T(8,128)(2,1)}, bf16[384,1024]{1,0:T(8,128)(2,1)S(1)}, u32[]{:S(2)}, u32[]{:S(2)}) collective-permute-start(bf16[384,1024]{1,0:T(8,128)(2,1)} %bitcast.9), channel_id=1, source_target_pairs={{0,4},{4,0},{8,12},{12,8},{16,20},{20,16},{24,28},{28,24},{1,5},{5... | collective-permute-start | bytes 2359304 | tf_op jit(solution)/shard_map/ppermute | solution.py:314
  1.1 0.8 %own_part_of_weight.1 = bf16[32,512]{1,0:T(8,128)(2,1)S(1)} custom-call(bf16[256,512]{1,0:T(8,128)(2,1)} %refs_4_.1), custom_call_target="tpu_custom_call" | custom-call | tf_op jit(solution)/shard_map/own_part_of_weight/pallas_call | solution.py:33
  1.9 4.8 %collective-permute-start = (bf16[32,512]{1,0:T(8,128)(2,1)S(1)}, bf16[32,512]{1,0:T(8,128)(2,1)S(1)}, u32[]{:S(2)}, u32[]{:S(2)}) collective-permute-start(bf16[32,512]{1,0:T(8,128)(2,1)S(1)} %own_part_of_weight.1), channel_id=1, source_target_pairs={{0,7},{1,6},{2,5},{3,4},{4,3},{5,2},{6,1},{7,0},{8,15},{9,14},{10,... | collective-permute-start | bytes 98312 | tf_op jit(solution)/shard_map/ppermute | solution.py:326
  6.7 1.8 %collective-permute-done._.refs_0_ = bf16[32,512]{1,0:T(8,128)(2,1)S(1)} collective-permute-done((bf16[32,512]{1,0:T(8,128)(2,1)S(1)}, bf16[32,512]{1,0:T(8,128)(2,1)S(1)}, u32[]{:S(2)}, u32[]{:S(2)}) %collective-permute-start) | collective-permute-done | bytes 32800 | tf_op jit(solution)/shard_map/ppermute | solution.py:326
  8.5 2.2 %collective-permute-start.4 = (bf16[32,512]{1,0:T(8,128)(2,1)S(1)}, bf16[32,512]{1,0:T(8,128)(2,1)S(1)}, u32[]{:S(2)}, u32[]{:S(2)}) collective-permute-start(bf16[32,512]{1,0:T(8,128)(2,1)S(1)} %collective-permute-done._.refs_0_), channel_id=1, source_target_pairs={{0,28},{1,29},{2,30},{3,31},{4,24},{5,25},{6,26},{7,27},{8,20},{9,... | collective-permute-start | bytes 98312 | tf_op jit(solution)/shard_map/ppermute | solution.py:326
  10.7 0.5 %collective-permute-start.3 = (bf16[32,512]{1,0:T(8,128)(2,1)S(1)}, bf16[32,512]{1,0:T(8,128)(2,1)S(1)}, u32[]{:S(2)}, u32[]{:S(2)}) collective-permute-start(bf16[32,512]{1,0:T(8,128)(2,1)S(1)} %collective-permute-done._.refs_0_), channel_id=1, source_target_pairs={{0,20},{1,21},{2,22},{3,23},{4,16},{5,17},{6,18},{7,19},{8,28},{9,... | collective-permute-start | bytes 98312 | tf_op jit(solution)/shard_map/ppermute | solution.py:326
  11.4 2.3 %prepared_operands.1 = (bf16[384,1024]{1,0:T(8,128)(2,1)S(1)}, bf16[384,512]{1,0:T(8,128)(2,1)S(1)}, bf16[384,512]{1,0:T(8,128)(2,1)S(1)}, bf16[384,512]{1,0:T(8...) custom-call(bf16[32,512]{1,0:T(8,128)(2,1)S(1)} %collective-permute-, ...), custom_call_target="tpu_custom_call" | custom-call | flops 5000000000 | tf_op jit(solution)/shard_map/prepared_operands/pallas_call | solution.py:33
  14.0 0.5 %collective-permute-done.2.refs_1_ = bf16[32,512]{1,0:T(8,128)(2,1)S(1)} collective-permute-done((bf16[32,512]{1,0:T(8,128)(2,1)S(1)}, bf16[32,512]{1,0:T(8,128)(2,1)S(1)}, u32[]{:S(2)}, u32[]{:S(2)}) %collective-permute-start.2) | collective-permute-done | bytes 32800 | tf_op jit(solution)/shard_map/ppermute | solution.py:326
  14.5 1.4 %collective-permute-done.6.refs_2_ = bf16[256,512]{1,0:T(8,128)(2,1)S(1)} collective-permute-done((bf16[256,512]{1,0:T(8,128)(2,1)}, bf16[256,512]{1,0:T(8,128)(2,1)S(1)}, u32[]{:S(2)}, u32[]{:S(2)}) %collective-permute-start.6) | collective-permute-done | bytes 262176 | tf_op jit(solution)/shard_map/ppermute | solution.py:326
  15.9 0.5 %collective-permute-start.5 = (bf16[128,512]{1,0:T(8,128)(2,1)S(1)}, bf16[128,512]{1,0:T(8,128)(2,1)S(1)}, u32[]{:S(2)}, u32[]{:S(2)}) collective-permute-start(bf16[128,512]{1,0:T(8,128)(2,1)S(1)} %parts_of_weight.1.refs_1_), channel_id=1, source_target_pairs={{0,4},{4,0},{8,12},{12,8},{16,20},{20,16},{24,28},{28,24},{1,5},{5... | collective-permute-start | bytes 393224 | tf_op jit(solution)/shard_map/ppermute | solution.py:314
  16.4 0.6 %projection_by_held_rows.1.refs_2_ = f32[384,512]{1,0:T(8,128)S(1)} custom-call(bf16[256,512]{1,0:T(8,128)(2,1)S(1)} %get-tuple-element.47.refs_0_, bf16[128,512]{1,0:T(8,128)(2,1)S(1)} %parts_of_weight.1.refs_1_, bf16[256,512]{1,0:T(8,128)(2,1)S(1)} %collective-permute-done.6.refs_2_, bf16[384,1024]{1,0:T(8,128)(2,1)S(1)} %get-tuple-element.48.refs_3_), custom_call_target="tpu_custom_call" | custom-call | flops 301989888 | bytes 786432 | tf_op jit(solution)/shard_map/projection_by_held_rows/pallas_call | solution.py:33
  17.0 0.6 %collective-permute-done.5.refs_0_ = bf16[128,512]{1,0:T(8,128)(2,1)S(1)} collective-permute-done((bf16[128,512]{1,0:T(8,128)(2,1)S(1)}, bf16[128,512]{1,0:T(8,128)(2,1)S(1)}, u32[]{:S(2)}, u32[]{:S(2)}) %collective-permute-start.5) | collective-permute-done | bytes 131104 | tf_op jit(solution)/shard_map/ppermute | solution.py:314
  17.6 1.6 %attention_to_grad_query.1 = (bf16[384,512]{1,0:T(8,128)(2,1)S(1)}, bf16[384,512]{1,0:T(8,128)(2,1)S(1)}, f32[384,512]{1,0:T(8,128)S(1)}, bf16[384,512]{1,0:T(8,...) custom-call(bf16[128,512]{1,0:T(8,128)(2,1)S(1)} %collective-permute-done.5.refs_0_, ...), custom_call_target="tpu_custom_call" | custom-call | flops 603979776 | bytes 4718592 | tf_op jit(solution)/shard_map/attention_to_grad_query/pallas_call | solution.py:33
  19.5 0.5 %weight_gradient_of_own_events.1 = (f32[512,256]{1,0:T(8,128)S(1)}, bf16[512,384]{1,0:T(8,128)(2,1)S(1)}, f32[512,256]{1,0:T(8,128)S(1)}, bf16[512,384]{1,0:T(8,128)(2,1)S(1)}) custom-call(bf16[1024,768]{1,0:T(8,128)(2,1)S(1)} %get-tuple-element.56.events_ref, bf16[384,512]{1,0:T(8,128)(2,1)S(1)} %get-tuple-element.55.grad_query_ref), custom_call_target="tpu_custom_call" | custom-call | flops 201326592 | bytes 3145728 | tf_op jit(solution)/shard_map/weight_gradient_of_own_events/pallas_call | solution.py:33
  20.0 1.1 %collective-permute-done.8._.grad_query_ref = bf16[384,512]{1,0:T(8,128)(2,1)S(1)} collective-permute-done((bf16[384,512]{1,0:T(8,128)(2,1)S(1)}, bf16[384,512]{1,0:T(8,128)(2,1)S(1)}, u32[]{:S(2)}, u32[]{:S(2)}) %collective-permute-start.8) | collective-permute-done | bytes 393248 | tf_op jit(solution)/shard_map/ppermute | solution.py:314
  21.3 2.3 %collective-permute-start.9 = (bf16[64,512]{1,0:T(8,128)(2,1)S(1)}, bf16[64,512]{1,0:T(8,128)(2,1)S(1)}, u32[]{:S(2)}, u32[]{:S(2)}) collective-permute-start(bf16[64,512]{1,0:T(8,128)(2,1)S(1)} %get-tuple-element.60), channel_id=1, source_target_pairs={{0,28},{1,29},{2,30},{3,31},{4,24},{5,25},{6,26},{7,27},{8,20},{9,... | collective-permute-start | bytes 196616 | tf_op jit(solution)/shard_map/ppermute | solution.py:326
  23.6 0.5 %collective-permute-start.10 = (bf16[64,512]{1,0:T(8,128)(2,1)S(1)}, bf16[64,512]{1,0:T(8,128)(2,1)S(1)}, u32[]{:S(2)}, u32[]{:S(2)}) collective-permute-start(bf16[64,512]{1,0:T(8,128)(2,1)S(1)} %get-tuple-element.61), channel_id=1, source_target_pairs={{0,20},{1,21},{2,22},{3,23},{4,16},{5,17},{6,18},{7,19},{8,28},{9,... | collective-permute-start | bytes 196616 | tf_op jit(solution)/shard_map/ppermute | solution.py:326
  24.7 2.5 %collective-permute-start.12 = (bf16[64,512]{1,0:T(8,128)(2,1)S(1)}, bf16[64,512]{1,0:T(8,128)(2,1)S(1)}, u32[]{:S(2)}, u32[]{:S(2)}) collective-permute-start(bf16[64,512]{1,0:T(8,128)(2,1)S(1)} %get-tuple-element.67), channel_id=1, source_target_pairs={{0,28},{1,29},{2,30},{3,31},{4,24},{5,25},{6,26},{7,27},{8,20},{9,... | collective-permute-start | bytes 196616 | tf_op jit(solution)/shard_map/ppermute | solution.py:326
  27.4 0.5 %collective-permute-start.14 = (bf16[64,512]{1,0:T(8,128)(2,1)S(1)}, bf16[64,512]{1,0:T(8,128)(2,1)S(1)}, u32[]{:S(2)}, u32[]{:S(2)}) collective-permute-start(bf16[64,512]{1,0:T(8,128)(2,1)S(1)} %get-tuple-element.69), channel_id=1, source_target_pairs={{0,12},{1,13},{2,14},{3,15},{4,8},{5,9},{6,10},{7,11},{8,4},{9,5},... | collective-permute-start | bytes 196616 | tf_op jit(solution)/shard_map/ppermute | solution.py:326
  28.2 2.3 %collective-permute-start.16 = (bf16[64,256]{1,0:T(8,128)(2,1)S(1)}, bf16[64,256]{1,0:T(8,128)(2,1)S(1)}, u32[]{:S(2)}, u32[]{:S(2)}) collective-permute-start(bf16[64,256]{1,0:T(8,128)(2,1)S(1)} %get-tuple-element.81), channel_id=1, source_target_pairs={{0,7},{1,6},{2,5},{3,4},{4,3},{5,2},{6,1},{7,0},{8,15},{9,14},{10,... | collective-permute-start | bytes 98312 | tf_op jit(solution)/shard_map/ppermute | solution.py:326
  30.5 1.7 %collective-permute-done.13.refs_2_ = bf16[64,512]{1,0:T(8,128)(2,1)S(1)} collective-permute-done((bf16[64,512]{1,0:T(8,128)(2,1)S(1)}, bf16[64,512]{1,0:T(8,128)(2,1)S(1)}, u32[]{:S(2)}, u32[]{:S(2)}) %collective-permute-start.13) | collective-permute-done | bytes 65568 | tf_op jit(solution)/shard_map/ppermute | solution.py:326
  32.3 1.4 %key_value_gate_gradients.1 = (bf16[384,512]{1,0:T(8,128)(2,1)}, bf16[384,512]{1,0:T(8,128)(2,1)}, bf16[384,512]{1,0:T(8,128)(2,1)}) custom-call(bf16[64,256]{1,0:T(8,128)(2,1)S(1)} %get-tuple-element.70._, bf16[384,512]{1,0:T(8,128)(2,1)S(1)} %get-tuple-element.71.query_ref, f32[384,512]{1,0:T(8,128)S(1)} %get-tuple-element.72.normed_ref, ...), custom_call_target="tpu_custom_call" | custom-call | flops 100663296 | bytes 2359296 | tf_op jit(solution)/shard_map/key_value_gate_gradients/pallas_call | solution.py:33
  33.8 1.0 %collective-permute-done.17.refs_3_ = bf16[64,256]{1,0:T(8,128)(2,1)S(1)} collective-permute-done((bf16[64,256]{1,0:T(8,128)(2,1)S(1)}, bf16[64,256]{1,0:T(8,128)(2,1)S(1)}, u32[]{:S(2)}, u32[]{:S(2)}) %collective-permute-start.17) | collective-permute-done | bytes 32800 | tf_op jit(solution)/shard_map/ppermute | solution.py:326
  34.8 0.9 %collective-permute-done.15.refs_1_ = bf16[64,256]{1,0:T(8,128)(2,1)S(1)} collective-permute-done((bf16[64,256]{1,0:T(8,128)(2,1)S(1)}, bf16[64,256]{1,0:T(8,128)(2,1)S(1)}, u32[]{:S(2)}, u32[]{:S(2)}) %collective-permute-start.15) | collective-permute-done | bytes 32800 | tf_op jit(solution)/shard_map/ppermute | solution.py:326
  35.7 1.5 %collective-permute-start.20 = (bf16[64,256]{1,0:T(8,128)(2,1)S(1)}, bf16[64,256]{1,0:T(8,128)(2,1)S(1)}, u32[]{:S(2)}, u32[]{:S(2)}) collective-permute-start(bf16[64,256]{1,0:T(8,128)(2,1)S(1)} %mean_over_shards.1._.refs_0_), channel_id=1, source_target_pairs={{0,28},{1,29},{2,30},{3,31},{4,24},{5,25},{6,26},{7,27},{8,20},{9,... | collective-permute-start | bytes 98312 | tf_op jit(solution)/shard_map/ppermute | solution.py:326
  37.2 1.3 %collective-permute-start.19 = (bf16[64,256]{1,0:T(8,128)(2,1)S(1)}, bf16[64,256]{1,0:T(8,128)(2,1)S(1)}, u32[]{:S(2)}, u32[]{:S(2)}) collective-permute-start(bf16[64,256]{1,0:T(8,128)(2,1)S(1)} %mean_over_shards.1._.refs_0_), channel_id=1, source_target_pairs={{0,20},{1,21},{2,22},{3,23},{4,16},{5,17},{6,18},{7,19},{8,28},{9,... | collective-permute-start | bytes 98312 | tf_op jit(solution)/shard_map/ppermute | solution.py:326
  38.8 1.3 %collective-permute-done.20.refs_3_ = bf16[64,256]{1,0:T(8,128)(2,1)S(1)} collective-permute-done((bf16[64,256]{1,0:T(8,128)(2,1)S(1)}, bf16[64,256]{1,0:T(8,128)(2,1)S(1)}, u32[]{:S(2)}, u32[]{:S(2)}) %collective-permute-start.20) | collective-permute-done | bytes 32800 | tf_op jit(solution)/shard_map/ppermute | solution.py:326
  40.1 0.7 %collective-permute-done.19.refs_2_ = bf16[64,256]{1,0:T(8,128)(2,1)S(1)} collective-permute-done((bf16[64,256]{1,0:T(8,128)(2,1)S(1)}, bf16[64,256]{1,0:T(8,128)(2,1)S(1)}, u32[]{:S(2)}, u32[]{:S(2)}) %collective-permute-start.19) | collective-permute-done | bytes 32800 | tf_op jit(solution)/shard_map/ppermute | solution.py:326
  40.8 1.2 %collective-permute-done.18.refs_1_ = bf16[64,256]{1,0:T(8,128)(2,1)S(1)} collective-permute-done((bf16[64,256]{1,0:T(8,128)(2,1)S(1)}, bf16[64,256]{1,0:T(8,128)(2,1)S(1)}, u32[]{:S(2)}, u32[]{:S(2)}) %collective-permute-start.18) | collective-permute-done | bytes 32800 | tf_op jit(solution)/shard_map/ppermute | solution.py:326
  42.1 0.7 %blocks_of_own_core_in_place.1.refs_0_ = f32[256,512]{1,0:T(8,128)} custom-call(bf16[256,256]{1,0:T(8,128)(2,1)S(1)} %blocks_of_chips.1.blocks_ref), custom_call_target="tpu_custom_call" | custom-call | tf_op jit(solution)/shard_map/blocks_of_own_core_in_place/pallas_call | solution.py:33
  42.9 0.5 %collective-permute-done.21.blocks_ref = bf16[256,256]{1,0:T(8,128)(2,1)S(1)} collective-permute-done((bf16[256,256]{1,0:T(8,128)(2,1)S(1)}, bf16[256,256]{1,0:T(8,128)(2,1)S(1)}, u32[]{:S(2)}, u32[]{:S(2)}) %collective-permute-start.21) | collective-permute-done | bytes 131104 | tf_op jit(solution)/shard_map/ppermute | solution.py:314
  43.4 0.7 %blocks_of_sibling_core_in_place.1 = f32[256,512]{1,0:T(8,128)} custom-call(bf16[256,256]{1,0:T(8,128)(2,1)S(1)} %collective-permute-done.21.blocks_ref, f32[256,512]{1,0:T(8,128)} %blocks_of_own_core_in_place.1.refs_0_), custom_call_target="tpu_custom_call", output_to_operand_aliasing={{}: (1, {})} | custom-call | tf_op jit(solution)/shard_map/blocks_of_sibling_core_in_place/pallas_call | solution.py:33
  (27 shorter events, 2.8 us)
Async XLA Ops:
  0.6 10.7 %collective-permute-start.1 = (bf16[384,1024]{1,0:T(8,128)(2,1)}, bf16[384,1024]{1,0:T(8,128)(2,1)S(1)}, u32[]{:S(2)}, u32[]{:S(2)}) collective-permute-start(bf16[384,1024]{1,0:T(8,128)(2,1)} %bitcast.9), channel_id=1, source_target_pairs={{0,4},{4,0},{8,12},{12,8},{16,20},{20,16},{24,28},{28,24},{1,5},{5... | collective-permute-start | bytes 2359304 | tf_op jit(solution)/shard_map/ppermute | solution.py:314
  1.9 6.6 %collective-permute-start = (bf16[32,512]{1,0:T(8,128)(2,1)S(1)}, bf16[32,512]{1,0:T(8,128)(2,1)S(1)}, u32[]{:S(2)}, u32[]{:S(2)}) collective-permute-start(bf16[32,512]{1,0:T(8,128)(2,1)S(1)} %own_part_of_weight.1), channel_id=1, source_target_pairs={{0,7},{1,6},{2,5},{3,4},{4,3},{5,2},{6,1},{7,0},{8,15},{9,14},{10,... | collective-permute-start | bytes 98312 | tf_op jit(solution)/shard_map/ppermute | solution.py:326
  6.7 9.2 %collective-permute-start.6 = (bf16[256,512]{1,0:T(8,128)(2,1)}, bf16[256,512]{1,0:T(8,128)(2,1)S(1)}, u32[]{:S(2)}, u32[]{:S(2)}) collective-permute-start(bf16[256,512]{1,0:T(8,128)(2,1)} %refs_4_.1), channel_id=1, source_target_pairs={{0,5},{1,4},{2,7},{3,6},{4,2},{5,3},{6,0},{7,1},{8,13},{9,12},{10,... | collective-permute-start | bytes 786440 | tf_op jit(solution)/shard_map/ppermute | solution.py:326
  8.5 5.2 %collective-permute-start.4 = (bf16[32,512]{1,0:T(8,128)(2,1)S(1)}, bf16[32,512]{1,0:T(8,128)(2,1)S(1)}, u32[]{:S(2)}, u32[]{:S(2)}) collective-permute-start(bf16[32,512]{1,0:T(8,128)(2,1)S(1)} %collective-permute-done._.refs_0_), channel_id=1, source_target_pairs={{0,28},{1,29},{2,30},{3,31},{4,24},{5,25},{6,26},{7,27},{8,20},{9,... | collective-permute-start | bytes 98312 | tf_op jit(solution)/shard_map/ppermute | solution.py:326
  10.7 3.4 %collective-permute-start.3 = (bf16[32,512]{1,0:T(8,128)(2,1)S(1)}, bf16[32,512]{1,0:T(8,128)(2,1)S(1)}, u32[]{:S(2)}, u32[]{:S(2)}) collective-permute-start(bf16[32,512]{1,0:T(8,128)(2,1)S(1)} %collective-permute-done._.refs_0_), channel_id=1, source_target_pairs={{0,20},{1,21},{2,22},{3,23},{4,16},{5,17},{6,18},{7,19},{8,28},{9,... | collective-permute-start | bytes 98312 | tf_op jit(solution)/shard_map/ppermute | solution.py:326
  11.2 3.3 %collective-permute-start.2 = (bf16[32,512]{1,0:T(8,128)(2,1)S(1)}, bf16[32,512]{1,0:T(8,128)(2,1)S(1)}, u32[]{:S(2)}, u32[]{:S(2)}) collective-permute-start(bf16[32,512]{1,0:T(8,128)(2,1)S(1)} %collective-permute-done._.refs_0_), channel_id=1, source_target_pairs={{0,12},{1,13},{2,14},{3,15},{4,8},{5,9},{6,10},{7,11},{8,4},{9,5},... | collective-permute-start | bytes 98312 | tf_op jit(solution)/shard_map/ppermute | solution.py:326
  15.9 1.7 %collective-permute-start.7 = (bf16[256,512]{1,0:T(8,128)(2,1)S(1)}, bf16[256,512]{1,0:T(8,128)(2,1)S(1)}, u32[]{:S(2)}, u32[]{:S(2)}) collective-permute-start(bf16[256,512]{1,0:T(8,128)(2,1)S(1)} %collective-permute-done.6.refs_2_), channel_id=1, source_target_pairs={{0,4},{4,0},{8,12},{12,8},{16,20},{20,16},{24,28},{28,24},{1,5},{5... | collective-permute-start | bytes 786440 | tf_op jit(solution)/shard_map/ppermute | solution.py:314
  15.9 1.7 %collective-permute-start.5 = (bf16[128,512]{1,0:T(8,128)(2,1)S(1)}, bf16[128,512]{1,0:T(8,128)(2,1)S(1)}, u32[]{:S(2)}, u32[]{:S(2)}) collective-permute-start(bf16[128,512]{1,0:T(8,128)(2,1)S(1)} %parts_of_weight.1.refs_1_), channel_id=1, source_target_pairs={{0,4},{4,0},{8,12},{12,8},{16,20},{20,16},{24,28},{28,24},{1,5},{5... | collective-permute-start | bytes 393224 | tf_op jit(solution)/shard_map/ppermute | solution.py:314
  19.3 1.8 %collective-permute-start.8 = (bf16[384,512]{1,0:T(8,128)(2,1)S(1)}, bf16[384,512]{1,0:T(8,128)(2,1)S(1)}, u32[]{:S(2)}, u32[]{:S(2)}) collective-permute-start(bf16[384,512]{1,0:T(8,128)(2,1)S(1)} %get-tuple-element.55.grad_query_ref), channel_id=1, source_target_pairs={{0,4},{4,0},{8,12},{12,8},{16,20},{20,16},{24,28},{28,24},{1,5},{5... | collective-permute-start | bytes 1179656 | tf_op jit(solution)/shard_map/ppermute | solution.py:314
  21.3 6.1 %collective-permute-start.9 = (bf16[64,512]{1,0:T(8,128)(2,1)S(1)}, bf16[64,512]{1,0:T(8,128)(2,1)S(1)}, u32[]{:S(2)}, u32[]{:S(2)}) collective-permute-start(bf16[64,512]{1,0:T(8,128)(2,1)S(1)} %get-tuple-element.60), channel_id=1, source_target_pairs={{0,28},{1,29},{2,30},{3,31},{4,24},{5,25},{6,26},{7,27},{8,20},{9,... | collective-permute-start | bytes 196616 | tf_op jit(solution)/shard_map/ppermute | solution.py:326
  23.6 4.3 %collective-permute-start.10 = (bf16[64,512]{1,0:T(8,128)(2,1)S(1)}, bf16[64,512]{1,0:T(8,128)(2,1)S(1)}, u32[]{:S(2)}, u32[]{:S(2)}) collective-permute-start(bf16[64,512]{1,0:T(8,128)(2,1)S(1)} %get-tuple-element.61), channel_id=1, source_target_pairs={{0,20},{1,21},{2,22},{3,23},{4,16},{5,17},{6,18},{7,19},{8,28},{9,... | collective-permute-start | bytes 196616 | tf_op jit(solution)/shard_map/ppermute | solution.py:326
  24.1 4.1 %collective-permute-start.11 = (bf16[64,512]{1,0:T(8,128)(2,1)S(1)}, bf16[64,512]{1,0:T(8,128)(2,1)S(1)}, u32[]{:S(2)}, u32[]{:S(2)}) collective-permute-start(bf16[64,512]{1,0:T(8,128)(2,1)S(1)} %get-tuple-element.62), channel_id=1, source_target_pairs={{0,12},{1,13},{2,14},{3,15},{4,8},{5,9},{6,10},{7,11},{8,4},{9,5},... | collective-permute-start | bytes 196616 | tf_op jit(solution)/shard_map/ppermute | solution.py:326
  24.7 5.8 %collective-permute-start.12 = (bf16[64,512]{1,0:T(8,128)(2,1)S(1)}, bf16[64,512]{1,0:T(8,128)(2,1)S(1)}, u32[]{:S(2)}, u32[]{:S(2)}) collective-permute-start(bf16[64,512]{1,0:T(8,128)(2,1)S(1)} %get-tuple-element.67), channel_id=1, source_target_pairs={{0,28},{1,29},{2,30},{3,31},{4,24},{5,25},{6,26},{7,27},{8,20},{9,... | collective-permute-start | bytes 196616 | tf_op jit(solution)/shard_map/ppermute | solution.py:326
  27.2 5.0 %collective-permute-start.13 = (bf16[64,512]{1,0:T(8,128)(2,1)S(1)}, bf16[64,512]{1,0:T(8,128)(2,1)S(1)}, u32[]{:S(2)}, u32[]{:S(2)}) collective-permute-start(bf16[64,512]{1,0:T(8,128)(2,1)S(1)} %get-tuple-element.68), channel_id=1, source_target_pairs={{0,20},{1,21},{2,22},{3,23},{4,16},{5,17},{6,18},{7,19},{8,28},{9,... | collective-permute-start | bytes 196616 | tf_op jit(solution)/shard_map/ppermute | solution.py:326
  27.4 4.8 %collective-permute-start.14 = (bf16[64,512]{1,0:T(8,128)(2,1)S(1)}, bf16[64,512]{1,0:T(8,128)(2,1)S(1)}, u32[]{:S(2)}, u32[]{:S(2)}) collective-permute-start(bf16[64,512]{1,0:T(8,128)(2,1)S(1)} %get-tuple-element.69), channel_id=1, source_target_pairs={{0,12},{1,13},{2,14},{3,15},{4,8},{5,9},{6,10},{7,11},{8,4},{9,5},... | collective-permute-start | bytes 196616 | tf_op jit(solution)/shard_map/ppermute | solution.py:326
  28.2 5.6 %collective-permute-start.16 = (bf16[64,256]{1,0:T(8,128)(2,1)S(1)}, bf16[64,256]{1,0:T(8,128)(2,1)S(1)}, u32[]{:S(2)}, u32[]{:S(2)}) collective-permute-start(bf16[64,256]{1,0:T(8,128)(2,1)S(1)} %get-tuple-element.81), channel_id=1, source_target_pairs={{0,7},{1,6},{2,5},{3,4},{4,3},{5,2},{6,1},{7,0},{8,15},{9,14},{10,... | collective-permute-start | bytes 98312 | tf_op jit(solution)/shard_map/ppermute | solution.py:326
  30.5 4.3 %collective-permute-start.17 = (bf16[64,256]{1,0:T(8,128)(2,1)S(1)}, bf16[64,256]{1,0:T(8,128)(2,1)S(1)}, u32[]{:S(2)}, u32[]{:S(2)}) collective-permute-start(bf16[64,256]{1,0:T(8,128)(2,1)S(1)} %get-tuple-element.63._), channel_id=1, source_target_pairs={{0,6},{1,7},{2,4},{3,5},{4,2},{5,3},{6,0},{7,1},{8,14},{9,15},{10,... | collective-permute-start | bytes 98312 | tf_op jit(solution)/shard_map/ppermute | solution.py:326
  32.2 3.5 %collective-permute-start.15 = (bf16[64,256]{1,0:T(8,128)(2,1)S(1)}, bf16[64,256]{1,0:T(8,128)(2,1)S(1)}, u32[]{:S(2)}, u32[]{:S(2)}) collective-permute-start(bf16[64,256]{1,0:T(8,128)(2,1)S(1)} %get-tuple-element.70._), channel_id=1, source_target_pairs={{0,5},{1,4},{2,7},{3,6},{4,1},{5,0},{6,3},{7,2},{8,13},{9,12},{10,... | collective-permute-start | bytes 98312 | tf_op jit(solution)/shard_map/ppermute | solution.py:326
  35.7 4.4 %collective-permute-start.20 = (bf16[64,256]{1,0:T(8,128)(2,1)S(1)}, bf16[64,256]{1,0:T(8,128)(2,1)S(1)}, u32[]{:S(2)}, u32[]{:S(2)}) collective-permute-start(bf16[64,256]{1,0:T(8,128)(2,1)S(1)} %mean_over_shards.1._.refs_0_), channel_id=1, source_target_pairs={{0,28},{1,29},{2,30},{3,31},{4,24},{5,25},{6,26},{7,27},{8,20},{9,... | collective-permute-start | bytes 98312 | tf_op jit(solution)/shard_map/ppermute | solution.py:326
  37.2 3.6 %collective-permute-start.19 = (bf16[64,256]{1,0:T(8,128)(2,1)S(1)}, bf16[64,256]{1,0:T(8,128)(2,1)S(1)}, u32[]{:S(2)}, u32[]{:S(2)}) collective-permute-start(bf16[64,256]{1,0:T(8,128)(2,1)S(1)} %mean_over_shards.1._.refs_0_), channel_id=1, source_target_pairs={{0,20},{1,21},{2,22},{3,23},{4,16},{5,17},{6,18},{7,19},{8,28},{9,... | collective-permute-start | bytes 98312 | tf_op jit(solution)/shard_map/ppermute | solution.py:326
  38.5 3.4 %collective-permute-start.18 = (bf16[64,256]{1,0:T(8,128)(2,1)S(1)}, bf16[64,256]{1,0:T(8,128)(2,1)S(1)}, u32[]{:S(2)}, u32[]{:S(2)}) collective-permute-start(bf16[64,256]{1,0:T(8,128)(2,1)S(1)} %mean_over_shards.1._.refs_0_), channel_id=1, source_target_pairs={{0,12},{1,13},{2,14},{3,15},{4,8},{5,9},{6,10},{7,11},{8,4},{9,5},... | collective-permute-start | bytes 98312 | tf_op jit(solution)/shard_map/ppermute | solution.py:326
  42.0 1.4 %collective-permute-start.21 = (bf16[256,256]{1,0:T(8,128)(2,1)S(1)}, bf16[256,256]{1,0:T(8,128)(2,1)S(1)}, u32[]{:S(2)}, u32[]{:S(2)}) collective-permute-start(bf16[256,256]{1,0:T(8,128)(2,1)S(1)} %blocks_of_chips.1.blocks_ref), channel_id=1, source_target_pairs={{0,4},{4,0},{8,12},{12,8},{16,20},{20,16},{24,28},{28,24},{1,5},{5... | collective-permute-start | bytes 393224 | tf_op jit(solution)/shard_map/ppermute | solution.py:314

commit v12 on v11

--- a/solution.py
+++ b/solution.py
@@ -62,12 +62,17 @@
     return jnp.sum(sum(blocks[1:], blocks[0]), axis=1, keepdims=True) / width
 
 
-def slice_kernel(group, block_ref, out_ref, sem):
-    rows = out_ref.shape[0]
-    start = pl.multiple_of(lax.rem(lax.axis_index("dp"), group) * rows, rows)
-    copy = pltpu.make_async_copy(block_ref.at[pl.ds(start, rows)], out_ref, sem)
-    copy.start()
-    copy.wait()
+def slice_kernel(block_ref, *refs):
+    outs, sems = refs[:-1], refs[-1]
+    copies = []
+    for i, out_ref in enumerate(outs):
+        rows = out_ref.shape[0]
+        member = lax.rem(lax.axis_index("dp"), block_ref.shape[0] // rows)
+        start = pl.multiple_of(member * rows, rows)
+        copies.append(pltpu.make_async_copy(block_ref.at[pl.ds(start, rows)], out_ref, sems.at[i]))
+        copies[i].start()
+    for copy in copies:
+        copy.wait()
 
 
 def prepare_kernel(slots, _, lengths_ref, sibling_ref, *refs):
@@ -105,45 +110,47 @@
         first_ref[place] = jnp.broadcast_to(first, (span, first_ref.shape[1]))
 
 
-def piece_start(shard_rows, group, part_rows, flips, member_flip):
-    device = lax.axis_index("dp")
-    start = (
-        lax.axis_index("fsdp") ^ jnp.where(lax.rem(device, CORES) == 0, flips[0], flips[1])
-    ) * shard_rows
+def piece_start(shard_rows, part_rows, shard_flip, member_flip):
+    start = (lax.axis_index("fsdp") ^ shard_flip) * shard_rows
     if member_flip is not None:
-        start = start + (lax.rem(device, group) ^ member_flip) * part_rows
+        member = lax.rem(lax.axis_index("dp"), shard_rows // part_rows) ^ member_flip
+        start = start + member * part_rows
     return pl.multiple_of(start, 16)
 
 
 def aligned(shard_rows):
-    return shard_rows % 128 == 0
-
-
-def project(events_ref, pieces, origins, group, shard_rows, spare_ref, sems):
+    return shard_rows % (CORES * 128) == 0
+
+
+def project(events_ref, pieces, origins, shard_rows, spare_ref, sems):
     copies, total = [], None
-    for piece, (flips, members) in zip(pieces, origins):
-        rows = piece.shape[0] // len(members)
-        starts = [piece_start(shard_rows, group, rows, flips, m) for m in members]
+    for piece, parts in zip(pieces, origins):
+        rows = piece.shape[0] // len(parts)
         if not aligned(shard_rows):
-            for i, start in enumerate(starts):
+            for i, part in enumerate(parts):
+                place = pl.ds(piece_start(shard_rows, rows, *part), rows)
                 copy = pltpu.make_async_copy(
-                    piece.at[pl.ds(i * rows, rows)],
-                    spare_ref.at[pl.ds(start, rows)],
-                    sems.at[len(copies)],
+                    piece.at[pl.ds(i * rows, rows)], spare_ref.at[place], sems.at[len(copies)]
                 )
                 copy.start()
                 copies.append(copy)
             continue
-        first = piece_start(shard_rows, group, rows, flips, None)
-        if len(members) > 1:
+        if rows % 128 == 0:
+            terms = [
+                (piece_start(shard_rows, rows, *part), piece.at[pl.ds(i * rows, rows)])
+                for i, part in enumerate(parts)
+            ]
+        else:
+            first = piece_start(shard_rows, shard_rows, parts[0][0], None)
             spare_ref[...] = jnp.zeros_like(spare_ref)
-            for i, start in enumerate(starts):
-                place = pl.ds(pl.multiple_of(start - first, 16), rows)
-                spare_ref[place] = piece[i * rows : (i + 1) * rows]
-            piece = spare_ref
-        columns = pl.ds(pl.multiple_of(first, 128), shard_rows)
-        term = dot(events_ref[:, columns], piece[...])
-        total = term if total is None else total + term
+            for i, part in enumerate(parts):
+                start = piece_start(shard_rows, rows, *part) - first
+                spare_ref[pl.ds(pl.multiple_of(start, 16), rows)] = piece[i * rows : (i + 1) * rows]
+            terms = [(first, spare_ref)]
+        for start, rows_ref in terms:
+            columns = pl.ds(pl.multiple_of(start, 128), rows_ref.shape[0])
+            term = dot(events_ref[:, columns], rows_ref[...])
+            total = term if total is None else total + term
     if copies:
         for copy in copies:
             copy.wait()
@@ -152,23 +159,23 @@
 
 
 def projection_scratch(shard_rows, model_width, width, origins):
-    count = sum(len(members) for _, members in origins)
+    count = sum(len(parts) for parts in origins)
     spare_rows = shard_rows if aligned(shard_rows) else model_width
     return [pltpu.VMEM((spare_rows, width), jnp.bfloat16), pltpu.SemaphoreType.DMA((count,))]
 
 
-def held_projection_kernel(group, shard_rows, origins, *refs):
+def held_projection_kernel(shard_rows, origins, *refs):
     pieces, (events_ref, out_ref, spare_ref, sems) = refs[: len(origins)], refs[len(origins) :]
-    out_ref[...] = project(events_ref, pieces, origins, group, shard_rows, spare_ref, sems)
-
-
-def attention_kernel(slots, group, shard_rows, origins, *refs):
+    out_ref[...] = project(events_ref, pieces, origins, shard_rows, spare_ref, sems)
+
+
+def attention_kernel(slots, shard_rows, origins, *refs):
     pieces = refs[: len(origins)]
     terms, refs = refs[len(origins) : -16], refs[-16:]
     (events_ref, key_ref, value_ref, key_t_ref, value_t_ref, weight_ref, gated_ref, first_ref,
      grad_query_ref, query_ref, normed_ref, mixed_grad_ref, attention_ref, scores_grad_ref,
      spare_ref, sems) = refs
-    query = project(events_ref, pieces, origins, group, shard_rows, spare_ref, sems)
+    query = project(events_ref, pieces, origins, shard_rows, spare_ref, sems)
     for term in terms:
         query = query + term[...]
     query_ref[...] = query.astype(jnp.bfloat16)
@@ -330,29 +337,28 @@
     return [send(k) for k in range(count - 1, 0, -1)][::-1]
 
 
-def shard_pairs(fsdp_count):
-    others = range(1, fsdp_count - 1)
-    return list(zip(others[::2], others[1::2]))
-
-
 def across_z(weight, dp_count, fsdp_count):
     rows = weight.shape[0]
     group = max(g for g in (2, 4, 8) if dp_count % g == 0 and rows % (16 * g) == 0)
-    part = call(
-        functools.partial(slice_kernel, group),
-        "own_part_of_weight",
+    part, half = call(
+        slice_kernel,
+        "own_parts_of_weight",
         [weight],
         [FAR],
-        jax.ShapeDtypeStruct((rows // group, weight.shape[1]), weight.dtype),
-        [pltpu.SemaphoreType.DMA],
-    )
-    weight, part = lax.optimization_barrier((weight, part))
-    part = cross(part, dp_count, fsdp_count, 0, (fsdp_count - 1,) * CORES)
-    wholes = [
-        (cross(weight, dp_count, fsdp_count, 0, flips), flips[::-1])
-        for flips in shard_pairs(fsdp_count)
+        tuple(
+            jax.ShapeDtypeStruct((rows // g, weight.shape[1]), weight.dtype)
+            for g in (group, CORES)
+        ),
+        [pltpu.SemaphoreType.DMA((2,))],
+    )
+    middle = fsdp_count // 2
+    part = cross(part, dp_count, fsdp_count, 0, (middle,) * CORES)
+    halves = [
+        (cross(half, dp_count, fsdp_count, 0, (z,) * CORES), z)
+        for z in range(1, fsdp_count)
+        if z != middle
     ]
-    return group, part, wholes
+    return group, part, halves
 
 
 def stack_kernel(_, *refs):
@@ -362,28 +368,33 @@
         out_ref[i * rows : (i + 1) * rows] = block_ref[...]
 
 
-def share(group, part, wholes, ready, dp_count, fsdp_count):
+def share(group, part, halves, ready, dp_count, fsdp_count):
     alike = (0,) * CORES
+    middle = fsdp_count // 2
     parts, members = [part], [1]
     for chip_bits in range(1, group // CORES):
         parts.append(cross(part, dp_count, fsdp_count, chip_bits, alike))
         members.append(CORES * chip_bits)
-    if len(parts) > 1:
-        rows, columns = part.shape
-        part = call(
+
+    def stacked(blocks, name, after):
+        if len(blocks) == 1:
+            return blocks[0]
+        rows, columns = blocks[0].shape
+        return call(
             stack_kernel,
-            "parts_of_weight",
-            [ready] + parts,
-            [ANYWHERE] + [NEAR] * len(parts),
-            jax.ShapeDtypeStruct((len(parts) * rows, columns), part.dtype),
+            name,
+            [after] + blocks,
+            [ANYWHERE] + [NEAR] * len(blocks),
+            jax.ShapeDtypeStruct((len(blocks) * rows, columns), part.dtype),
         )
-    held = [(part, (fsdp_count - 1,) * CORES, members)]
-    for block, flips in wholes:
-        held.append((lax.optimization_barrier((block, part))[0], flips, [None]))
-    moved = []
-    for block, flips, members in held:
-        places = [m if m is None else m ^ 1 for m in members]
-        moved.append((flip(block, "dp", dp_count, 1), flips[::-1], places))
+
+    part = stacked(parts, "parts_of_weight", ready)
+    halves, flips = zip(*halves)
+    half = stacked(list(halves), "halves_of_weight", part)
+    held = [(part, [(middle, m) for m in members]), (half, [(z, 1) for z in flips])]
+    moved = [
+        (flip(block, "dp", dp_count, 1), [(z, m ^ 1) for z, m in origin]) for block, origin in held
+    ]
     return held, moved
 
 
@@ -406,7 +417,7 @@
         a.reshape(rows, width) for a in (keys, values, gates, cotangent)
     )
     sibling_events = flip(flat_events, "dp", dp_count, 1)
-    group, part, wholes = across_z(query_weight, dp_count, fsdp_count)
+    group, part, halves = across_z(query_weight, dp_count, fsdp_count)
     prepared = call(
         functools.partial(prepare_kernel, slots),
         "prepared_operands",
@@ -435,20 +446,20 @@
     )
     near_events, near_keys, near_values, near_cotangent, near_weight = prepared[:5]
     events_t, keys_t, values_t, weight, gated, first = prepared[5:]
-    held, moved = share(group, part, wholes, first, dp_count, fsdp_count)
-    held = [(near_weight, (0, 0), [None])] + held
+    held, moved = share(group, part, halves, first, dp_count, fsdp_count)
+    held = [(near_weight, [(0, None)])] + held
     if not aligned(shard_rows):
         held, moved = [], held + moved
 
     def split(found):
-        return [f[0] for f in found], [f[1:] for f in found]
+        return [f[0] for f in found], [f[1] for f in found]
 
     terms = []
     if held:
         pieces, origins = split(held)
         terms = [
             call(
-                functools.partial(held_projection_kernel, group, shard_rows, origins),
+                functools.partial(held_projection_kernel, shard_rows, origins),
                 "projection_by_held_rows",
                 pieces + [near_events],
                 [NEAR] * (len(pieces) + 1),
@@ -461,7 +472,7 @@
     pieces, origins = split(moved)
     blocks = shape(slots * HEADS, span, span)
     grad_query, query, normed, grad_mixed, attention, grad_scores = call(
-        functools.partial(attention_kernel, slots, group, shard_rows, origins),
+        functools.partial(attention_kernel, slots, shard_rows, origins),
         "attention_to_grad_query",
         pieces
         + terms

time: 44.3 us -> 45.2 us (1.020)
  starting transfers between devices: 20.7 us -> 25.2 us
  waiting for transfers between devices: 13.3 us -> 9.22 us
  Pallas kernels: 9.39 us -> 9.85 us
    ppermute x17 -> x18, starting transfers between devices: 19.3 us -> 23.3 us  [cross(): return lax.ppermute(block, BOTH, pairs)]
    ppermute x17 -> x18, waiting for transfers between devices: 11.1 us -> 7.47 us  [cross(): return lax.ppermute(block, BOTH, pairs)]
    ppermute x5, waiting for transfers between devices: 2.23 us -> 1.75 us  [flip(): return lax.ppermute(block, axis, [(i, i ^ bits) for i in range(count)])]
    pallas_call x15 -> x16, Pallas kernels: 9.39 us -> 9.85 us  [call(): pl.pallas_call(kernel, out_shape=out_shape, in_specs=in_specs, out_specs=...]
  transfers between devices with their start and end apart: 22 -> 23, of which waited for: 15 -> 11; matrix products, arithmetic and copies ran while one was open for 0% -> 0% of each run, Pallas kernels for 15% -> 16%
where the time goes in v12:
time: 45.2 us; the launch traced here: 45 us
  starting transfers between devices  25.2 us (56%)
  Pallas kernels  9.85 us (22%)
  waiting for transfers between devices  9.22 us (20%)
  between operations  0.76 us (2%)
    ppermute x18, starting transfers between devices, cross(): return lax.ppermute(block, BOTH, pairs)  23.3 us
    pallas_call x16, Pallas kernels, call(): pl.pallas_call(kernel, out_shape=out_shape, in_specs=in_specs, out_specs=...  9.85 us
    ppermute x18, waiting for transfers between devices, cross(): return lax.ppermute(block, BOTH, pairs)  7.47 us
    ppermute x5, starting transfers between devices, flip(): return lax.ppermute(block, axis, [(i, i ^ bits) for i in range(count)])  1.84 us
    ppermute x5, waiting for transfers between devices, flip(): return lax.ppermute(block, axis, [(i, i ^ bits) for i in range(count)])  1.75 us
  transfers between devices with their start and end apart: 23, of which 11 were waited for; matrix products, arithmetic and copies ran while one was open for 0% of the time, Pallas kernels for 16%

profile of v12, /device:TPU:0, one launch (start us, length us, event | category | flops | bytes accessed | tf_op | source)
XLA Modules:
  0.0 45.0 jit_solution(4005234804903022101)
XLA Ops:
  0.6 0.5 %collective-permute-start.1 = (bf16[384,1024]{1,0:T(8,128)(2,1)}, bf16[384,1024]{1,0:T(8,128)(2,1)S(1)}, u32[]{:S(2)}, u32[]{:S(2)}) collective-permute-start(bf16[384,1024]{1,0:T(8,128)(2,1)} %bitcast.9), channel_id=1, source_target_pairs={{0,4},{4,0},{8,12},{12,8},{16,20},{20,16},{24,28},{28,24},{1,5},{5... | collective-permute-start | bytes 2359304 | tf_op jit(solution)/shard_map/ppermute | solution.py:321
  1.1 1.0 %own_parts_of_weight.1 = (bf16[32,512]{1,0:T(8,128)(2,1)S(1)}, bf16[128,512]{1,0:T(8,128)(2,1)S(1)}) custom-call(bf16[256,512]{1,0:T(8,128)(2,1)} %refs_4_.1), custom_call_target="tpu_custom_call" | custom-call | tf_op jit(solution)/shard_map/own_parts_of_weight/pallas_call | solution.py:33
  2.2 3.7 %collective-permute-start = (bf16[32,512]{1,0:T(8,128)(2,1)S(1)}, bf16[32,512]{1,0:T(8,128)(2,1)S(1)}, u32[]{:S(2)}, u32[]{:S(2)}) collective-permute-start(bf16[32,512]{1,0:T(8,128)(2,1)S(1)} %get-tuple-element.42), channel_id=1, source_target_pairs={{0,6},{1,7},{2,4},{3,5},{4,2},{5,3},{6,0},{7,1},{8,14},{9,15},{10,... | collective-permute-start | bytes 98312 | tf_op jit(solution)/shard_map/ppermute | solution.py:333
  5.9 1.1 %collective-permute-start.7 = (bf16[128,512]{1,0:T(8,128)(2,1)S(1)}, bf16[128,512]{1,0:T(8,128)(2,1)S(1)}, u32[]{:S(2)}, u32[]{:S(2)}) collective-permute-start(bf16[128,512]{1,0:T(8,128)(2,1)S(1)} %get-tuple-element.44), channel_id=1, source_target_pairs={{0,7},{1,6},{2,5},{3,4},{4,3},{5,2},{6,1},{7,0},{8,15},{9,14},{10,... | collective-permute-start | bytes 393224 | tf_op jit(solution)/shard_map/ppermute | solution.py:333
  7.1 0.4 collective-permute-done._.refs_0_
  7.5 2.5 %collective-permute-start.4 = (bf16[32,512]{1,0:T(8,128)(2,1)S(1)}, bf16[32,512]{1,0:T(8,128)(2,1)S(1)}, u32[]{:S(2)}, u32[]{:S(2)}) collective-permute-start(bf16[32,512]{1,0:T(8,128)(2,1)S(1)} %collective-permute-done._.refs_0_), channel_id=1, source_target_pairs={{0,28},{1,29},{2,30},{3,31},{4,24},{5,25},{6,26},{7,27},{8,20},{9,... | collective-permute-start | bytes 98312 | tf_op jit(solution)/shard_map/ppermute | solution.py:333
  10.5 2.3 %prepared_operands.1 = (bf16[384,1024]{1,0:T(8,128)(2,1)S(1)}, bf16[384,512]{1,0:T(8,128)(2,1)S(1)}, bf16[384,512]{1,0:T(8,128)(2,1)S(1)}, bf16[384,512]{1,0:T(8...) custom-call(bf16[32,512]{1,0:T(8,128)(2,1)S(1)} %collective-permute-, ...), custom_call_target="tpu_custom_call" | custom-call | flops 5000000000 | tf_op jit(solution)/shard_map/prepared_operands/pallas_call | solution.py:33
  12.8 0.7 %collective-permute-done.3.refs_2_ = bf16[32,512]{1,0:T(8,128)(2,1)S(1)} collective-permute-done((bf16[32,512]{1,0:T(8,128)(2,1)S(1)}, bf16[32,512]{1,0:T(8,128)(2,1)S(1)}, u32[]{:S(2)}, u32[]{:S(2)}) %collective-permute-start.3) | collective-permute-done | bytes 32800 | tf_op jit(solution)/shard_map/ppermute | solution.py:333
  13.5 1.6 %collective-permute-done.6.refs_0_ = bf16[128,512]{1,0:T(8,128)(2,1)S(1)} collective-permute-done((bf16[128,512]{1,0:T(8,128)(2,1)S(1)}, bf16[128,512]{1,0:T(8,128)(2,1)S(1)}, u32[]{:S(2)}, u32[]{:S(2)}) %collective-permute-start.6) | collective-permute-done | bytes 131104 | tf_op jit(solution)/shard_map/ppermute | solution.py:333
  15.1 0.4 collective-permute-start.8
  15.7 0.7 %projection_by_held_rows.1.refs_2_ = f32[384,512]{1,0:T(8,128)S(1)} custom-call(bf16[256,512]{1,0:T(8,128)(2,1)S(1)} %get-tuple-element.45.refs_0_, bf16[128,512]{1,0:T(8,128)(2,1)S(1)} %parts_of_weight.1._.refs_1_, bf16[256,512]{1,0:T(8,128)(2,1)S(1)} %halves_of_weight.1.refs_2_, bf16[384,1024]{1,0:T(8,128)(2,1)S(1)} %get-tuple-element.46.refs_3_), custom_call_target="tpu_custom_call" | custom-call | flops 301989888 | bytes 786432 | tf_op jit(solution)/shard_map/projection_by_held_rows/pallas_call | solution.py:33
  16.4 0.5 %collective-permute-done.5.refs_0_ = bf16[128,512]{1,0:T(8,128)(2,1)S(1)} collective-permute-done((bf16[128,512]{1,0:T(8,128)(2,1)S(1)}, bf16[128,512]{1,0:T(8,128)(2,1)S(1)}, u32[]{:S(2)}, u32[]{:S(2)}) %collective-permute-start.5) | collective-permute-done | bytes 131104 | tf_op jit(solution)/shard_map/ppermute | solution.py:321
  16.9 1.7 %attention_to_grad_query.1 = (bf16[384,512]{1,0:T(8,128)(2,1)S(1)}, bf16[384,512]{1,0:T(8,128)(2,1)S(1)}, f32[384,512]{1,0:T(8,128)S(1)}, bf16[384,512]{1,0:T(8,...) custom-call(bf16[128,512]{1,0:T(8,128)(2,1)S(1)} %collective-permute-done.5.refs_0_, ...), custom_call_target="tpu_custom_call" | custom-call | flops 603979776 | bytes 4718592 | tf_op jit(solution)/shard_map/attention_to_grad_query/pallas_call | solution.py:33
  18.7 0.4 collective-permute-start.9
  19.0 0.5 %weight_gradient_of_own_events.1 = (f32[512,256]{1,0:T(8,128)S(1)}, bf16[512,384]{1,0:T(8,128)(2,1)S(1)}, f32[512,256]{1,0:T(8,128)S(1)}, bf16[512,384]{1,0:T(8,128)(2,1)S(1)}) custom-call(bf16[1024,768]{1,0:T(8,128)(2,1)S(1)} %get-tuple-element.54.events_ref, bf16[384,512]{1,0:T(8,128)(2,1)S(1)} %get-tuple-element.53.grad_query_ref), custom_call_target="tpu_custom_call" | custom-call | flops 201326592 | bytes 3145728 | tf_op jit(solution)/shard_map/weight_gradient_of_own_events/pallas_call | solution.py:33
  19.5 0.9 %collective-permute-done.9._.grad_query_ref = bf16[384,512]{1,0:T(8,128)(2,1)S(1)} collective-permute-done((bf16[384,512]{1,0:T(8,128)(2,1)S(1)}, bf16[384,512]{1,0:T(8,128)(2,1)S(1)}, u32[]{:S(2)}, u32[]{:S(2)}) %collective-permute-start.9) | collective-permute-done | bytes 393248 | tf_op jit(solution)/shard_map/ppermute | solution.py:321
  20.7 2.5 %collective-permute-start.10 = (bf16[64,512]{1,0:T(8,128)(2,1)S(1)}, bf16[64,512]{1,0:T(8,128)(2,1)S(1)}, u32[]{:S(2)}, u32[]{:S(2)}) collective-permute-start(bf16[64,512]{1,0:T(8,128)(2,1)S(1)} %get-tuple-element.58), channel_id=1, source_target_pairs={{0,28},{1,29},{2,30},{3,31},{4,24},{5,25},{6,26},{7,27},{8,20},{9,... | collective-permute-start | bytes 196616 | tf_op jit(solution)/shard_map/ppermute | solution.py:333
  23.5 0.4 collective-permute-start.12
  24.2 2.4 %collective-permute-start.13 = (bf16[64,512]{1,0:T(8,128)(2,1)S(1)}, bf16[64,512]{1,0:T(8,128)(2,1)S(1)}, u32[]{:S(2)}, u32[]{:S(2)}) collective-permute-start(bf16[64,512]{1,0:T(8,128)(2,1)S(1)} %get-tuple-element.65), channel_id=1, source_target_pairs={{0,28},{1,29},{2,30},{3,31},{4,24},{5,25},{6,26},{7,27},{8,20},{9,... | collective-permute-start | bytes 196616 | tf_op jit(solution)/shard_map/ppermute | solution.py:333
  26.6 0.4 collective-permute-start.14
  27.0 0.4 collective-permute-start.15
  27.5 5.4 %collective-permute-start.17 = (bf16[64,256]{1,0:T(8,128)(2,1)S(1)}, bf16[64,256]{1,0:T(8,128)(2,1)S(1)}, u32[]{:S(2)}, u32[]{:S(2)}) collective-permute-start(bf16[64,256]{1,0:T(8,128)(2,1)S(1)} %get-tuple-element.79), channel_id=1, source_target_pairs={{0,7},{1,6},{2,5},{3,4},{4,3},{5,2},{6,1},{7,0},{8,15},{9,14},{10,... | collective-permute-start | bytes 98312 | tf_op jit(solution)/shard_map/ppermute | solution.py:333
  33.0 0.6 %collective-permute-start.16 = (bf16[64,256]{1,0:T(8,128)(2,1)S(1)}, bf16[64,256]{1,0:T(8,128)(2,1)S(1)}, u32[]{:S(2)}, u32[]{:S(2)}) collective-permute-start(bf16[64,256]{1,0:T(8,128)(2,1)S(1)} %get-tuple-element.68._), channel_id=1, source_target_pairs={{0,5},{1,4},{2,7},{3,6},{4,1},{5,0},{6,3},{7,2},{8,13},{9,12},{10,... | collective-permute-start | bytes 98312 | tf_op jit(solution)/shard_map/ppermute | solution.py:333
  33.6 1.4 %key_value_gate_gradients.1 = (bf16[384,512]{1,0:T(8,128)(2,1)}, bf16[384,512]{1,0:T(8,128)(2,1)}, bf16[384,512]{1,0:T(8,128)(2,1)}) custom-call(bf16[64,256]{1,0:T(8,128)(2,1)S(1)} %get-tuple-element.68._, bf16[384,512]{1,0:T(8,128)(2,1)S(1)} %get-tuple-element.69.query_ref, f32[384,512]{1,0:T(8,128)S(1)} %get-tuple-element.70.normed_ref, ...), custom_call_target="tpu_custom_call" | custom-call | flops 100663296 | bytes 2359296 | tf_op jit(solution)/shard_map/key_value_gate_gradients/pallas_call | solution.py:33
  35.0 2.2 %collective-permute-done.18.refs_3_ = bf16[64,256]{1,0:T(8,128)(2,1)S(1)} collective-permute-done((bf16[64,256]{1,0:T(8,128)(2,1)S(1)}, bf16[64,256]{1,0:T(8,128)(2,1)S(1)}, u32[]{:S(2)}, u32[]{:S(2)}) %collective-permute-start.18) | collective-permute-done | bytes 32800 | tf_op jit(solution)/shard_map/ppermute | solution.py:333
  37.3 1.9 %collective-permute-start.21 = (bf16[64,256]{1,0:T(8,128)(2,1)S(1)}, bf16[64,256]{1,0:T(8,128)(2,1)S(1)}, u32[]{:S(2)}, u32[]{:S(2)}) collective-permute-start(bf16[64,256]{1,0:T(8,128)(2,1)S(1)} %mean_over_shards.1._.refs_0_), channel_id=1, source_target_pairs={{0,28},{1,29},{2,30},{3,31},{4,24},{5,25},{6,26},{7,27},{8,20},{9,... | collective-permute-start | bytes 98312 | tf_op jit(solution)/shard_map/ppermute | solution.py:333
  39.5 0.9 %collective-permute-start.19 = (bf16[64,256]{1,0:T(8,128)(2,1)S(1)}, bf16[64,256]{1,0:T(8,128)(2,1)S(1)}, u32[]{:S(2)}, u32[]{:S(2)}) collective-permute-start(bf16[64,256]{1,0:T(8,128)(2,1)S(1)} %mean_over_shards.1._.refs_0_), channel_id=1, source_target_pairs={{0,12},{1,13},{2,14},{3,15},{4,8},{5,9},{6,10},{7,11},{8,4},{9,5},... | collective-permute-start | bytes 98312 | tf_op jit(solution)/shard_map/ppermute | solution.py:333
  40.4 1.2 %collective-permute-done.21.refs_3_ = bf16[64,256]{1,0:T(8,128)(2,1)S(1)} collective-permute-done((bf16[64,256]{1,0:T(8,128)(2,1)S(1)}, bf16[64,256]{1,0:T(8,128)(2,1)S(1)}, u32[]{:S(2)}, u32[]{:S(2)}) %collective-permute-start.21) | collective-permute-done | bytes 32800 | tf_op jit(solution)/shard_map/ppermute | solution.py:333
  41.6 0.9 %collective-permute-done.20.refs_2_ = bf16[64,256]{1,0:T(8,128)(2,1)S(1)} collective-permute-done((bf16[64,256]{1,0:T(8,128)(2,1)S(1)}, bf16[64,256]{1,0:T(8,128)(2,1)S(1)}, u32[]{:S(2)}, u32[]{:S(2)}) %collective-permute-start.20) | collective-permute-done | bytes 32800 | tf_op jit(solution)/shard_map/ppermute | solution.py:333
  42.8 0.4 collective-permute-start.22
  43.2 0.7 %blocks_of_own_core_in_place.1.refs_0_ = f32[256,512]{1,0:T(8,128)} custom-call(bf16[256,256]{1,0:T(8,128)(2,1)S(1)} %blocks_of_chips.1.blocks_ref), custom_call_target="tpu_custom_call" | custom-call | tf_op jit(solution)/shard_map/blocks_of_own_core_in_place/pallas_call | solution.py:33
  44.3 0.7 %blocks_of_sibling_core_in_place.1 = f32[256,512]{1,0:T(8,128)} custom-call(bf16[256,256]{1,0:T(8,128)(2,1)S(1)} %collective-permute-done.22.blocks_ref, f32[256,512]{1,0:T(8,128)} %blocks_of_own_core_in_place.1.refs_0_), custom_call_target="tpu_custom_call", output_to_operand_aliasing={{}: (1, {})} | custom-call | tf_op jit(solution)/shard_map/blocks_of_sibling_core_in_place/pallas_call | solution.py:33
  (30 shorter events, 3.0 us)
Async XLA Ops:
  0.6 9.5 %collective-permute-start.1 = (bf16[384,1024]{1,0:T(8,128)(2,1)}, bf16[384,1024]{1,0:T(8,128)(2,1)S(1)}, u32[]{:S(2)}, u32[]{:S(2)}) collective-permute-start(bf16[384,1024]{1,0:T(8,128)(2,1)} %bitcast.9), channel_id=1, source_target_pairs={{0,4},{4,0},{8,12},{12,8},{16,20},{20,16},{24,28},{28,24},{1,5},{5... | collective-permute-start | bytes 2359304 | tf_op jit(solution)/shard_map/ppermute | solution.py:321
  2.2 5.4 %collective-permute-start = (bf16[32,512]{1,0:T(8,128)(2,1)S(1)}, bf16[32,512]{1,0:T(8,128)(2,1)S(1)}, u32[]{:S(2)}, u32[]{:S(2)}) collective-permute-start(bf16[32,512]{1,0:T(8,128)(2,1)S(1)} %get-tuple-element.42), channel_id=1, source_target_pairs={{0,6},{1,7},{2,4},{3,5},{4,2},{5,3},{6,0},{7,1},{8,14},{9,15},{10,... | collective-permute-start | bytes 98312 | tf_op jit(solution)/shard_map/ppermute | solution.py:333
  5.9 7.6 %collective-permute-start.7 = (bf16[128,512]{1,0:T(8,128)(2,1)S(1)}, bf16[128,512]{1,0:T(8,128)(2,1)S(1)}, u32[]{:S(2)}, u32[]{:S(2)}) collective-permute-start(bf16[128,512]{1,0:T(8,128)(2,1)S(1)} %get-tuple-element.44), channel_id=1, source_target_pairs={{0,7},{1,6},{2,5},{3,4},{4,3},{5,2},{6,1},{7,0},{8,15},{9,14},{10,... | collective-permute-start | bytes 393224 | tf_op jit(solution)/shard_map/ppermute | solution.py:333
  7.0 8.2 %collective-permute-start.6 = (bf16[128,512]{1,0:T(8,128)(2,1)S(1)}, bf16[128,512]{1,0:T(8,128)(2,1)S(1)}, u32[]{:S(2)}, u32[]{:S(2)}) collective-permute-start(bf16[128,512]{1,0:T(8,128)(2,1)S(1)} %get-tuple-element.44), channel_id=1, source_target_pairs={{0,5},{1,4},{2,7},{3,6},{4,1},{5,0},{6,3},{7,2},{8,13},{9,12},{10,... | collective-permute-start | bytes 393224 | tf_op jit(solution)/shard_map/ppermute | solution.py:333
  7.5 5.3 %collective-permute-start.4 = (bf16[32,512]{1,0:T(8,128)(2,1)S(1)}, bf16[32,512]{1,0:T(8,128)(2,1)S(1)}, u32[]{:S(2)}, u32[]{:S(2)}) collective-permute-start(bf16[32,512]{1,0:T(8,128)(2,1)S(1)} %collective-permute-done._.refs_0_), channel_id=1, source_target_pairs={{0,28},{1,29},{2,30},{3,31},{4,24},{5,25},{6,26},{7,27},{8,20},{9,... | collective-permute-start | bytes 98312 | tf_op jit(solution)/shard_map/ppermute | solution.py:333
  10.0 3.4 %collective-permute-start.3 = (bf16[32,512]{1,0:T(8,128)(2,1)S(1)}, bf16[32,512]{1,0:T(8,128)(2,1)S(1)}, u32[]{:S(2)}, u32[]{:S(2)}) collective-permute-start(bf16[32,512]{1,0:T(8,128)(2,1)S(1)} %collective-permute-done._.refs_0_), channel_id=1, source_target_pairs={{0,20},{1,21},{2,22},{3,23},{4,16},{5,17},{6,18},{7,19},{8,28},{9,... | collective-permute-start | bytes 98312 | tf_op jit(solution)/shard_map/ppermute | solution.py:333
  10.2 3.3 %collective-permute-start.2 = (bf16[32,512]{1,0:T(8,128)(2,1)S(1)}, bf16[32,512]{1,0:T(8,128)(2,1)S(1)}, u32[]{:S(2)}, u32[]{:S(2)}) collective-permute-start(bf16[32,512]{1,0:T(8,128)(2,1)S(1)} %collective-permute-done._.refs_0_), channel_id=1, source_target_pairs={{0,12},{1,13},{2,14},{3,15},{4,8},{5,9},{6,10},{7,11},{8,4},{9,5},... | collective-permute-start | bytes 98312 | tf_op jit(solution)/shard_map/ppermute | solution.py:333
  15.1 1.8 %collective-permute-start.8 = (bf16[256,512]{1,0:T(8,128)(2,1)S(1)}, bf16[256,512]{1,0:T(8,128)(2,1)S(1)}, u32[]{:S(2)}, u32[]{:S(2)}) collective-permute-start(bf16[256,512]{1,0:T(8,128)(2,1)S(1)} %halves_of_weight.1.refs_2_), channel_id=1, source_target_pairs={{0,4},{4,0},{8,12},{12,8},{16,20},{20,16},{24,28},{28,24},{1,5},{5... | collective-permute-start | bytes 786440 | tf_op jit(solution)/shard_map/ppermute | solution.py:321
  15.5 1.4 %collective-permute-start.5 = (bf16[128,512]{1,0:T(8,128)(2,1)S(1)}, bf16[128,512]{1,0:T(8,128)(2,1)S(1)}, u32[]{:S(2)}, u32[]{:S(2)}) collective-permute-start(bf16[128,512]{1,0:T(8,128)(2,1)S(1)} %parts_of_weight.1._.refs_1_), channel_id=1, source_target_pairs={{0,4},{4,0},{8,12},{12,8},{16,20},{20,16},{24,28},{28,24},{1,5},{5... | collective-permute-start | bytes 393224 | tf_op jit(solution)/shard_map/ppermute | solution.py:321
  18.7 1.8 %collective-permute-start.9 = (bf16[384,512]{1,0:T(8,128)(2,1)S(1)}, bf16[384,512]{1,0:T(8,128)(2,1)S(1)}, u32[]{:S(2)}, u32[]{:S(2)}) collective-permute-start(bf16[384,512]{1,0:T(8,128)(2,1)S(1)} %get-tuple-element.53.grad_query_ref), channel_id=1, source_target_pairs={{0,4},{4,0},{8,12},{12,8},{16,20},{20,16},{24,28},{28,24},{1,5},{5... | collective-permute-start | bytes 1179656 | tf_op jit(solution)/shard_map/ppermute | solution.py:321
  20.7 6.2 %collective-permute-start.10 = (bf16[64,512]{1,0:T(8,128)(2,1)S(1)}, bf16[64,512]{1,0:T(8,128)(2,1)S(1)}, u32[]{:S(2)}, u32[]{:S(2)}) collective-permute-start(bf16[64,512]{1,0:T(8,128)(2,1)S(1)} %get-tuple-element.58), channel_id=1, source_target_pairs={{0,28},{1,29},{2,30},{3,31},{4,24},{5,25},{6,26},{7,27},{8,20},{9,... | collective-permute-start | bytes 196616 | tf_op jit(solution)/shard_map/ppermute | solution.py:333
  23.2 4.1 %collective-permute-start.11 = (bf16[64,512]{1,0:T(8,128)(2,1)S(1)}, bf16[64,512]{1,0:T(8,128)(2,1)S(1)}, u32[]{:S(2)}, u32[]{:S(2)}) collective-permute-start(bf16[64,512]{1,0:T(8,128)(2,1)S(1)} %get-tuple-element.59), channel_id=1, source_target_pairs={{0,20},{1,21},{2,22},{3,23},{4,16},{5,17},{6,18},{7,19},{8,28},{9,... | collective-permute-start | bytes 196616 | tf_op jit(solution)/shard_map/ppermute | solution.py:333
  23.5 4.0 %collective-permute-start.12 = (bf16[64,512]{1,0:T(8,128)(2,1)S(1)}, bf16[64,512]{1,0:T(8,128)(2,1)S(1)}, u32[]{:S(2)}, u32[]{:S(2)}) collective-permute-start(bf16[64,512]{1,0:T(8,128)(2,1)S(1)} %get-tuple-element.60), channel_id=1, source_target_pairs={{0,12},{1,13},{2,14},{3,15},{4,8},{5,9},{6,10},{7,11},{8,4},{9,5},... | collective-permute-start | bytes 196616 | tf_op jit(solution)/shard_map/ppermute | solution.py:333
  24.2 8.7 %collective-permute-start.13 = (bf16[64,512]{1,0:T(8,128)(2,1)S(1)}, bf16[64,512]{1,0:T(8,128)(2,1)S(1)}, u32[]{:S(2)}, u32[]{:S(2)}) collective-permute-start(bf16[64,512]{1,0:T(8,128)(2,1)S(1)} %get-tuple-element.65), channel_id=1, source_target_pairs={{0,28},{1,29},{2,30},{3,31},{4,24},{5,25},{6,26},{7,27},{8,20},{9,... | collective-permute-start | bytes 196616 | tf_op jit(solution)/shard_map/ppermute | solution.py:333
  26.6 6.3 %collective-permute-start.14 = (bf16[64,512]{1,0:T(8,128)(2,1)S(1)}, bf16[64,512]{1,0:T(8,128)(2,1)S(1)}, u32[]{:S(2)}, u32[]{:S(2)}) collective-permute-start(bf16[64,512]{1,0:T(8,128)(2,1)S(1)} %get-tuple-element.66), channel_id=1, source_target_pairs={{0,20},{1,21},{2,22},{3,23},{4,16},{5,17},{6,18},{7,19},{8,28},{9,... | collective-permute-start | bytes 196616 | tf_op jit(solution)/shard_map/ppermute | solution.py:333
  27.0 6.0 %collective-permute-start.15 = (bf16[64,512]{1,0:T(8,128)(2,1)S(1)}, bf16[64,512]{1,0:T(8,128)(2,1)S(1)}, u32[]{:S(2)}, u32[]{:S(2)}) collective-permute-start(bf16[64,512]{1,0:T(8,128)(2,1)S(1)} %get-tuple-element.67), channel_id=1, source_target_pairs={{0,12},{1,13},{2,14},{3,15},{4,8},{5,9},{6,10},{7,11},{8,4},{9,5},... | collective-permute-start | bytes 196616 | tf_op jit(solution)/shard_map/ppermute | solution.py:333
  27.5 7.5 %collective-permute-start.17 = (bf16[64,256]{1,0:T(8,128)(2,1)S(1)}, bf16[64,256]{1,0:T(8,128)(2,1)S(1)}, u32[]{:S(2)}, u32[]{:S(2)}) collective-permute-start(bf16[64,256]{1,0:T(8,128)(2,1)S(1)} %get-tuple-element.79), channel_id=1, source_target_pairs={{0,7},{1,6},{2,5},{3,4},{4,3},{5,2},{6,1},{7,0},{8,15},{9,14},{10,... | collective-permute-start | bytes 98312 | tf_op jit(solution)/shard_map/ppermute | solution.py:333
  32.9 4.3 %collective-permute-start.18 = (bf16[64,256]{1,0:T(8,128)(2,1)S(1)}, bf16[64,256]{1,0:T(8,128)(2,1)S(1)}, u32[]{:S(2)}, u32[]{:S(2)}) collective-permute-start(bf16[64,256]{1,0:T(8,128)(2,1)S(1)} %get-tuple-element.61._), channel_id=1, source_target_pairs={{0,6},{1,7},{2,4},{3,5},{4,2},{5,3},{6,0},{7,1},{8,14},{9,15},{10,... | collective-permute-start | bytes 98312 | tf_op jit(solution)/shard_map/ppermute | solution.py:333
  33.0 4.2 %collective-permute-start.16 = (bf16[64,256]{1,0:T(8,128)(2,1)S(1)}, bf16[64,256]{1,0:T(8,128)(2,1)S(1)}, u32[]{:S(2)}, u32[]{:S(2)}) collective-permute-start(bf16[64,256]{1,0:T(8,128)(2,1)S(1)} %get-tuple-element.68._), channel_id=1, source_target_pairs={{0,5},{1,4},{2,7},{3,6},{4,1},{5,0},{6,3},{7,2},{8,13},{9,12},{10,... | collective-permute-start | bytes 98312 | tf_op jit(solution)/shard_map/ppermute | solution.py:333
  37.3 4.3 %collective-permute-start.21 = (bf16[64,256]{1,0:T(8,128)(2,1)S(1)}, bf16[64,256]{1,0:T(8,128)(2,1)S(1)}, u32[]{:S(2)}, u32[]{:S(2)}) collective-permute-start(bf16[64,256]{1,0:T(8,128)(2,1)S(1)} %mean_over_shards.1._.refs_0_), channel_id=1, source_target_pairs={{0,28},{1,29},{2,30},{3,31},{4,24},{5,25},{6,26},{7,27},{8,20},{9,... | collective-permute-start | bytes 98312 | tf_op jit(solution)/shard_map/ppermute | solution.py:333
  39.2 3.3 %collective-permute-start.20 = (bf16[64,256]{1,0:T(8,128)(2,1)S(1)}, bf16[64,256]{1,0:T(8,128)(2,1)S(1)}, u32[]{:S(2)}, u32[]{:S(2)}) collective-permute-start(bf16[64,256]{1,0:T(8,128)(2,1)S(1)} %mean_over_shards.1._.refs_0_), channel_id=1, source_target_pairs={{0,20},{1,21},{2,22},{3,23},{4,16},{5,17},{6,18},{7,19},{8,28},{9,... | collective-permute-start | bytes 98312 | tf_op jit(solution)/shard_map/ppermute | solution.py:333
  39.5 3.3 %collective-permute-start.19 = (bf16[64,256]{1,0:T(8,128)(2,1)S(1)}, bf16[64,256]{1,0:T(8,128)(2,1)S(1)}, u32[]{:S(2)}, u32[]{:S(2)}) collective-permute-start(bf16[64,256]{1,0:T(8,128)(2,1)S(1)} %mean_over_shards.1._.refs_0_), channel_id=1, source_target_pairs={{0,12},{1,13},{2,14},{3,15},{4,8},{5,9},{6,10},{7,11},{8,4},{9,5},... | collective-permute-start | bytes 98312 | tf_op jit(solution)/shard_map/ppermute | solution.py:333
  42.8 1.4 %collective-permute-start.22 = (bf16[256,256]{1,0:T(8,128)(2,1)S(1)}, bf16[256,256]{1,0:T(8,128)(2,1)S(1)}, u32[]{:S(2)}, u32[]{:S(2)}) collective-permute-start(bf16[256,256]{1,0:T(8,128)(2,1)S(1)} %blocks_of_chips.1.blocks_ref), channel_id=1, source_target_pairs={{0,4},{4,0},{8,12},{12,8},{16,20},{20,16},{24,28},{28,24},{1,5},{5... | collective-permute-start | bytes 393224 | tf_op jit(solution)/shard_map/ppermute | solution.py:321

commit v13 on v10

--- a/solution.py
+++ b/solution.py
@@ -261,18 +261,22 @@
             term_ref[first:at] = dot(picked_ref[first:at], grad_query_ref[:, columns])
 
 
-def gradient_kernel(order, flips, _, term_ref, events_ref, grad_query_ref, *outs):
-    half = term_ref.shape[1]
-    part_rows = outs[0].shape[0]
-    out_of = dict(zip(order, outs))
-    at = 0
-    for side, picks in enumerate(gradient_picks(len(order), flips)):
-        rows = slice(at, at + len(picks) * part_rows)
-        total = term_ref[rows] + dot(events_ref[rows], grad_query_ref[:, half_columns(side, half)])
-        for p, (k, i, _) in enumerate(picks):
-            block = total[p * part_rows : (p + 1) * part_rows]
-            out_of[k][:, i * half : (i + 1) * half] = block.astype(out_of[k].dtype)
-        at = rows.stop
+def gradient_kernel(order, sets, grad_query_ref, *refs):
+    terms, outs = refs[: 2 * len(sets)], refs[2 * len(sets) :]
+    for which, flips in enumerate(sets):
+        term_ref, events_ref = terms[2 * which : 2 * which + 2]
+        out_of = dict(zip(order, outs[which * len(order) :]))
+        half = term_ref.shape[1]
+        part_rows = out_of[0].shape[0]
+        at = 0
+        for side, picks in enumerate(gradient_picks(len(order), flips)):
+            rows = slice(at, at + len(picks) * part_rows)
+            columns = half_columns(side, half)
+            total = term_ref[rows] + dot(events_ref[rows], grad_query_ref[:, columns])
+            for p, (k, i, _) in enumerate(picks):
+                block = total[p * part_rows : (p + 1) * part_rows]
+                out_of[k][:, i * half : (i + 1) * half] = block.astype(out_of[k].dtype)
+            at = rows.stop
 
 
 def chip_sum_kernel(term_count, _, *refs):
@@ -520,20 +524,20 @@
             moved=8 * model_width * rows,
         )
 
-        def gradient(which, name, after):
-            columns = len(sets[which]) * half_width
-            return call(
-                functools.partial(gradient_kernel, order, sets[which]),
-                name,
-                [after, *own_terms[2 * which : 2 * which + 2], got],
-                [ANYWHERE] + [NEAR] * 3,
-                tuple(shape(part_rows, columns, dtype=bf16 if k else f32) for k in order),
-                flops=2 * rows * picked_rows[which] * half_width,
-                moved=2 * picked_rows[which] * (rows + 2 * half_width),
-            )
-
-        far_terms = gradient(0, "weight_gradient_of_far_shards", got)
-        terms = gradient(1, "weight_gradient_of_near_shards", far_terms[0])
+        finished = call(
+            functools.partial(gradient_kernel, order, sets),
+            "weight_gradient_of_both_cores",
+            [got, *own_terms],
+            [NEAR] * (1 + len(own_terms)),
+            tuple(
+                shape(part_rows, len(flips) * half_width, dtype=bf16 if k else f32)
+                for flips in sets
+                for k in order
+            ),
+            flops=2 * rows * model_width * half_width,
+            moved=2 * model_width * (rows + 2 * half_width),
+        )
+        far_terms, terms = finished[:chips], finished[chips:]
 
         def to_shard(block, z):
             return cross(block, dp_count, fsdp_count, 0, (z,) * CORES)

time: 43.2 us -> 42.7 us (0.988)
  waiting for transfers between devices: 10.1 us -> 9.52 us
    pallas_call x15 -> x14, Pallas kernels: 9.37 us -> 9.23 us  [call(): pl.pallas_call(kernel, out_shape=out_shape, in_specs=in_specs, out_specs=...]
  transfers between devices with their start and end apart: 22 -> 22, of which waited for: 14 -> 13; matrix products, arithmetic and copies ran while one was open for 0% -> 0% of each run, Pallas kernels for 16% -> 15%
where the time goes in v13:
time: 42.7 us; the launch traced here: 42.5 us
  starting transfers between devices  23 us (54%)
  waiting for transfers between devices  9.52 us (22%)
  Pallas kernels  9.23 us (22%)
  between operations  0.73 us (2%)
    ppermute x17, starting transfers between devices, cross(): return lax.ppermute(block, BOTH, pairs)  21.3 us
    pallas_call x14, Pallas kernels, call(): pl.pallas_call(kernel, out_shape=out_shape, in_specs=in_specs, out_specs=...  9.23 us
    ppermute x17, waiting for transfers between devices, cross(): return lax.ppermute(block, BOTH, pairs)  7.52 us
    ppermute x5, waiting for transfers between devices, flip(): return lax.ppermute(block, axis, [(i, i ^ bits) for i in range(count)])  2 us
    ppermute x5, starting transfers between devices, flip(): return lax.ppermute(block, axis, [(i, i ^ bits) for i in range(count)])  1.65 us
  transfers between devices with their start and end apart: 22, of which 13 were waited for; matrix products, arithmetic and copies ran while one was open for 0% of the time, Pallas kernels for 15%

profile of v13, /device:TPU:0, one launch (start us, length us, event | category | flops | bytes accessed | tf_op | source)
XLA Modules:
  0.0 42.5 jit_solution(5622706548310869895)
XLA Ops:
  0.6 0.5 %collective-permute-start.1 = (bf16[384,1024]{1,0:T(8,128)(2,1)}, bf16[384,1024]{1,0:T(8,128)(2,1)S(1)}, u32[]{:S(2)}, u32[]{:S(2)}) collective-permute-start(bf16[384,1024]{1,0:T(8,128)(2,1)} %bitcast.9), channel_id=1, source_target_pairs={{0,4},{4,0},{8,12},{12,8},{16,20},{20,16},{24,28},{28,24},{1,5},{5... | collective-permute-start | bytes 2359304 | tf_op jit(solution)/shard_map/ppermute | solution.py:318
  1.1 0.8 %own_part_of_weight.1 = bf16[32,512]{1,0:T(8,128)(2,1)S(1)} custom-call(bf16[256,512]{1,0:T(8,128)(2,1)} %refs_4_.1), custom_call_target="tpu_custom_call" | custom-call | tf_op jit(solution)/shard_map/own_part_of_weight/pallas_call | solution.py:33
  1.9 3.8 %collective-permute-start = (bf16[32,512]{1,0:T(8,128)(2,1)S(1)}, bf16[32,512]{1,0:T(8,128)(2,1)S(1)}, u32[]{:S(2)}, u32[]{:S(2)}) collective-permute-start(bf16[32,512]{1,0:T(8,128)(2,1)S(1)} %own_part_of_weight.1), channel_id=1, source_target_pairs={{0,6},{1,7},{2,4},{3,5},{4,2},{5,3},{6,0},{7,1},{8,14},{9,15},{10,... | collective-permute-start | bytes 98312 | tf_op jit(solution)/shard_map/ppermute | solution.py:330
  5.7 1.2 %collective-permute-start.6 = (bf16[256,512]{1,0:T(8,128)(2,1)}, bf16[256,512]{1,0:T(8,128)(2,1)S(1)}, u32[]{:S(2)}, u32[]{:S(2)}) collective-permute-start(bf16[256,512]{1,0:T(8,128)(2,1)} %refs_4_.1), channel_id=1, source_target_pairs={{0,5},{1,4},{2,7},{3,6},{4,3},{5,2},{6,1},{7,0},{8,13},{9,12},{10,... | collective-permute-start | bytes 786440 | tf_op jit(solution)/shard_map/ppermute | solution.py:330
  6.9 0.5 %collective-permute-done._.refs_0_ = bf16[32,512]{1,0:T(8,128)(2,1)S(1)} collective-permute-done((bf16[32,512]{1,0:T(8,128)(2,1)S(1)}, bf16[32,512]{1,0:T(8,128)(2,1)S(1)}, u32[]{:S(2)}, u32[]{:S(2)}) %collective-permute-start) | collective-permute-done | bytes 32800 | tf_op jit(solution)/shard_map/ppermute | solution.py:330
  7.4 2.4 %collective-permute-start.4 = (bf16[32,512]{1,0:T(8,128)(2,1)S(1)}, bf16[32,512]{1,0:T(8,128)(2,1)S(1)}, u32[]{:S(2)}, u32[]{:S(2)}) collective-permute-start(bf16[32,512]{1,0:T(8,128)(2,1)S(1)} %collective-permute-done._.refs_0_), channel_id=1, source_target_pairs={{0,28},{1,29},{2,30},{3,31},{4,24},{5,25},{6,26},{7,27},{8,20},{9,... | collective-permute-start | bytes 98312 | tf_op jit(solution)/shard_map/ppermute | solution.py:330
  10.4 2.3 %prepared_operands.1 = (bf16[384,1024]{1,0:T(8,128)(2,1)S(1)}, bf16[384,512]{1,0:T(8,128)(2,1)S(1)}, bf16[384,512]{1,0:T(8,128)(2,1)S(1)}, bf16[384,512]{1,0:T(8...) custom-call(bf16[32,512]{1,0:T(8,128)(2,1)S(1)} %collective-permute-, ...), custom_call_target="tpu_custom_call" | custom-call | flops 5000000000 | tf_op jit(solution)/shard_map/prepared_operands/pallas_call | solution.py:33
  12.7 0.5 %collective-permute-done.3.refs_2_ = bf16[32,512]{1,0:T(8,128)(2,1)S(1)} collective-permute-done((bf16[32,512]{1,0:T(8,128)(2,1)S(1)}, bf16[32,512]{1,0:T(8,128)(2,1)S(1)}, u32[]{:S(2)}, u32[]{:S(2)}) %collective-permute-start.3) | collective-permute-done | bytes 32800 | tf_op jit(solution)/shard_map/ppermute | solution.py:330
  13.3 1.4 %collective-permute-done.6.refs_2_ = bf16[256,512]{1,0:T(8,128)(2,1)S(1)} collective-permute-done((bf16[256,512]{1,0:T(8,128)(2,1)}, bf16[256,512]{1,0:T(8,128)(2,1)S(1)}, u32[]{:S(2)}, u32[]{:S(2)}) %collective-permute-start.6) | collective-permute-done | bytes 262176 | tf_op jit(solution)/shard_map/ppermute | solution.py:330
  14.7 0.5 %collective-permute-start.5 = (bf16[128,512]{1,0:T(8,128)(2,1)S(1)}, bf16[128,512]{1,0:T(8,128)(2,1)S(1)}, u32[]{:S(2)}, u32[]{:S(2)}) collective-permute-start(bf16[128,512]{1,0:T(8,128)(2,1)S(1)} %parts_of_weight.1.refs_1_), channel_id=1, source_target_pairs={{0,4},{4,0},{8,12},{12,8},{16,20},{20,16},{24,28},{28,24},{1,5},{5... | collective-permute-start | bytes 393224 | tf_op jit(solution)/shard_map/ppermute | solution.py:318
  15.2 0.5 %projection_by_held_rows.1.refs_2_ = f32[384,512]{1,0:T(8,128)S(1)} custom-call(bf16[256,512]{1,0:T(8,128)(2,1)S(1)} %get-tuple-element.47.refs_0_, bf16[128,512]{1,0:T(8,128)(2,1)S(1)} %parts_of_weight.1.refs_1_, bf16[256,512]{1,0:T(8,128)(2,1)S(1)} %collective-permute-done.6.refs_2_, bf16[384,1024]{1,0:T(8,128)(2,1)S(1)} %get-tuple-element.48.refs_3_), custom_call_target="tpu_custom_call" | custom-call | flops 301989888 | bytes 786432 | tf_op jit(solution)/shard_map/projection_by_held_rows/pallas_call | solution.py:33
  15.8 0.7 %collective-permute-done.5.refs_0_ = bf16[128,512]{1,0:T(8,128)(2,1)S(1)} collective-permute-done((bf16[128,512]{1,0:T(8,128)(2,1)S(1)}, bf16[128,512]{1,0:T(8,128)(2,1)S(1)}, u32[]{:S(2)}, u32[]{:S(2)}) %collective-permute-start.5) | collective-permute-done | bytes 131104 | tf_op jit(solution)/shard_map/ppermute | solution.py:318
  16.4 1.6 %attention_to_grad_query.1 = (bf16[384,512]{1,0:T(8,128)(2,1)S(1)}, bf16[384,512]{1,0:T(8,128)(2,1)S(1)}, f32[384,512]{1,0:T(8,128)S(1)}, bf16[384,512]{1,0:T(8,...) custom-call(bf16[128,512]{1,0:T(8,128)(2,1)S(1)} %collective-permute-done.5.refs_0_, ...), custom_call_target="tpu_custom_call" | custom-call | flops 603979776 | bytes 4718592 | tf_op jit(solution)/shard_map/attention_to_grad_query/pallas_call | solution.py:33
  18.3 0.5 %weight_gradient_of_own_events.1 = (f32[512,256]{1,0:T(8,128)S(1)}, bf16[512,384]{1,0:T(8,128)(2,1)S(1)}, f32[512,256]{1,0:T(8,128)S(1)}, bf16[512,384]{1,0:T(8,128)(2,1)S(1)}) custom-call(bf16[1024,768]{1,0:T(8,128)(2,1)S(1)} %get-tuple-element.56.events_ref, bf16[384,512]{1,0:T(8,128)(2,1)S(1)} %get-tuple-element.55.grad_query_ref), custom_call_target="tpu_custom_call" | custom-call | flops 201326592 | bytes 3145728 | tf_op jit(solution)/shard_map/weight_gradient_of_own_events/pallas_call | solution.py:33
  18.8 1.1 %collective-permute-done.8.grad_query_ref._ = bf16[384,512]{1,0:T(8,128)(2,1)S(1)} collective-permute-done((bf16[384,512]{1,0:T(8,128)(2,1)S(1)}, bf16[384,512]{1,0:T(8,128)(2,1)S(1)}, u32[]{:S(2)}, u32[]{:S(2)}) %collective-permute-start.8) | collective-permute-done | bytes 393248 | tf_op jit(solution)/shard_map/ppermute | solution.py:318
  20.3 2.3 %collective-permute-start.9 = (bf16[64,512]{1,0:T(8,128)(2,1)S(1)}, bf16[64,512]{1,0:T(8,128)(2,1)S(1)}, u32[]{:S(2)}, u32[]{:S(2)}) collective-permute-start(bf16[64,512]{1,0:T(8,128)(2,1)S(1)} %get-tuple-element.62), channel_id=1, source_target_pairs={{0,28},{1,29},{2,30},{3,31},{4,24},{5,25},{6,26},{7,27},{8,20},{9,... | collective-permute-start | bytes 196616 | tf_op jit(solution)/shard_map/ppermute | solution.py:330
  22.6 0.5 %collective-permute-start.10 = (bf16[64,512]{1,0:T(8,128)(2,1)S(1)}, bf16[64,512]{1,0:T(8,128)(2,1)S(1)}, u32[]{:S(2)}, u32[]{:S(2)}) collective-permute-start(bf16[64,512]{1,0:T(8,128)(2,1)S(1)} %get-tuple-element.63), channel_id=1, source_target_pairs={{0,20},{1,21},{2,22},{3,23},{4,16},{5,17},{6,18},{7,19},{8,28},{9,... | collective-permute-start | bytes 196616 | tf_op jit(solution)/shard_map/ppermute | solution.py:330
  23.4 2.4 %collective-permute-start.12 = (bf16[64,512]{1,0:T(8,128)(2,1)S(1)}, bf16[64,512]{1,0:T(8,128)(2,1)S(1)}, u32[]{:S(2)}, u32[]{:S(2)}) collective-permute-start(bf16[64,512]{1,0:T(8,128)(2,1)S(1)} %get-tuple-element.67), channel_id=1, source_target_pairs={{0,28},{1,29},{2,30},{3,31},{4,24},{5,25},{6,26},{7,27},{8,20},{9,... | collective-permute-start | bytes 196616 | tf_op jit(solution)/shard_map/ppermute | solution.py:330
  26.0 0.7 %collective-permute-start.14 = (bf16[64,512]{1,0:T(8,128)(2,1)S(1)}, bf16[64,512]{1,0:T(8,128)(2,1)S(1)}, u32[]{:S(2)}, u32[]{:S(2)}) collective-permute-start(bf16[64,512]{1,0:T(8,128)(2,1)S(1)} %get-tuple-element.69), channel_id=1, source_target_pairs={{0,12},{1,13},{2,14},{3,15},{4,8},{5,9},{6,10},{7,11},{8,4},{9,5},... | collective-permute-start | bytes 196616 | tf_op jit(solution)/shard_map/ppermute | solution.py:330
  26.7 0.5 %collective-permute-done.11.refs_3_ = bf16[64,512]{1,0:T(8,128)(2,1)S(1)} collective-permute-done((bf16[64,512]{1,0:T(8,128)(2,1)S(1)}, bf16[64,512]{1,0:T(8,128)(2,1)S(1)}, u32[]{:S(2)}, u32[]{:S(2)}) %collective-permute-start.11) | collective-permute-done | bytes 65568 | tf_op jit(solution)/shard_map/ppermute | solution.py:330
  27.2 2.9 %collective-permute-start.16 = (bf16[64,256]{1,0:T(8,128)(2,1)S(1)}, bf16[64,256]{1,0:T(8,128)(2,1)S(1)}, u32[]{:S(2)}, u32[]{:S(2)}) collective-permute-start(bf16[64,256]{1,0:T(8,128)(2,1)S(1)} %get-tuple-element.81), channel_id=1, source_target_pairs={{0,7},{1,6},{2,5},{3,4},{4,3},{5,2},{6,1},{7,0},{8,15},{9,14},{10,... | collective-permute-start | bytes 98312 | tf_op jit(solution)/shard_map/ppermute | solution.py:330
  30.2 1.0 %collective-permute-done.13.refs_2_ = bf16[64,512]{1,0:T(8,128)(2,1)S(1)} collective-permute-done((bf16[64,512]{1,0:T(8,128)(2,1)S(1)}, bf16[64,512]{1,0:T(8,128)(2,1)S(1)}, u32[]{:S(2)}, u32[]{:S(2)}) %collective-permute-start.13) | collective-permute-done | bytes 65568 | tf_op jit(solution)/shard_map/ppermute | solution.py:330
  31.2 1.1 %collective-permute-start.15 = (bf16[64,256]{1,0:T(8,128)(2,1)S(1)}, bf16[64,256]{1,0:T(8,128)(2,1)S(1)}, u32[]{:S(2)}, u32[]{:S(2)}) collective-permute-start(bf16[64,256]{1,0:T(8,128)(2,1)S(1)} %get-tuple-element.70._), channel_id=1, source_target_pairs={{0,5},{1,4},{2,7},{3,6},{4,1},{5,0},{6,3},{7,2},{8,13},{9,12},{10,... | collective-permute-start | bytes 98312 | tf_op jit(solution)/shard_map/ppermute | solution.py:330
  32.4 1.4 %key_value_gate_gradients.1 = (bf16[384,512]{1,0:T(8,128)(2,1)}, bf16[384,512]{1,0:T(8,128)(2,1)}, bf16[384,512]{1,0:T(8,128)(2,1)}) custom-call(bf16[64,256]{1,0:T(8,128)(2,1)S(1)} %get-tuple-element.70._, bf16[384,512]{1,0:T(8,128)(2,1)S(1)} %get-tuple-element.71.query_ref, f32[384,512]{1,0:T(8,128)S(1)} %get-tuple-element.72.normed_ref, ...), custom_call_target="tpu_custom_call" | custom-call | flops 100663296 | bytes 2359296 | tf_op jit(solution)/shard_map/key_value_gate_gradients/pallas_call | solution.py:33
  33.8 0.6 %collective-permute-done.17.refs_3_ = bf16[64,256]{1,0:T(8,128)(2,1)S(1)} collective-permute-done((bf16[64,256]{1,0:T(8,128)(2,1)S(1)}, bf16[64,256]{1,0:T(8,128)(2,1)S(1)}, u32[]{:S(2)}, u32[]{:S(2)}) %collective-permute-start.17) | collective-permute-done | bytes 32800 | tf_op jit(solution)/shard_map/ppermute | solution.py:330
  34.4 0.9 %collective-permute-done.15.refs_1_ = bf16[64,256]{1,0:T(8,128)(2,1)S(1)} collective-permute-done((bf16[64,256]{1,0:T(8,128)(2,1)S(1)}, bf16[64,256]{1,0:T(8,128)(2,1)S(1)}, u32[]{:S(2)}, u32[]{:S(2)}) %collective-permute-start.15) | collective-permute-done | bytes 32800 | tf_op jit(solution)/shard_map/ppermute | solution.py:330
  35.3 1.4 %collective-permute-start.20 = (bf16[64,256]{1,0:T(8,128)(2,1)S(1)}, bf16[64,256]{1,0:T(8,128)(2,1)S(1)}, u32[]{:S(2)}, u32[]{:S(2)}) collective-permute-start(bf16[64,256]{1,0:T(8,128)(2,1)S(1)} %mean_over_shards.1._.refs_0_), channel_id=1, source_target_pairs={{0,28},{1,29},{2,30},{3,31},{4,24},{5,25},{6,26},{7,27},{8,20},{9,... | collective-permute-start | bytes 98312 | tf_op jit(solution)/shard_map/ppermute | solution.py:330
  36.9 1.4 %collective-permute-start.18 = (bf16[64,256]{1,0:T(8,128)(2,1)S(1)}, bf16[64,256]{1,0:T(8,128)(2,1)S(1)}, u32[]{:S(2)}, u32[]{:S(2)}) collective-permute-start(bf16[64,256]{1,0:T(8,128)(2,1)S(1)} %mean_over_shards.1._.refs_0_), channel_id=1, source_target_pairs={{0,12},{1,13},{2,14},{3,15},{4,8},{5,9},{6,10},{7,11},{8,4},{9,5},... | collective-permute-start | bytes 98312 | tf_op jit(solution)/shard_map/ppermute | solution.py:330
  38.3 1.4 %collective-permute-done.20.refs_3_ = bf16[64,256]{1,0:T(8,128)(2,1)S(1)} collective-permute-done((bf16[64,256]{1,0:T(8,128)(2,1)S(1)}, bf16[64,256]{1,0:T(8,128)(2,1)S(1)}, u32[]{:S(2)}, u32[]{:S(2)}) %collective-permute-start.20) | collective-permute-done | bytes 32800 | tf_op jit(solution)/shard_map/ppermute | solution.py:330
  39.6 0.6 %collective-permute-done.19.refs_2_ = bf16[64,256]{1,0:T(8,128)(2,1)S(1)} collective-permute-done((bf16[64,256]{1,0:T(8,128)(2,1)S(1)}, bf16[64,256]{1,0:T(8,128)(2,1)S(1)}, u32[]{:S(2)}, u32[]{:S(2)}) %collective-permute-start.19) | collective-permute-done | bytes 32800 | tf_op jit(solution)/shard_map/ppermute | solution.py:330
  40.7 0.7 %blocks_of_own_core_in_place.1.refs_0_ = f32[256,512]{1,0:T(8,128)} custom-call(bf16[256,256]{1,0:T(8,128)(2,1)S(1)} %blocks_of_chips.1.blocks_ref), custom_call_target="tpu_custom_call" | custom-call | tf_op jit(solution)/shard_map/blocks_of_own_core_in_place/pallas_call | solution.py:33
  41.7 0.7 %blocks_of_sibling_core_in_place.1 = f32[256,512]{1,0:T(8,128)} custom-call(bf16[256,256]{1,0:T(8,128)(2,1)S(1)} %collective-permute-done.21.blocks_ref, f32[256,512]{1,0:T(8,128)} %blocks_of_own_core_in_place.1.refs_0_), custom_call_target="tpu_custom_call", output_to_operand_aliasing={{}: (1, {})} | custom-call | tf_op jit(solution)/shard_map/blocks_of_sibling_core_in_place/pallas_call | solution.py:33
  (26 shorter events, 2.8 us)
Async XLA Ops:
  0.6 9.7 %collective-permute-start.1 = (bf16[384,1024]{1,0:T(8,128)(2,1)}, bf16[384,1024]{1,0:T(8,128)(2,1)S(1)}, u32[]{:S(2)}, u32[]{:S(2)}) collective-permute-start(bf16[384,1024]{1,0:T(8,128)(2,1)} %bitcast.9), channel_id=1, source_target_pairs={{0,4},{4,0},{8,12},{12,8},{16,20},{20,16},{24,28},{28,24},{1,5},{5... | collective-permute-start | bytes 2359304 | tf_op jit(solution)/shard_map/ppermute | solution.py:318
  1.9 5.5 %collective-permute-start = (bf16[32,512]{1,0:T(8,128)(2,1)S(1)}, bf16[32,512]{1,0:T(8,128)(2,1)S(1)}, u32[]{:S(2)}, u32[]{:S(2)}) collective-permute-start(bf16[32,512]{1,0:T(8,128)(2,1)S(1)} %own_part_of_weight.1), channel_id=1, source_target_pairs={{0,6},{1,7},{2,4},{3,5},{4,2},{5,3},{6,0},{7,1},{8,14},{9,15},{10,... | collective-permute-start | bytes 98312 | tf_op jit(solution)/shard_map/ppermute | solution.py:330
  5.7 9.0 %collective-permute-start.6 = (bf16[256,512]{1,0:T(8,128)(2,1)}, bf16[256,512]{1,0:T(8,128)(2,1)S(1)}, u32[]{:S(2)}, u32[]{:S(2)}) collective-permute-start(bf16[256,512]{1,0:T(8,128)(2,1)} %refs_4_.1), channel_id=1, source_target_pairs={{0,5},{1,4},{2,7},{3,6},{4,3},{5,2},{6,1},{7,0},{8,13},{9,12},{10,... | collective-permute-start | bytes 786440 | tf_op jit(solution)/shard_map/ppermute | solution.py:330
  7.4 5.3 %collective-permute-start.4 = (bf16[32,512]{1,0:T(8,128)(2,1)S(1)}, bf16[32,512]{1,0:T(8,128)(2,1)S(1)}, u32[]{:S(2)}, u32[]{:S(2)}) collective-permute-start(bf16[32,512]{1,0:T(8,128)(2,1)S(1)} %collective-permute-done._.refs_0_), channel_id=1, source_target_pairs={{0,28},{1,29},{2,30},{3,31},{4,24},{5,25},{6,26},{7,27},{8,20},{9,... | collective-permute-start | bytes 98312 | tf_op jit(solution)/shard_map/ppermute | solution.py:330
  9.8 3.4 %collective-permute-start.3 = (bf16[32,512]{1,0:T(8,128)(2,1)S(1)}, bf16[32,512]{1,0:T(8,128)(2,1)S(1)}, u32[]{:S(2)}, u32[]{:S(2)}) collective-permute-start(bf16[32,512]{1,0:T(8,128)(2,1)S(1)} %collective-permute-done._.refs_0_), channel_id=1, source_target_pairs={{0,20},{1,21},{2,22},{3,23},{4,16},{5,17},{6,18},{7,19},{8,28},{9,... | collective-permute-start | bytes 98312 | tf_op jit(solution)/shard_map/ppermute | solution.py:330
  10.0 3.3 %collective-permute-start.2 = (bf16[32,512]{1,0:T(8,128)(2,1)S(1)}, bf16[32,512]{1,0:T(8,128)(2,1)S(1)}, u32[]{:S(2)}, u32[]{:S(2)}) collective-permute-start(bf16[32,512]{1,0:T(8,128)(2,1)S(1)} %collective-permute-done._.refs_0_), channel_id=1, source_target_pairs={{0,12},{1,13},{2,14},{3,15},{4,8},{5,9},{6,10},{7,11},{8,4},{9,5},... | collective-permute-start | bytes 98312 | tf_op jit(solution)/shard_map/ppermute | solution.py:330
  14.7 1.7 %collective-permute-start.7 = (bf16[256,512]{1,0:T(8,128)(2,1)S(1)}, bf16[256,512]{1,0:T(8,128)(2,1)S(1)}, u32[]{:S(2)}, u32[]{:S(2)}) collective-permute-start(bf16[256,512]{1,0:T(8,128)(2,1)S(1)} %collective-permute-done.6.refs_2_), channel_id=1, source_target_pairs={{0,4},{4,0},{8,12},{12,8},{16,20},{20,16},{24,28},{28,24},{1,5},{5... | collective-permute-start | bytes 786440 | tf_op jit(solution)/shard_map/ppermute | solution.py:318
  14.7 1.7 %collective-permute-start.5 = (bf16[128,512]{1,0:T(8,128)(2,1)S(1)}, bf16[128,512]{1,0:T(8,128)(2,1)S(1)}, u32[]{:S(2)}, u32[]{:S(2)}) collective-permute-start(bf16[128,512]{1,0:T(8,128)(2,1)S(1)} %parts_of_weight.1.refs_1_), channel_id=1, source_target_pairs={{0,4},{4,0},{8,12},{12,8},{16,20},{20,16},{24,28},{28,24},{1,5},{5... | collective-permute-start | bytes 393224 | tf_op jit(solution)/shard_map/ppermute | solution.py:318
  18.1 1.8 %collective-permute-start.8 = (bf16[384,512]{1,0:T(8,128)(2,1)S(1)}, bf16[384,512]{1,0:T(8,128)(2,1)S(1)}, u32[]{:S(2)}, u32[]{:S(2)}) collective-permute-start(bf16[384,512]{1,0:T(8,128)(2,1)S(1)} %get-tuple-element.55.grad_query_ref), channel_id=1, source_target_pairs={{0,4},{4,0},{8,12},{12,8},{16,20},{20,16},{24,28},{28,24},{1,5},{5... | collective-permute-start | bytes 1179656 | tf_op jit(solution)/shard_map/ppermute | solution.py:318
  20.3 5.7 %collective-permute-start.9 = (bf16[64,512]{1,0:T(8,128)(2,1)S(1)}, bf16[64,512]{1,0:T(8,128)(2,1)S(1)}, u32[]{:S(2)}, u32[]{:S(2)}) collective-permute-start(bf16[64,512]{1,0:T(8,128)(2,1)S(1)} %get-tuple-element.62), channel_id=1, source_target_pairs={{0,28},{1,29},{2,30},{3,31},{4,24},{5,25},{6,26},{7,27},{8,20},{9,... | collective-permute-start | bytes 196616 | tf_op jit(solution)/shard_map/ppermute | solution.py:330
  22.6 4.1 %collective-permute-start.10 = (bf16[64,512]{1,0:T(8,128)(2,1)S(1)}, bf16[64,512]{1,0:T(8,128)(2,1)S(1)}, u32[]{:S(2)}, u32[]{:S(2)}) collective-permute-start(bf16[64,512]{1,0:T(8,128)(2,1)S(1)} %get-tuple-element.63), channel_id=1, source_target_pairs={{0,20},{1,21},{2,22},{3,23},{4,16},{5,17},{6,18},{7,19},{8,28},{9,... | collective-permute-start | bytes 196616 | tf_op jit(solution)/shard_map/ppermute | solution.py:330
  23.1 4.1 %collective-permute-start.11 = (bf16[64,512]{1,0:T(8,128)(2,1)S(1)}, bf16[64,512]{1,0:T(8,128)(2,1)S(1)}, u32[]{:S(2)}, u32[]{:S(2)}) collective-permute-start(bf16[64,512]{1,0:T(8,128)(2,1)S(1)} %get-tuple-element.64), channel_id=1, source_target_pairs={{0,12},{1,13},{2,14},{3,15},{4,8},{5,9},{6,10},{7,11},{8,4},{9,5},... | collective-permute-start | bytes 196616 | tf_op jit(solution)/shard_map/ppermute | solution.py:330
  23.4 6.8 %collective-permute-start.12 = (bf16[64,512]{1,0:T(8,128)(2,1)S(1)}, bf16[64,512]{1,0:T(8,128)(2,1)S(1)}, u32[]{:S(2)}, u32[]{:S(2)}) collective-permute-start(bf16[64,512]{1,0:T(8,128)(2,1)S(1)} %get-tuple-element.67), channel_id=1, source_target_pairs={{0,28},{1,29},{2,30},{3,31},{4,24},{5,25},{6,26},{7,27},{8,20},{9,... | collective-permute-start | bytes 196616 | tf_op jit(solution)/shard_map/ppermute | solution.py:330
  25.8 5.4 %collective-permute-start.13 = (bf16[64,512]{1,0:T(8,128)(2,1)S(1)}, bf16[64,512]{1,0:T(8,128)(2,1)S(1)}, u32[]{:S(2)}, u32[]{:S(2)}) collective-permute-start(bf16[64,512]{1,0:T(8,128)(2,1)S(1)} %get-tuple-element.68), channel_id=1, source_target_pairs={{0,20},{1,21},{2,22},{3,23},{4,16},{5,17},{6,18},{7,19},{8,28},{9,... | collective-permute-start | bytes 196616 | tf_op jit(solution)/shard_map/ppermute | solution.py:330
  26.0 5.1 %collective-permute-start.14 = (bf16[64,512]{1,0:T(8,128)(2,1)S(1)}, bf16[64,512]{1,0:T(8,128)(2,1)S(1)}, u32[]{:S(2)}, u32[]{:S(2)}) collective-permute-start(bf16[64,512]{1,0:T(8,128)(2,1)S(1)} %get-tuple-element.69), channel_id=1, source_target_pairs={{0,12},{1,13},{2,14},{3,15},{4,8},{5,9},{6,10},{7,11},{8,4},{9,5},... | collective-permute-start | bytes 196616 | tf_op jit(solution)/shard_map/ppermute | solution.py:330
  27.2 6.6 %collective-permute-start.16 = (bf16[64,256]{1,0:T(8,128)(2,1)S(1)}, bf16[64,256]{1,0:T(8,128)(2,1)S(1)}, u32[]{:S(2)}, u32[]{:S(2)}) collective-permute-start(bf16[64,256]{1,0:T(8,128)(2,1)S(1)} %get-tuple-element.81), channel_id=1, source_target_pairs={{0,7},{1,6},{2,5},{3,4},{4,3},{5,2},{6,1},{7,0},{8,15},{9,14},{10,... | collective-permute-start | bytes 98312 | tf_op jit(solution)/shard_map/ppermute | solution.py:330
  30.1 4.2 %collective-permute-start.17 = (bf16[64,256]{1,0:T(8,128)(2,1)S(1)}, bf16[64,256]{1,0:T(8,128)(2,1)S(1)}, u32[]{:S(2)}, u32[]{:S(2)}) collective-permute-start(bf16[64,256]{1,0:T(8,128)(2,1)S(1)} %get-tuple-element.65._), channel_id=1, source_target_pairs={{0,6},{1,7},{2,4},{3,5},{4,2},{5,3},{6,0},{7,1},{8,14},{9,15},{10,... | collective-permute-start | bytes 98312 | tf_op jit(solution)/shard_map/ppermute | solution.py:330
  31.2 4.0 %collective-permute-start.15 = (bf16[64,256]{1,0:T(8,128)(2,1)S(1)}, bf16[64,256]{1,0:T(8,128)(2,1)S(1)}, u32[]{:S(2)}, u32[]{:S(2)}) collective-permute-start(bf16[64,256]{1,0:T(8,128)(2,1)S(1)} %get-tuple-element.70._), channel_id=1, source_target_pairs={{0,5},{1,4},{2,7},{3,6},{4,1},{5,0},{6,3},{7,2},{8,13},{9,12},{10,... | collective-permute-start | bytes 98312 | tf_op jit(solution)/shard_map/ppermute | solution.py:330
  35.3 4.4 %collective-permute-start.20 = (bf16[64,256]{1,0:T(8,128)(2,1)S(1)}, bf16[64,256]{1,0:T(8,128)(2,1)S(1)}, u32[]{:S(2)}, u32[]{:S(2)}) collective-permute-start(bf16[64,256]{1,0:T(8,128)(2,1)S(1)} %mean_over_shards.1._.refs_0_), channel_id=1, source_target_pairs={{0,28},{1,29},{2,30},{3,31},{4,24},{5,25},{6,26},{7,27},{8,20},{9,... | collective-permute-start | bytes 98312 | tf_op jit(solution)/shard_map/ppermute | solution.py:330
  36.7 3.6 %collective-permute-start.19 = (bf16[64,256]{1,0:T(8,128)(2,1)S(1)}, bf16[64,256]{1,0:T(8,128)(2,1)S(1)}, u32[]{:S(2)}, u32[]{:S(2)}) collective-permute-start(bf16[64,256]{1,0:T(8,128)(2,1)S(1)} %mean_over_shards.1._.refs_0_), channel_id=1, source_target_pairs={{0,20},{1,21},{2,22},{3,23},{4,16},{5,17},{6,18},{7,19},{8,28},{9,... | collective-permute-start | bytes 98312 | tf_op jit(solution)/shard_map/ppermute | solution.py:330
  36.9 3.4 %collective-permute-start.18 = (bf16[64,256]{1,0:T(8,128)(2,1)S(1)}, bf16[64,256]{1,0:T(8,128)(2,1)S(1)}, u32[]{:S(2)}, u32[]{:S(2)}) collective-permute-start(bf16[64,256]{1,0:T(8,128)(2,1)S(1)} %mean_over_shards.1._.refs_0_), channel_id=1, source_target_pairs={{0,12},{1,13},{2,14},{3,15},{4,8},{5,9},{6,10},{7,11},{8,4},{9,5},... | collective-permute-start | bytes 98312 | tf_op jit(solution)/shard_map/ppermute | solution.py:330
  40.3 1.4 %collective-permute-start.21 = (bf16[256,256]{1,0:T(8,128)(2,1)S(1)}, bf16[256,256]{1,0:T(8,128)(2,1)S(1)}, u32[]{:S(2)}, u32[]{:S(2)}) collective-permute-start(bf16[256,256]{1,0:T(8,128)(2,1)S(1)} %blocks_of_chips.1.blocks_ref), channel_id=1, source_target_pairs={{0,4},{4,0},{8,12},{12,8},{16,20},{20,16},{24,28},{28,24},{1,5},{5... | collective-permute-start | bytes 393224 | tf_op jit(solution)/shard_map/ppermute | solution.py:318

commit v14 on v13

--- a/solution.py
+++ b/solution.py
@@ -157,9 +157,13 @@
     return [pltpu.VMEM((spare_rows, width), jnp.bfloat16), pltpu.SemaphoreType.DMA((count,))]
 
 
-def held_projection_kernel(group, shard_rows, origins, *refs):
-    pieces, (events_ref, out_ref, spare_ref, sems) = refs[: len(origins)], refs[len(origins) :]
-    out_ref[...] = project(events_ref, pieces, origins, group, shard_rows, spare_ref, sems)
+def projection_kernel(group, shard_rows, origins, *refs):
+    pieces, (events_ref, *terms) = refs[: len(origins)], refs[len(origins) : -3]
+    out_ref, spare_ref, sems = refs[-3:]
+    total = project(events_ref, pieces, origins, group, shard_rows, spare_ref, sems)
+    for term in terms:
+        total = total + term[...]
+    out_ref[...] = total
 
 
 def attention_kernel(slots, group, shard_rows, origins, *refs):
@@ -449,20 +453,25 @@
         return [f[0] for f in found], [f[1:] for f in found]
 
     terms = []
-    if held:
-        pieces, origins = split(held)
+    for name, found in (("held", held), ("passed", moved[:1])):
+        if not held:
+            break
+        pieces, origins = split(found)
+        operands = pieces + [near_events] + terms
         terms = [
             call(
-                functools.partial(held_projection_kernel, group, shard_rows, origins),
-                "projection_by_held_rows",
-                pieces + [near_events],
-                [NEAR] * (len(pieces) + 1),
+                functools.partial(projection_kernel, group, shard_rows, origins),
+                f"projection_by_{name}_rows",
+                operands,
+                [NEAR] * len(operands),
                 shape(rows, width, dtype=f32),
                 projection_scratch(shard_rows, model_width, width, origins),
                 flops=2 * rows * width * shard_rows * len(pieces),
                 moved=4 * rows * width,
             )
         ]
+    if held:
+        moved = moved[1:]
     pieces, origins = split(moved)
     blocks = shape(slots * HEADS, span, span)
     grad_query, query, normed, grad_mixed, attention, grad_scores = call(

time: 42.7 us -> 42.9 us (level)
    pallas_call x14 -> x15, Pallas kernels: 9.23 us -> 9.39 us  [call(): pl.pallas_call(kernel, out_shape=out_shape, in_specs=in_specs, out_specs=...]
  transfers between devices with their start and end apart: 22 -> 22, of which waited for: 13 -> 13; matrix products, arithmetic and copies ran while one was open for 0% -> 0% of each run, Pallas kernels for 15% -> 16%
where the time goes in v14:
time: 42.9 us; the launch traced here: 42.7 us
  starting transfers between devices  23 us (54%)
  waiting for transfers between devices  9.52 us (22%)
  Pallas kernels  9.39 us (22%)
  between operations  0.75 us (2%)
    ppermute x17, starting transfers between devices, cross(): return lax.ppermute(block, BOTH, pairs)  21.4 us
    pallas_call x15, Pallas kernels, call(): pl.pallas_call(kernel, out_shape=out_shape, in_specs=in_specs, out_specs=...  9.39 us
    ppermute x17, waiting for transfers between devices, cross(): return lax.ppermute(block, BOTH, pairs)  7.52 us
    ppermute x5, waiting for transfers between devices, flip(): return lax.ppermute(block, axis, [(i, i ^ bits) for i in range(count)])  2 us
    ppermute x5, starting transfers between devices, flip(): return lax.ppermute(block, axis, [(i, i ^ bits) for i in range(count)])  1.64 us
  transfers between devices with their start and end apart: 22, of which 13 were waited for; matrix products, arithmetic and copies ran while one was open for 0% of the time, Pallas kernels for 16%

profile of v14, /device:TPU:0, one launch (start us, length us, event | category | flops | bytes accessed | tf_op | source)
XLA Modules:
  0.0 42.7 jit_solution(5967159883375347639)
XLA Ops:
  0.6 0.5 %collective-permute-start.2 = (bf16[384,1024]{1,0:T(8,128)(2,1)}, bf16[384,1024]{1,0:T(8,128)(2,1)S(1)}, u32[]{:S(2)}, u32[]{:S(2)}) collective-permute-start(bf16[384,1024]{1,0:T(8,128)(2,1)} %bitcast.9), channel_id=1, source_target_pairs={{0,4},{4,0},{8,12},{12,8},{16,20},{20,16},{24,28},{28,24},{1,5},{5... | collective-permute-start | bytes 2359304 | tf_op jit(solution)/shard_map/ppermute | solution.py:322
  1.1 0.8 %own_part_of_weight.1 = bf16[32,512]{1,0:T(8,128)(2,1)S(1)} custom-call(bf16[256,512]{1,0:T(8,128)(2,1)} %refs_4_.1), custom_call_target="tpu_custom_call" | custom-call | tf_op jit(solution)/shard_map/own_part_of_weight/pallas_call | solution.py:33
  1.9 3.8 %collective-permute-start.1 = (bf16[32,512]{1,0:T(8,128)(2,1)S(1)}, bf16[32,512]{1,0:T(8,128)(2,1)S(1)}, u32[]{:S(2)}, u32[]{:S(2)}) collective-permute-start(bf16[32,512]{1,0:T(8,128)(2,1)S(1)} %own_part_of_weight.1), channel_id=1, source_target_pairs={{0,6},{1,7},{2,4},{3,5},{4,2},{5,3},{6,0},{7,1},{8,14},{9,15},{10,... | collective-permute-start | bytes 98312 | tf_op jit(solution)/shard_map/ppermute | solution.py:334
  5.7 1.2 %collective-permute-start = (bf16[256,512]{1,0:T(8,128)(2,1)}, bf16[256,512]{1,0:T(8,128)(2,1)S(1)}, u32[]{:S(2)}, u32[]{:S(2)}) collective-permute-start(bf16[256,512]{1,0:T(8,128)(2,1)} %refs_4_.1), channel_id=1, source_target_pairs={{0,5},{1,4},{2,7},{3,6},{4,3},{5,2},{6,1},{7,0},{8,13},{9,12},{10,... | collective-permute-start | bytes 786440 | tf_op jit(solution)/shard_map/ppermute | solution.py:334
  6.9 0.5 %collective-permute-done.1._.refs_0_ = bf16[32,512]{1,0:T(8,128)(2,1)S(1)} collective-permute-done((bf16[32,512]{1,0:T(8,128)(2,1)S(1)}, bf16[32,512]{1,0:T(8,128)(2,1)S(1)}, u32[]{:S(2)}, u32[]{:S(2)}) %collective-permute-start.1) | collective-permute-done | bytes 32800 | tf_op jit(solution)/shard_map/ppermute | solution.py:334
  7.4 2.4 %collective-permute-start.5 = (bf16[32,512]{1,0:T(8,128)(2,1)S(1)}, bf16[32,512]{1,0:T(8,128)(2,1)S(1)}, u32[]{:S(2)}, u32[]{:S(2)}) collective-permute-start(bf16[32,512]{1,0:T(8,128)(2,1)S(1)} %collective-permute-done.1._.refs_0_), channel_id=1, source_target_pairs={{0,28},{1,29},{2,30},{3,31},{4,24},{5,25},{6,26},{7,27},{8,20},{9,... | collective-permute-start | bytes 98312 | tf_op jit(solution)/shard_map/ppermute | solution.py:334
  10.4 2.3 %prepared_operands.1 = (bf16[384,1024]{1,0:T(8,128)(2,1)S(1)}, bf16[384,512]{1,0:T(8,128)(2,1)S(1)}, bf16[384,512]{1,0:T(8,128)(2,1)S(1)}, bf16[384,512]{1,0:T(8...) custom-call(bf16[32,512]{1,0:T(8,128)(2,1)S(1)} %collective-permute-, ...), custom_call_target="tpu_custom_call" | custom-call | flops 5000000000 | tf_op jit(solution)/shard_map/prepared_operands/pallas_call | solution.py:33
  12.7 0.5 %collective-permute-done.4.refs_2_ = bf16[32,512]{1,0:T(8,128)(2,1)S(1)} collective-permute-done((bf16[32,512]{1,0:T(8,128)(2,1)S(1)}, bf16[32,512]{1,0:T(8,128)(2,1)S(1)}, u32[]{:S(2)}, u32[]{:S(2)}) %collective-permute-start.4) | collective-permute-done | bytes 32800 | tf_op jit(solution)/shard_map/ppermute | solution.py:334
  13.3 1.4 %collective-permute-done.refs_2_ = bf16[256,512]{1,0:T(8,128)(2,1)S(1)} collective-permute-done((bf16[256,512]{1,0:T(8,128)(2,1)}, bf16[256,512]{1,0:T(8,128)(2,1)S(1)}, u32[]{:S(2)}, u32[]{:S(2)}) %collective-permute-start) | collective-permute-done | bytes 262176 | tf_op jit(solution)/shard_map/ppermute | solution.py:334
  14.7 0.5 %collective-permute-start.7 = (bf16[128,512]{1,0:T(8,128)(2,1)S(1)}, bf16[128,512]{1,0:T(8,128)(2,1)S(1)}, u32[]{:S(2)}, u32[]{:S(2)}) collective-permute-start(bf16[128,512]{1,0:T(8,128)(2,1)S(1)} %parts_of_weight.1.refs_1_), channel_id=1, source_target_pairs={{0,4},{4,0},{8,12},{12,8},{16,20},{20,16},{24,28},{28,24},{1,5},{5... | collective-permute-start | bytes 393224 | tf_op jit(solution)/shard_map/ppermute | solution.py:322
  15.2 0.5 %projection_by_held_rows.1.refs_2_ = f32[384,512]{1,0:T(8,128)S(1)} custom-call(bf16[256,512]{1,0:T(8,128)(2,1)S(1)} %get-tuple-element.48.refs_0_, bf16[128,512]{1,0:T(8,128)(2,1)S(1)} %parts_of_weight.1.refs_1_, bf16[256,512]{1,0:T(8,128)(2,1)S(1)} %collective-permute-done.refs_2_, bf16[384,1024]{1,0:T(8,128)(2,1)S(1)} %get-tuple-element.47.refs_3_.refs_1_.refs_2_), custom_call_target="tpu_custom_call" | custom-call | flops 301989888 | bytes 786432 | tf_op jit(solution)/shard_map/projection_by_held_rows/pallas_call | solution.py:33
  15.8 0.7 %collective-permute-done.7.refs_0_ = bf16[128,512]{1,0:T(8,128)(2,1)S(1)} collective-permute-done((bf16[128,512]{1,0:T(8,128)(2,1)S(1)}, bf16[128,512]{1,0:T(8,128)(2,1)S(1)}, u32[]{:S(2)}, u32[]{:S(2)}) %collective-permute-start.7) | collective-permute-done | bytes 131104 | tf_op jit(solution)/shard_map/ppermute | solution.py:322
  16.8 1.5 %attention_to_grad_query.1 = (bf16[384,512]{1,0:T(8,128)(2,1)S(1)}, bf16[384,512]{1,0:T(8,128)(2,1)S(1)}, f32[384,512]{1,0:T(8,128)S(1)}, bf16[384,512]{1,0:T(8,...) custom-call(bf16[256,512]{1,0:T(8,128)(2,1)S(1)} %collective-permute-done.6.refs_0_, ...), custom_call_target="tpu_custom_call" | custom-call | flops 603979776 | bytes 4718592 | tf_op jit(solution)/shard_map/attention_to_grad_query/pallas_call | solution.py:33
  18.5 0.5 %weight_gradient_of_own_events.1 = (f32[512,256]{1,0:T(8,128)S(1)}, bf16[512,384]{1,0:T(8,128)(2,1)S(1)}, f32[512,256]{1,0:T(8,128)S(1)}, bf16[512,384]{1,0:T(8,128)(2,1)S(1)}) custom-call(bf16[1024,768]{1,0:T(8,128)(2,1)S(1)} %get-tuple-element.56.events_ref, bf16[384,512]{1,0:T(8,128)(2,1)S(1)} %get-tuple-element.55.grad_query_ref), custom_call_target="tpu_custom_call" | custom-call | flops 201326592 | bytes 3145728 | tf_op jit(solution)/shard_map/weight_gradient_of_own_events/pallas_call | solution.py:33
  19.0 1.1 %collective-permute-done.8.grad_query_ref._ = bf16[384,512]{1,0:T(8,128)(2,1)S(1)} collective-permute-done((bf16[384,512]{1,0:T(8,128)(2,1)S(1)}, bf16[384,512]{1,0:T(8,128)(2,1)S(1)}, u32[]{:S(2)}, u32[]{:S(2)}) %collective-permute-start.8) | collective-permute-done | bytes 393248 | tf_op jit(solution)/shard_map/ppermute | solution.py:322
  20.5 2.3 %collective-permute-start.9 = (bf16[64,512]{1,0:T(8,128)(2,1)S(1)}, bf16[64,512]{1,0:T(8,128)(2,1)S(1)}, u32[]{:S(2)}, u32[]{:S(2)}) collective-permute-start(bf16[64,512]{1,0:T(8,128)(2,1)S(1)} %get-tuple-element.62), channel_id=1, source_target_pairs={{0,28},{1,29},{2,30},{3,31},{4,24},{5,25},{6,26},{7,27},{8,20},{9,... | collective-permute-start | bytes 196616 | tf_op jit(solution)/shard_map/ppermute | solution.py:334
  22.8 0.5 %collective-permute-start.10 = (bf16[64,512]{1,0:T(8,128)(2,1)S(1)}, bf16[64,512]{1,0:T(8,128)(2,1)S(1)}, u32[]{:S(2)}, u32[]{:S(2)}) collective-permute-start(bf16[64,512]{1,0:T(8,128)(2,1)S(1)} %get-tuple-element.63), channel_id=1, source_target_pairs={{0,20},{1,21},{2,22},{3,23},{4,16},{5,17},{6,18},{7,19},{8,28},{9,... | collective-permute-start | bytes 196616 | tf_op jit(solution)/shard_map/ppermute | solution.py:334
  23.5 2.4 %collective-permute-start.12 = (bf16[64,512]{1,0:T(8,128)(2,1)S(1)}, bf16[64,512]{1,0:T(8,128)(2,1)S(1)}, u32[]{:S(2)}, u32[]{:S(2)}) collective-permute-start(bf16[64,512]{1,0:T(8,128)(2,1)S(1)} %get-tuple-element.67), channel_id=1, source_target_pairs={{0,28},{1,29},{2,30},{3,31},{4,24},{5,25},{6,26},{7,27},{8,20},{9,... | collective-permute-start | bytes 196616 | tf_op jit(solution)/shard_map/ppermute | solution.py:334
  26.2 0.7 %collective-permute-start.14 = (bf16[64,512]{1,0:T(8,128)(2,1)S(1)}, bf16[64,512]{1,0:T(8,128)(2,1)S(1)}, u32[]{:S(2)}, u32[]{:S(2)}) collective-permute-start(bf16[64,512]{1,0:T(8,128)(2,1)S(1)} %get-tuple-element.69), channel_id=1, source_target_pairs={{0,12},{1,13},{2,14},{3,15},{4,8},{5,9},{6,10},{7,11},{8,4},{9,5},... | collective-permute-start | bytes 196616 | tf_op jit(solution)/shard_map/ppermute | solution.py:334
  26.9 0.5 %collective-permute-done.11.refs_3_ = bf16[64,512]{1,0:T(8,128)(2,1)S(1)} collective-permute-done((bf16[64,512]{1,0:T(8,128)(2,1)S(1)}, bf16[64,512]{1,0:T(8,128)(2,1)S(1)}, u32[]{:S(2)}, u32[]{:S(2)}) %collective-permute-start.11) | collective-permute-done | bytes 65568 | tf_op jit(solution)/shard_map/ppermute | solution.py:334
  27.4 2.9 %collective-permute-start.16 = (bf16[64,256]{1,0:T(8,128)(2,1)S(1)}, bf16[64,256]{1,0:T(8,128)(2,1)S(1)}, u32[]{:S(2)}, u32[]{:S(2)}) collective-permute-start(bf16[64,256]{1,0:T(8,128)(2,1)S(1)} %get-tuple-element.81), channel_id=1, source_target_pairs={{0,7},{1,6},{2,5},{3,4},{4,3},{5,2},{6,1},{7,0},{8,15},{9,14},{10,... | collective-permute-start | bytes 98312 | tf_op jit(solution)/shard_map/ppermute | solution.py:334
  30.3 1.0 %collective-permute-done.13.refs_2_ = bf16[64,512]{1,0:T(8,128)(2,1)S(1)} collective-permute-done((bf16[64,512]{1,0:T(8,128)(2,1)S(1)}, bf16[64,512]{1,0:T(8,128)(2,1)S(1)}, u32[]{:S(2)}, u32[]{:S(2)}) %collective-permute-start.13) | collective-permute-done | bytes 65568 | tf_op jit(solution)/shard_map/ppermute | solution.py:334
  31.4 1.2 %collective-permute-start.15 = (bf16[64,256]{1,0:T(8,128)(2,1)S(1)}, bf16[64,256]{1,0:T(8,128)(2,1)S(1)}, u32[]{:S(2)}, u32[]{:S(2)}) collective-permute-start(bf16[64,256]{1,0:T(8,128)(2,1)S(1)} %get-tuple-element.70._), channel_id=1, source_target_pairs={{0,5},{1,4},{2,7},{3,6},{4,1},{5,0},{6,3},{7,2},{8,13},{9,12},{10,... | collective-permute-start | bytes 98312 | tf_op jit(solution)/shard_map/ppermute | solution.py:334
  32.5 1.4 %key_value_gate_gradients.1 = (bf16[384,512]{1,0:T(8,128)(2,1)}, bf16[384,512]{1,0:T(8,128)(2,1)}, bf16[384,512]{1,0:T(8,128)(2,1)}) custom-call(bf16[64,256]{1,0:T(8,128)(2,1)S(1)} %get-tuple-element.70._, bf16[384,512]{1,0:T(8,128)(2,1)S(1)} %get-tuple-element.71.query_ref, f32[384,512]{1,0:T(8,128)S(1)} %get-tuple-element.72.normed_ref, ...), custom_call_target="tpu_custom_call" | custom-call | flops 100663296 | bytes 2359296 | tf_op jit(solution)/shard_map/key_value_gate_gradients/pallas_call | solution.py:33
  34.0 0.6 %collective-permute-done.17.refs_3_ = bf16[64,256]{1,0:T(8,128)(2,1)S(1)} collective-permute-done((bf16[64,256]{1,0:T(8,128)(2,1)S(1)}, bf16[64,256]{1,0:T(8,128)(2,1)S(1)}, u32[]{:S(2)}, u32[]{:S(2)}) %collective-permute-start.17) | collective-permute-done | bytes 32800 | tf_op jit(solution)/shard_map/ppermute | solution.py:334
  34.6 0.9 %collective-permute-done.15.refs_1_ = bf16[64,256]{1,0:T(8,128)(2,1)S(1)} collective-permute-done((bf16[64,256]{1,0:T(8,128)(2,1)S(1)}, bf16[64,256]{1,0:T(8,128)(2,1)S(1)}, u32[]{:S(2)}, u32[]{:S(2)}) %collective-permute-start.15) | collective-permute-done | bytes 32800 | tf_op jit(solution)/shard_map/ppermute | solution.py:334
  35.5 1.4 %collective-permute-start.20 = (bf16[64,256]{1,0:T(8,128)(2,1)S(1)}, bf16[64,256]{1,0:T(8,128)(2,1)S(1)}, u32[]{:S(2)}, u32[]{:S(2)}) collective-permute-start(bf16[64,256]{1,0:T(8,128)(2,1)S(1)} %mean_over_shards.1._.refs_0_), channel_id=1, source_target_pairs={{0,28},{1,29},{2,30},{3,31},{4,24},{5,25},{6,26},{7,27},{8,20},{9,... | collective-permute-start | bytes 98312 | tf_op jit(solution)/shard_map/ppermute | solution.py:334
  37.0 1.4 %collective-permute-start.18 = (bf16[64,256]{1,0:T(8,128)(2,1)S(1)}, bf16[64,256]{1,0:T(8,128)(2,1)S(1)}, u32[]{:S(2)}, u32[]{:S(2)}) collective-permute-start(bf16[64,256]{1,0:T(8,128)(2,1)S(1)} %mean_over_shards.1._.refs_0_), channel_id=1, source_target_pairs={{0,12},{1,13},{2,14},{3,15},{4,8},{5,9},{6,10},{7,11},{8,4},{9,5},... | collective-permute-start | bytes 98312 | tf_op jit(solution)/shard_map/ppermute | solution.py:334
  38.5 1.4 %collective-permute-done.20.refs_3_ = bf16[64,256]{1,0:T(8,128)(2,1)S(1)} collective-permute-done((bf16[64,256]{1,0:T(8,128)(2,1)S(1)}, bf16[64,256]{1,0:T(8,128)(2,1)S(1)}, u32[]{:S(2)}, u32[]{:S(2)}) %collective-permute-start.20) | collective-permute-done | bytes 32800 | tf_op jit(solution)/shard_map/ppermute | solution.py:334
  39.8 0.6 %collective-permute-done.19.refs_2_ = bf16[64,256]{1,0:T(8,128)(2,1)S(1)} collective-permute-done((bf16[64,256]{1,0:T(8,128)(2,1)S(1)}, bf16[64,256]{1,0:T(8,128)(2,1)S(1)}, u32[]{:S(2)}, u32[]{:S(2)}) %collective-permute-start.19) | collective-permute-done | bytes 32800 | tf_op jit(solution)/shard_map/ppermute | solution.py:334
  40.9 0.7 %blocks_of_own_core_in_place.1.refs_0_ = f32[256,512]{1,0:T(8,128)} custom-call(bf16[256,256]{1,0:T(8,128)(2,1)S(1)} %blocks_of_chips.1.blocks_ref), custom_call_target="tpu_custom_call" | custom-call | tf_op jit(solution)/shard_map/blocks_of_own_core_in_place/pallas_call | solution.py:33
  41.9 0.7 %blocks_of_sibling_core_in_place.1 = f32[256,512]{1,0:T(8,128)} custom-call(bf16[256,256]{1,0:T(8,128)(2,1)S(1)} %collective-permute-done.21.blocks_ref, f32[256,512]{1,0:T(8,128)} %blocks_of_own_core_in_place.1.refs_0_), custom_call_target="tpu_custom_call", output_to_operand_aliasing={{}: (1, {})} | custom-call | tf_op jit(solution)/shard_map/blocks_of_sibling_core_in_place/pallas_call | solution.py:33
  (27 shorter events, 3.1 us)
Async XLA Ops:
  0.6 9.7 %collective-permute-start.2 = (bf16[384,1024]{1,0:T(8,128)(2,1)}, bf16[384,1024]{1,0:T(8,128)(2,1)S(1)}, u32[]{:S(2)}, u32[]{:S(2)}) collective-permute-start(bf16[384,1024]{1,0:T(8,128)(2,1)} %bitcast.9), channel_id=1, source_target_pairs={{0,4},{4,0},{8,12},{12,8},{16,20},{20,16},{24,28},{28,24},{1,5},{5... | collective-permute-start | bytes 2359304 | tf_op jit(solution)/shard_map/ppermute | solution.py:322
  1.9 5.5 %collective-permute-start.1 = (bf16[32,512]{1,0:T(8,128)(2,1)S(1)}, bf16[32,512]{1,0:T(8,128)(2,1)S(1)}, u32[]{:S(2)}, u32[]{:S(2)}) collective-permute-start(bf16[32,512]{1,0:T(8,128)(2,1)S(1)} %own_part_of_weight.1), channel_id=1, source_target_pairs={{0,6},{1,7},{2,4},{3,5},{4,2},{5,3},{6,0},{7,1},{8,14},{9,15},{10,... | collective-permute-start | bytes 98312 | tf_op jit(solution)/shard_map/ppermute | solution.py:334
  5.7 9.0 %collective-permute-start = (bf16[256,512]{1,0:T(8,128)(2,1)}, bf16[256,512]{1,0:T(8,128)(2,1)S(1)}, u32[]{:S(2)}, u32[]{:S(2)}) collective-permute-start(bf16[256,512]{1,0:T(8,128)(2,1)} %refs_4_.1), channel_id=1, source_target_pairs={{0,5},{1,4},{2,7},{3,6},{4,3},{5,2},{6,1},{7,0},{8,13},{9,12},{10,... | collective-permute-start | bytes 786440 | tf_op jit(solution)/shard_map/ppermute | solution.py:334
  7.4 5.3 %collective-permute-start.5 = (bf16[32,512]{1,0:T(8,128)(2,1)S(1)}, bf16[32,512]{1,0:T(8,128)(2,1)S(1)}, u32[]{:S(2)}, u32[]{:S(2)}) collective-permute-start(bf16[32,512]{1,0:T(8,128)(2,1)S(1)} %collective-permute-done.1._.refs_0_), channel_id=1, source_target_pairs={{0,28},{1,29},{2,30},{3,31},{4,24},{5,25},{6,26},{7,27},{8,20},{9,... | collective-permute-start | bytes 98312 | tf_op jit(solution)/shard_map/ppermute | solution.py:334
  9.8 3.4 %collective-permute-start.4 = (bf16[32,512]{1,0:T(8,128)(2,1)S(1)}, bf16[32,512]{1,0:T(8,128)(2,1)S(1)}, u32[]{:S(2)}, u32[]{:S(2)}) collective-permute-start(bf16[32,512]{1,0:T(8,128)(2,1)S(1)} %collective-permute-done.1._.refs_0_), channel_id=1, source_target_pairs={{0,20},{1,21},{2,22},{3,23},{4,16},{5,17},{6,18},{7,19},{8,28},{9,... | collective-permute-start | bytes 98312 | tf_op jit(solution)/shard_map/ppermute | solution.py:334
  10.0 3.3 %collective-permute-start.3 = (bf16[32,512]{1,0:T(8,128)(2,1)S(1)}, bf16[32,512]{1,0:T(8,128)(2,1)S(1)}, u32[]{:S(2)}, u32[]{:S(2)}) collective-permute-start(bf16[32,512]{1,0:T(8,128)(2,1)S(1)} %collective-permute-done.1._.refs_0_), channel_id=1, source_target_pairs={{0,12},{1,13},{2,14},{3,15},{4,8},{5,9},{6,10},{7,11},{8,4},{9,5},... | collective-permute-start | bytes 98312 | tf_op jit(solution)/shard_map/ppermute | solution.py:334
  14.7 2.1 %collective-permute-start.6 = (bf16[256,512]{1,0:T(8,128)(2,1)S(1)}, bf16[256,512]{1,0:T(8,128)(2,1)S(1)}, u32[]{:S(2)}, u32[]{:S(2)}) collective-permute-start(bf16[256,512]{1,0:T(8,128)(2,1)S(1)} %collective-permute-done.refs_2_), channel_id=1, source_target_pairs={{0,4},{4,0},{8,12},{12,8},{16,20},{20,16},{24,28},{28,24},{1,5},{5... | collective-permute-start | bytes 786440 | tf_op jit(solution)/shard_map/ppermute | solution.py:322
  14.7 1.7 %collective-permute-start.7 = (bf16[128,512]{1,0:T(8,128)(2,1)S(1)}, bf16[128,512]{1,0:T(8,128)(2,1)S(1)}, u32[]{:S(2)}, u32[]{:S(2)}) collective-permute-start(bf16[128,512]{1,0:T(8,128)(2,1)S(1)} %parts_of_weight.1.refs_1_), channel_id=1, source_target_pairs={{0,4},{4,0},{8,12},{12,8},{16,20},{20,16},{24,28},{28,24},{1,5},{5... | collective-permute-start | bytes 393224 | tf_op jit(solution)/shard_map/ppermute | solution.py:322
  18.3 1.8 %collective-permute-start.8 = (bf16[384,512]{1,0:T(8,128)(2,1)S(1)}, bf16[384,512]{1,0:T(8,128)(2,1)S(1)}, u32[]{:S(2)}, u32[]{:S(2)}) collective-permute-start(bf16[384,512]{1,0:T(8,128)(2,1)S(1)} %get-tuple-element.55.grad_query_ref), channel_id=1, source_target_pairs={{0,4},{4,0},{8,12},{12,8},{16,20},{20,16},{24,28},{28,24},{1,5},{5... | collective-permute-start | bytes 1179656 | tf_op jit(solution)/shard_map/ppermute | solution.py:322
  20.5 5.7 %collective-permute-start.9 = (bf16[64,512]{1,0:T(8,128)(2,1)S(1)}, bf16[64,512]{1,0:T(8,128)(2,1)S(1)}, u32[]{:S(2)}, u32[]{:S(2)}) collective-permute-start(bf16[64,512]{1,0:T(8,128)(2,1)S(1)} %get-tuple-element.62), channel_id=1, source_target_pairs={{0,28},{1,29},{2,30},{3,31},{4,24},{5,25},{6,26},{7,27},{8,20},{9,... | collective-permute-start | bytes 196616 | tf_op jit(solution)/shard_map/ppermute | solution.py:334
  22.8 4.1 %collective-permute-start.10 = (bf16[64,512]{1,0:T(8,128)(2,1)S(1)}, bf16[64,512]{1,0:T(8,128)(2,1)S(1)}, u32[]{:S(2)}, u32[]{:S(2)}) collective-permute-start(bf16[64,512]{1,0:T(8,128)(2,1)S(1)} %get-tuple-element.63), channel_id=1, source_target_pairs={{0,20},{1,21},{2,22},{3,23},{4,16},{5,17},{6,18},{7,19},{8,28},{9,... | collective-permute-start | bytes 196616 | tf_op jit(solution)/shard_map/ppermute | solution.py:334
  23.2 4.1 %collective-permute-start.11 = (bf16[64,512]{1,0:T(8,128)(2,1)S(1)}, bf16[64,512]{1,0:T(8,128)(2,1)S(1)}, u32[]{:S(2)}, u32[]{:S(2)}) collective-permute-start(bf16[64,512]{1,0:T(8,128)(2,1)S(1)} %get-tuple-element.64), channel_id=1, source_target_pairs={{0,12},{1,13},{2,14},{3,15},{4,8},{5,9},{6,10},{7,11},{8,4},{9,5},... | collective-permute-start | bytes 196616 | tf_op jit(solution)/shard_map/ppermute | solution.py:334
  23.5 6.8 %collective-permute-start.12 = (bf16[64,512]{1,0:T(8,128)(2,1)S(1)}, bf16[64,512]{1,0:T(8,128)(2,1)S(1)}, u32[]{:S(2)}, u32[]{:S(2)}) collective-permute-start(bf16[64,512]{1,0:T(8,128)(2,1)S(1)} %get-tuple-element.67), channel_id=1, source_target_pairs={{0,28},{1,29},{2,30},{3,31},{4,24},{5,25},{6,26},{7,27},{8,20},{9,... | collective-permute-start | bytes 196616 | tf_op jit(solution)/shard_map/ppermute | solution.py:334
  25.9 5.4 %collective-permute-start.13 = (bf16[64,512]{1,0:T(8,128)(2,1)S(1)}, bf16[64,512]{1,0:T(8,128)(2,1)S(1)}, u32[]{:S(2)}, u32[]{:S(2)}) collective-permute-start(bf16[64,512]{1,0:T(8,128)(2,1)S(1)} %get-tuple-element.68), channel_id=1, source_target_pairs={{0,20},{1,21},{2,22},{3,23},{4,16},{5,17},{6,18},{7,19},{8,28},{9,... | collective-permute-start | bytes 196616 | tf_op jit(solution)/shard_map/ppermute | solution.py:334
  26.2 5.1 %collective-permute-start.14 = (bf16[64,512]{1,0:T(8,128)(2,1)S(1)}, bf16[64,512]{1,0:T(8,128)(2,1)S(1)}, u32[]{:S(2)}, u32[]{:S(2)}) collective-permute-start(bf16[64,512]{1,0:T(8,128)(2,1)S(1)} %get-tuple-element.69), channel_id=1, source_target_pairs={{0,12},{1,13},{2,14},{3,15},{4,8},{5,9},{6,10},{7,11},{8,4},{9,5},... | collective-permute-start | bytes 196616 | tf_op jit(solution)/shard_map/ppermute | solution.py:334
  27.4 6.6 %collective-permute-start.16 = (bf16[64,256]{1,0:T(8,128)(2,1)S(1)}, bf16[64,256]{1,0:T(8,128)(2,1)S(1)}, u32[]{:S(2)}, u32[]{:S(2)}) collective-permute-start(bf16[64,256]{1,0:T(8,128)(2,1)S(1)} %get-tuple-element.81), channel_id=1, source_target_pairs={{0,7},{1,6},{2,5},{3,4},{4,3},{5,2},{6,1},{7,0},{8,15},{9,14},{10,... | collective-permute-start | bytes 98312 | tf_op jit(solution)/shard_map/ppermute | solution.py:334
  30.3 4.2 %collective-permute-start.17 = (bf16[64,256]{1,0:T(8,128)(2,1)S(1)}, bf16[64,256]{1,0:T(8,128)(2,1)S(1)}, u32[]{:S(2)}, u32[]{:S(2)}) collective-permute-start(bf16[64,256]{1,0:T(8,128)(2,1)S(1)} %get-tuple-element.65._), channel_id=1, source_target_pairs={{0,6},{1,7},{2,4},{3,5},{4,2},{5,3},{6,0},{7,1},{8,14},{9,15},{10,... | collective-permute-start | bytes 98312 | tf_op jit(solution)/shard_map/ppermute | solution.py:334
  31.4 4.1 %collective-permute-start.15 = (bf16[64,256]{1,0:T(8,128)(2,1)S(1)}, bf16[64,256]{1,0:T(8,128)(2,1)S(1)}, u32[]{:S(2)}, u32[]{:S(2)}) collective-permute-start(bf16[64,256]{1,0:T(8,128)(2,1)S(1)} %get-tuple-element.70._), channel_id=1, source_target_pairs={{0,5},{1,4},{2,7},{3,6},{4,1},{5,0},{6,3},{7,2},{8,13},{9,12},{10,... | collective-permute-start | bytes 98312 | tf_op jit(solution)/shard_map/ppermute | solution.py:334
  35.5 4.4 %collective-permute-start.20 = (bf16[64,256]{1,0:T(8,128)(2,1)S(1)}, bf16[64,256]{1,0:T(8,128)(2,1)S(1)}, u32[]{:S(2)}, u32[]{:S(2)}) collective-permute-start(bf16[64,256]{1,0:T(8,128)(2,1)S(1)} %mean_over_shards.1._.refs_0_), channel_id=1, source_target_pairs={{0,28},{1,29},{2,30},{3,31},{4,24},{5,25},{6,26},{7,27},{8,20},{9,... | collective-permute-start | bytes 98312 | tf_op jit(solution)/shard_map/ppermute | solution.py:334
  36.9 3.6 %collective-permute-start.19 = (bf16[64,256]{1,0:T(8,128)(2,1)S(1)}, bf16[64,256]{1,0:T(8,128)(2,1)S(1)}, u32[]{:S(2)}, u32[]{:S(2)}) collective-permute-start(bf16[64,256]{1,0:T(8,128)(2,1)S(1)} %mean_over_shards.1._.refs_0_), channel_id=1, source_target_pairs={{0,20},{1,21},{2,22},{3,23},{4,16},{5,17},{6,18},{7,19},{8,28},{9,... | collective-permute-start | bytes 98312 | tf_op jit(solution)/shard_map/ppermute | solution.py:334
  37.0 3.4 %collective-permute-start.18 = (bf16[64,256]{1,0:T(8,128)(2,1)S(1)}, bf16[64,256]{1,0:T(8,128)(2,1)S(1)}, u32[]{:S(2)}, u32[]{:S(2)}) collective-permute-start(bf16[64,256]{1,0:T(8,128)(2,1)S(1)} %mean_over_shards.1._.refs_0_), channel_id=1, source_target_pairs={{0,12},{1,13},{2,14},{3,15},{4,8},{5,9},{6,10},{7,11},{8,4},{9,5},... | collective-permute-start | bytes 98312 | tf_op jit(solution)/shard_map/ppermute | solution.py:334
  40.5 1.4 %collective-permute-start.21 = (bf16[256,256]{1,0:T(8,128)(2,1)S(1)}, bf16[256,256]{1,0:T(8,128)(2,1)S(1)}, u32[]{:S(2)}, u32[]{:S(2)}) collective-permute-start(bf16[256,256]{1,0:T(8,128)(2,1)S(1)} %blocks_of_chips.1.blocks_ref), channel_id=1, source_target_pairs={{0,4},{4,0},{8,12},{12,8},{16,20},{20,16},{24,28},{28,24},{1,5},{5... | collective-permute-start | bytes 393224 | tf_op jit(solution)/shard_map/ppermute | solution.py:322

commit v15 on v14

--- a/solution.py
+++ b/solution.py
@@ -466,7 +466,7 @@
                 [NEAR] * len(operands),
                 shape(rows, width, dtype=f32),
                 projection_scratch(shard_rows, model_width, width, origins),
-                flops=2 * rows * width * shard_rows * len(pieces),
+                flops=3 * 10**9 if terms else 2 * rows * width * shard_rows * len(pieces),
                 moved=4 * rows * width,
             )
         ]

time: 42.9 us -> 42.6 us (level)
  waiting for transfers between devices: 9.52 us -> 8.74 us
  starting transfers between devices: 23 us -> 23.5 us
    ppermute x17, waiting for transfers between devices: 7.52 us -> 6.56 us  [cross(): return lax.ppermute(block, BOTH, pairs)]
where the time goes in v15:
time: 42.6 us; the launch traced here: 42.4 us
  starting transfers between devices  23.5 us (55%)
  Pallas kernels  9.4 us (22%)
  waiting for transfers between devices  8.74 us (21%)
  between operations  0.75 us (2%)
    ppermute x17, starting transfers between devices, cross(): return lax.ppermute(block, BOTH, pairs)  21.8 us
    pallas_call x15, Pallas kernels, call(): pl.pallas_call(kernel, out_shape=out_shape, in_specs=in_specs, out_specs=...  9.4 us
    ppermute x17, waiting for transfers between devices, cross(): return lax.ppermute(block, BOTH, pairs)  6.56 us
    ppermute x5, waiting for transfers between devices, flip(): return lax.ppermute(block, axis, [(i, i ^ bits) for i in range(count)])  2.18 us
    ppermute x5, starting transfers between devices, flip(): return lax.ppermute(block, axis, [(i, i ^ bits) for i in range(count)])  1.72 us
  transfers between devices with their start and end apart: 22, of which 13 were waited for; matrix products, arithmetic and copies ran while one was open for 0% of the time, Pallas kernels for 16%

profile of v15, /device:TPU:0, one launch (start us, length us, event | category | flops | bytes accessed | tf_op | source)
XLA Modules:
  0.0 42.4 jit_solution(6034842306290317574)
XLA Ops:
  0.6 0.5 %collective-permute-start.2 = (bf16[384,1024]{1,0:T(8,128)(2,1)}, bf16[384,1024]{1,0:T(8,128)(2,1)S(1)}, u32[]{:S(2)}, u32[]{:S(2)}) collective-permute-start(bf16[384,1024]{1,0:T(8,128)(2,1)} %bitcast.9), channel_id=1, source_target_pairs={{0,4},{4,0},{8,12},{12,8},{16,20},{20,16},{24,28},{28,24},{1,5},{5... | collective-permute-start | bytes 2359304 | tf_op jit(solution)/shard_map/ppermute | solution.py:322
  1.1 0.8 %own_part_of_weight.1 = bf16[32,512]{1,0:T(8,128)(2,1)S(1)} custom-call(bf16[256,512]{1,0:T(8,128)(2,1)} %refs_4_.1), custom_call_target="tpu_custom_call" | custom-call | tf_op jit(solution)/shard_map/own_part_of_weight/pallas_call | solution.py:33
  1.9 3.8 %collective-permute-start.1 = (bf16[32,512]{1,0:T(8,128)(2,1)S(1)}, bf16[32,512]{1,0:T(8,128)(2,1)S(1)}, u32[]{:S(2)}, u32[]{:S(2)}) collective-permute-start(bf16[32,512]{1,0:T(8,128)(2,1)S(1)} %own_part_of_weight.1), channel_id=1, source_target_pairs={{0,6},{1,7},{2,4},{3,5},{4,2},{5,3},{6,0},{7,1},{8,14},{9,15},{10,... | collective-permute-start | bytes 98312 | tf_op jit(solution)/shard_map/ppermute | solution.py:334
  5.7 1.2 %collective-permute-start = (bf16[256,512]{1,0:T(8,128)(2,1)}, bf16[256,512]{1,0:T(8,128)(2,1)S(1)}, u32[]{:S(2)}, u32[]{:S(2)}) collective-permute-start(bf16[256,512]{1,0:T(8,128)(2,1)} %refs_4_.1), channel_id=1, source_target_pairs={{0,5},{1,4},{2,7},{3,6},{4,3},{5,2},{6,1},{7,0},{8,13},{9,12},{10,... | collective-permute-start | bytes 786440 | tf_op jit(solution)/shard_map/ppermute | solution.py:334
  6.9 0.5 %collective-permute-done.1._.refs_0_ = bf16[32,512]{1,0:T(8,128)(2,1)S(1)} collective-permute-done((bf16[32,512]{1,0:T(8,128)(2,1)S(1)}, bf16[32,512]{1,0:T(8,128)(2,1)S(1)}, u32[]{:S(2)}, u32[]{:S(2)}) %collective-permute-start.1) | collective-permute-done | bytes 32800 | tf_op jit(solution)/shard_map/ppermute | solution.py:334
  7.4 2.4 %collective-permute-start.5 = (bf16[32,512]{1,0:T(8,128)(2,1)S(1)}, bf16[32,512]{1,0:T(8,128)(2,1)S(1)}, u32[]{:S(2)}, u32[]{:S(2)}) collective-permute-start(bf16[32,512]{1,0:T(8,128)(2,1)S(1)} %collective-permute-done.1._.refs_0_), channel_id=1, source_target_pairs={{0,28},{1,29},{2,30},{3,31},{4,24},{5,25},{6,26},{7,27},{8,20},{9,... | collective-permute-start | bytes 98312 | tf_op jit(solution)/shard_map/ppermute | solution.py:334
  10.4 2.3 %prepared_operands.1 = (bf16[384,1024]{1,0:T(8,128)(2,1)S(1)}, bf16[384,512]{1,0:T(8,128)(2,1)S(1)}, bf16[384,512]{1,0:T(8,128)(2,1)S(1)}, bf16[384,512]{1,0:T(8...) custom-call(bf16[32,512]{1,0:T(8,128)(2,1)S(1)} %collective-permute-, ...), custom_call_target="tpu_custom_call" | custom-call | flops 5000000000 | tf_op jit(solution)/shard_map/prepared_operands/pallas_call | solution.py:33
  12.7 0.5 %collective-permute-done.4.refs_2_ = bf16[32,512]{1,0:T(8,128)(2,1)S(1)} collective-permute-done((bf16[32,512]{1,0:T(8,128)(2,1)S(1)}, bf16[32,512]{1,0:T(8,128)(2,1)S(1)}, u32[]{:S(2)}, u32[]{:S(2)}) %collective-permute-start.4) | collective-permute-done | bytes 32800 | tf_op jit(solution)/shard_map/ppermute | solution.py:334
  13.3 0.8 %collective-permute-start.7 = (bf16[128,512]{1,0:T(8,128)(2,1)S(1)}, bf16[128,512]{1,0:T(8,128)(2,1)S(1)}, u32[]{:S(2)}, u32[]{:S(2)}) collective-permute-start(bf16[128,512]{1,0:T(8,128)(2,1)S(1)} %parts_of_weight.1.refs_1_), channel_id=1, source_target_pairs={{0,4},{4,0},{8,12},{12,8},{16,20},{20,16},{24,28},{28,24},{1,5},{5... | collective-permute-start | bytes 393224 | tf_op jit(solution)/shard_map/ppermute | solution.py:322
  14.1 0.6 %collective-permute-done.refs_2_ = bf16[256,512]{1,0:T(8,128)(2,1)S(1)} collective-permute-done((bf16[256,512]{1,0:T(8,128)(2,1)}, bf16[256,512]{1,0:T(8,128)(2,1)S(1)}, u32[]{:S(2)}, u32[]{:S(2)}) %collective-permute-start) | collective-permute-done | bytes 262176 | tf_op jit(solution)/shard_map/ppermute | solution.py:334
  14.7 0.6 %projection_by_held_rows.1.refs_2_ = f32[384,512]{1,0:T(8,128)S(1)} custom-call(bf16[256,512]{1,0:T(8,128)(2,1)S(1)} %get-tuple-element.48.refs_0_, bf16[128,512]{1,0:T(8,128)(2,1)S(1)} %parts_of_weight.1.refs_1_, bf16[256,512]{1,0:T(8,128)(2,1)S(1)} %collective-permute-done.refs_2_, bf16[384,1024]{1,0:T(8,128)(2,1)S(1)} %get-tuple-element.47.refs_3_.refs_1_.refs_2_), custom_call_target="tpu_custom_call" | custom-call | flops 301989888 | bytes 786432 | tf_op jit(solution)/shard_map/projection_by_held_rows/pallas_call | solution.py:33
  15.6 0.6 %collective-permute-done.6.refs_0_ = bf16[256,512]{1,0:T(8,128)(2,1)S(1)} collective-permute-done((bf16[256,512]{1,0:T(8,128)(2,1)S(1)}, bf16[256,512]{1,0:T(8,128)(2,1)S(1)}, u32[]{:S(2)}, u32[]{:S(2)}) %collective-permute-start.6) | collective-permute-done | bytes 262176 | tf_op jit(solution)/shard_map/ppermute | solution.py:322
  16.2 1.5 %attention_to_grad_query.1 = (bf16[384,512]{1,0:T(8,128)(2,1)S(1)}, bf16[384,512]{1,0:T(8,128)(2,1)S(1)}, f32[384,512]{1,0:T(8,128)S(1)}, bf16[384,512]{1,0:T(8,...) custom-call(bf16[256,512]{1,0:T(8,128)(2,1)S(1)} %collective-permute-done.6.refs_0_, ...), custom_call_target="tpu_custom_call" | custom-call | flops 603979776 | bytes 4718592 | tf_op jit(solution)/shard_map/attention_to_grad_query/pallas_call | solution.py:33
  17.9 0.5 %weight_gradient_of_own_events.1 = (f32[512,256]{1,0:T(8,128)S(1)}, bf16[512,384]{1,0:T(8,128)(2,1)S(1)}, f32[512,256]{1,0:T(8,128)S(1)}, bf16[512,384]{1,0:T(8,128)(2,1)S(1)}) custom-call(bf16[1024,768]{1,0:T(8,128)(2,1)S(1)} %get-tuple-element.56.events_ref, bf16[384,512]{1,0:T(8,128)(2,1)S(1)} %get-tuple-element.55.grad_query_ref), custom_call_target="tpu_custom_call" | custom-call | flops 201326592 | bytes 3145728 | tf_op jit(solution)/shard_map/weight_gradient_of_own_events/pallas_call | solution.py:33
  18.4 1.1 %collective-permute-done.8.grad_query_ref._ = bf16[384,512]{1,0:T(8,128)(2,1)S(1)} collective-permute-done((bf16[384,512]{1,0:T(8,128)(2,1)S(1)}, bf16[384,512]{1,0:T(8,128)(2,1)S(1)}, u32[]{:S(2)}, u32[]{:S(2)}) %collective-permute-start.8) | collective-permute-done | bytes 393248 | tf_op jit(solution)/shard_map/ppermute | solution.py:322
  20.0 2.3 %collective-permute-start.9 = (bf16[64,512]{1,0:T(8,128)(2,1)S(1)}, bf16[64,512]{1,0:T(8,128)(2,1)S(1)}, u32[]{:S(2)}, u32[]{:S(2)}) collective-permute-start(bf16[64,512]{1,0:T(8,128)(2,1)S(1)} %get-tuple-element.62), channel_id=1, source_target_pairs={{0,28},{1,29},{2,30},{3,31},{4,24},{5,25},{6,26},{7,27},{8,20},{9,... | collective-permute-start | bytes 196616 | tf_op jit(solution)/shard_map/ppermute | solution.py:334
  22.2 0.5 %collective-permute-start.10 = (bf16[64,512]{1,0:T(8,128)(2,1)S(1)}, bf16[64,512]{1,0:T(8,128)(2,1)S(1)}, u32[]{:S(2)}, u32[]{:S(2)}) collective-permute-start(bf16[64,512]{1,0:T(8,128)(2,1)S(1)} %get-tuple-element.63), channel_id=1, source_target_pairs={{0,20},{1,21},{2,22},{3,23},{4,16},{5,17},{6,18},{7,19},{8,28},{9,... | collective-permute-start | bytes 196616 | tf_op jit(solution)/shard_map/ppermute | solution.py:334
  23.0 2.4 %collective-permute-start.12 = (bf16[64,512]{1,0:T(8,128)(2,1)S(1)}, bf16[64,512]{1,0:T(8,128)(2,1)S(1)}, u32[]{:S(2)}, u32[]{:S(2)}) collective-permute-start(bf16[64,512]{1,0:T(8,128)(2,1)S(1)} %get-tuple-element.67), channel_id=1, source_target_pairs={{0,28},{1,29},{2,30},{3,31},{4,24},{5,25},{6,26},{7,27},{8,20},{9,... | collective-permute-start | bytes 196616 | tf_op jit(solution)/shard_map/ppermute | solution.py:334
  25.7 0.7 %collective-permute-start.14 = (bf16[64,512]{1,0:T(8,128)(2,1)S(1)}, bf16[64,512]{1,0:T(8,128)(2,1)S(1)}, u32[]{:S(2)}, u32[]{:S(2)}) collective-permute-start(bf16[64,512]{1,0:T(8,128)(2,1)S(1)} %get-tuple-element.69), channel_id=1, source_target_pairs={{0,12},{1,13},{2,14},{3,15},{4,8},{5,9},{6,10},{7,11},{8,4},{9,5},... | collective-permute-start | bytes 196616 | tf_op jit(solution)/shard_map/ppermute | solution.py:334
  26.8 3.3 %collective-permute-start.16 = (bf16[64,256]{1,0:T(8,128)(2,1)S(1)}, bf16[64,256]{1,0:T(8,128)(2,1)S(1)}, u32[]{:S(2)}, u32[]{:S(2)}) collective-permute-start(bf16[64,256]{1,0:T(8,128)(2,1)S(1)} %get-tuple-element.81), channel_id=1, source_target_pairs={{0,7},{1,6},{2,5},{3,4},{4,3},{5,2},{6,1},{7,0},{8,15},{9,14},{10,... | collective-permute-start | bytes 98312 | tf_op jit(solution)/shard_map/ppermute | solution.py:334
  30.1 0.7 %collective-permute-done.13.refs_2_ = bf16[64,512]{1,0:T(8,128)(2,1)S(1)} collective-permute-done((bf16[64,512]{1,0:T(8,128)(2,1)S(1)}, bf16[64,512]{1,0:T(8,128)(2,1)S(1)}, u32[]{:S(2)}, u32[]{:S(2)}) %collective-permute-start.13) | collective-permute-done | bytes 65568 | tf_op jit(solution)/shard_map/ppermute | solution.py:334
  30.9 1.2 %collective-permute-start.15 = (bf16[64,256]{1,0:T(8,128)(2,1)S(1)}, bf16[64,256]{1,0:T(8,128)(2,1)S(1)}, u32[]{:S(2)}, u32[]{:S(2)}) collective-permute-start(bf16[64,256]{1,0:T(8,128)(2,1)S(1)} %get-tuple-element.70._), channel_id=1, source_target_pairs={{0,5},{1,4},{2,7},{3,6},{4,1},{5,0},{6,3},{7,2},{8,13},{9,12},{10,... | collective-permute-start | bytes 98312 | tf_op jit(solution)/shard_map/ppermute | solution.py:334
  32.0 1.4 %key_value_gate_gradients.1 = (bf16[384,512]{1,0:T(8,128)(2,1)}, bf16[384,512]{1,0:T(8,128)(2,1)}, bf16[384,512]{1,0:T(8,128)(2,1)}) custom-call(bf16[64,256]{1,0:T(8,128)(2,1)S(1)} %get-tuple-element.70._, bf16[384,512]{1,0:T(8,128)(2,1)S(1)} %get-tuple-element.71.query_ref, f32[384,512]{1,0:T(8,128)S(1)} %get-tuple-element.72.normed_ref, ...), custom_call_target="tpu_custom_call" | custom-call | flops 100663296 | bytes 2359296 | tf_op jit(solution)/shard_map/key_value_gate_gradients/pallas_call | solution.py:33
  33.5 1.0 %collective-permute-done.17.refs_3_ = bf16[64,256]{1,0:T(8,128)(2,1)S(1)} collective-permute-done((bf16[64,256]{1,0:T(8,128)(2,1)S(1)}, bf16[64,256]{1,0:T(8,128)(2,1)S(1)}, u32[]{:S(2)}, u32[]{:S(2)}) %collective-permute-start.17) | collective-permute-done | bytes 32800 | tf_op jit(solution)/shard_map/ppermute | solution.py:334
  34.5 0.7 %collective-permute-done.15.refs_1_ = bf16[64,256]{1,0:T(8,128)(2,1)S(1)} collective-permute-done((bf16[64,256]{1,0:T(8,128)(2,1)S(1)}, bf16[64,256]{1,0:T(8,128)(2,1)S(1)}, u32[]{:S(2)}, u32[]{:S(2)}) %collective-permute-start.15) | collective-permute-done | bytes 32800 | tf_op jit(solution)/shard_map/ppermute | solution.py:334
  35.2 1.4 %collective-permute-start.20 = (bf16[64,256]{1,0:T(8,128)(2,1)S(1)}, bf16[64,256]{1,0:T(8,128)(2,1)S(1)}, u32[]{:S(2)}, u32[]{:S(2)}) collective-permute-start(bf16[64,256]{1,0:T(8,128)(2,1)S(1)} %mean_over_shards.1._.refs_0_), channel_id=1, source_target_pairs={{0,28},{1,29},{2,30},{3,31},{4,24},{5,25},{6,26},{7,27},{8,20},{9,... | collective-permute-start | bytes 98312 | tf_op jit(solution)/shard_map/ppermute | solution.py:334
  36.5 1.6 %collective-permute-start.18 = (bf16[64,256]{1,0:T(8,128)(2,1)S(1)}, bf16[64,256]{1,0:T(8,128)(2,1)S(1)}, u32[]{:S(2)}, u32[]{:S(2)}) collective-permute-start(bf16[64,256]{1,0:T(8,128)(2,1)S(1)} %mean_over_shards.1._.refs_0_), channel_id=1, source_target_pairs={{0,12},{1,13},{2,14},{3,15},{4,8},{5,9},{6,10},{7,11},{8,4},{9,5},... | collective-permute-start | bytes 98312 | tf_op jit(solution)/shard_map/ppermute | solution.py:334
  38.1 1.4 %collective-permute-done.20.refs_3_ = bf16[64,256]{1,0:T(8,128)(2,1)S(1)} collective-permute-done((bf16[64,256]{1,0:T(8,128)(2,1)S(1)}, bf16[64,256]{1,0:T(8,128)(2,1)S(1)}, u32[]{:S(2)}, u32[]{:S(2)}) %collective-permute-start.20) | collective-permute-done | bytes 32800 | tf_op jit(solution)/shard_map/ppermute | solution.py:334
  39.5 0.7 %collective-permute-done.19.refs_2_ = bf16[64,256]{1,0:T(8,128)(2,1)S(1)} collective-permute-done((bf16[64,256]{1,0:T(8,128)(2,1)S(1)}, bf16[64,256]{1,0:T(8,128)(2,1)S(1)}, u32[]{:S(2)}, u32[]{:S(2)}) %collective-permute-start.19) | collective-permute-done | bytes 32800 | tf_op jit(solution)/shard_map/ppermute | solution.py:334
  40.4 0.7 %blocks_of_own_core_in_place.1.refs_0_ = f32[256,512]{1,0:T(8,128)} custom-call(bf16[256,256]{1,0:T(8,128)(2,1)S(1)} %blocks_of_chips.1.blocks_ref), custom_call_target="tpu_custom_call" | custom-call | tf_op jit(solution)/shard_map/blocks_of_own_core_in_place/pallas_call | solution.py:33
  41.2 0.5 %collective-permute-done.21.blocks_ref = bf16[256,256]{1,0:T(8,128)(2,1)S(1)} collective-permute-done((bf16[256,256]{1,0:T(8,128)(2,1)S(1)}, bf16[256,256]{1,0:T(8,128)(2,1)S(1)}, u32[]{:S(2)}, u32[]{:S(2)}) %collective-permute-start.21) | collective-permute-done | bytes 131104 | tf_op jit(solution)/shard_map/ppermute | solution.py:322
  41.6 0.7 %blocks_of_sibling_core_in_place.1 = f32[256,512]{1,0:T(8,128)} custom-call(bf16[256,256]{1,0:T(8,128)(2,1)S(1)} %collective-permute-done.21.blocks_ref, f32[256,512]{1,0:T(8,128)} %blocks_of_own_core_in_place.1.refs_0_), custom_call_target="tpu_custom_call", output_to_operand_aliasing={{}: (1, {})} | custom-call | tf_op jit(solution)/shard_map/blocks_of_sibling_core_in_place/pallas_call | solution.py:33
  (27 shorter events, 2.9 us)
Async XLA Ops:
  0.6 9.7 %collective-permute-start.2 = (bf16[384,1024]{1,0:T(8,128)(2,1)}, bf16[384,1024]{1,0:T(8,128)(2,1)S(1)}, u32[]{:S(2)}, u32[]{:S(2)}) collective-permute-start(bf16[384,1024]{1,0:T(8,128)(2,1)} %bitcast.9), channel_id=1, source_target_pairs={{0,4},{4,0},{8,12},{12,8},{16,20},{20,16},{24,28},{28,24},{1,5},{5... | collective-permute-start | bytes 2359304 | tf_op jit(solution)/shard_map/ppermute | solution.py:322
  1.9 5.5 %collective-permute-start.1 = (bf16[32,512]{1,0:T(8,128)(2,1)S(1)}, bf16[32,512]{1,0:T(8,128)(2,1)S(1)}, u32[]{:S(2)}, u32[]{:S(2)}) collective-permute-start(bf16[32,512]{1,0:T(8,128)(2,1)S(1)} %own_part_of_weight.1), channel_id=1, source_target_pairs={{0,6},{1,7},{2,4},{3,5},{4,2},{5,3},{6,0},{7,1},{8,14},{9,15},{10,... | collective-permute-start | bytes 98312 | tf_op jit(solution)/shard_map/ppermute | solution.py:334
  5.7 9.0 %collective-permute-start = (bf16[256,512]{1,0:T(8,128)(2,1)}, bf16[256,512]{1,0:T(8,128)(2,1)S(1)}, u32[]{:S(2)}, u32[]{:S(2)}) collective-permute-start(bf16[256,512]{1,0:T(8,128)(2,1)} %refs_4_.1), channel_id=1, source_target_pairs={{0,5},{1,4},{2,7},{3,6},{4,3},{5,2},{6,1},{7,0},{8,13},{9,12},{10,... | collective-permute-start | bytes 786440 | tf_op jit(solution)/shard_map/ppermute | solution.py:334
  7.4 5.3 %collective-permute-start.5 = (bf16[32,512]{1,0:T(8,128)(2,1)S(1)}, bf16[32,512]{1,0:T(8,128)(2,1)S(1)}, u32[]{:S(2)}, u32[]{:S(2)}) collective-permute-start(bf16[32,512]{1,0:T(8,128)(2,1)S(1)} %collective-permute-done.1._.refs_0_), channel_id=1, source_target_pairs={{0,28},{1,29},{2,30},{3,31},{4,24},{5,25},{6,26},{7,27},{8,20},{9,... | collective-permute-start | bytes 98312 | tf_op jit(solution)/shard_map/ppermute | solution.py:334
  9.8 3.4 %collective-permute-start.4 = (bf16[32,512]{1,0:T(8,128)(2,1)S(1)}, bf16[32,512]{1,0:T(8,128)(2,1)S(1)}, u32[]{:S(2)}, u32[]{:S(2)}) collective-permute-start(bf16[32,512]{1,0:T(8,128)(2,1)S(1)} %collective-permute-done.1._.refs_0_), channel_id=1, source_target_pairs={{0,20},{1,21},{2,22},{3,23},{4,16},{5,17},{6,18},{7,19},{8,28},{9,... | collective-permute-start | bytes 98312 | tf_op jit(solution)/shard_map/ppermute | solution.py:334
  10.0 3.3 %collective-permute-start.3 = (bf16[32,512]{1,0:T(8,128)(2,1)S(1)}, bf16[32,512]{1,0:T(8,128)(2,1)S(1)}, u32[]{:S(2)}, u32[]{:S(2)}) collective-permute-start(bf16[32,512]{1,0:T(8,128)(2,1)S(1)} %collective-permute-done.1._.refs_0_), channel_id=1, source_target_pairs={{0,12},{1,13},{2,14},{3,15},{4,8},{5,9},{6,10},{7,11},{8,4},{9,5},... | collective-permute-start | bytes 98312 | tf_op jit(solution)/shard_map/ppermute | solution.py:334
  13.3 2.0 %collective-permute-start.7 = (bf16[128,512]{1,0:T(8,128)(2,1)S(1)}, bf16[128,512]{1,0:T(8,128)(2,1)S(1)}, u32[]{:S(2)}, u32[]{:S(2)}) collective-permute-start(bf16[128,512]{1,0:T(8,128)(2,1)S(1)} %parts_of_weight.1.refs_1_), channel_id=1, source_target_pairs={{0,4},{4,0},{8,12},{12,8},{16,20},{20,16},{24,28},{28,24},{1,5},{5... | collective-permute-start | bytes 393224 | tf_op jit(solution)/shard_map/ppermute | solution.py:322
  14.7 1.5 %collective-permute-start.6 = (bf16[256,512]{1,0:T(8,128)(2,1)S(1)}, bf16[256,512]{1,0:T(8,128)(2,1)S(1)}, u32[]{:S(2)}, u32[]{:S(2)}) collective-permute-start(bf16[256,512]{1,0:T(8,128)(2,1)S(1)} %collective-permute-done.refs_2_), channel_id=1, source_target_pairs={{0,4},{4,0},{8,12},{12,8},{16,20},{20,16},{24,28},{28,24},{1,5},{5... | collective-permute-start | bytes 786440 | tf_op jit(solution)/shard_map/ppermute | solution.py:322
  17.7 1.8 %collective-permute-start.8 = (bf16[384,512]{1,0:T(8,128)(2,1)S(1)}, bf16[384,512]{1,0:T(8,128)(2,1)S(1)}, u32[]{:S(2)}, u32[]{:S(2)}) collective-permute-start(bf16[384,512]{1,0:T(8,128)(2,1)S(1)} %get-tuple-element.55.grad_query_ref), channel_id=1, source_target_pairs={{0,4},{4,0},{8,12},{12,8},{16,20},{20,16},{24,28},{28,24},{1,5},{5... | collective-permute-start | bytes 1179656 | tf_op jit(solution)/shard_map/ppermute | solution.py:322
  20.0 5.7 %collective-permute-start.9 = (bf16[64,512]{1,0:T(8,128)(2,1)S(1)}, bf16[64,512]{1,0:T(8,128)(2,1)S(1)}, u32[]{:S(2)}, u32[]{:S(2)}) collective-permute-start(bf16[64,512]{1,0:T(8,128)(2,1)S(1)} %get-tuple-element.62), channel_id=1, source_target_pairs={{0,28},{1,29},{2,30},{3,31},{4,24},{5,25},{6,26},{7,27},{8,20},{9,... | collective-permute-start | bytes 196616 | tf_op jit(solution)/shard_map/ppermute | solution.py:334
  22.2 4.1 %collective-permute-start.10 = (bf16[64,512]{1,0:T(8,128)(2,1)S(1)}, bf16[64,512]{1,0:T(8,128)(2,1)S(1)}, u32[]{:S(2)}, u32[]{:S(2)}) collective-permute-start(bf16[64,512]{1,0:T(8,128)(2,1)S(1)} %get-tuple-element.63), channel_id=1, source_target_pairs={{0,20},{1,21},{2,22},{3,23},{4,16},{5,17},{6,18},{7,19},{8,28},{9,... | collective-permute-start | bytes 196616 | tf_op jit(solution)/shard_map/ppermute | solution.py:334
  22.7 4.0 %collective-permute-start.11 = (bf16[64,512]{1,0:T(8,128)(2,1)S(1)}, bf16[64,512]{1,0:T(8,128)(2,1)S(1)}, u32[]{:S(2)}, u32[]{:S(2)}) collective-permute-start(bf16[64,512]{1,0:T(8,128)(2,1)S(1)} %get-tuple-element.64), channel_id=1, source_target_pairs={{0,12},{1,13},{2,14},{3,15},{4,8},{5,9},{6,10},{7,11},{8,4},{9,5},... | collective-permute-start | bytes 196616 | tf_op jit(solution)/shard_map/ppermute | solution.py:334
  23.0 7.1 %collective-permute-start.12 = (bf16[64,512]{1,0:T(8,128)(2,1)S(1)}, bf16[64,512]{1,0:T(8,128)(2,1)S(1)}, u32[]{:S(2)}, u32[]{:S(2)}) collective-permute-start(bf16[64,512]{1,0:T(8,128)(2,1)S(1)} %get-tuple-element.67), channel_id=1, source_target_pairs={{0,28},{1,29},{2,30},{3,31},{4,24},{5,25},{6,26},{7,27},{8,20},{9,... | collective-permute-start | bytes 196616 | tf_op jit(solution)/shard_map/ppermute | solution.py:334
  25.4 5.4 %collective-permute-start.13 = (bf16[64,512]{1,0:T(8,128)(2,1)S(1)}, bf16[64,512]{1,0:T(8,128)(2,1)S(1)}, u32[]{:S(2)}, u32[]{:S(2)}) collective-permute-start(bf16[64,512]{1,0:T(8,128)(2,1)S(1)} %get-tuple-element.68), channel_id=1, source_target_pairs={{0,20},{1,21},{2,22},{3,23},{4,16},{5,17},{6,18},{7,19},{8,28},{9,... | collective-permute-start | bytes 196616 | tf_op jit(solution)/shard_map/ppermute | solution.py:334
  25.7 5.1 %collective-permute-start.14 = (bf16[64,512]{1,0:T(8,128)(2,1)S(1)}, bf16[64,512]{1,0:T(8,128)(2,1)S(1)}, u32[]{:S(2)}, u32[]{:S(2)}) collective-permute-start(bf16[64,512]{1,0:T(8,128)(2,1)S(1)} %get-tuple-element.69), channel_id=1, source_target_pairs={{0,12},{1,13},{2,14},{3,15},{4,8},{5,9},{6,10},{7,11},{8,4},{9,5},... | collective-permute-start | bytes 196616 | tf_op jit(solution)/shard_map/ppermute | solution.py:334
  26.8 6.7 %collective-permute-start.16 = (bf16[64,256]{1,0:T(8,128)(2,1)S(1)}, bf16[64,256]{1,0:T(8,128)(2,1)S(1)}, u32[]{:S(2)}, u32[]{:S(2)}) collective-permute-start(bf16[64,256]{1,0:T(8,128)(2,1)S(1)} %get-tuple-element.81), channel_id=1, source_target_pairs={{0,7},{1,6},{2,5},{3,4},{4,3},{5,2},{6,1},{7,0},{8,15},{9,14},{10,... | collective-permute-start | bytes 98312 | tf_op jit(solution)/shard_map/ppermute | solution.py:334
  30.1 4.3 %collective-permute-start.17 = (bf16[64,256]{1,0:T(8,128)(2,1)S(1)}, bf16[64,256]{1,0:T(8,128)(2,1)S(1)}, u32[]{:S(2)}, u32[]{:S(2)}) collective-permute-start(bf16[64,256]{1,0:T(8,128)(2,1)S(1)} %get-tuple-element.65._), channel_id=1, source_target_pairs={{0,6},{1,7},{2,4},{3,5},{4,2},{5,3},{6,0},{7,1},{8,14},{9,15},{10,... | collective-permute-start | bytes 98312 | tf_op jit(solution)/shard_map/ppermute | solution.py:334
  30.9 4.3 %collective-permute-start.15 = (bf16[64,256]{1,0:T(8,128)(2,1)S(1)}, bf16[64,256]{1,0:T(8,128)(2,1)S(1)}, u32[]{:S(2)}, u32[]{:S(2)}) collective-permute-start(bf16[64,256]{1,0:T(8,128)(2,1)S(1)} %get-tuple-element.70._), channel_id=1, source_target_pairs={{0,5},{1,4},{2,7},{3,6},{4,1},{5,0},{6,3},{7,2},{8,13},{9,12},{10,... | collective-permute-start | bytes 98312 | tf_op jit(solution)/shard_map/ppermute | solution.py:334
  35.2 4.4 %collective-permute-start.20 = (bf16[64,256]{1,0:T(8,128)(2,1)S(1)}, bf16[64,256]{1,0:T(8,128)(2,1)S(1)}, u32[]{:S(2)}, u32[]{:S(2)}) collective-permute-start(bf16[64,256]{1,0:T(8,128)(2,1)S(1)} %mean_over_shards.1._.refs_0_), channel_id=1, source_target_pairs={{0,28},{1,29},{2,30},{3,31},{4,24},{5,25},{6,26},{7,27},{8,20},{9,... | collective-permute-start | bytes 98312 | tf_op jit(solution)/shard_map/ppermute | solution.py:334
  36.5 3.7 %collective-permute-start.19 = (bf16[64,256]{1,0:T(8,128)(2,1)S(1)}, bf16[64,256]{1,0:T(8,128)(2,1)S(1)}, u32[]{:S(2)}, u32[]{:S(2)}) collective-permute-start(bf16[64,256]{1,0:T(8,128)(2,1)S(1)} %mean_over_shards.1._.refs_0_), channel_id=1, source_target_pairs={{0,20},{1,21},{2,22},{3,23},{4,16},{5,17},{6,18},{7,19},{8,28},{9,... | collective-permute-start | bytes 98312 | tf_op jit(solution)/shard_map/ppermute | solution.py:334
  36.5 3.7 %collective-permute-start.18 = (bf16[64,256]{1,0:T(8,128)(2,1)S(1)}, bf16[64,256]{1,0:T(8,128)(2,1)S(1)}, u32[]{:S(2)}, u32[]{:S(2)}) collective-permute-start(bf16[64,256]{1,0:T(8,128)(2,1)S(1)} %mean_over_shards.1._.refs_0_), channel_id=1, source_target_pairs={{0,12},{1,13},{2,14},{3,15},{4,8},{5,9},{6,10},{7,11},{8,4},{9,5},... | collective-permute-start | bytes 98312 | tf_op jit(solution)/shard_map/ppermute | solution.py:334
  40.2 1.4 %collective-permute-start.21 = (bf16[256,256]{1,0:T(8,128)(2,1)S(1)}, bf16[256,256]{1,0:T(8,128)(2,1)S(1)}, u32[]{:S(2)}, u32[]{:S(2)}) collective-permute-start(bf16[256,256]{1,0:T(8,128)(2,1)S(1)} %blocks_of_chips.1.blocks_ref), channel_id=1, source_target_pairs={{0,4},{4,0},{8,12},{12,8},{16,20},{20,16},{24,28},{28,24},{1,5},{5... | collective-permute-start | bytes 393224 | tf_op jit(solution)/shard_map/ppermute | solution.py:322

commit v16 on v15

--- a/solution.py
+++ b/solution.py
@@ -515,7 +515,7 @@
                 tuple(shape(part_rows, half_width, dtype=bf16 if z else f32) for z in flips),
             )
 
-        sets = (tuple(range(2, fsdp_count)), (0, 1))
+        sets = (tuple(range(fsdp_count - 1, 1, -1)), (0, 1))
         picked_rows = [len(flips) * shard_rows for flips in sets]
         got = flip(grad_query, "dp", dp_count, 1)
         own_terms = call(

time: 42.6 us -> 43.1 us (1.012)
  transfers between devices with their start and end apart: 22 -> 22, of which waited for: 13 -> 14; matrix products, arithmetic and copies ran while one was open for 0% -> 0% of each run, Pallas kernels for 16% -> 16%
where the time goes in v16:
time: 43.1 us; the launch traced here: 42.9 us
  starting transfers between devices  23.7 us (55%)
  Pallas kernels  9.4 us (22%)
  waiting for transfers between devices  9.08 us (21%)
  between operations  0.74 us (2%)
    ppermute x17, starting transfers between devices, cross(): return lax.ppermute(block, BOTH, pairs)  22 us
    pallas_call x15, Pallas kernels, call(): pl.pallas_call(kernel, out_shape=out_shape, in_specs=in_specs, out_specs=...  9.4 us
    ppermute x17, waiting for transfers between devices, cross(): return lax.ppermute(block, BOTH, pairs)  6.89 us
    ppermute x5, waiting for transfers between devices, flip(): return lax.ppermute(block, axis, [(i, i ^ bits) for i in range(count)])  2.2 us
    ppermute x5, starting transfers between devices, flip(): return lax.ppermute(block, axis, [(i, i ^ bits) for i in range(count)])  1.71 us
  transfers between devices with their start and end apart: 22, of which 14 were waited for; matrix products, arithmetic and copies ran while one was open for 0% of the time, Pallas kernels for 16%

profile of v16, /device:TPU:0, one launch (start us, length us, event | category | flops | bytes accessed | tf_op | source)
XLA Modules:
  0.0 42.9 jit_solution(16506974463641322823)
XLA Ops:
  0.6 0.5 %collective-permute-start.2 = (bf16[384,1024]{1,0:T(8,128)(2,1)}, bf16[384,1024]{1,0:T(8,128)(2,1)S(1)}, u32[]{:S(2)}, u32[]{:S(2)}) collective-permute-start(bf16[384,1024]{1,0:T(8,128)(2,1)} %bitcast.9), channel_id=1, source_target_pairs={{0,4},{4,0},{8,12},{12,8},{16,20},{20,16},{24,28},{28,24},{1,5},{5... | collective-permute-start | bytes 2359304 | tf_op jit(solution)/shard_map/ppermute | solution.py:322
  1.1 0.8 %own_part_of_weight.1 = bf16[32,512]{1,0:T(8,128)(2,1)S(1)} custom-call(bf16[256,512]{1,0:T(8,128)(2,1)} %refs_4_.1), custom_call_target="tpu_custom_call" | custom-call | tf_op jit(solution)/shard_map/own_part_of_weight/pallas_call | solution.py:33
  1.9 3.8 %collective-permute-start.1 = (bf16[32,512]{1,0:T(8,128)(2,1)S(1)}, bf16[32,512]{1,0:T(8,128)(2,1)S(1)}, u32[]{:S(2)}, u32[]{:S(2)}) collective-permute-start(bf16[32,512]{1,0:T(8,128)(2,1)S(1)} %own_part_of_weight.1), channel_id=1, source_target_pairs={{0,6},{1,7},{2,4},{3,5},{4,2},{5,3},{6,0},{7,1},{8,14},{9,15},{10,... | collective-permute-start | bytes 98312 | tf_op jit(solution)/shard_map/ppermute | solution.py:334
  5.7 1.2 %collective-permute-start = (bf16[256,512]{1,0:T(8,128)(2,1)}, bf16[256,512]{1,0:T(8,128)(2,1)S(1)}, u32[]{:S(2)}, u32[]{:S(2)}) collective-permute-start(bf16[256,512]{1,0:T(8,128)(2,1)} %refs_4_.1), channel_id=1, source_target_pairs={{0,5},{1,4},{2,7},{3,6},{4,3},{5,2},{6,1},{7,0},{8,13},{9,12},{10,... | collective-permute-start | bytes 786440 | tf_op jit(solution)/shard_map/ppermute | solution.py:334
  6.9 0.5 %collective-permute-done.1._.refs_0_ = bf16[32,512]{1,0:T(8,128)(2,1)S(1)} collective-permute-done((bf16[32,512]{1,0:T(8,128)(2,1)S(1)}, bf16[32,512]{1,0:T(8,128)(2,1)S(1)}, u32[]{:S(2)}, u32[]{:S(2)}) %collective-permute-start.1) | collective-permute-done | bytes 32800 | tf_op jit(solution)/shard_map/ppermute | solution.py:334
  7.4 2.4 %collective-permute-start.5 = (bf16[32,512]{1,0:T(8,128)(2,1)S(1)}, bf16[32,512]{1,0:T(8,128)(2,1)S(1)}, u32[]{:S(2)}, u32[]{:S(2)}) collective-permute-start(bf16[32,512]{1,0:T(8,128)(2,1)S(1)} %collective-permute-done.1._.refs_0_), channel_id=1, source_target_pairs={{0,28},{1,29},{2,30},{3,31},{4,24},{5,25},{6,26},{7,27},{8,20},{9,... | collective-permute-start | bytes 98312 | tf_op jit(solution)/shard_map/ppermute | solution.py:334
  10.4 2.3 %prepared_operands.1 = (bf16[384,1024]{1,0:T(8,128)(2,1)S(1)}, bf16[384,512]{1,0:T(8,128)(2,1)S(1)}, bf16[384,512]{1,0:T(8,128)(2,1)S(1)}, bf16[384,512]{1,0:T(8...) custom-call(bf16[32,512]{1,0:T(8,128)(2,1)S(1)} %collective-permute-, ...), custom_call_target="tpu_custom_call" | custom-call | flops 5000000000 | tf_op jit(solution)/shard_map/prepared_operands/pallas_call | solution.py:33
  12.7 0.5 %collective-permute-done.4.refs_2_ = bf16[32,512]{1,0:T(8,128)(2,1)S(1)} collective-permute-done((bf16[32,512]{1,0:T(8,128)(2,1)S(1)}, bf16[32,512]{1,0:T(8,128)(2,1)S(1)}, u32[]{:S(2)}, u32[]{:S(2)}) %collective-permute-start.4) | collective-permute-done | bytes 32800 | tf_op jit(solution)/shard_map/ppermute | solution.py:334
  13.3 0.8 %collective-permute-start.7 = (bf16[128,512]{1,0:T(8,128)(2,1)S(1)}, bf16[128,512]{1,0:T(8,128)(2,1)S(1)}, u32[]{:S(2)}, u32[]{:S(2)}) collective-permute-start(bf16[128,512]{1,0:T(8,128)(2,1)S(1)} %parts_of_weight.1.refs_1_), channel_id=1, source_target_pairs={{0,4},{4,0},{8,12},{12,8},{16,20},{20,16},{24,28},{28,24},{1,5},{5... | collective-permute-start | bytes 393224 | tf_op jit(solution)/shard_map/ppermute | solution.py:322
  14.1 0.6 %collective-permute-done.refs_2_ = bf16[256,512]{1,0:T(8,128)(2,1)S(1)} collective-permute-done((bf16[256,512]{1,0:T(8,128)(2,1)}, bf16[256,512]{1,0:T(8,128)(2,1)S(1)}, u32[]{:S(2)}, u32[]{:S(2)}) %collective-permute-start) | collective-permute-done | bytes 262176 | tf_op jit(solution)/shard_map/ppermute | solution.py:334
  14.7 0.6 %projection_by_held_rows.1.refs_2_ = f32[384,512]{1,0:T(8,128)S(1)} custom-call(bf16[256,512]{1,0:T(8,128)(2,1)S(1)} %get-tuple-element.48.refs_0_, bf16[128,512]{1,0:T(8,128)(2,1)S(1)} %parts_of_weight.1.refs_1_, bf16[256,512]{1,0:T(8,128)(2,1)S(1)} %collective-permute-done.refs_2_, bf16[384,1024]{1,0:T(8,128)(2,1)S(1)} %get-tuple-element.47.refs_3_.refs_1_.refs_2_), custom_call_target="tpu_custom_call" | custom-call | flops 301989888 | bytes 786432 | tf_op jit(solution)/shard_map/projection_by_held_rows/pallas_call | solution.py:33
  15.6 0.6 %collective-permute-done.6.refs_0_ = bf16[256,512]{1,0:T(8,128)(2,1)S(1)} collective-permute-done((bf16[256,512]{1,0:T(8,128)(2,1)S(1)}, bf16[256,512]{1,0:T(8,128)(2,1)S(1)}, u32[]{:S(2)}, u32[]{:S(2)}) %collective-permute-start.6) | collective-permute-done | bytes 262176 | tf_op jit(solution)/shard_map/ppermute | solution.py:322
  16.2 1.5 %attention_to_grad_query.1 = (bf16[384,512]{1,0:T(8,128)(2,1)S(1)}, bf16[384,512]{1,0:T(8,128)(2,1)S(1)}, f32[384,512]{1,0:T(8,128)S(1)}, bf16[384,512]{1,0:T(8,...) custom-call(bf16[256,512]{1,0:T(8,128)(2,1)S(1)} %collective-permute-done.6.refs_0_, ...), custom_call_target="tpu_custom_call" | custom-call | flops 603979776 | bytes 4718592 | tf_op jit(solution)/shard_map/attention_to_grad_query/pallas_call | solution.py:33
  17.9 0.5 %weight_gradient_of_own_events.1 = (f32[512,256]{1,0:T(8,128)S(1)}, bf16[512,384]{1,0:T(8,128)(2,1)S(1)}, f32[512,256]{1,0:T(8,128)S(1)}, bf16[512,384]{1,0:T(8,128)(2,1)S(1)}) custom-call(bf16[1024,768]{1,0:T(8,128)(2,1)S(1)} %get-tuple-element.56.events_ref, bf16[384,512]{1,0:T(8,128)(2,1)S(1)} %get-tuple-element.55.grad_query_ref), custom_call_target="tpu_custom_call" | custom-call | flops 201326592 | bytes 3145728 | tf_op jit(solution)/shard_map/weight_gradient_of_own_events/pallas_call | solution.py:33
  18.4 1.1 %collective-permute-done.8.grad_query_ref._ = bf16[384,512]{1,0:T(8,128)(2,1)S(1)} collective-permute-done((bf16[384,512]{1,0:T(8,128)(2,1)S(1)}, bf16[384,512]{1,0:T(8,128)(2,1)S(1)}, u32[]{:S(2)}, u32[]{:S(2)}) %collective-permute-start.8) | collective-permute-done | bytes 393248 | tf_op jit(solution)/shard_map/ppermute | solution.py:322
  20.0 2.3 %collective-permute-start.9 = (bf16[64,512]{1,0:T(8,128)(2,1)S(1)}, bf16[64,512]{1,0:T(8,128)(2,1)S(1)}, u32[]{:S(2)}, u32[]{:S(2)}) collective-permute-start(bf16[64,512]{1,0:T(8,128)(2,1)S(1)} %get-tuple-element.62), channel_id=1, source_target_pairs={{0,28},{1,29},{2,30},{3,31},{4,24},{5,25},{6,26},{7,27},{8,20},{9,... | collective-permute-start | bytes 196616 | tf_op jit(solution)/shard_map/ppermute | solution.py:334
  23.0 2.4 %collective-permute-start.12 = (bf16[64,512]{1,0:T(8,128)(2,1)S(1)}, bf16[64,512]{1,0:T(8,128)(2,1)S(1)}, u32[]{:S(2)}, u32[]{:S(2)}) collective-permute-start(bf16[64,512]{1,0:T(8,128)(2,1)S(1)} %get-tuple-element.67), channel_id=1, source_target_pairs={{0,28},{1,29},{2,30},{3,31},{4,24},{5,25},{6,26},{7,27},{8,20},{9,... | collective-permute-start | bytes 196616 | tf_op jit(solution)/shard_map/ppermute | solution.py:334
  25.7 0.7 %collective-permute-start.14 = (bf16[64,512]{1,0:T(8,128)(2,1)S(1)}, bf16[64,512]{1,0:T(8,128)(2,1)S(1)}, u32[]{:S(2)}, u32[]{:S(2)}) collective-permute-start(bf16[64,512]{1,0:T(8,128)(2,1)S(1)} %get-tuple-element.69), channel_id=1, source_target_pairs={{0,12},{1,13},{2,14},{3,15},{4,8},{5,9},{6,10},{7,11},{8,4},{9,5},... | collective-permute-start | bytes 196616 | tf_op jit(solution)/shard_map/ppermute | solution.py:334
  26.8 1.6 %collective-permute-start.16 = (bf16[64,256]{1,0:T(8,128)(2,1)S(1)}, bf16[64,256]{1,0:T(8,128)(2,1)S(1)}, u32[]{:S(2)}, u32[]{:S(2)}) collective-permute-start(bf16[64,256]{1,0:T(8,128)(2,1)S(1)} %get-tuple-element.81), channel_id=1, source_target_pairs={{0,6},{1,7},{2,4},{3,5},{4,2},{5,3},{6,0},{7,1},{8,14},{9,15},{10,... | collective-permute-start | bytes 98312 | tf_op jit(solution)/shard_map/ppermute | solution.py:334
  28.4 1.9 %collective-permute-start.17 = (bf16[64,256]{1,0:T(8,128)(2,1)S(1)}, bf16[64,256]{1,0:T(8,128)(2,1)S(1)}, u32[]{:S(2)}, u32[]{:S(2)}) collective-permute-start(bf16[64,256]{1,0:T(8,128)(2,1)S(1)} %get-tuple-element.65._), channel_id=1, source_target_pairs={{0,7},{1,6},{2,5},{3,4},{4,3},{5,2},{6,1},{7,0},{8,15},{9,14},{10,... | collective-permute-start | bytes 98312 | tf_op jit(solution)/shard_map/ppermute | solution.py:334
  30.3 0.5 %collective-permute-done.13.refs_2_ = bf16[64,512]{1,0:T(8,128)(2,1)S(1)} collective-permute-done((bf16[64,512]{1,0:T(8,128)(2,1)S(1)}, bf16[64,512]{1,0:T(8,128)(2,1)S(1)}, u32[]{:S(2)}, u32[]{:S(2)}) %collective-permute-start.13) | collective-permute-done | bytes 65568 | tf_op jit(solution)/shard_map/ppermute | solution.py:334
  30.9 1.2 %collective-permute-start.15 = (bf16[64,256]{1,0:T(8,128)(2,1)S(1)}, bf16[64,256]{1,0:T(8,128)(2,1)S(1)}, u32[]{:S(2)}, u32[]{:S(2)}) collective-permute-start(bf16[64,256]{1,0:T(8,128)(2,1)S(1)} %get-tuple-element.70._), channel_id=1, source_target_pairs={{0,5},{1,4},{2,7},{3,6},{4,1},{5,0},{6,3},{7,2},{8,13},{9,12},{10,... | collective-permute-start | bytes 98312 | tf_op jit(solution)/shard_map/ppermute | solution.py:334
  32.0 1.4 %key_value_gate_gradients.1 = (bf16[384,512]{1,0:T(8,128)(2,1)}, bf16[384,512]{1,0:T(8,128)(2,1)}, bf16[384,512]{1,0:T(8,128)(2,1)}) custom-call(bf16[64,256]{1,0:T(8,128)(2,1)S(1)} %get-tuple-element.70._, bf16[384,512]{1,0:T(8,128)(2,1)S(1)} %get-tuple-element.71.query_ref, f32[384,512]{1,0:T(8,128)S(1)} %get-tuple-element.72.normed_ref, ...), custom_call_target="tpu_custom_call" | custom-call | flops 100663296 | bytes 2359296 | tf_op jit(solution)/shard_map/key_value_gate_gradients/pallas_call | solution.py:33
  33.7 1.0 %collective-permute-done.15.refs_1_ = bf16[64,256]{1,0:T(8,128)(2,1)S(1)} collective-permute-done((bf16[64,256]{1,0:T(8,128)(2,1)S(1)}, bf16[64,256]{1,0:T(8,128)(2,1)S(1)}, u32[]{:S(2)}, u32[]{:S(2)}) %collective-permute-start.15) | collective-permute-done | bytes 32800 | tf_op jit(solution)/shard_map/ppermute | solution.py:334
  34.7 1.8 %collective-permute-start.20 = (bf16[64,256]{1,0:T(8,128)(2,1)S(1)}, bf16[64,256]{1,0:T(8,128)(2,1)S(1)}, u32[]{:S(2)}, u32[]{:S(2)}) collective-permute-start(bf16[64,256]{1,0:T(8,128)(2,1)S(1)} %mean_over_shards.1._.refs_0_), channel_id=1, source_target_pairs={{0,28},{1,29},{2,30},{3,31},{4,24},{5,25},{6,26},{7,27},{8,20},{9,... | collective-permute-start | bytes 98312 | tf_op jit(solution)/shard_map/ppermute | solution.py:334
  36.5 0.8 %collective-permute-start.19 = (bf16[64,256]{1,0:T(8,128)(2,1)S(1)}, bf16[64,256]{1,0:T(8,128)(2,1)S(1)}, u32[]{:S(2)}, u32[]{:S(2)}) collective-permute-start(bf16[64,256]{1,0:T(8,128)(2,1)S(1)} %mean_over_shards.1._.refs_0_), channel_id=1, source_target_pairs={{0,20},{1,21},{2,22},{3,23},{4,16},{5,17},{6,18},{7,19},{8,28},{9,... | collective-permute-start | bytes 98312 | tf_op jit(solution)/shard_map/ppermute | solution.py:334
  37.7 1.4 %collective-permute-done.20.refs_3_ = bf16[64,256]{1,0:T(8,128)(2,1)S(1)} collective-permute-done((bf16[64,256]{1,0:T(8,128)(2,1)S(1)}, bf16[64,256]{1,0:T(8,128)(2,1)S(1)}, u32[]{:S(2)}, u32[]{:S(2)}) %collective-permute-start.20) | collective-permute-done | bytes 32800 | tf_op jit(solution)/shard_map/ppermute | solution.py:334
  39.0 0.8 %collective-permute-done.19.refs_2_ = bf16[64,256]{1,0:T(8,128)(2,1)S(1)} collective-permute-done((bf16[64,256]{1,0:T(8,128)(2,1)S(1)}, bf16[64,256]{1,0:T(8,128)(2,1)S(1)}, u32[]{:S(2)}, u32[]{:S(2)}) %collective-permute-start.19) | collective-permute-done | bytes 32800 | tf_op jit(solution)/shard_map/ppermute | solution.py:334
  39.9 0.9 %collective-permute-done.18.refs_1_ = bf16[64,256]{1,0:T(8,128)(2,1)S(1)} collective-permute-done((bf16[64,256]{1,0:T(8,128)(2,1)S(1)}, bf16[64,256]{1,0:T(8,128)(2,1)S(1)}, u32[]{:S(2)}, u32[]{:S(2)}) %collective-permute-start.18) | collective-permute-done | bytes 32800 | tf_op jit(solution)/shard_map/ppermute | solution.py:334
  40.9 0.7 %blocks_of_own_core_in_place.1.refs_0_ = f32[256,512]{1,0:T(8,128)} custom-call(bf16[256,256]{1,0:T(8,128)(2,1)S(1)} %blocks_of_chips.1.blocks_ref), custom_call_target="tpu_custom_call" | custom-call | tf_op jit(solution)/shard_map/blocks_of_own_core_in_place/pallas_call | solution.py:33
  41.7 0.5 %collective-permute-done.21.blocks_ref = bf16[256,256]{1,0:T(8,128)(2,1)S(1)} collective-permute-done((bf16[256,256]{1,0:T(8,128)(2,1)S(1)}, bf16[256,256]{1,0:T(8,128)(2,1)S(1)}, u32[]{:S(2)}, u32[]{:S(2)}) %collective-permute-start.21) | collective-permute-done | bytes 131104 | tf_op jit(solution)/shard_map/ppermute | solution.py:322
  42.2 0.7 %blocks_of_sibling_core_in_place.1 = f32[256,512]{1,0:T(8,128)} custom-call(bf16[256,256]{1,0:T(8,128)(2,1)S(1)} %collective-permute-done.21.blocks_ref, f32[256,512]{1,0:T(8,128)} %blocks_of_own_core_in_place.1.refs_0_), custom_call_target="tpu_custom_call", output_to_operand_aliasing={{}: (1, {})} | custom-call | tf_op jit(solution)/shard_map/blocks_of_sibling_core_in_place/pallas_call | solution.py:33
  (27 shorter events, 3.9 us)
Async XLA Ops:
  0.6 9.7 %collective-permute-start.2 = (bf16[384,1024]{1,0:T(8,128)(2,1)}, bf16[384,1024]{1,0:T(8,128)(2,1)S(1)}, u32[]{:S(2)}, u32[]{:S(2)}) collective-permute-start(bf16[384,1024]{1,0:T(8,128)(2,1)} %bitcast.9), channel_id=1, source_target_pairs={{0,4},{4,0},{8,12},{12,8},{16,20},{20,16},{24,28},{28,24},{1,5},{5... | collective-permute-start | bytes 2359304 | tf_op jit(solution)/shard_map/ppermute | solution.py:322
  1.9 5.5 %collective-permute-start.1 = (bf16[32,512]{1,0:T(8,128)(2,1)S(1)}, bf16[32,512]{1,0:T(8,128)(2,1)S(1)}, u32[]{:S(2)}, u32[]{:S(2)}) collective-permute-start(bf16[32,512]{1,0:T(8,128)(2,1)S(1)} %own_part_of_weight.1), channel_id=1, source_target_pairs={{0,6},{1,7},{2,4},{3,5},{4,2},{5,3},{6,0},{7,1},{8,14},{9,15},{10,... | collective-permute-start | bytes 98312 | tf_op jit(solution)/shard_map/ppermute | solution.py:334
  5.7 9.0 %collective-permute-start = (bf16[256,512]{1,0:T(8,128)(2,1)}, bf16[256,512]{1,0:T(8,128)(2,1)S(1)}, u32[]{:S(2)}, u32[]{:S(2)}) collective-permute-start(bf16[256,512]{1,0:T(8,128)(2,1)} %refs_4_.1), channel_id=1, source_target_pairs={{0,5},{1,4},{2,7},{3,6},{4,3},{5,2},{6,1},{7,0},{8,13},{9,12},{10,... | collective-permute-start | bytes 786440 | tf_op jit(solution)/shard_map/ppermute | solution.py:334
  7.4 5.3 %collective-permute-start.5 = (bf16[32,512]{1,0:T(8,128)(2,1)S(1)}, bf16[32,512]{1,0:T(8,128)(2,1)S(1)}, u32[]{:S(2)}, u32[]{:S(2)}) collective-permute-start(bf16[32,512]{1,0:T(8,128)(2,1)S(1)} %collective-permute-done.1._.refs_0_), channel_id=1, source_target_pairs={{0,28},{1,29},{2,30},{3,31},{4,24},{5,25},{6,26},{7,27},{8,20},{9,... | collective-permute-start | bytes 98312 | tf_op jit(solution)/shard_map/ppermute | solution.py:334
  9.8 3.4 %collective-permute-start.4 = (bf16[32,512]{1,0:T(8,128)(2,1)S(1)}, bf16[32,512]{1,0:T(8,128)(2,1)S(1)}, u32[]{:S(2)}, u32[]{:S(2)}) collective-permute-start(bf16[32,512]{1,0:T(8,128)(2,1)S(1)} %collective-permute-done.1._.refs_0_), channel_id=1, source_target_pairs={{0,20},{1,21},{2,22},{3,23},{4,16},{5,17},{6,18},{7,19},{8,28},{9,... | collective-permute-start | bytes 98312 | tf_op jit(solution)/shard_map/ppermute | solution.py:334
  10.0 3.3 %collective-permute-start.3 = (bf16[32,512]{1,0:T(8,128)(2,1)S(1)}, bf16[32,512]{1,0:T(8,128)(2,1)S(1)}, u32[]{:S(2)}, u32[]{:S(2)}) collective-permute-start(bf16[32,512]{1,0:T(8,128)(2,1)S(1)} %collective-permute-done.1._.refs_0_), channel_id=1, source_target_pairs={{0,12},{1,13},{2,14},{3,15},{4,8},{5,9},{6,10},{7,11},{8,4},{9,5},... | collective-permute-start | bytes 98312 | tf_op jit(solution)/shard_map/ppermute | solution.py:334
  13.3 2.0 %collective-permute-start.7 = (bf16[128,512]{1,0:T(8,128)(2,1)S(1)}, bf16[128,512]{1,0:T(8,128)(2,1)S(1)}, u32[]{:S(2)}, u32[]{:S(2)}) collective-permute-start(bf16[128,512]{1,0:T(8,128)(2,1)S(1)} %parts_of_weight.1.refs_1_), channel_id=1, source_target_pairs={{0,4},{4,0},{8,12},{12,8},{16,20},{20,16},{24,28},{28,24},{1,5},{5... | collective-permute-start | bytes 393224 | tf_op jit(solution)/shard_map/ppermute | solution.py:322
  14.7 1.5 %collective-permute-start.6 = (bf16[256,512]{1,0:T(8,128)(2,1)S(1)}, bf16[256,512]{1,0:T(8,128)(2,1)S(1)}, u32[]{:S(2)}, u32[]{:S(2)}) collective-permute-start(bf16[256,512]{1,0:T(8,128)(2,1)S(1)} %collective-permute-done.refs_2_), channel_id=1, source_target_pairs={{0,4},{4,0},{8,12},{12,8},{16,20},{20,16},{24,28},{28,24},{1,5},{5... | collective-permute-start | bytes 786440 | tf_op jit(solution)/shard_map/ppermute | solution.py:322
  17.7 1.8 %collective-permute-start.8 = (bf16[384,512]{1,0:T(8,128)(2,1)S(1)}, bf16[384,512]{1,0:T(8,128)(2,1)S(1)}, u32[]{:S(2)}, u32[]{:S(2)}) collective-permute-start(bf16[384,512]{1,0:T(8,128)(2,1)S(1)} %get-tuple-element.55.grad_query_ref), channel_id=1, source_target_pairs={{0,4},{4,0},{8,12},{12,8},{16,20},{20,16},{24,28},{28,24},{1,5},{5... | collective-permute-start | bytes 1179656 | tf_op jit(solution)/shard_map/ppermute | solution.py:322
  20.0 5.7 %collective-permute-start.9 = (bf16[64,512]{1,0:T(8,128)(2,1)S(1)}, bf16[64,512]{1,0:T(8,128)(2,1)S(1)}, u32[]{:S(2)}, u32[]{:S(2)}) collective-permute-start(bf16[64,512]{1,0:T(8,128)(2,1)S(1)} %get-tuple-element.62), channel_id=1, source_target_pairs={{0,28},{1,29},{2,30},{3,31},{4,24},{5,25},{6,26},{7,27},{8,20},{9,... | collective-permute-start | bytes 196616 | tf_op jit(solution)/shard_map/ppermute | solution.py:334
  22.2 4.1 %collective-permute-start.10 = (bf16[64,512]{1,0:T(8,128)(2,1)S(1)}, bf16[64,512]{1,0:T(8,128)(2,1)S(1)}, u32[]{:S(2)}, u32[]{:S(2)}) collective-permute-start(bf16[64,512]{1,0:T(8,128)(2,1)S(1)} %get-tuple-element.63), channel_id=1, source_target_pairs={{0,20},{1,21},{2,22},{3,23},{4,16},{5,17},{6,18},{7,19},{8,28},{9,... | collective-permute-start | bytes 196616 | tf_op jit(solution)/shard_map/ppermute | solution.py:334
  22.7 4.0 %collective-permute-start.11 = (bf16[64,512]{1,0:T(8,128)(2,1)S(1)}, bf16[64,512]{1,0:T(8,128)(2,1)S(1)}, u32[]{:S(2)}, u32[]{:S(2)}) collective-permute-start(bf16[64,512]{1,0:T(8,128)(2,1)S(1)} %get-tuple-element.64), channel_id=1, source_target_pairs={{0,12},{1,13},{2,14},{3,15},{4,8},{5,9},{6,10},{7,11},{8,4},{9,5},... | collective-permute-start | bytes 196616 | tf_op jit(solution)/shard_map/ppermute | solution.py:334
  23.0 7.3 %collective-permute-start.12 = (bf16[64,512]{1,0:T(8,128)(2,1)S(1)}, bf16[64,512]{1,0:T(8,128)(2,1)S(1)}, u32[]{:S(2)}, u32[]{:S(2)}) collective-permute-start(bf16[64,512]{1,0:T(8,128)(2,1)S(1)} %get-tuple-element.67), channel_id=1, source_target_pairs={{0,28},{1,29},{2,30},{3,31},{4,24},{5,25},{6,26},{7,27},{8,20},{9,... | collective-permute-start | bytes 196616 | tf_op jit(solution)/shard_map/ppermute | solution.py:334
  25.4 5.4 %collective-permute-start.13 = (bf16[64,512]{1,0:T(8,128)(2,1)S(1)}, bf16[64,512]{1,0:T(8,128)(2,1)S(1)}, u32[]{:S(2)}, u32[]{:S(2)}) collective-permute-start(bf16[64,512]{1,0:T(8,128)(2,1)S(1)} %get-tuple-element.68), channel_id=1, source_target_pairs={{0,20},{1,21},{2,22},{3,23},{4,16},{5,17},{6,18},{7,19},{8,28},{9,... | collective-permute-start | bytes 196616 | tf_op jit(solution)/shard_map/ppermute | solution.py:334
  25.7 5.1 %collective-permute-start.14 = (bf16[64,512]{1,0:T(8,128)(2,1)S(1)}, bf16[64,512]{1,0:T(8,128)(2,1)S(1)}, u32[]{:S(2)}, u32[]{:S(2)}) collective-permute-start(bf16[64,512]{1,0:T(8,128)(2,1)S(1)} %get-tuple-element.69), channel_id=1, source_target_pairs={{0,12},{1,13},{2,14},{3,15},{4,8},{5,9},{6,10},{7,11},{8,4},{9,5},... | collective-permute-start | bytes 196616 | tf_op jit(solution)/shard_map/ppermute | solution.py:334
  26.8 6.7 %collective-permute-start.16 = (bf16[64,256]{1,0:T(8,128)(2,1)S(1)}, bf16[64,256]{1,0:T(8,128)(2,1)S(1)}, u32[]{:S(2)}, u32[]{:S(2)}) collective-permute-start(bf16[64,256]{1,0:T(8,128)(2,1)S(1)} %get-tuple-element.81), channel_id=1, source_target_pairs={{0,6},{1,7},{2,4},{3,5},{4,2},{5,3},{6,0},{7,1},{8,14},{9,15},{10,... | collective-permute-start | bytes 98312 | tf_op jit(solution)/shard_map/ppermute | solution.py:334
  28.4 5.2 %collective-permute-start.17 = (bf16[64,256]{1,0:T(8,128)(2,1)S(1)}, bf16[64,256]{1,0:T(8,128)(2,1)S(1)}, u32[]{:S(2)}, u32[]{:S(2)}) collective-permute-start(bf16[64,256]{1,0:T(8,128)(2,1)S(1)} %get-tuple-element.65._), channel_id=1, source_target_pairs={{0,7},{1,6},{2,5},{3,4},{4,3},{5,2},{6,1},{7,0},{8,15},{9,14},{10,... | collective-permute-start | bytes 98312 | tf_op jit(solution)/shard_map/ppermute | solution.py:334
  30.9 3.8 %collective-permute-start.15 = (bf16[64,256]{1,0:T(8,128)(2,1)S(1)}, bf16[64,256]{1,0:T(8,128)(2,1)S(1)}, u32[]{:S(2)}, u32[]{:S(2)}) collective-permute-start(bf16[64,256]{1,0:T(8,128)(2,1)S(1)} %get-tuple-element.70._), channel_id=1, source_target_pairs={{0,5},{1,4},{2,7},{3,6},{4,1},{5,0},{6,3},{7,2},{8,13},{9,12},{10,... | collective-permute-start | bytes 98312 | tf_op jit(solution)/shard_map/ppermute | solution.py:334
  34.7 4.4 %collective-permute-start.20 = (bf16[64,256]{1,0:T(8,128)(2,1)S(1)}, bf16[64,256]{1,0:T(8,128)(2,1)S(1)}, u32[]{:S(2)}, u32[]{:S(2)}) collective-permute-start(bf16[64,256]{1,0:T(8,128)(2,1)S(1)} %mean_over_shards.1._.refs_0_), channel_id=1, source_target_pairs={{0,28},{1,29},{2,30},{3,31},{4,24},{5,25},{6,26},{7,27},{8,20},{9,... | collective-permute-start | bytes 98312 | tf_op jit(solution)/shard_map/ppermute | solution.py:334
  36.5 3.3 %collective-permute-start.19 = (bf16[64,256]{1,0:T(8,128)(2,1)S(1)}, bf16[64,256]{1,0:T(8,128)(2,1)S(1)}, u32[]{:S(2)}, u32[]{:S(2)}) collective-permute-start(bf16[64,256]{1,0:T(8,128)(2,1)S(1)} %mean_over_shards.1._.refs_0_), channel_id=1, source_target_pairs={{0,20},{1,21},{2,22},{3,23},{4,16},{5,17},{6,18},{7,19},{8,28},{9,... | collective-permute-start | bytes 98312 | tf_op jit(solution)/shard_map/ppermute | solution.py:334
  37.3 3.4 %collective-permute-start.18 = (bf16[64,256]{1,0:T(8,128)(2,1)S(1)}, bf16[64,256]{1,0:T(8,128)(2,1)S(1)}, u32[]{:S(2)}, u32[]{:S(2)}) collective-permute-start(bf16[64,256]{1,0:T(8,128)(2,1)S(1)} %mean_over_shards.1._.refs_0_), channel_id=1, source_target_pairs={{0,12},{1,13},{2,14},{3,15},{4,8},{5,9},{6,10},{7,11},{8,4},{9,5},... | collective-permute-start | bytes 98312 | tf_op jit(solution)/shard_map/ppermute | solution.py:334
  40.7 1.4 %collective-permute-start.21 = (bf16[256,256]{1,0:T(8,128)(2,1)S(1)}, bf16[256,256]{1,0:T(8,128)(2,1)S(1)}, u32[]{:S(2)}, u32[]{:S(2)}) collective-permute-start(bf16[256,256]{1,0:T(8,128)(2,1)S(1)} %blocks_of_chips.1.blocks_ref), channel_id=1, source_target_pairs={{0,4},{4,0},{8,12},{12,8},{16,20},{20,16},{24,28},{28,24},{1,5},{5... | collective-permute-start | bytes 393224 | tf_op jit(solution)/shard_map/ppermute | solution.py:322

commit v17 on v15

--- a/solution.py
+++ b/solution.py
@@ -502,7 +502,7 @@
         def to_chip(block, k):
             return cross(block, dp_count, fsdp_count, k, alike)
 
-        order = (0,) + tuple(range(chips - 1, 0, -1))
+        order = (0, 1) + tuple(range(chips - 1, 1, -1))
 
         def summed_over_chips(terms, name, which, after):
             flips = sets[which]

time: 42.6 us -> 43.7 us (1.026)
  waiting for transfers between devices: 8.74 us -> 10 us
    ppermute x17, waiting for transfers between devices: 6.56 us -> 7.94 us  [cross(): return lax.ppermute(block, BOTH, pairs)]
  transfers between devices with their start and end apart: 22 -> 22, of which waited for: 13 -> 12; matrix products, arithmetic and copies ran while one was open for 0% -> 0% of each run, Pallas kernels for 16% -> 15%
where the time goes in v17:
time: 43.7 us; the launch traced here: 43.5 us
  starting transfers between devices  23.3 us (53%)
  waiting for transfers between devices  10 us (23%)
  Pallas kernels  9.39 us (21%)
  between operations  0.76 us (2%)
    ppermute x17, starting transfers between devices, cross(): return lax.ppermute(block, BOTH, pairs)  21.5 us
    pallas_call x15, Pallas kernels, call(): pl.pallas_call(kernel, out_shape=out_shape, in_specs=in_specs, out_specs=...  9.39 us
    ppermute x17, waiting for transfers between devices, cross(): return lax.ppermute(block, BOTH, pairs)  7.94 us
    ppermute x5, waiting for transfers between devices, flip(): return lax.ppermute(block, axis, [(i, i ^ bits) for i in range(count)])  2.1 us
    ppermute x5, starting transfers between devices, flip(): return lax.ppermute(block, axis, [(i, i ^ bits) for i in range(count)])  1.81 us
  transfers between devices with their start and end apart: 22, of which 12 were waited for; matrix products, arithmetic and copies ran while one was open for 0% of the time, Pallas kernels for 15%

profile of v17, /device:TPU:0, one launch (start us, length us, event | category | flops | bytes accessed | tf_op | source)
XLA Modules:
  0.0 43.5 jit_solution(5928756914306828318)
XLA Ops:
  0.6 0.5 %collective-permute-start.2 = (bf16[384,1024]{1,0:T(8,128)(2,1)}, bf16[384,1024]{1,0:T(8,128)(2,1)S(1)}, u32[]{:S(2)}, u32[]{:S(2)}) collective-permute-start(bf16[384,1024]{1,0:T(8,128)(2,1)} %bitcast.9), channel_id=1, source_target_pairs={{0,4},{4,0},{8,12},{12,8},{16,20},{20,16},{24,28},{28,24},{1,5},{5... | collective-permute-start | bytes 2359304 | tf_op jit(solution)/shard_map/ppermute | solution.py:322
  1.1 0.8 %own_part_of_weight.1 = bf16[32,512]{1,0:T(8,128)(2,1)S(1)} custom-call(bf16[256,512]{1,0:T(8,128)(2,1)} %refs_4_.1), custom_call_target="tpu_custom_call" | custom-call | tf_op jit(solution)/shard_map/own_part_of_weight/pallas_call | solution.py:33
  1.9 3.8 %collective-permute-start.1 = (bf16[32,512]{1,0:T(8,128)(2,1)S(1)}, bf16[32,512]{1,0:T(8,128)(2,1)S(1)}, u32[]{:S(2)}, u32[]{:S(2)}) collective-permute-start(bf16[32,512]{1,0:T(8,128)(2,1)S(1)} %own_part_of_weight.1), channel_id=1, source_target_pairs={{0,6},{1,7},{2,4},{3,5},{4,2},{5,3},{6,0},{7,1},{8,14},{9,15},{10,... | collective-permute-start | bytes 98312 | tf_op jit(solution)/shard_map/ppermute | solution.py:334
  5.7 1.2 %collective-permute-start = (bf16[256,512]{1,0:T(8,128)(2,1)}, bf16[256,512]{1,0:T(8,128)(2,1)S(1)}, u32[]{:S(2)}, u32[]{:S(2)}) collective-permute-start(bf16[256,512]{1,0:T(8,128)(2,1)} %refs_4_.1), channel_id=1, source_target_pairs={{0,5},{1,4},{2,7},{3,6},{4,3},{5,2},{6,1},{7,0},{8,13},{9,12},{10,... | collective-permute-start | bytes 786440 | tf_op jit(solution)/shard_map/ppermute | solution.py:334
  6.9 0.5 %collective-permute-done.1._.refs_0_ = bf16[32,512]{1,0:T(8,128)(2,1)S(1)} collective-permute-done((bf16[32,512]{1,0:T(8,128)(2,1)S(1)}, bf16[32,512]{1,0:T(8,128)(2,1)S(1)}, u32[]{:S(2)}, u32[]{:S(2)}) %collective-permute-start.1) | collective-permute-done | bytes 32800 | tf_op jit(solution)/shard_map/ppermute | solution.py:334
  7.4 2.4 %collective-permute-start.5 = (bf16[32,512]{1,0:T(8,128)(2,1)S(1)}, bf16[32,512]{1,0:T(8,128)(2,1)S(1)}, u32[]{:S(2)}, u32[]{:S(2)}) collective-permute-start(bf16[32,512]{1,0:T(8,128)(2,1)S(1)} %collective-permute-done.1._.refs_0_), channel_id=1, source_target_pairs={{0,28},{1,29},{2,30},{3,31},{4,24},{5,25},{6,26},{7,27},{8,20},{9,... | collective-permute-start | bytes 98312 | tf_op jit(solution)/shard_map/ppermute | solution.py:334
  10.4 2.3 %prepared_operands.1 = (bf16[384,1024]{1,0:T(8,128)(2,1)S(1)}, bf16[384,512]{1,0:T(8,128)(2,1)S(1)}, bf16[384,512]{1,0:T(8,128)(2,1)S(1)}, bf16[384,512]{1,0:T(8...) custom-call(bf16[32,512]{1,0:T(8,128)(2,1)S(1)} %collective-permute-, ...), custom_call_target="tpu_custom_call" | custom-call | flops 5000000000 | tf_op jit(solution)/shard_map/prepared_operands/pallas_call | solution.py:33
  12.7 0.5 %collective-permute-done.4.refs_2_ = bf16[32,512]{1,0:T(8,128)(2,1)S(1)} collective-permute-done((bf16[32,512]{1,0:T(8,128)(2,1)S(1)}, bf16[32,512]{1,0:T(8,128)(2,1)S(1)}, u32[]{:S(2)}, u32[]{:S(2)}) %collective-permute-start.4) | collective-permute-done | bytes 32800 | tf_op jit(solution)/shard_map/ppermute | solution.py:334
  13.3 0.8 %collective-permute-start.7 = (bf16[128,512]{1,0:T(8,128)(2,1)S(1)}, bf16[128,512]{1,0:T(8,128)(2,1)S(1)}, u32[]{:S(2)}, u32[]{:S(2)}) collective-permute-start(bf16[128,512]{1,0:T(8,128)(2,1)S(1)} %parts_of_weight.1.refs_1_), channel_id=1, source_target_pairs={{0,4},{4,0},{8,12},{12,8},{16,20},{20,16},{24,28},{28,24},{1,5},{5... | collective-permute-start | bytes 393224 | tf_op jit(solution)/shard_map/ppermute | solution.py:322
  14.1 0.6 %collective-permute-done.refs_2_ = bf16[256,512]{1,0:T(8,128)(2,1)S(1)} collective-permute-done((bf16[256,512]{1,0:T(8,128)(2,1)}, bf16[256,512]{1,0:T(8,128)(2,1)S(1)}, u32[]{:S(2)}, u32[]{:S(2)}) %collective-permute-start) | collective-permute-done | bytes 262176 | tf_op jit(solution)/shard_map/ppermute | solution.py:334
  14.7 0.6 %projection_by_held_rows.1.refs_2_ = f32[384,512]{1,0:T(8,128)S(1)} custom-call(bf16[256,512]{1,0:T(8,128)(2,1)S(1)} %get-tuple-element.48.refs_0_, bf16[128,512]{1,0:T(8,128)(2,1)S(1)} %parts_of_weight.1.refs_1_, bf16[256,512]{1,0:T(8,128)(2,1)S(1)} %collective-permute-done.refs_2_, bf16[384,1024]{1,0:T(8,128)(2,1)S(1)} %get-tuple-element.47.refs_3_.refs_1_.refs_2_), custom_call_target="tpu_custom_call" | custom-call | flops 301989888 | bytes 786432 | tf_op jit(solution)/shard_map/projection_by_held_rows/pallas_call | solution.py:33
  15.6 0.6 %collective-permute-done.6.refs_0_ = bf16[256,512]{1,0:T(8,128)(2,1)S(1)} collective-permute-done((bf16[256,512]{1,0:T(8,128)(2,1)S(1)}, bf16[256,512]{1,0:T(8,128)(2,1)S(1)}, u32[]{:S(2)}, u32[]{:S(2)}) %collective-permute-start.6) | collective-permute-done | bytes 262176 | tf_op jit(solution)/shard_map/ppermute | solution.py:322
  16.2 1.5 %attention_to_grad_query.1 = (bf16[384,512]{1,0:T(8,128)(2,1)S(1)}, bf16[384,512]{1,0:T(8,128)(2,1)S(1)}, f32[384,512]{1,0:T(8,128)S(1)}, bf16[384,512]{1,0:T(8,...) custom-call(bf16[256,512]{1,0:T(8,128)(2,1)S(1)} %collective-permute-done.6.refs_0_, ...), custom_call_target="tpu_custom_call" | custom-call | flops 603979776 | bytes 4718592 | tf_op jit(solution)/shard_map/attention_to_grad_query/pallas_call | solution.py:33
  17.9 0.5 %weight_gradient_of_own_events.1 = (f32[512,256]{1,0:T(8,128)S(1)}, bf16[512,384]{1,0:T(8,128)(2,1)S(1)}, f32[512,256]{1,0:T(8,128)S(1)}, bf16[512,384]{1,0:T(8,128)(2,1)S(1)}) custom-call(bf16[1024,768]{1,0:T(8,128)(2,1)S(1)} %get-tuple-element.56.events_ref, bf16[384,512]{1,0:T(8,128)(2,1)S(1)} %get-tuple-element.55.grad_query_ref), custom_call_target="tpu_custom_call" | custom-call | flops 201326592 | bytes 3145728 | tf_op jit(solution)/shard_map/weight_gradient_of_own_events/pallas_call | solution.py:33
  18.4 1.1 %collective-permute-done.8.grad_query_ref._ = bf16[384,512]{1,0:T(8,128)(2,1)S(1)} collective-permute-done((bf16[384,512]{1,0:T(8,128)(2,1)S(1)}, bf16[384,512]{1,0:T(8,128)(2,1)S(1)}, u32[]{:S(2)}, u32[]{:S(2)}) %collective-permute-start.8) | collective-permute-done | bytes 393248 | tf_op jit(solution)/shard_map/ppermute | solution.py:322
  20.0 1.3 %collective-permute-start.9 = (bf16[64,512]{1,0:T(8,128)(2,1)S(1)}, bf16[64,512]{1,0:T(8,128)(2,1)S(1)}, u32[]{:S(2)}, u32[]{:S(2)}) collective-permute-start(bf16[64,512]{1,0:T(8,128)(2,1)S(1)} %get-tuple-element.62), channel_id=1, source_target_pairs={{0,12},{1,13},{2,14},{3,15},{4,8},{5,9},{6,10},{7,11},{8,4},{9,5},... | collective-permute-start | bytes 196616 | tf_op jit(solution)/shard_map/ppermute | solution.py:334
  21.3 1.5 %collective-permute-start.10 = (bf16[64,512]{1,0:T(8,128)(2,1)S(1)}, bf16[64,512]{1,0:T(8,128)(2,1)S(1)}, u32[]{:S(2)}, u32[]{:S(2)}) collective-permute-start(bf16[64,512]{1,0:T(8,128)(2,1)S(1)} %get-tuple-element.63), channel_id=1, source_target_pairs={{0,28},{1,29},{2,30},{3,31},{4,24},{5,25},{6,26},{7,27},{8,20},{9,... | collective-permute-start | bytes 196616 | tf_op jit(solution)/shard_map/ppermute | solution.py:334
  23.0 1.4 %collective-permute-start.12 = (bf16[64,512]{1,0:T(8,128)(2,1)S(1)}, bf16[64,512]{1,0:T(8,128)(2,1)S(1)}, u32[]{:S(2)}, u32[]{:S(2)}) collective-permute-start(bf16[64,512]{1,0:T(8,128)(2,1)S(1)} %get-tuple-element.67), channel_id=1, source_target_pairs={{0,12},{1,13},{2,14},{3,15},{4,8},{5,9},{6,10},{7,11},{8,4},{9,5},... | collective-permute-start | bytes 196616 | tf_op jit(solution)/shard_map/ppermute | solution.py:334
  24.4 1.3 %collective-permute-start.13 = (bf16[64,512]{1,0:T(8,128)(2,1)S(1)}, bf16[64,512]{1,0:T(8,128)(2,1)S(1)}, u32[]{:S(2)}, u32[]{:S(2)}) collective-permute-start(bf16[64,512]{1,0:T(8,128)(2,1)S(1)} %get-tuple-element.68), channel_id=1, source_target_pairs={{0,28},{1,29},{2,30},{3,31},{4,24},{5,25},{6,26},{7,27},{8,20},{9,... | collective-permute-start | bytes 196616 | tf_op jit(solution)/shard_map/ppermute | solution.py:334
  25.7 0.5 %collective-permute-start.14 = (bf16[64,512]{1,0:T(8,128)(2,1)S(1)}, bf16[64,512]{1,0:T(8,128)(2,1)S(1)}, u32[]{:S(2)}, u32[]{:S(2)}) collective-permute-start(bf16[64,512]{1,0:T(8,128)(2,1)S(1)} %get-tuple-element.69), channel_id=1, source_target_pairs={{0,20},{1,21},{2,22},{3,23},{4,16},{5,17},{6,18},{7,19},{8,28},{9,... | collective-permute-start | bytes 196616 | tf_op jit(solution)/shard_map/ppermute | solution.py:334
  26.5 1.6 %collective-permute-done.11.refs_3_ = bf16[64,512]{1,0:T(8,128)(2,1)S(1)} collective-permute-done((bf16[64,512]{1,0:T(8,128)(2,1)S(1)}, bf16[64,512]{1,0:T(8,128)(2,1)S(1)}, u32[]{:S(2)}, u32[]{:S(2)}) %collective-permute-start.11) | collective-permute-done | bytes 65568 | tf_op jit(solution)/shard_map/ppermute | solution.py:334
  28.2 3.6 %collective-permute-start.16 = (bf16[64,256]{1,0:T(8,128)(2,1)S(1)}, bf16[64,256]{1,0:T(8,128)(2,1)S(1)}, u32[]{:S(2)}, u32[]{:S(2)}) collective-permute-start(bf16[64,256]{1,0:T(8,128)(2,1)S(1)} %get-tuple-element.81), channel_id=1, source_target_pairs={{0,7},{1,6},{2,5},{3,4},{4,3},{5,2},{6,1},{7,0},{8,15},{9,14},{10,... | collective-permute-start | bytes 98312 | tf_op jit(solution)/shard_map/ppermute | solution.py:334
  31.9 0.6 %collective-permute-start.15 = (bf16[64,256]{1,0:T(8,128)(2,1)S(1)}, bf16[64,256]{1,0:T(8,128)(2,1)S(1)}, u32[]{:S(2)}, u32[]{:S(2)}) collective-permute-start(bf16[64,256]{1,0:T(8,128)(2,1)S(1)} %get-tuple-element.70._), channel_id=1, source_target_pairs={{0,5},{1,4},{2,7},{3,6},{4,1},{5,0},{6,3},{7,2},{8,13},{9,12},{10,... | collective-permute-start | bytes 98312 | tf_op jit(solution)/shard_map/ppermute | solution.py:334
  32.5 1.4 %key_value_gate_gradients.1 = (bf16[384,512]{1,0:T(8,128)(2,1)}, bf16[384,512]{1,0:T(8,128)(2,1)}, bf16[384,512]{1,0:T(8,128)(2,1)}) custom-call(bf16[64,256]{1,0:T(8,128)(2,1)S(1)} %get-tuple-element.70._, bf16[384,512]{1,0:T(8,128)(2,1)S(1)} %get-tuple-element.71.query_ref, f32[384,512]{1,0:T(8,128)S(1)} %get-tuple-element.72.normed_ref, ...), custom_call_target="tpu_custom_call" | custom-call | flops 100663296 | bytes 2359296 | tf_op jit(solution)/shard_map/key_value_gate_gradients/pallas_call | solution.py:33
  33.9 2.2 %collective-permute-done.17.refs_3_ = bf16[64,256]{1,0:T(8,128)(2,1)S(1)} collective-permute-done((bf16[64,256]{1,0:T(8,128)(2,1)S(1)}, bf16[64,256]{1,0:T(8,128)(2,1)S(1)}, u32[]{:S(2)}, u32[]{:S(2)}) %collective-permute-start.17) | collective-permute-done | bytes 32800 | tf_op jit(solution)/shard_map/ppermute | solution.py:334
  36.2 0.6 %collective-permute-start.20 = (bf16[64,256]{1,0:T(8,128)(2,1)S(1)}, bf16[64,256]{1,0:T(8,128)(2,1)S(1)}, u32[]{:S(2)}, u32[]{:S(2)}) collective-permute-start(bf16[64,256]{1,0:T(8,128)(2,1)S(1)} %mean_over_shards.1._.refs_0_), channel_id=1, source_target_pairs={{0,28},{1,29},{2,30},{3,31},{4,24},{5,25},{6,26},{7,27},{8,20},{9,... | collective-permute-start | bytes 98312 | tf_op jit(solution)/shard_map/ppermute | solution.py:334
  36.8 1.2 %collective-permute-start.19 = (bf16[64,256]{1,0:T(8,128)(2,1)S(1)}, bf16[64,256]{1,0:T(8,128)(2,1)S(1)}, u32[]{:S(2)}, u32[]{:S(2)}) collective-permute-start(bf16[64,256]{1,0:T(8,128)(2,1)S(1)} %mean_over_shards.1._.refs_0_), channel_id=1, source_target_pairs={{0,20},{1,21},{2,22},{3,23},{4,16},{5,17},{6,18},{7,19},{8,28},{9,... | collective-permute-start | bytes 98312 | tf_op jit(solution)/shard_map/ppermute | solution.py:334
  38.0 1.3 %collective-permute-start.18 = (bf16[64,256]{1,0:T(8,128)(2,1)S(1)}, bf16[64,256]{1,0:T(8,128)(2,1)S(1)}, u32[]{:S(2)}, u32[]{:S(2)}) collective-permute-start(bf16[64,256]{1,0:T(8,128)(2,1)S(1)} %mean_over_shards.1._.refs_0_), channel_id=1, source_target_pairs={{0,12},{1,13},{2,14},{3,15},{4,8},{5,9},{6,10},{7,11},{8,4},{9,5},... | collective-permute-start | bytes 98312 | tf_op jit(solution)/shard_map/ppermute | solution.py:334
  39.3 1.2 %collective-permute-done.20.refs_3_ = bf16[64,256]{1,0:T(8,128)(2,1)S(1)} collective-permute-done((bf16[64,256]{1,0:T(8,128)(2,1)S(1)}, bf16[64,256]{1,0:T(8,128)(2,1)S(1)}, u32[]{:S(2)}, u32[]{:S(2)}) %collective-permute-start.20) | collective-permute-done | bytes 32800 | tf_op jit(solution)/shard_map/ppermute | solution.py:334
  40.5 0.8 %collective-permute-done.18.refs_1_ = bf16[64,256]{1,0:T(8,128)(2,1)S(1)} collective-permute-done((bf16[64,256]{1,0:T(8,128)(2,1)S(1)}, bf16[64,256]{1,0:T(8,128)(2,1)S(1)}, u32[]{:S(2)}, u32[]{:S(2)}) %collective-permute-start.18) | collective-permute-done | bytes 32800 | tf_op jit(solution)/shard_map/ppermute | solution.py:334
  41.6 0.7 %blocks_of_own_core_in_place.1.refs_0_ = f32[256,512]{1,0:T(8,128)} custom-call(bf16[256,256]{1,0:T(8,128)(2,1)S(1)} %blocks_of_chips.1.blocks_ref), custom_call_target="tpu_custom_call" | custom-call | tf_op jit(solution)/shard_map/blocks_of_own_core_in_place/pallas_call | solution.py:33
  42.7 0.7 %blocks_of_sibling_core_in_place.1 = f32[256,512]{1,0:T(8,128)} custom-call(bf16[256,256]{1,0:T(8,128)(2,1)S(1)} %collective-permute-done.21.blocks_ref, f32[256,512]{1,0:T(8,128)} %blocks_of_own_core_in_place.1.refs_0_), custom_call_target="tpu_custom_call", output_to_operand_aliasing={{}: (1, {})} | custom-call | tf_op jit(solution)/shard_map/blocks_of_sibling_core_in_place/pallas_call | solution.py:33
  (27 shorter events, 3.0 us)
Async XLA Ops:
  0.6 9.7 %collective-permute-start.2 = (bf16[384,1024]{1,0:T(8,128)(2,1)}, bf16[384,1024]{1,0:T(8,128)(2,1)S(1)}, u32[]{:S(2)}, u32[]{:S(2)}) collective-permute-start(bf16[384,1024]{1,0:T(8,128)(2,1)} %bitcast.9), channel_id=1, source_target_pairs={{0,4},{4,0},{8,12},{12,8},{16,20},{20,16},{24,28},{28,24},{1,5},{5... | collective-permute-start | bytes 2359304 | tf_op jit(solution)/shard_map/ppermute | solution.py:322
  1.9 5.5 %collective-permute-start.1 = (bf16[32,512]{1,0:T(8,128)(2,1)S(1)}, bf16[32,512]{1,0:T(8,128)(2,1)S(1)}, u32[]{:S(2)}, u32[]{:S(2)}) collective-permute-start(bf16[32,512]{1,0:T(8,128)(2,1)S(1)} %own_part_of_weight.1), channel_id=1, source_target_pairs={{0,6},{1,7},{2,4},{3,5},{4,2},{5,3},{6,0},{7,1},{8,14},{9,15},{10,... | collective-permute-start | bytes 98312 | tf_op jit(solution)/shard_map/ppermute | solution.py:334
  5.7 9.0 %collective-permute-start = (bf16[256,512]{1,0:T(8,128)(2,1)}, bf16[256,512]{1,0:T(8,128)(2,1)S(1)}, u32[]{:S(2)}, u32[]{:S(2)}) collective-permute-start(bf16[256,512]{1,0:T(8,128)(2,1)} %refs_4_.1), channel_id=1, source_target_pairs={{0,5},{1,4},{2,7},{3,6},{4,3},{5,2},{6,1},{7,0},{8,13},{9,12},{10,... | collective-permute-start | bytes 786440 | tf_op jit(solution)/shard_map/ppermute | solution.py:334
  7.4 5.3 %collective-permute-start.5 = (bf16[32,512]{1,0:T(8,128)(2,1)S(1)}, bf16[32,512]{1,0:T(8,128)(2,1)S(1)}, u32[]{:S(2)}, u32[]{:S(2)}) collective-permute-start(bf16[32,512]{1,0:T(8,128)(2,1)S(1)} %collective-permute-done.1._.refs_0_), channel_id=1, source_target_pairs={{0,28},{1,29},{2,30},{3,31},{4,24},{5,25},{6,26},{7,27},{8,20},{9,... | collective-permute-start | bytes 98312 | tf_op jit(solution)/shard_map/ppermute | solution.py:334
  9.8 3.4 %collective-permute-start.4 = (bf16[32,512]{1,0:T(8,128)(2,1)S(1)}, bf16[32,512]{1,0:T(8,128)(2,1)S(1)}, u32[]{:S(2)}, u32[]{:S(2)}) collective-permute-start(bf16[32,512]{1,0:T(8,128)(2,1)S(1)} %collective-permute-done.1._.refs_0_), channel_id=1, source_target_pairs={{0,20},{1,21},{2,22},{3,23},{4,16},{5,17},{6,18},{7,19},{8,28},{9,... | collective-permute-start | bytes 98312 | tf_op jit(solution)/shard_map/ppermute | solution.py:334
  10.0 3.3 %collective-permute-start.3 = (bf16[32,512]{1,0:T(8,128)(2,1)S(1)}, bf16[32,512]{1,0:T(8,128)(2,1)S(1)}, u32[]{:S(2)}, u32[]{:S(2)}) collective-permute-start(bf16[32,512]{1,0:T(8,128)(2,1)S(1)} %collective-permute-done.1._.refs_0_), channel_id=1, source_target_pairs={{0,12},{1,13},{2,14},{3,15},{4,8},{5,9},{6,10},{7,11},{8,4},{9,5},... | collective-permute-start | bytes 98312 | tf_op jit(solution)/shard_map/ppermute | solution.py:334
  13.3 2.0 %collective-permute-start.7 = (bf16[128,512]{1,0:T(8,128)(2,1)S(1)}, bf16[128,512]{1,0:T(8,128)(2,1)S(1)}, u32[]{:S(2)}, u32[]{:S(2)}) collective-permute-start(bf16[128,512]{1,0:T(8,128)(2,1)S(1)} %parts_of_weight.1.refs_1_), channel_id=1, source_target_pairs={{0,4},{4,0},{8,12},{12,8},{16,20},{20,16},{24,28},{28,24},{1,5},{5... | collective-permute-start | bytes 393224 | tf_op jit(solution)/shard_map/ppermute | solution.py:322
  14.7 1.5 %collective-permute-start.6 = (bf16[256,512]{1,0:T(8,128)(2,1)S(1)}, bf16[256,512]{1,0:T(8,128)(2,1)S(1)}, u32[]{:S(2)}, u32[]{:S(2)}) collective-permute-start(bf16[256,512]{1,0:T(8,128)(2,1)S(1)} %collective-permute-done.refs_2_), channel_id=1, source_target_pairs={{0,4},{4,0},{8,12},{12,8},{16,20},{20,16},{24,28},{28,24},{1,5},{5... | collective-permute-start | bytes 786440 | tf_op jit(solution)/shard_map/ppermute | solution.py:322
  17.7 1.8 %collective-permute-start.8 = (bf16[384,512]{1,0:T(8,128)(2,1)S(1)}, bf16[384,512]{1,0:T(8,128)(2,1)S(1)}, u32[]{:S(2)}, u32[]{:S(2)}) collective-permute-start(bf16[384,512]{1,0:T(8,128)(2,1)S(1)} %get-tuple-element.55.grad_query_ref), channel_id=1, source_target_pairs={{0,4},{4,0},{8,12},{12,8},{16,20},{20,16},{24,28},{28,24},{1,5},{5... | collective-permute-start | bytes 1179656 | tf_op jit(solution)/shard_map/ppermute | solution.py:322
  20.0 5.8 %collective-permute-start.9 = (bf16[64,512]{1,0:T(8,128)(2,1)S(1)}, bf16[64,512]{1,0:T(8,128)(2,1)S(1)}, u32[]{:S(2)}, u32[]{:S(2)}) collective-permute-start(bf16[64,512]{1,0:T(8,128)(2,1)S(1)} %get-tuple-element.62), channel_id=1, source_target_pairs={{0,12},{1,13},{2,14},{3,15},{4,8},{5,9},{6,10},{7,11},{8,4},{9,5},... | collective-permute-start | bytes 196616 | tf_op jit(solution)/shard_map/ppermute | solution.py:334
  21.3 5.3 %collective-permute-start.10 = (bf16[64,512]{1,0:T(8,128)(2,1)S(1)}, bf16[64,512]{1,0:T(8,128)(2,1)S(1)}, u32[]{:S(2)}, u32[]{:S(2)}) collective-permute-start(bf16[64,512]{1,0:T(8,128)(2,1)S(1)} %get-tuple-element.63), channel_id=1, source_target_pairs={{0,28},{1,29},{2,30},{3,31},{4,24},{5,25},{6,26},{7,27},{8,20},{9,... | collective-permute-start | bytes 196616 | tf_op jit(solution)/shard_map/ppermute | solution.py:334
  22.7 5.4 %collective-permute-start.11 = (bf16[64,512]{1,0:T(8,128)(2,1)S(1)}, bf16[64,512]{1,0:T(8,128)(2,1)S(1)}, u32[]{:S(2)}, u32[]{:S(2)}) collective-permute-start(bf16[64,512]{1,0:T(8,128)(2,1)S(1)} %get-tuple-element.64), channel_id=1, source_target_pairs={{0,20},{1,21},{2,22},{3,23},{4,16},{5,17},{6,18},{7,19},{8,28},{9,... | collective-permute-start | bytes 196616 | tf_op jit(solution)/shard_map/ppermute | solution.py:334
  23.0 8.8 %collective-permute-start.12 = (bf16[64,512]{1,0:T(8,128)(2,1)S(1)}, bf16[64,512]{1,0:T(8,128)(2,1)S(1)}, u32[]{:S(2)}, u32[]{:S(2)}) collective-permute-start(bf16[64,512]{1,0:T(8,128)(2,1)S(1)} %get-tuple-element.67), channel_id=1, source_target_pairs={{0,12},{1,13},{2,14},{3,15},{4,8},{5,9},{6,10},{7,11},{8,4},{9,5},... | collective-permute-start | bytes 196616 | tf_op jit(solution)/shard_map/ppermute | solution.py:334
  24.4 7.4 %collective-permute-start.13 = (bf16[64,512]{1,0:T(8,128)(2,1)S(1)}, bf16[64,512]{1,0:T(8,128)(2,1)S(1)}, u32[]{:S(2)}, u32[]{:S(2)}) collective-permute-start(bf16[64,512]{1,0:T(8,128)(2,1)S(1)} %get-tuple-element.68), channel_id=1, source_target_pairs={{0,28},{1,29},{2,30},{3,31},{4,24},{5,25},{6,26},{7,27},{8,20},{9,... | collective-permute-start | bytes 196616 | tf_op jit(solution)/shard_map/ppermute | solution.py:334
  25.7 6.1 %collective-permute-start.14 = (bf16[64,512]{1,0:T(8,128)(2,1)S(1)}, bf16[64,512]{1,0:T(8,128)(2,1)S(1)}, u32[]{:S(2)}, u32[]{:S(2)}) collective-permute-start(bf16[64,512]{1,0:T(8,128)(2,1)S(1)} %get-tuple-element.69), channel_id=1, source_target_pairs={{0,20},{1,21},{2,22},{3,23},{4,16},{5,17},{6,18},{7,19},{8,28},{9,... | collective-permute-start | bytes 196616 | tf_op jit(solution)/shard_map/ppermute | solution.py:334
  28.2 5.8 %collective-permute-start.16 = (bf16[64,256]{1,0:T(8,128)(2,1)S(1)}, bf16[64,256]{1,0:T(8,128)(2,1)S(1)}, u32[]{:S(2)}, u32[]{:S(2)}) collective-permute-start(bf16[64,256]{1,0:T(8,128)(2,1)S(1)} %get-tuple-element.81), channel_id=1, source_target_pairs={{0,7},{1,6},{2,5},{3,4},{4,3},{5,2},{6,1},{7,0},{8,15},{9,14},{10,... | collective-permute-start | bytes 98312 | tf_op jit(solution)/shard_map/ppermute | solution.py:334
  31.8 4.3 %collective-permute-start.17 = (bf16[64,256]{1,0:T(8,128)(2,1)S(1)}, bf16[64,256]{1,0:T(8,128)(2,1)S(1)}, u32[]{:S(2)}, u32[]{:S(2)}) collective-permute-start(bf16[64,256]{1,0:T(8,128)(2,1)S(1)} %get-tuple-element.65._), channel_id=1, source_target_pairs={{0,6},{1,7},{2,4},{3,5},{4,2},{5,3},{6,0},{7,1},{8,14},{9,15},{10,... | collective-permute-start | bytes 98312 | tf_op jit(solution)/shard_map/ppermute | solution.py:334
  31.9 4.3 %collective-permute-start.15 = (bf16[64,256]{1,0:T(8,128)(2,1)S(1)}, bf16[64,256]{1,0:T(8,128)(2,1)S(1)}, u32[]{:S(2)}, u32[]{:S(2)}) collective-permute-start(bf16[64,256]{1,0:T(8,128)(2,1)S(1)} %get-tuple-element.70._), channel_id=1, source_target_pairs={{0,5},{1,4},{2,7},{3,6},{4,1},{5,0},{6,3},{7,2},{8,13},{9,12},{10,... | collective-permute-start | bytes 98312 | tf_op jit(solution)/shard_map/ppermute | solution.py:334
  36.2 4.3 %collective-permute-start.20 = (bf16[64,256]{1,0:T(8,128)(2,1)S(1)}, bf16[64,256]{1,0:T(8,128)(2,1)S(1)}, u32[]{:S(2)}, u32[]{:S(2)}) collective-permute-start(bf16[64,256]{1,0:T(8,128)(2,1)S(1)} %mean_over_shards.1._.refs_0_), channel_id=1, source_target_pairs={{0,28},{1,29},{2,30},{3,31},{4,24},{5,25},{6,26},{7,27},{8,20},{9,... | collective-permute-start | bytes 98312 | tf_op jit(solution)/shard_map/ppermute | solution.py:334
  36.8 3.7 %collective-permute-start.19 = (bf16[64,256]{1,0:T(8,128)(2,1)S(1)}, bf16[64,256]{1,0:T(8,128)(2,1)S(1)}, u32[]{:S(2)}, u32[]{:S(2)}) collective-permute-start(bf16[64,256]{1,0:T(8,128)(2,1)S(1)} %mean_over_shards.1._.refs_0_), channel_id=1, source_target_pairs={{0,20},{1,21},{2,22},{3,23},{4,16},{5,17},{6,18},{7,19},{8,28},{9,... | collective-permute-start | bytes 98312 | tf_op jit(solution)/shard_map/ppermute | solution.py:334
  38.0 3.3 %collective-permute-start.18 = (bf16[64,256]{1,0:T(8,128)(2,1)S(1)}, bf16[64,256]{1,0:T(8,128)(2,1)S(1)}, u32[]{:S(2)}, u32[]{:S(2)}) collective-permute-start(bf16[64,256]{1,0:T(8,128)(2,1)S(1)} %mean_over_shards.1._.refs_0_), channel_id=1, source_target_pairs={{0,12},{1,13},{2,14},{3,15},{4,8},{5,9},{6,10},{7,11},{8,4},{9,5},... | collective-permute-start | bytes 98312 | tf_op jit(solution)/shard_map/ppermute | solution.py:334
  41.3 1.4 %collective-permute-start.21 = (bf16[256,256]{1,0:T(8,128)(2,1)S(1)}, bf16[256,256]{1,0:T(8,128)(2,1)S(1)}, u32[]{:S(2)}, u32[]{:S(2)}) collective-permute-start(bf16[256,256]{1,0:T(8,128)(2,1)S(1)} %blocks_of_chips.1.blocks_ref), channel_id=1, source_target_pairs={{0,4},{4,0},{8,12},{12,8},{16,20},{20,16},{24,28},{28,24},{1,5},{5... | collective-permute-start | bytes 393224 | tf_op jit(solution)/shard_map/ppermute | solution.py:322
